TPU v7x, 256 devices: a whole 4x4x8 slice. The times are simulated.
256 devices in a mesh: gx: 4 (over x), gy: 8 (over z), gz: 8 (over y, core).
Axes of the slice: x: 4, y: 4, z: 8, core: 2. Of those that a mesh axis runs over, the one named last changes fastest.
Arguments:
- right_side: float32 [64, 128, 1024], P('gx', 'gy', 'gz'), may hold values from -8 to 8
- classes: int32 [64, 128, 1024], P('gx', 'gy', 'gz'), may hold values from 0 to 15
- table: float32 [16], replicated, may hold values from 0.001 to 0.5
Outputs:
- solution_field: float32 [64, 128, 1024], P('gx', 'gy', 'gz')
- residual: float32 [64, 128, 1024], P('gx', 'gy', 'gz')
All inputs are finite; a program needn't handle non-finite values.
Results may differ from a plain program's by a relative error of at most 0.0003.
Values sent between devices are 32-bit elements; how exact they have to be, the bound alone decides.
No kernel may reach another device: no remote copies, remote signals or barrier semaphores. Data moves between devices by JAX's collectives and lax.ppermute only.
A program may use at most 64 MiB of HBM per device.

v0:
```python
import jax
import jax.numpy as jnp
from jax import lax
from jax.sharding import PartitionSpec as P

CLASSES = 16
ITERS = 3
COARSE_SWEEPS = 6


OMEGA = 0.8


def with_halo(block, sides, width):
    for axis, dim in sides:
        count = lax.axis_size(axis)
        forward = [(i, i + 1) for i in range(count - 1)]
        backward = [(target, source) for source, target in forward]
        low = lax.ppermute(
            lax.slice_in_dim(block, block.shape[dim] - width, None, axis=dim), axis, forward
        )
        high = lax.ppermute(lax.slice_in_dim(block, 0, width, axis=dim), axis, backward)
        block = jnp.concatenate([low, block, high], axis=dim)
    return block


def lookup(classes, table):
    kap = jnp.zeros(classes.shape, jnp.float32)
    for index in range(CLASSES):
        kap = kap + jnp.where(classes == index, table[index], jnp.float32(0.0))
    return kap


def restrict(v):
    a, b, c = v.shape
    return jnp.mean(v.reshape(a // 2, 2, b // 2, 2, c // 2, 2), axis=(1, 3, 5))


def prolong(v):
    return jnp.repeat(jnp.repeat(jnp.repeat(v, 2, axis=0), 2, axis=1), 2, axis=2)


def neighbours(padded):
    beside = padded[2:, 1:-1, 1:-1] + padded[:-2, 1:-1, 1:-1]
    beside = beside + padded[1:-1, 2:, 1:-1] + padded[1:-1, :-2, 1:-1]
    beside = beside + padded[1:-1, 1:-1, 2:] + padded[1:-1, 1:-1, :-2]
    return beside


def operate(u, padded, kap, scale):
    return (kap + 6.0 * scale) * u - scale * neighbours(padded)


def fine_halo(u):
    return with_halo(u, (("gx", 0), ("gy", 1), ("gz", 2)), 1)


def mid_halo(u):
    return with_halo(u, (("gx", 0), ("gy", 1), ("gz", 2)), 1)


def coarse_halo(u):
    return with_halo(u, (("gx", 0), ("gy", 1), ("gz", 2)), 1)


def alignment(residual, precond):
    return lax.psum(jnp.sum(residual * precond), ("gx", "gy", "gz"))


def coarse_solve(r2, kap2, diag2):
    x2 = OMEGA * r2 / diag2
    for sweep in range(COARSE_SWEEPS - 1):
        x2 = x2 + OMEGA * (r2 - operate(x2, coarse_halo(x2), kap2, 0.0625)) / diag2
    return x2


def vcycle(r, kaps, diags):
    x0 = OMEGA * r / diags[0]
    first_cycle = fine_halo(x0)
    r1 = restrict(r - operate(x0, first_cycle, kaps[0], 1.0))
    x1 = OMEGA * r1 / diags[1]
    r2 = restrict(r1 - operate(x1, mid_halo(x1), kaps[1], 0.25))
    x2 = coarse_solve(r2, kaps[2], diags[2])
    x1 = x1 + prolong(x2)
    x1 = x1 + OMEGA * (r1 - operate(x1, mid_halo(x1), kaps[1], 0.25)) / diags[1]
    x0 = x0 + prolong(x1)
    padded = fine_halo(x0)
    return x0 + OMEGA * (r - operate(x0, padded, kaps[0], 1.0)) / diags[0]


def local(right_side, classes, table):
    kap0 = lookup(classes, table)
    kap1 = restrict(kap0)
    kap2 = restrict(kap1)
    kaps = (kap0, kap1, kap2)
    diags = (kap0 + 6.0, kap1 + 6.0 * 0.25, kap2 + 6.0 * 0.0625)
    solution_field = jnp.zeros_like(right_side)
    residual = right_side
    precond = vcycle(residual, kaps, diags)
    direction = precond
    rz_now = alignment(residual, precond)
    for step in range(ITERS):
        image = operate(direction, fine_halo(direction), kap0, 1.0)
        curve = lax.psum(jnp.sum(direction * image), ("gx", "gy", "gz"))
        alpha = rz_now / curve
        solution_field = solution_field + alpha * direction
        residual = residual - alpha * image
        if step + 1 < ITERS:
            precond = vcycle(residual, kaps, diags)
            rz_next = alignment(residual, precond)
            direction = precond + rz_next / rz_now * direction
            rz_now = rz_next
    return (solution_field, residual)


def solution(mesh):
    in_specs = (P("gx", "gy", "gz"), P("gx", "gy", "gz"), P())
    out_specs = (P("gx", "gy", "gz"), P("gx", "gy", "gz"))
    return jax.shard_map(local, mesh=mesh, in_specs=in_specs, out_specs=out_specs, check_vma=False)
```

profile of v0, /device:TPU:1, one launch (start us, length us, event | category | flops | bytes accessed | tf_op | source)
XLA Modules:
  0.0 1197.0 jit_solution(4084699347328201193)
XLA Ops:
  2.6 11.1 multiply_divide_fusion.2
  38.8 9.7 reshape.84
  52.7 9.7 reshape.83
  135.7 7.1 collective-permute-start.23
  159.0 7.1 collective-permute-start.29
  182.4 7.1 collective-permute-start.35
  205.7 7.1 collective-permute-start.41
  229.4 7.1 collective-permute-start.47
  254.4 7.1 collective-permute-start.53
  280.4 7.0 collective-permute-start.59
  291.0 75.2 %all-reduce = (f32[]{:T(128)}, f32[]{:T(128)}) all-reduce(f32[]{:T(128)} %get-tuple-element.11, f32[]{:T(128)} %get-tuple-element.10), channel_id=1, replica_groups=mesh['gx'=4,'gy'=8,'gz'=8] {'gx','gy','gz'}, use_global_device_ids=true, to_apply=%region_5.6 | all-reduce | flops 2 | bytes 16 | tf_op jit(solution)/shard_map/psum | solution.py:67
  392.0 9.7 reshape.92
  422.7 5.7 collective-permute-start.71
  450.3 6.9 collective-permute-start.77
  474.2 7.1 collective-permute-start.83
  497.6 7.1 collective-permute-start.89
  520.9 7.1 collective-permute-start.95
  544.2 7.1 collective-permute-start.101
  568.0 7.1 collective-permute-start.107
  593.0 7.1 collective-permute-start.113
  603.8 73.8 %psum.44 = f32[]{:T(128)} all-reduce(f32[]{:T(128)} %get-tuple-element.22), channel_id=1, replica_groups=mesh['gx'=4,'gy'=8,'gz'=8] {'gx','gy','gz'}, use_global_device_ids=true, to_apply=%region_11.12 | all-reduce | flops 1 | bytes 8 | tf_op jit(solution)/shard_map/psum | solution.py:67
  703.9 76.8 %psum.45 = f32[]{:T(128)} all-reduce(f32[]{:T(128)} %get-tuple-element.20), channel_id=1, replica_groups=mesh['gx'=4,'gy'=8,'gz'=8] {'gx','gy','gz'}, use_global_device_ids=true, to_apply=%region_13.14 | all-reduce | flops 1 | bytes 8 | tf_op jit(solution)/shard_map/psum | solution.py:104
  805.3 9.7 reshape.100
  864.7 6.9 collective-permute-start.137
  888.6 7.1 collective-permute-start.143
  912.0 7.1 collective-permute-start.149
  935.3 7.1 collective-permute-start.155
  958.6 7.1 collective-permute-start.161
  982.4 7.1 collective-permute-start.167
  1007.4 7.1 collective-permute-start.173
  1018.2 73.8 %psum.46 = f32[]{:T(128)} all-reduce(f32[]{:T(128)} %get-tuple-element.16), channel_id=1, replica_groups=mesh['gx'=4,'gy'=8,'gz'=8] {'gx','gy','gz'}, use_global_device_ids=true, to_apply=%region_17.18 | all-reduce | flops 1 | bytes 8 | tf_op jit(solution)/shard_map/psum | solution.py:67
  1118.3 76.6 %psum.47 = f32[]{:T(128)} all-reduce(f32[]{:T(128)} %get-tuple-element.14), channel_id=1, replica_groups=mesh['gx'=4,'gy'=8,'gz'=8] {'gx','gy','gz'}, use_global_device_ids=true, to_apply=%region_19.20 | all-reduce | flops 1 | bytes 8 | tf_op jit(solution)/shard_map/psum | solution.py:104
  (556 shorter events, 606.6 us)
Async XLA Ops:
  30.4 22.1 %collective-permute-start.4 = (f32[18,18,1]{2,1,0:T(8,128)S(1)}, f32[18,18,1]{2,1,0:T(8,128)S(1)}, u32[]{:S(2)}, u32[]{:S(2)}) collective-permute-start(f32[18,18,1]{2,1,0:T(8,128)S(1)} %get-tuple-element.45), channel_id=1, source_target_pairs={{1,0},{2,1},{3,2},{4,3},{5,4},{6,5},{7,6},{9,8},{10,9},{11,10},{12... | collective-permute-start | bytes 3896 | tf_op jit(solution)/shard_map/ppermute | solution.py:22
  35.6 16.9 %collective-permute-start.5 = (f32[18,18,1]{2,1,0:T(8,128)S(1)}, f32[18,18,1]{2,1,0:T(8,128)S(1)}, u32[]{:S(2)}, u32[]{:S(2)}) collective-permute-start(f32[18,18,1]{2,1,0:T(8,128)S(1)} %get-tuple-element.46), channel_id=1, source_target_pairs={{0,1},{1,2},{2,3},{3,4},{4,5},{5,6},{6,7},{8,9},{9,10},{10,11},{11... | collective-permute-start | bytes 3896 | tf_op jit(solution)/shard_map/ppermute | solution.py:19
  133.8 9.0 collective-permute-start.22
  157.1 9.0 collective-permute-start.28
  180.4 9.0 collective-permute-start.34
  203.8 9.0 collective-permute-start.40
  227.5 9.2 collective-permute-start.46
  252.5 10.8 collective-permute-start.52
  254.4 10.0 collective-permute-start.53
  278.4 10.6 collective-permute-start.58
  280.4 9.8 collective-permute-start.59
  381.1 9.5 collective-permute-start.64
  419.4 9.1 collective-permute-start.70
  472.3 9.0 collective-permute-start.82
  495.7 9.0 collective-permute-start.88
  519.0 9.0 collective-permute-start.94
  542.3 9.0 collective-permute-start.100
  566.0 9.2 collective-permute-start.106
  591.0 10.8 collective-permute-start.112
  593.0 10.0 collective-permute-start.113
  692.5 9.5 collective-permute-start.118
  794.5 9.5 collective-permute-start.124
  833.8 9.0 collective-permute-start.130
  862.8 8.8 collective-permute-start.136
  886.7 9.0 collective-permute-start.142
  910.1 9.0 collective-permute-start.148
  933.4 9.0 collective-permute-start.154
  956.7 9.0 collective-permute-start.160
  980.4 9.2 collective-permute-start.166
  1005.4 10.8 collective-permute-start.172
  1007.4 10.0 collective-permute-start.173
  1106.9 9.5 collective-permute-start.178
  (149 other events, 718.9 us)
where the time goes:
time: 1200 us
  starting transfers between devices  492 us (41%)
  blocking collectives  376 us (31%)
  waiting for transfers between devices  231 us (19%)
  local copies, waits for them, and re-layouts  51.1 us (4%)
  other arithmetic  37.1 us (3%)
    ppermute x90, starting transfers between devices, with_halo(): lax.ppermute(lax.slice_in_dim(block, block.shape[dim] - width, None, axis...  333 us
    psum x3, blocking collectives, alignment(): return lax.psum(jnp.sum(residual * precond), ('gx', 'gy', 'gz'))  223 us
    ppermute x90, waiting for transfers between devices, with_halo(): lax.ppermute(lax.slice_in_dim(block, 0, width, axis=dim), axis, backward)  201 us
    ppermute x90, starting transfers between devices, with_halo(): lax.ppermute(lax.slice_in_dim(block, 0, width, axis=dim), axis, backward)  159 us
    psum x2, blocking collectives, local(): curve = lax.psum(jnp.sum(direction * image), ('gx', 'gy', 'gz'))  153 us
    reshape x7, local copies, waits for them, and re-layouts, restrict(): return jnp.mean(v.reshape(a // 2, 2, b // 2, 2, c // 2, 2), axis=(1, 3, 5))  42.1 us
    ppermute x90, waiting for transfers between devices, with_halo(): lax.ppermute(lax.slice_in_dim(block, block.shape[dim] - width, None, axis...  29.9 us
  transfers between devices with their start and end apart: 180, of which 102 were waited for; matrix products, arithmetic and copies ran while one was open for 1% of the time, Pallas kernels for 0%

commit v1 on v0

v1 whole, which is shorter than its diff:
```python
import jax
import jax.numpy as jnp
from jax import lax
from jax.experimental import pallas as pl
from jax.experimental.pallas import tpu as pltpu
from jax.sharding import PartitionSpec as P

CLASSES = 16
COARSE_SWEEPS = 6
OMEGA = 0.8
KEEP = 1.0 - OMEGA
F32 = jnp.float32
SLABS, MIDS = 26, 12
VMEM = pl.BlockSpec(memory_space=pltpu.VMEM)
SMEM = pl.BlockSpec(memory_space=pltpu.SMEM)


def iota(shape, dim):
    return lax.broadcasted_iota(jnp.int32, shape, dim)


def roll(v, shift, axis):
    shift = shift % v.shape[axis]
    return v if shift == 0 else pltpu.roll(v, shift, axis)


def around(v, rows, lanes):
    return (roll(v, rows, 0) + roll(v, -rows, 0)) + (roll(v, lanes, 1) + roll(v, -lanes, 1))


def pair_mean(v, step):
    rows = (iota(v.shape, 0) // step) % 2 == 0
    v = v + jnp.where(rows, roll(v, -step, 0), roll(v, step, 0))
    lanes = (iota(v.shape, 1) // step) % 2 == 0
    v = v + jnp.where(lanes, roll(v, -step, 1), roll(v, step, 1))
    return v * 0.125


def pack_fine(read, low_ref, high_ref):
    chunk = iota((16, 128), 1) // 8
    low = high = jnp.zeros((16, 128), F32)
    for k in range(16):
        v = read(k)
        low = jnp.where(chunk == k, roll(v, 8 * k, 1), low)
        high = jnp.where(chunk == k, roll(v, 8 * k + 8, 1), high)
    low_ref[...] = low
    high_ref[...] = high


def prepare_kernel(rhs, classes, table, kap, low, high):
    for k in range(16):
        c = classes[k]
        v = jnp.zeros((16, 128), F32)
        for index in range(CLASSES):
            v = jnp.where(c == index, table[index], v)
        kap[k] = v
    pack_fine(lambda k: rhs[k], low.at[0], high.at[0])
    pack_fine(lambda k: kap[k], low.at[1], high.at[1])


def slab_sources(i):
    x = i - 5
    if x < 0:
        return 18 + x + 5, 23, 24, 16 + x
    if x < 16:
        return x, 16, 17, x
    return 25 + x - 16, 30, 31, x - 16


def assemble_fine(body, upper, lower, i):
    def unit(u):
        return jnp.concatenate([body[u], upper[u], lower[u]], axis=0)

    main, above, below, k = slab_sources(i)
    lane = iota((32, 128), 1)
    side = jnp.where(lane >= 120, roll(unit(below), 120 - 8 * k, 1), 0.0)
    side = jnp.where(lane < 8, roll(unit(above), -8 * k, 1), side)
    return jnp.concatenate([unit(main), side], axis=1)


def inside_fine(place, sizes):
    row, lane = iota((32, 256), 0), iota((32, 256), 1)
    y = jnp.where(row < 24, row, row - 32) + 16 * place[1]
    z = jnp.where(lane < 192, lane, lane - 256) + 128 * place[2]
    near = (lane < 136) | (lane >= 248)
    return near & (y >= 0) & (y < 16 * sizes[1]) & (z >= 0) & (z < 128 * sizes[2])


def fine_weights(place, sizes, body, upper, lower, weight0, weight1, middle, quads, weight2):
    inside = inside_fine(place, sizes)
    for m in range(MIDS):
        pair = None
        for i in (2 * m + 1, 2 * m + 2):
            kap = assemble_fine(body, upper, lower, i)
            x = 16 * place[0] + (i - 5)
            weight0[i] = jnp.where(inside & (x >= 0) & (x < 16 * sizes[0]), OMEGA / (kap + 6.0), 0.0)
            pair = kap if pair is None else pair + kap
        kap1 = pair_mean(pair, 1)
        middle[m] = kap1
        x = 8 * place[0] + (m - 2)
        weight1[m] = jnp.where(inside & (x >= 0) & (x < 8 * sizes[0]), OMEGA / (kap1 + 1.5), 0.0)
    for i in (0, SLABS - 1):
        kap = assemble_fine(body, upper, lower, i)
        x = 16 * place[0] + (i - 5)
        weight0[i] = jnp.where(inside & (x >= 0) & (x < 16 * sizes[0]), OMEGA / (kap + 6.0), 0.0)
    for c in range(4):
        kap2 = pair_mean(middle[2 + 2 * c] + middle[3 + 2 * c], 2)[:16, :128]
        quads[c] = OMEGA / (kap2 + 0.375)
    pack_coarse(quads, weight2, 0)


def pack_coarse(quads, out, base):
    row, chunk = iota((8, 128), 0), iota((8, 128), 1) // 32
    ends = jnp.zeros((8, 128), F32)
    rows = [quads[c, pl.ds(0, 4, stride=4), :] for c in range(4)]
    for c in range(4):
        both = jnp.concatenate([rows[c], rows[c]], axis=0)
        both = jnp.where(row < 4, roll(both, 32 * c, 1), roll(both, 32 * c + 32, 1))
        ends = jnp.where(chunk == c, both, ends)
    out[base] = jnp.concatenate(rows[:2], axis=0)
    out[base + 1] = jnp.concatenate(rows[2:], axis=0)
    out[base + 2] = ends


def down_sweep(body, upper, lower, weight0, weight1, x0, x1, unit, r, r1, quads):
    for i in range(SLABS):
        v = assemble_fine(body, upper, lower, i)
        r[i] = v
        x0[i] = weight0[i] * v
    for m in range(MIDS):
        i = 2 * m + 1
        two = x0[i] + x0[i + 1]
        left = KEEP * (r[i] + r[i + 1]) + ((x0[i - 1] + x0[i + 2]) + two) + around(two, 1, 1)
        v = pair_mean(left, 1)
        r1[m] = v
        x1[m] = weight1[m] * v
    for c in range(4):
        m = 2 + 2 * c
        two = x1[m] + x1[m + 1]
        left = KEEP * (r1[m] + r1[m + 1]) + 0.25 * (((x1[m - 1] + x1[m + 2]) + two) + around(two, 2, 2))
        quads[c] = pair_mean(left, 2)[:16, :128]
    pack_coarse(quads, unit, 0)


def first_down_kernel(sizes, place, body, upper, lower, kbody, kupper, klower, weight0, weight1, x0, x1, unit, r, r1, quads):
    fine_weights(place, sizes, kbody, kupper, klower, weight0, weight1, r1, quads, unit.at[pl.ds(3, 3)])
    down_sweep(body, upper, lower, weight0, weight1, x0, x1, unit, r, r1, quads)


def down_kernel(body, upper, lower, weight0, weight1, x0, x1, unit, r, r1, quads):
    down_sweep(body, upper, lower, weight0, weight1, x0, x1, unit, r, r1, quads)


def assemble_coarse(place, blocks, base, out, first, change):
    own, up1, down1, up2, down2 = blocks
    lane = iota((16, 128), 1)
    for k in range(4):
        def rows(t, s):
            parts = [own[k, t, s:s + 4], up1[k, t, s:s + 4], up2[k, t, s:s + 2], down2[k, t, s + 2:s + 4], down1[k, t, s:s + 4]]
            return jnp.concatenate(parts, axis=0)

        above, below = rows(base + 2, 0), rows(base + 2, 4)
        start = 4 * lax.rem(place[0] + k, 4) + first
        for s in range(4):
            side = jnp.where(lane >= 96, roll(below, 96 - 32 * s, 1), 0.0)
            side = jnp.where(lane < 32, roll(above, -32 * s, 1), side)
            v = jnp.concatenate([rows(base + s // 2, 4 * (s % 2)), side], axis=1)
            out[start + s] = change(start + s, v)


def up_sweep(place, blocks, weight2, weight1, weight0, x0, x1, kap, u, w, low, high, a, b, rhs2, spread, middle, t1, t0):
    zero = jnp.zeros((16, 256), F32)
    for ref in (a, b):
        ref[0] = zero
        ref[17] = zero
    assemble_coarse(place, blocks, 0, rhs2, 1, lambda s, v: weight2[s] * v)
    for s in range(1, 17):
        a[s] = rhs2[s]
    for sweep in range(COARSE_SWEEPS - 1):
        old, new = (a, b) if sweep % 2 == 0 else (b, a)

        def step(s, carry, old=old, new=new):
            v = old[s]
            beside = (old[s - 1] + old[s + 1]) + around(v, 1, 4)
            new[s] = (KEEP * v + rhs2[s]) + weight2[s] * (0.0625 * beside)
            return carry

        lax.fori_loop(1, 17, step, 0, unroll=4)
    last = b if COARSE_SWEEPS % 2 == 0 else a
    half = iota((8, 256), 0) < 4
    for c in range(6):
        v = last[4 * place[0] + c]
        spread[c] = jnp.concatenate(
            [
                jnp.where(half, jnp.broadcast_to(v[j:j + 1], (8, 256)), jnp.broadcast_to(v[j + 1:j + 2], (8, 256)))
                for j in (0, 2, 4, 14)
            ],
            axis=0,
        )
    for m in range(MIDS):
        t1[m] = x1[m] + spread[m // 2]
    for m in range(1, MIDS - 1):
        v = t1[m]
        beside = (t1[m - 1] + t1[m + 1]) + around(v, 2, 2)
        middle[m] = (KEEP * v + x1[m]) + weight1[m] * (0.25 * beside)
    for i in range(3, SLABS - 3):
        t0[i] = x0[i] + middle[(i - 1) // 2]
    for i in range(4, SLABS - 4):
        v = t0[i]
        beside = (t0[i - 1] + t0[i + 1]) + around(v, 1, 1)
        middle_v = (KEEP * v + x0[i]) + weight0[i] * beside
        u[i] = middle_v
    for i in range(5, SLABS - 5):
        v = u[i]
        beside = (u[i - 1] + u[i + 1]) + around(v, 1, 1)
        w[i - 5] = (kap[i - 5] + 6.0) * v[:16, :128] - beside[:16, :128]
    pack_fine(lambda k: w[k], low, high)


def lanes_of(values, shape=(8, 128)):
    lane = iota(shape, 1)
    out = jnp.zeros(shape, F32)
    for k, v in enumerate(values):
        out = jnp.where(lane == k, jnp.sum(v), out)
    return out


def first_up_kernel(place, sizes, *refs):
    (own, up1, down1, up2, down2, weight1, weight0, x0, x1, kap, rhs,
     weight2, u, w, low, high, dots, a, b, rhs2, spread, middle, t1, t0, full) = refs
    blocks = (own, up1, down1, up2, down2)
    row, lane = iota((16, 256), 0), iota((16, 256), 1)
    y = jnp.where(row < 10, row, row - 16) + 4 * place[1]
    z = jnp.where(lane < 192, lane, lane - 256) + 128 * place[2]
    near = (lane < 160) | (lane >= 224)
    inside = near & (y >= 0) & (y < 4 * sizes[1]) & (z >= 0) & (z < 128 * sizes[2])
    assemble_coarse(place, blocks, 3, weight2, 1, lambda s, v: jnp.where(inside, v, 0.0))
    up_sweep(place, blocks, weight2, weight1, weight0, x0, x1, kap, full, w, low, high, a, b, rhs2, spread, middle, t1, t0)
    rz = curve = jnp.zeros((16, 128), F32)
    for k in range(16):
        v = full[k + 5][:16, :128]
        u[k] = v
        rz = rz + rhs[k] * v
        curve = curve + w[k] * v
    dots[...] = lanes_of([rz, curve])


def up_kernel(place, *refs):
    (own, up1, down1, up2, down2, weight2, weight1, weight0, x0, x1, kap,
     u, w, low, high, a, b, rhs2, spread, middle, t1, t0, full) = refs
    blocks = (own, up1, down1, up2, down2)
    up_sweep(place, blocks, weight2, weight1, weight0, x0, x1, kap, full, w, low, high, a, b, rhs2, spread, middle, t1, t0)
    for k in range(16):
        u[k] = full[k + 5][:16, :128]


def dots_kernel(first, r0, u0, w0, m0, n0, p, q, r1, u1, w1, m1, n1, dots):
    alpha = first[0:1, 0:1] / first[0:1, 1:2]
    sums = [jnp.zeros((16, 128), F32)] * 12
    for k in range(16):
        vw0, vm0, vn0 = w0[k], m0[k], n0[k]
        vr1 = r0[k] - alpha * vw0
        vu1 = u0[k] - alpha * vm0
        vw1 = vw0 - alpha * vn0
        vm1 = vm0 - alpha * p[k]
        vn1 = vn0 - alpha * q[k]
        r1[k], u1[k], w1[k], m1[k], n1[k] = vr1, vu1, vw1, vm1, vn1
        terms = [vr1 * vu1, vr1 * vm1, vr1 * vm0, vw1 * vu1, vw1 * vm1, vw1 * vm0,
                 vw0 * vu1, vw0 * vm1, vw0 * vm0, vn1 * vm1, vn1 * vm0, vn0 * vm0]
        sums = [s + t for s, t in zip(sums, terms)]
    dots[...] = lanes_of(sums)


def finish_kernel(first, second, u0, w0, m0, n0, r1, u1, w1, m1, n1, field, residual):
    g0, d0 = first[0:1, 0:1], first[0:1, 1:2]
    r1u1, r1m1, r1m0, w1u1, w1m1, w1m0, w0u1, w0m1, w0m0, n1m1, n1m0, n0m0 = [second[0:1, k:k + 1] for k in range(12)]
    alpha0 = g0 / d0
    beta1 = r1u1 / g0
    curve1 = w1u1 + 2.0 * beta1 * w0u1 + beta1 * beta1 * d0
    alpha1 = r1u1 / curve1
    ab = alpha1 * beta1
    su = w1u1 + beta1 * w0u1 - alpha1 * (w1m1 + beta1 * w0m1) - ab * (w1m0 + beta1 * w0m0)
    g2 = (r1u1 - alpha1 * r1m1 - ab * r1m0) - alpha1 * su
    beta2 = g2 / r1u1
    uw = (w1u1 - 2.0 * alpha1 * w1m1 - 2.0 * ab * w1m0) + (alpha1 * alpha1 * n1m1 + 2.0 * alpha1 * ab * n1m0 + ab * ab * n0m0)
    curve2 = uw + 2.0 * beta2 * su + beta2 * beta2 * curve1
    alpha2 = g2 / curve2
    mix = alpha1 + alpha2 * beta2
    cu0, cu1, cm1, cm0 = alpha0 + mix * beta1, mix + alpha2, alpha2 * alpha1, alpha2 * ab
    cw0 = mix * beta1
    for k in range(16):
        field[k] = (cu0 * u0[k] + cu1 * u1[k]) - (cm1 * m1[k] + cm0 * m0[k])
        residual[k] = r1[k] - (cw0 * w0[k] + cu1 * w1[k]) + (cm1 * n1[k] + cm0 * n0[k])


def shape(*dims):
    return jax.ShapeDtypeStruct(dims, F32)


def call(kernel, outs, scratch=(), scalars=0, count=0, smem=()):
    specs = [SMEM if (k < scalars or k in smem) else VMEM for k in range(count)]
    return pl.pallas_call(
        kernel,
        out_shape=outs,
        in_specs=specs,
        out_specs=[VMEM] * len(outs),
        scratch_shapes=[pltpu.VMEM(s, F32) for s in scratch],
        compiler_params=pltpu.CompilerParams(vmem_limit_bytes=40 * 1024 * 1024),
    )


def ring(axis, distance):
    count = lax.axis_size(axis)
    return [(i, (i + distance) % count) for i in range(count)]


def shift(v, axis, distance):
    return lax.ppermute(v, axis, ring(axis, -distance))


def fine_exchange(own, low, high):
    above, below = shift(low, "gz", 1), shift(high, "gz", -1)
    packs = [above[..., None, :, :], below[..., None, :, :]]
    first = jnp.concatenate([own[..., :5, :, :]] + packs, axis=-3)
    last = jnp.concatenate([own[..., 11:, :, :]] + packs, axis=-3)
    before, after = shift(last, "gx", -1), shift(first, "gx", 1)
    body = jnp.concatenate([own] + packs + [before, after], axis=-3)
    upper, lower = shift(body[..., :8, :], "gy", 1), shift(body[..., 8:, :], "gy", -1)
    return body, upper, lower


def coarse_exchange(unit):
    groups = []
    ends = unit[2::3]
    above, below = shift(ends, "gz", 1), shift(ends, "gz", -1)
    tiles = []
    for k in range(unit.shape[0] // 3):
        tiles += [unit[3 * k], unit[3 * k + 1], jnp.concatenate([above[k, :4], below[k, 4:]], axis=0)]
    unit = jnp.stack(tiles)
    groups = jnp.stack([unit] + [shift(unit, "gx", k) for k in (1, 2, 3)])
    return [groups] + [shift(groups, "gy", k) for k in (1, -1, 2, -2)]


def total(v):
    row = v[:1]
    for axes, count in ((("gx", "gy"), lax.axis_size("gx") * lax.axis_size("gy")), (("gz",), lax.axis_size("gz"))):
        parts = lax.all_to_all(jnp.broadcast_to(row[None], (count, 1, 128)), axes, 0, 0, tiled=True)
        row = parts.sum(0)
    return jnp.broadcast_to(row, (8, 128))


def local(right_side, classes, table):
    place = jnp.stack([lax.axis_index(axis) for axis in ("gx", "gy", "gz")]).astype(jnp.int32)
    sizes = jnp.array([lax.axis_size(axis) for axis in ("gx", "gy", "gz")], jnp.int32)
    block, halo = (16, 16, 128), (SLABS, 32, 256)
    mids = (MIDS, 32, 256)
    down_scratch = [halo, mids, (4, 16, 128)]
    up_scratch = [(18, 16, 256), (18, 16, 256), (18, 16, 256), (6, 32, 256), mids, mids, halo, halo]

    kap, low, high = call(
        prepare_kernel, [shape(*block), shape(2, 16, 128), shape(2, 16, 128)], count=3, smem=(2,)
    )(right_side, classes, table)
    body, upper, lower = fine_exchange(jnp.stack([right_side, kap]), low, high)
    weight0, weight1, x0, x1, unit = call(
        first_down_kernel, [shape(*halo), shape(*mids), shape(*halo), shape(*mids), shape(6, 8, 128)],
        down_scratch, scalars=2, count=8,
    )(sizes, place, body[0], upper[0], lower[0], body[1], upper[1], lower[1])
    blocks = coarse_exchange(unit)
    weight2, u0, w0, low, high, dots = call(
        first_up_kernel,
        [shape(18, 16, 256), shape(*block), shape(*block), shape(16, 128), shape(16, 128), shape(8, 128)],
        up_scratch, scalars=2, count=13,
    )(place, sizes, *blocks, weight1, weight0, x0, x1, kap, right_side)
    first = total(dots)

    def apply(v, low, high):
        body, upper, lower = fine_exchange(v, low, high)
        x0, x1, unit = call(
            down_kernel, [shape(*halo), shape(*mids), shape(3, 8, 128)], down_scratch, count=5
        )(body, upper, lower, weight0, weight1)
        blocks = coarse_exchange(unit)
        return call(
            up_kernel, [shape(*block), shape(*block), shape(16, 128), shape(16, 128)],
            up_scratch, scalars=1, count=12,
        )(place, *blocks, weight2, weight1, weight0, x0, x1, kap)

    m0, n0, low, high = apply(w0, low, high)
    p, q, _, _ = apply(n0, low, high)
    r1, u1, w1, m1, n1, dots = call(
        dots_kernel, [shape(*block)] * 5 + [shape(8, 128)], count=8
    )(first, right_side, u0, w0, m0, n0, p, q)
    second = total(dots)
    field, residual = call(finish_kernel, [shape(*block)] * 2, count=11)(
        first, second, u0, w0, m0, n0, r1, u1, w1, m1, n1
    )
    return field, residual


def solution(mesh):
    in_specs = (P("gx", "gy", "gz"), P("gx", "gy", "gz"), P())
    out_specs = (P("gx", "gy", "gz"), P("gx", "gy", "gz"))
    return jax.shard_map(local, mesh=mesh, in_specs=in_specs, out_specs=out_specs, check_vma=False)
```

time: 1200 us -> 196 us (0.16)
  starting transfers between devices: 492 us -> 74.1 us
  blocking collectives: 376 us -> 46.2 us
  waiting for transfers between devices: 231 us -> 47.5 us
  local copies, waits for them, and re-layouts: 51.1 us -> 5.18 us
  other arithmetic: 37.1 us -> 0.28 us
  Pallas kernels: 0 us -> 21.3 us
    ppermute x180 -> x45, starting transfers between devices: 492 us -> 74.1 us  [shift(): return lax.ppermute(v, axis, ring(axis, -distance))]
    psum x5 -> x0, blocking collectives: 376 us -> none  [the longest x3 223 us: alignment(): return lax.psum(jnp.sum(residual * precond), ('gx', 'gy', 'gz'))]
    ppermute x180 -> x45, waiting for transfers between devices: 231 us -> 47.5 us  [shift(): return lax.ppermute(v, axis, ring(axis, -distance))]
    all_to_all x0 -> x4, blocking collectives: none -> 46.2 us  [total(): lax.all_to_all(jnp.broadcast_to(row[None], (count, 1, 128)), axes, 0, 0,...]
    reshape x19 -> x0, local copies, waits for them, and re-layouts: 44.9 us -> none  [the longest x7 42.1 us: restrict(): return jnp.mean(v.reshape(a // 2, 2, b // 2, 2, c // 2, 2), axis=(1, 3, 5))]
    pallas_call x0 -> x9, Pallas kernels: none -> 21.3 us  [the longest x2 7.8 us: apply(): call(up_kernel, [shape(*block), shape(*block), shape(16, 128), shape(16,...]
    reduce_sum x13 -> x4, other arithmetic: 20.8 us -> 0.07 us  [total(): row = parts.sum(0)]
  transfers between devices with their start and end apart: 180 -> 45, of which waited for: 102 -> 29; matrix products, arithmetic and copies ran while one was open for 1% -> 0% of each run, Pallas kernels for 0% -> 0%
where the time goes in v1:
time: 196 us; the launch traced here: 195 us
  starting transfers between devices  74.1 us (38%)
  waiting for transfers between devices  47.5 us (24%)
  blocking collectives  46.2 us (24%)
  Pallas kernels  21.3 us (11%)
  local copies, waits for them, and re-layouts  5.18 us (3%)
    ppermute x45, starting transfers between devices, shift(): return lax.ppermute(v, axis, ring(axis, -distance))  74.1 us
    ppermute x45, waiting for transfers between devices, shift(): return lax.ppermute(v, axis, ring(axis, -distance))  47.5 us
    all_to_all x4, blocking collectives, total(): lax.all_to_all(jnp.broadcast_to(row[None], (count, 1, 128)), axes, 0, 0,...  46.2 us
    pallas_call x2, Pallas kernels, apply(): call(up_kernel, [shape(*block), shape(*block), shape(16, 128), shape(16,...  7.8 us
    unnamed x25, local copies, waits for them, and re-layouts  4.92 us
  transfers between devices with their start and end apart: 45, of which 29 were waited for; matrix products, arithmetic and copies ran while one was open for 0% of the time, Pallas kernels for 0%

profile of v1, /device:TPU:1, one launch (start us, length us, event | category | flops | bytes accessed | tf_op | source)
XLA Modules:
  0.0 195.5 jit_solution(13327739145484269172)
XLA Ops:
  3.9 3.2 %collective-permute-start = (f32[2,16,128]{2,1,0:T(8,128)S(1)}, f32[2,16,128]{2,1,0:T(8,128)S(1)}, u32[]{:S(2)}, u32[]{:S(2)}) collective-permute-start(f32[2,16,128]{2,1,0:T(8,128)S(1)} %get-tuple-element.35), channel_id=1, source_target_pairs={{0,7},{1,0},{2,1},{3,2},{4,3},{5,4},{6,5},{7,6},{8,15},{9,8},{10,9... | collective-permute-start | bytes 49160 | tf_op jit(solution)/shard_map/ppermute | solution.py:318
  8.5 2.6 %collective-permute-start.3 = (f32[2,7,16,128]{3,2,1,0:T(8,128)S(1)}, f32[2,7,16,128]{3,2,1,0:T(8,128)S(1)}, u32[]{:S(2)}, u32[]{:S(2)}) collective-permute-start(f32[2,7,16,128]{3,2,1,0:T(8,128)S(1)} %get-tuple-element.84), channel_id=1, source_target_pairs={{0,192},{64,0},{128,64},{192,128},{1,193},{65,1},{129,65},{193,129... | collective-permute-start | bytes 344072 | tf_op jit(solution)/shard_map/ppermute | solution.py:318
  11.1 4.8 %collective-permute-done.2 = f32[2,7,16,128]{3,2,1,0:T(8,128)S(1)} collective-permute-done((f32[2,7,16,128]{3,2,1,0:T(8,128)S(1)}, f32[2,7,16,128]{3,2,1,0:T(8,128)S(1)}, u32[]{:S(2)}, u32[]{:S(2)}) %collective-permute-start.2) | collective-permute-done | bytes 114720 | tf_op jit(solution)/shard_map/ppermute | solution.py:318
  17.8 4.0 %collective-permute-start.4 = (f32[2,32,8,128]{3,2,1,0:T(8,128)S(1)}, f32[2,32,8,128]{3,2,1,0:T(8,128)S(1)}, u32[]{:S(2)}, u32[]{:S(2)}) collective-permute-start(f32[2,32,8,128]{3,2,1,0:T(8,128)S(1)} %get-tuple-element.69), channel_id=1, source_target_pairs={{0,56},{8,0},{16,8},{24,16},{32,24},{40,32},{48,40},{56,48},{1,57}... | collective-permute-start | bytes 786440 | tf_op jit(solution)/shard_map/ppermute | solution.py:318
  21.8 3.6 %collective-permute-done.5 = f32[2,32,8,128]{3,2,1,0:T(8,128)S(1)} collective-permute-done((f32[2,32,8,128]{3,2,1,0:T(8,128)S(1)}, f32[2,32,8,128]{3,2,1,0:T(8,128)S(1)}, u32[]{:S(2)}, u32[]{:S(2)}) %collective-permute-start.5) | collective-permute-done | bytes 262176 | tf_op jit(solution)/shard_map/ppermute | solution.py:318
  26.2 3.6 %shard_map.60 = (f32[26,32,256]{2,1,0:T(8,128)S(1)}, f32[12,32,256]{2,1,0:T(8,128)S(1)}, f32[26,32,256]{2,1,0:T(8,128)S(1)}, f32[12,32,256]{2,1,0:T(8,128)S(1)}, f32[6,8,128]{2,1,0:T(8,128)S(1)}) custom-call(s32[3]{0:T(128)S(1)} %copy-done.5, s32[3]{0:T(128)S(1)} %pad_add_fusion.place, f32[32,16,128]{2,1,0:T(8,128)S(1)} %get-tuple-element.67.body, ...), custom_call_target="tpu_custom_call" | custom-call | tf_op jit(solution)/shard_map/pallas_call | solution.py:364
  29.8 4.7 %collective-permute-start.7 = (f32[2,8,128]{2,1,0:T(8,128)S(1)}, f32[2,8,128]{2,1,0:T(8,128)S(1)}, u32[]{:S(2)}, u32[]{:S(2)}) collective-permute-start(f32[2,8,128]{2,1,0:T(8,128)S(1)} %get-tuple-element.90), channel_id=1, source_target_pairs={{0,1},{1,2},{2,3},{3,4},{4,5},{5,6},{6,7},{7,0},{8,9},{9,10},{10,1... | collective-permute-start | bytes 24584 | tf_op jit(solution)/shard_map/ppermute | solution.py:318
  39.3 2.6 %collective-permute-done.9 = f32[6,8,128]{2,1,0:T(8,128)S(1)} collective-permute-done((f32[6,8,128]{2,1,0:T(8,128)S(1)}, f32[6,8,128]{2,1,0:T(8,128)S(1)}, u32[]{:S(2)}, u32[]{:S(2)}) %collective-permute-start.9) | collective-permute-done | bytes 24608 | tf_op jit(solution)/shard_map/ppermute | solution.py:318
  49.6 2.8 %collective-permute-done.12.refs_2_ = f32[4,6,8,128]{3,2,1,0:T(8,128)S(1)} collective-permute-done((f32[4,6,8,128]{3,2,1,0:T(8,128)S(1)}, f32[4,6,8,128]{3,2,1,0:T(8,128)S(1)}, u32[]{:S(2)}, u32[]{:S(2)}) %collective-permute-start.12) | collective-permute-done | bytes 98336 | tf_op jit(solution)/shard_map/ppermute | solution.py:318
  52.4 3.8 %shard_map.61 = (f32[18,16,256]{2,1,0:T(8,128)S(1)}, f32[16,16,128]{2,1,0:T(8,128)S(1)}, f32[16,16,128]{2,1,0:T(8,128)S(1)}, f32[16,128]{1,0:T(8,128)S(1)}, f32[16,128]{1,0:T(8,128)S(1)}, /*index=5*/f32[8,128]{1,0:T(8,128)S(1)}) custom-call(s32[3]{0:T(128)S(1)} %pad_add_fusion.place, s32[3]{0:T(128)S(1)} %copy-done.5, ...), custom_call_target="tpu_custom_call" | custom-call | tf_op jit(solution)/shard_map/pallas_call | solution.py:369
  56.2 4.8 %collective-permute-start.15 = (f32[16,128]{1,0:T(8,128)S(1)}, f32[16,128]{1,0:T(8,128)S(1)}, u32[]{:S(2)}, u32[]{:S(2)}) collective-permute-start(f32[16,128]{1,0:T(8,128)S(1)} %get-tuple-element.45), channel_id=1, source_target_pairs={{0,7},{1,0},{2,1},{3,2},{4,3},{5,4},{6,5},{7,6},{8,15},{9,8},{10,9... | collective-permute-start | bytes 24584 | tf_op jit(solution)/shard_map/ppermute | solution.py:318
  62.2 2.5 %collective-permute-done.16 = f32[16,128]{1,0:T(8,128)S(1)} collective-permute-done((f32[16,128]{1,0:T(8,128)S(1)}, f32[16,128]{1,0:T(8,128)S(1)}, u32[]{:S(2)}, u32[]{:S(2)}) %collective-permute-start.16) | collective-permute-done | bytes 8224 | tf_op jit(solution)/shard_map/ppermute | solution.py:318
  66.2 4.0 %collective-permute-done.17 = f32[7,16,128]{2,1,0:T(8,128)S(1)} collective-permute-done((f32[7,16,128]{2,1,0:T(8,128)S(1)}, f32[7,16,128]{2,1,0:T(8,128)S(1)}, u32[]{:S(2)}, u32[]{:S(2)}) %collective-permute-start.17) | collective-permute-done | bytes 57376 | tf_op jit(solution)/shard_map/ppermute | solution.py:318
  71.0 2.1 %collective-permute-start.19 = (f32[32,8,128]{2,1,0:T(8,128)S(1)}, f32[32,8,128]{2,1,0:T(8,128)S(1)}, u32[]{:S(2)}, u32[]{:S(2)}) collective-permute-start(f32[32,8,128]{2,1,0:T(8,128)S(1)} %get-tuple-element.73), channel_id=1, source_target_pairs={{0,56},{8,0},{16,8},{24,16},{32,24},{40,32},{48,40},{56,48},{1,57}... | collective-permute-start | bytes 393224 | tf_op jit(solution)/shard_map/ppermute | solution.py:318
  73.0 2.4 %collective-permute-done.20.lower = f32[32,8,128]{2,1,0:T(8,128)S(1)} collective-permute-done((f32[32,8,128]{2,1,0:T(8,128)S(1)}, f32[32,8,128]{2,1,0:T(8,128)S(1)}, u32[]{:S(2)}, u32[]{:S(2)}) %collective-permute-start.20) | collective-permute-done | bytes 131104 | tf_op jit(solution)/shard_map/ppermute | solution.py:318
  77.5 2.4 %collective-permute-start.22 = (f32[1,8,128]{2,1,0:T(8,128)S(1)}, f32[1,8,128]{2,1,0:T(8,128)S(1)}, u32[]{:S(2)}, u32[]{:S(2)}) collective-permute-start(f32[1,8,128]{2,1,0:T(8,128)S(1)} %slice.138), channel_id=1, source_target_pairs={{0,1},{1,2},{2,3},{3,4},{4,5},{5,6},{6,7},{7,0},{8,9},{9,10},{10,1... | collective-permute-start | bytes 12296 | tf_op jit(solution)/shard_map/ppermute | solution.py:318
  79.9 3.8 %collective-permute-start.21 = (f32[1,8,128]{2,1,0:T(8,128)S(1)}, f32[1,8,128]{2,1,0:T(8,128)S(1)}, u32[]{:S(2)}, u32[]{:S(2)}) collective-permute-start(f32[1,8,128]{2,1,0:T(8,128)S(1)} %slice.138), channel_id=1, source_target_pairs={{0,7},{1,0},{2,1},{3,2},{4,3},{5,4},{6,5},{7,6},{8,15},{9,8},{10,9... | collective-permute-start | bytes 12296 | tf_op jit(solution)/shard_map/ppermute | solution.py:318
  86.2 2.5 %collective-permute-done.24 = f32[3,8,128]{2,1,0:T(8,128)S(1)} collective-permute-done((f32[3,8,128]{2,1,0:T(8,128)S(1)}, f32[3,8,128]{2,1,0:T(8,128)S(1)}, u32[]{:S(2)}, u32[]{:S(2)}) %collective-permute-start.24) | collective-permute-done | bytes 12320 | tf_op jit(solution)/shard_map/ppermute | solution.py:318
  89.5 2.4 %collective-permute-start.29 = (f32[4,3,8,128]{3,2,1,0:T(8,128)S(1)}, f32[4,3,8,128]{3,2,1,0:T(8,128)S(1)}, u32[]{:S(2)}, u32[]{:S(2)}) collective-permute-start(f32[4,3,8,128]{3,2,1,0:T(8,128)S(1)} %pad_maximum_fusion.14.refs_0_), channel_id=1, source_target_pairs={{0,16},{8,24},{16,32},{24,40},{32,48},{40,56},{48,0},{56,8},{1,17}... | collective-permute-start | bytes 147464 | tf_op jit(solution)/shard_map/ppermute | solution.py:318
  97.7 3.6 %shard_map.63 = (f32[16,16,128]{2,1,0:T(8,128)S(1)}, f32[16,16,128]{2,1,0:T(8,128)S(1)}, f32[16,128]{1,0:T(8,128)S(1)}, f32[16,128]{1,0:T(8,128)S(1)}) custom-call(s32[3]{0:T(128)S(1)} %pad_add_fusion.place, f32[4,3,8,128]{3,2,1,0:T(8,128)S(1)} %pad_maximum_fusion.14.refs_0_, f32[4,3,8,128]{3,2,1,0:T(8,128)S(1)} %collective-permute-done.26.refs_1_, ...), custom_call_target="tpu_custom_call" | custom-call | tf_op jit(solution)/shard_map/pallas_call | solution.py:382
  101.3 7.2 %collective-permute-start.30 = (f32[16,128]{1,0:T(8,128)S(1)}, f32[16,128]{1,0:T(8,128)S(1)}, u32[]{:S(2)}, u32[]{:S(2)}) collective-permute-start(f32[16,128]{1,0:T(8,128)S(1)} %get-tuple-element.53), channel_id=1, source_target_pairs={{0,7},{1,0},{2,1},{3,2},{4,3},{5,4},{6,5},{7,6},{8,15},{9,8},{10,9... | collective-permute-start | bytes 24584 | tf_op jit(solution)/shard_map/ppermute | solution.py:318
  111.4 3.8 %collective-permute-done.32 = f32[7,16,128]{2,1,0:T(8,128)S(1)} collective-permute-done((f32[7,16,128]{2,1,0:T(8,128)S(1)}, f32[7,16,128]{2,1,0:T(8,128)S(1)}, u32[]{:S(2)}, u32[]{:S(2)}) %collective-permute-start.32) | collective-permute-done | bytes 57376 | tf_op jit(solution)/shard_map/ppermute | solution.py:318
  115.3 2.7 %collective-permute-start.34 = (f32[32,8,128]{2,1,0:T(8,128)S(1)}, f32[32,8,128]{2,1,0:T(8,128)S(1)}, u32[]{:S(2)}, u32[]{:S(2)}) collective-permute-start(f32[32,8,128]{2,1,0:T(8,128)S(1)} %get-tuple-element.71), channel_id=1, source_target_pairs={{0,56},{8,0},{16,8},{24,16},{32,24},{40,32},{48,40},{56,48},{1,57}... | collective-permute-start | bytes 393224 | tf_op jit(solution)/shard_map/ppermute | solution.py:318
  118.0 2.4 %collective-permute-done.35.lower = f32[32,8,128]{2,1,0:T(8,128)S(1)} collective-permute-done((f32[32,8,128]{2,1,0:T(8,128)S(1)}, f32[32,8,128]{2,1,0:T(8,128)S(1)}, u32[]{:S(2)}, u32[]{:S(2)}) %collective-permute-start.35) | collective-permute-done | bytes 131104 | tf_op jit(solution)/shard_map/ppermute | solution.py:318
  122.9 4.5 %collective-permute-start.37 = (f32[1,8,128]{2,1,0:T(8,128)S(1)}, f32[1,8,128]{2,1,0:T(8,128)S(1)}, u32[]{:S(2)}, u32[]{:S(2)}) collective-permute-start(f32[1,8,128]{2,1,0:T(8,128)S(1)} %slice.146), channel_id=1, source_target_pairs={{0,1},{1,2},{2,3},{3,4},{4,5},{5,6},{6,7},{7,0},{8,9},{9,10},{10,1... | collective-permute-start | bytes 12296 | tf_op jit(solution)/shard_map/ppermute | solution.py:318
  132.2 2.4 %collective-permute-done.39 = f32[3,8,128]{2,1,0:T(8,128)S(1)} collective-permute-done((f32[3,8,128]{2,1,0:T(8,128)S(1)}, f32[3,8,128]{2,1,0:T(8,128)S(1)}, u32[]{:S(2)}, u32[]{:S(2)}) %collective-permute-start.39) | collective-permute-done | bytes 12320 | tf_op jit(solution)/shard_map/ppermute | solution.py:318
  140.2 2.0 %collective-permute-start.41 = (f32[4,3,8,128]{3,2,1,0:T(8,128)S(1)}, f32[4,3,8,128]{3,2,1,0:T(8,128)S(1)}, u32[]{:S(2)}, u32[]{:S(2)}) collective-permute-start(f32[4,3,8,128]{3,2,1,0:T(8,128)S(1)} %pad_maximum_fusion.15.refs_0_), channel_id=1, source_target_pairs={{0,56},{8,0},{16,8},{24,16},{32,24},{40,32},{48,40},{56,48},{1,57}... | collective-permute-start | bytes 147464 | tf_op jit(solution)/shard_map/ppermute | solution.py:318
  142.2 12.5 %all_to_all.20 = f32[32,1,128]{2,1,0:T(1,128)S(1)} all-to-all(f32[32,1,128]{2,1,0:T(1,128)S(1)} %broadcast_in_dim.59), channel_id=1, replica_groups=mesh['gx'=4,'gy'=8,'gz'=8] {'gx','gy'}, dimensions={0} | all-to-all | bytes 32768 | tf_op jit(solution)/shard_map/all_to_all | solution.py:347
  154.7 13.4 %all_to_all.21 = f32[8,1,128]{2,1,0:T(1,128)S(1)} all-to-all(f32[8,1,128]{2,1,0:T(1,128)S(1)} %broadcast_in_dim.60), channel_id=1, replica_groups=mesh['gx'=4,'gy'=8,'gz'=8] {'gz'}, dimensions={0} | all-to-all | bytes 8192 | tf_op jit(solution)/shard_map/all_to_all | solution.py:347
  169.1 4.2 %shard_map.65 = (f32[16,16,128]{2,1,0:T(8,128)S(1)}, f32[16,16,128]{2,1,0:T(8,128)S(1)}, f32[16,128]{1,0:T(8,128)}, f32[16,128]{1,0:T(8,128)}) custom-call(s32[3]{0:T(128)S(1)} %pad_add_fusion.place, f32[4,3,8,128]{3,2,1,0:T(8,128)S(1)} %pad_maximum_fusion.15.refs_0_, f32[4,3,8,128]{3,2,1,0:T(8,128)S(1)} %collective-permute-done.41.refs_1_, ...), custom_call_target="tpu_custom_call" | custom-call | tf_op jit(solution)/shard_map/pallas_call | solution.py:382
  173.8 11.6 %all_to_all.22 = f32[32,1,128]{2,1,0:T(1,128)S(1)} all-to-all(f32[32,1,128]{2,1,0:T(1,128)S(1)} %broadcast_in_dim.67), channel_id=1, replica_groups=mesh['gx'=4,'gy'=8,'gz'=8] {'gx','gy'}, dimensions={0} | all-to-all | bytes 32768 | tf_op jit(solution)/shard_map/all_to_all | solution.py:347
  185.4 8.8 %all_to_all.23 = f32[8,1,128]{2,1,0:T(1,128)S(1)} all-to-all(f32[8,1,128]{2,1,0:T(1,128)S(1)} %broadcast_in_dim.68), channel_id=1, replica_groups=mesh['gx'=4,'gy'=8,'gz'=8] {'gz'}, dimensions={0} | all-to-all | bytes 8192 | tf_op jit(solution)/shard_map/all_to_all | solution.py:347
  (145 shorter events, 53.1 us)
Async XLA Ops:
  8.5 7.4 %collective-permute-start.3 = (f32[2,7,16,128]{3,2,1,0:T(8,128)S(1)}, f32[2,7,16,128]{3,2,1,0:T(8,128)S(1)}, u32[]{:S(2)}, u32[]{:S(2)}) collective-permute-start(f32[2,7,16,128]{3,2,1,0:T(8,128)S(1)} %get-tuple-element.84), channel_id=1, source_target_pairs={{0,192},{64,0},{128,64},{192,128},{1,193},{65,1},{129,65},{193,129... | collective-permute-start | bytes 344072 | tf_op jit(solution)/shard_map/ppermute | solution.py:318
  11.1 4.9 %collective-permute-start.2 = (f32[2,7,16,128]{3,2,1,0:T(8,128)S(1)}, f32[2,7,16,128]{3,2,1,0:T(8,128)S(1)}, u32[]{:S(2)}, u32[]{:S(2)}) collective-permute-start(f32[2,7,16,128]{3,2,1,0:T(8,128)S(1)} %get-tuple-element.85), channel_id=1, source_target_pairs={{0,64},{64,128},{128,192},{192,0},{1,65},{65,129},{129,193},{193,1... | collective-permute-start | bytes 344072 | tf_op jit(solution)/shard_map/ppermute | solution.py:318
  16.0 9.4 %collective-permute-start.5 = (f32[2,32,8,128]{3,2,1,0:T(8,128)S(1)}, f32[2,32,8,128]{3,2,1,0:T(8,128)S(1)}, u32[]{:S(2)}, u32[]{:S(2)}) collective-permute-start(f32[2,32,8,128]{3,2,1,0:T(8,128)S(1)} %get-tuple-element.68), channel_id=1, source_target_pairs={{0,8},{8,16},{16,24},{24,32},{32,40},{40,48},{48,56},{56,0},{1,9},... | collective-permute-start | bytes 786440 | tf_op jit(solution)/shard_map/ppermute | solution.py:318
  17.8 7.6 %collective-permute-start.4 = (f32[2,32,8,128]{3,2,1,0:T(8,128)S(1)}, f32[2,32,8,128]{3,2,1,0:T(8,128)S(1)}, u32[]{:S(2)}, u32[]{:S(2)}) collective-permute-start(f32[2,32,8,128]{3,2,1,0:T(8,128)S(1)} %get-tuple-element.69), channel_id=1, source_target_pairs={{0,56},{8,0},{16,8},{24,16},{32,24},{40,32},{48,40},{56,48},{1,57}... | collective-permute-start | bytes 786440 | tf_op jit(solution)/shard_map/ppermute | solution.py:318
  29.8 6.7 %collective-permute-start.7 = (f32[2,8,128]{2,1,0:T(8,128)S(1)}, f32[2,8,128]{2,1,0:T(8,128)S(1)}, u32[]{:S(2)}, u32[]{:S(2)}) collective-permute-start(f32[2,8,128]{2,1,0:T(8,128)S(1)} %get-tuple-element.90), channel_id=1, source_target_pairs={{0,1},{1,2},{2,3},{3,4},{4,5},{5,6},{6,7},{7,0},{8,9},{9,10},{10,1... | collective-permute-start | bytes 24584 | tf_op jit(solution)/shard_map/ppermute | solution.py:318
  37.7 4.3 %collective-permute-start.9 = (f32[6,8,128]{2,1,0:T(8,128)S(1)}, f32[6,8,128]{2,1,0:T(8,128)S(1)}, u32[]{:S(2)}, u32[]{:S(2)}) collective-permute-start(f32[6,8,128]{2,1,0:T(8,128)S(1)} %get-tuple-element.87), channel_id=1, source_target_pairs={{0,128},{64,192},{128,0},{192,64},{1,129},{65,193},{129,1},{193,65... | collective-permute-start | bytes 73736 | tf_op jit(solution)/shard_map/ppermute | solution.py:318
  37.8 4.2 %collective-permute-start.8 = (f32[6,8,128]{2,1,0:T(8,128)S(1)}, f32[6,8,128]{2,1,0:T(8,128)S(1)}, u32[]{:S(2)}, u32[]{:S(2)}) collective-permute-start(f32[6,8,128]{2,1,0:T(8,128)S(1)} %get-tuple-element.87), channel_id=1, source_target_pairs={{0,192},{64,0},{128,64},{192,128},{1,193},{65,1},{129,65},{193,129... | collective-permute-start | bytes 73736 | tf_op jit(solution)/shard_map/ppermute | solution.py:318
  43.1 6.3 %collective-permute-start.14 = (f32[4,6,8,128]{3,2,1,0:T(8,128)S(1)}, f32[4,6,8,128]{3,2,1,0:T(8,128)S(1)}, u32[]{:S(2)}, u32[]{:S(2)}) collective-permute-start(f32[4,6,8,128]{3,2,1,0:T(8,128)S(1)} %pad_maximum_fusion.5.refs_0_), channel_id=1, source_target_pairs={{0,16},{8,24},{16,32},{24,40},{32,48},{40,56},{48,0},{56,8},{1,17}... | collective-permute-start | bytes 294920 | tf_op jit(solution)/shard_map/ppermute | solution.py:318
  45.2 4.4 %collective-permute-start.13 = (f32[4,6,8,128]{3,2,1,0:T(8,128)S(1)}, f32[4,6,8,128]{3,2,1,0:T(8,128)S(1)}, u32[]{:S(2)}, u32[]{:S(2)}) collective-permute-start(f32[4,6,8,128]{3,2,1,0:T(8,128)S(1)} %pad_maximum_fusion.5.refs_0_), channel_id=1, source_target_pairs={{0,48},{8,56},{16,0},{24,8},{32,16},{40,24},{48,32},{56,40},{1,49}... | collective-permute-start | bytes 294920 | tf_op jit(solution)/shard_map/ppermute | solution.py:318
  46.8 5.6 %collective-permute-start.12 = (f32[4,6,8,128]{3,2,1,0:T(8,128)S(1)}, f32[4,6,8,128]{3,2,1,0:T(8,128)S(1)}, u32[]{:S(2)}, u32[]{:S(2)}) collective-permute-start(f32[4,6,8,128]{3,2,1,0:T(8,128)S(1)} %pad_maximum_fusion.5.refs_0_), channel_id=1, source_target_pairs={{0,8},{8,16},{16,24},{24,32},{32,40},{40,48},{48,56},{56,0},{1,9},... | collective-permute-start | bytes 294920 | tf_op jit(solution)/shard_map/ppermute | solution.py:318
  47.8 4.6 %collective-permute-start.11 = (f32[4,6,8,128]{3,2,1,0:T(8,128)S(1)}, f32[4,6,8,128]{3,2,1,0:T(8,128)S(1)}, u32[]{:S(2)}, u32[]{:S(2)}) collective-permute-start(f32[4,6,8,128]{3,2,1,0:T(8,128)S(1)} %pad_maximum_fusion.5.refs_0_), channel_id=1, source_target_pairs={{0,56},{8,0},{16,8},{24,16},{32,24},{40,32},{48,40},{56,48},{1,57}... | collective-permute-start | bytes 294920 | tf_op jit(solution)/shard_map/ppermute | solution.py:318
  56.2 6.0 %collective-permute-start.15 = (f32[16,128]{1,0:T(8,128)S(1)}, f32[16,128]{1,0:T(8,128)S(1)}, u32[]{:S(2)}, u32[]{:S(2)}) collective-permute-start(f32[16,128]{1,0:T(8,128)S(1)} %get-tuple-element.45), channel_id=1, source_target_pairs={{0,7},{1,0},{2,1},{3,2},{4,3},{5,4},{6,5},{7,6},{8,15},{9,8},{10,9... | collective-permute-start | bytes 24584 | tf_op jit(solution)/shard_map/ppermute | solution.py:318
  64.7 5.5 %collective-permute-start.18 = (f32[7,16,128]{2,1,0:T(8,128)S(1)}, f32[7,16,128]{2,1,0:T(8,128)S(1)}, u32[]{:S(2)}, u32[]{:S(2)}) collective-permute-start(f32[7,16,128]{2,1,0:T(8,128)S(1)} %get-tuple-element.93), channel_id=1, source_target_pairs={{0,192},{64,0},{128,64},{192,128},{1,193},{65,1},{129,65},{193,129... | collective-permute-start | bytes 172040 | tf_op jit(solution)/shard_map/ppermute | solution.py:318
  66.0 4.2 %collective-permute-start.17 = (f32[7,16,128]{2,1,0:T(8,128)S(1)}, f32[7,16,128]{2,1,0:T(8,128)S(1)}, u32[]{:S(2)}, u32[]{:S(2)}) collective-permute-start(f32[7,16,128]{2,1,0:T(8,128)S(1)} %get-tuple-element.94), channel_id=1, source_target_pairs={{0,64},{64,128},{128,192},{192,0},{1,65},{65,129},{129,193},{193,1... | collective-permute-start | bytes 172040 | tf_op jit(solution)/shard_map/ppermute | solution.py:318
  70.3 5.1 %collective-permute-start.20 = (f32[32,8,128]{2,1,0:T(8,128)S(1)}, f32[32,8,128]{2,1,0:T(8,128)S(1)}, u32[]{:S(2)}, u32[]{:S(2)}) collective-permute-start(f32[32,8,128]{2,1,0:T(8,128)S(1)} %get-tuple-element.72), channel_id=1, source_target_pairs={{0,8},{8,16},{16,24},{24,32},{32,40},{40,48},{48,56},{56,0},{1,9},... | collective-permute-start | bytes 393224 | tf_op jit(solution)/shard_map/ppermute | solution.py:318
  71.0 4.7 %collective-permute-start.19 = (f32[32,8,128]{2,1,0:T(8,128)S(1)}, f32[32,8,128]{2,1,0:T(8,128)S(1)}, u32[]{:S(2)}, u32[]{:S(2)}) collective-permute-start(f32[32,8,128]{2,1,0:T(8,128)S(1)} %get-tuple-element.73), channel_id=1, source_target_pairs={{0,56},{8,0},{16,8},{24,16},{32,24},{40,32},{48,40},{56,48},{1,57}... | collective-permute-start | bytes 393224 | tf_op jit(solution)/shard_map/ppermute | solution.py:318
  77.5 6.9 %collective-permute-start.22 = (f32[1,8,128]{2,1,0:T(8,128)S(1)}, f32[1,8,128]{2,1,0:T(8,128)S(1)}, u32[]{:S(2)}, u32[]{:S(2)}) collective-permute-start(f32[1,8,128]{2,1,0:T(8,128)S(1)} %slice.138), channel_id=1, source_target_pairs={{0,1},{1,2},{2,3},{3,4},{4,5},{5,6},{6,7},{7,0},{8,9},{9,10},{10,1... | collective-permute-start | bytes 12296 | tf_op jit(solution)/shard_map/ppermute | solution.py:318
  79.9 4.6 %collective-permute-start.21 = (f32[1,8,128]{2,1,0:T(8,128)S(1)}, f32[1,8,128]{2,1,0:T(8,128)S(1)}, u32[]{:S(2)}, u32[]{:S(2)}) collective-permute-start(f32[1,8,128]{2,1,0:T(8,128)S(1)} %slice.138), channel_id=1, source_target_pairs={{0,7},{1,0},{2,1},{3,2},{4,3},{5,4},{6,5},{7,6},{8,15},{9,8},{10,9... | collective-permute-start | bytes 12296 | tf_op jit(solution)/shard_map/ppermute | solution.py:318
  84.5 4.1 %collective-permute-start.24 = (f32[3,8,128]{2,1,0:T(8,128)S(1)}, f32[3,8,128]{2,1,0:T(8,128)S(1)}, u32[]{:S(2)}, u32[]{:S(2)}) collective-permute-start(f32[3,8,128]{2,1,0:T(8,128)S(1)} %get-tuple-element.98), channel_id=1, source_target_pairs={{0,128},{64,192},{128,0},{192,64},{1,129},{65,193},{129,1},{193,65... | collective-permute-start | bytes 36872 | tf_op jit(solution)/shard_map/ppermute | solution.py:318
  89.5 6.3 %collective-permute-start.29 = (f32[4,3,8,128]{3,2,1,0:T(8,128)S(1)}, f32[4,3,8,128]{3,2,1,0:T(8,128)S(1)}, u32[]{:S(2)}, u32[]{:S(2)}) collective-permute-start(f32[4,3,8,128]{3,2,1,0:T(8,128)S(1)} %pad_maximum_fusion.14.refs_0_), channel_id=1, source_target_pairs={{0,16},{8,24},{16,32},{24,40},{32,48},{40,56},{48,0},{56,8},{1,17}... | collective-permute-start | bytes 147464 | tf_op jit(solution)/shard_map/ppermute | solution.py:318
  93.1 4.2 %collective-permute-start.27 = (f32[4,3,8,128]{3,2,1,0:T(8,128)S(1)}, f32[4,3,8,128]{3,2,1,0:T(8,128)S(1)}, u32[]{:S(2)}, u32[]{:S(2)}) collective-permute-start(f32[4,3,8,128]{3,2,1,0:T(8,128)S(1)} %pad_maximum_fusion.14.refs_0_), channel_id=1, source_target_pairs={{0,8},{8,16},{16,24},{24,32},{32,40},{40,48},{48,56},{56,0},{1,9},... | collective-permute-start | bytes 147464 | tf_op jit(solution)/shard_map/ppermute | solution.py:318
  101.3 8.0 %collective-permute-start.30 = (f32[16,128]{1,0:T(8,128)S(1)}, f32[16,128]{1,0:T(8,128)S(1)}, u32[]{:S(2)}, u32[]{:S(2)}) collective-permute-start(f32[16,128]{1,0:T(8,128)S(1)} %get-tuple-element.53), channel_id=1, source_target_pairs={{0,7},{1,0},{2,1},{3,2},{4,3},{5,4},{6,5},{7,6},{8,15},{9,8},{10,9... | collective-permute-start | bytes 24584 | tf_op jit(solution)/shard_map/ppermute | solution.py:318
  109.6 5.5 %collective-permute-start.33 = (f32[7,16,128]{2,1,0:T(8,128)S(1)}, f32[7,16,128]{2,1,0:T(8,128)S(1)}, u32[]{:S(2)}, u32[]{:S(2)}) collective-permute-start(f32[7,16,128]{2,1,0:T(8,128)S(1)} %get-tuple-element.91), channel_id=1, source_target_pairs={{0,192},{64,0},{128,64},{192,128},{1,193},{65,1},{129,65},{193,129... | collective-permute-start | bytes 172040 | tf_op jit(solution)/shard_map/ppermute | solution.py:318
  110.9 4.2 %collective-permute-start.32 = (f32[7,16,128]{2,1,0:T(8,128)S(1)}, f32[7,16,128]{2,1,0:T(8,128)S(1)}, u32[]{:S(2)}, u32[]{:S(2)}) collective-permute-start(f32[7,16,128]{2,1,0:T(8,128)S(1)} %get-tuple-element.92), channel_id=1, source_target_pairs={{0,64},{64,128},{128,192},{192,0},{1,65},{65,129},{129,193},{193,1... | collective-permute-start | bytes 172040 | tf_op jit(solution)/shard_map/ppermute | solution.py:318
  115.2 5.1 %collective-permute-start.35 = (f32[32,8,128]{2,1,0:T(8,128)S(1)}, f32[32,8,128]{2,1,0:T(8,128)S(1)}, u32[]{:S(2)}, u32[]{:S(2)}) collective-permute-start(f32[32,8,128]{2,1,0:T(8,128)S(1)} %get-tuple-element.70), channel_id=1, source_target_pairs={{0,8},{8,16},{16,24},{24,32},{32,40},{40,48},{48,56},{56,0},{1,9},... | collective-permute-start | bytes 393224 | tf_op jit(solution)/shard_map/ppermute | solution.py:318
  115.3 5.0 %collective-permute-start.34 = (f32[32,8,128]{2,1,0:T(8,128)S(1)}, f32[32,8,128]{2,1,0:T(8,128)S(1)}, u32[]{:S(2)}, u32[]{:S(2)}) collective-permute-start(f32[32,8,128]{2,1,0:T(8,128)S(1)} %get-tuple-element.71), channel_id=1, source_target_pairs={{0,56},{8,0},{16,8},{24,16},{32,24},{40,32},{48,40},{56,48},{1,57}... | collective-permute-start | bytes 393224 | tf_op jit(solution)/shard_map/ppermute | solution.py:318
  122.9 6.4 %collective-permute-start.37 = (f32[1,8,128]{2,1,0:T(8,128)S(1)}, f32[1,8,128]{2,1,0:T(8,128)S(1)}, u32[]{:S(2)}, u32[]{:S(2)}) collective-permute-start(f32[1,8,128]{2,1,0:T(8,128)S(1)} %slice.146), channel_id=1, source_target_pairs={{0,1},{1,2},{2,3},{3,4},{4,5},{5,6},{6,7},{7,0},{8,9},{9,10},{10,1... | collective-permute-start | bytes 12296 | tf_op jit(solution)/shard_map/ppermute | solution.py:318
  130.4 4.1 %collective-permute-start.39 = (f32[3,8,128]{2,1,0:T(8,128)S(1)}, f32[3,8,128]{2,1,0:T(8,128)S(1)}, u32[]{:S(2)}, u32[]{:S(2)}) collective-permute-start(f32[3,8,128]{2,1,0:T(8,128)S(1)} %get-tuple-element.96), channel_id=1, source_target_pairs={{0,128},{64,192},{128,0},{192,64},{1,129},{65,193},{129,1},{193,65... | collective-permute-start | bytes 36872 | tf_op jit(solution)/shard_map/ppermute | solution.py:318
  135.9 32.2 %collective-permute-start.44 = (f32[4,3,8,128]{3,2,1,0:T(8,128)S(1)}, f32[4,3,8,128]{3,2,1,0:T(8,128)S(1)}, u32[]{:S(2)}, u32[]{:S(2)}) collective-permute-start(f32[4,3,8,128]{3,2,1,0:T(8,128)S(1)} %pad_maximum_fusion.15.refs_0_), channel_id=1, source_target_pairs={{0,16},{8,24},{16,32},{24,40},{32,48},{40,56},{48,0},{56,8},{1,17}... | collective-permute-start | bytes 147464 | tf_op jit(solution)/shard_map/ppermute | solution.py:318
  137.7 30.4 %collective-permute-start.43 = (f32[4,3,8,128]{3,2,1,0:T(8,128)S(1)}, f32[4,3,8,128]{3,2,1,0:T(8,128)S(1)}, u32[]{:S(2)}, u32[]{:S(2)}) collective-permute-start(f32[4,3,8,128]{3,2,1,0:T(8,128)S(1)} %pad_maximum_fusion.15.refs_0_), channel_id=1, source_target_pairs={{0,48},{8,56},{16,0},{24,8},{32,16},{40,24},{48,32},{56,40},{1,49}... | collective-permute-start | bytes 147464 | tf_op jit(solution)/shard_map/ppermute | solution.py:318
  139.5 28.6 %collective-permute-start.42 = (f32[4,3,8,128]{3,2,1,0:T(8,128)S(1)}, f32[4,3,8,128]{3,2,1,0:T(8,128)S(1)}, u32[]{:S(2)}, u32[]{:S(2)}) collective-permute-start(f32[4,3,8,128]{3,2,1,0:T(8,128)S(1)} %pad_maximum_fusion.15.refs_0_), channel_id=1, source_target_pairs={{0,8},{8,16},{16,24},{24,32},{32,40},{40,48},{48,56},{56,0},{1,9},... | collective-permute-start | bytes 147464 | tf_op jit(solution)/shard_map/ppermute | solution.py:318
  140.2 28.0 %collective-permute-start.41 = (f32[4,3,8,128]{3,2,1,0:T(8,128)S(1)}, f32[4,3,8,128]{3,2,1,0:T(8,128)S(1)}, u32[]{:S(2)}, u32[]{:S(2)}) collective-permute-start(f32[4,3,8,128]{3,2,1,0:T(8,128)S(1)} %pad_maximum_fusion.15.refs_0_), channel_id=1, source_target_pairs={{0,56},{8,0},{16,8},{24,16},{32,24},{40,32},{48,40},{56,48},{1,57}... | collective-permute-start | bytes 147464 | tf_op jit(solution)/shard_map/ppermute | solution.py:318
  (20 other events, 62.4 us)

commit v2 on v1

v2 whole, which is shorter than its diff:
```python
import jax
import jax.numpy as jnp
from jax import lax
from jax.experimental import pallas as pl
from jax.experimental.pallas import tpu as pltpu
from jax.sharding import PartitionSpec as P

CLASSES = 16
COARSE_SWEEPS = 6
OMEGA = 0.8
KEEP = 1.0 - OMEGA
F32 = jnp.float32
SLABS, MIDS = 26, 12
MARK = 64
BLOCK, HALO, MID = (16, 16, 128), (SLABS, 32, 256), (MIDS, 32, 256)
VMEM = pl.BlockSpec(memory_space=pltpu.VMEM)
ANY = pl.BlockSpec(memory_space=pl.ANY)


def iota(shape, dim):
    return lax.broadcasted_iota(jnp.int32, shape, dim)


def roll(v, shift, axis):
    shift = shift % v.shape[axis]
    return v if shift == 0 else pltpu.roll(v, shift, axis)


def around(v, rows, lanes):
    return (roll(v, rows, 0) + roll(v, -rows, 0)) + (roll(v, lanes, 1) + roll(v, -lanes, 1))


def pair_mean(v, step):
    rows = (iota(v.shape, 0) // step) % 2 == 0
    v = v + jnp.where(rows, roll(v, -step, 0), roll(v, step, 0))
    lanes = (iota(v.shape, 1) // step) % 2 == 0
    v = v + jnp.where(lanes, roll(v, -step, 1), roll(v, step, 1))
    return v * 0.125


def place():
    return tuple(lax.axis_index(axis) for axis in ("gx", "gy", "gz"))


def sizes():
    return tuple(lax.axis_size(axis) for axis in ("gx", "gy", "gz"))


def pack_fine(read, low_ref, high_ref):
    chunk = iota((16, 128), 1) // 32
    for g in range(4):
        low = high = None
        for j in range(4):
            v = read(4 * g + j)
            first, last = roll(v, 32 * j, 1), roll(v, 32 * j + 32, 1)
            low = first if j == 0 else jnp.where(chunk == j, first, low)
            high = last if j == 0 else jnp.where(chunk == j, last, high)
        low_ref[g] = low
        high_ref[g] = high


def prepare_kernel(rhs_in, classes_in, table_in, both, low, high, classes, table, sems):
    copies = [
        pltpu.make_async_copy(rhs_in, both.at[0], sems.at[0]),
        pltpu.make_async_copy(classes_in, classes, sems.at[1]),
        pltpu.make_async_copy(table_in, table, sems.at[2]),
    ]
    for copy in copies:
        copy.start()
    for copy in copies:
        copy.wait()
    for k in range(16):
        c = classes[k]
        v = jnp.zeros((16, 128), F32)
        for index in range(CLASSES):
            v = jnp.where(c == index, table[index], v)
        both[1, k] = v
    for t in range(2):
        pack_fine(lambda k, t=t: both[t, k], low.at[t], high.at[t])


def slab_sources(i):
    x = i - 5
    if x < 0:
        k = 16 + x
        return 24 + x + 5, 29 + k // 4 - 2, 31 + k // 4 - 2, k % 4
    if x < 16:
        return x, 16 + x // 4, 20 + x // 4, x % 4
    k = x - 16
    return 33 + k, 38 + k // 4, 40 + k // 4, k % 4


def assemble_fine(body, upper, lower, i):
    def unit(u):
        return jnp.concatenate([body[u], upper[u], lower[u]], axis=0)

    main, above, below, j = slab_sources(i)
    lane = iota((32, 128), 1)
    side = jnp.where(lane < 64, roll(unit(above), -32 * j, 1), roll(unit(below), 96 - 32 * j, 1))
    return jnp.concatenate([unit(main), side], axis=1)


def near(lane):
    return (lane < 160) | (lane >= 224)


def inside_lanes(lane):
    z = jnp.where(lane < 192, lane, lane - 256) + 128 * place()[2]
    return near(lane) & (z >= 0) & (z < 128 * sizes()[2])


def inside_fine():
    row, lane = iota((32, 256), 0), iota((32, 256), 1)
    y = jnp.where(row < 24, row, row - 32) + 16 * place()[1]
    return inside_lanes(lane) & (y >= 0) & (y < 16 * sizes()[1])


def fine_weights(body, upper, lower, weight0, weight1, middle, quads, unit):
    inside, gx, nx = inside_fine(), place()[0], sizes()[0]

    def weigh(i):
        kap = assemble_fine(body, upper, lower, i)
        x = 16 * gx + (i - 5)
        weight0[i] = jnp.where(inside & (x >= 0) & (x < 16 * nx), OMEGA / (kap + 6.0), 0.0)
        return kap

    weigh(0)
    weigh(SLABS - 1)
    for m in range(MIDS):
        kap1 = pair_mean(weigh(2 * m + 1) + weigh(2 * m + 2), 1)
        middle[m] = kap1
        x = 8 * gx + (m - 2)
        weight1[m] = jnp.where(inside & (x >= 0) & (x < 8 * nx), OMEGA / (kap1 + 1.5), 0.0)
    for c in range(4):
        kap2 = pair_mean(middle[2 + 2 * c] + middle[3 + 2 * c], 2)[:16]
        weight2 = OMEGA / (kap2 + 0.375)
        quads[0, c], quads[1, c] = weight2[:, :128], weight2[:, 128:]
    pack_coarse(quads, unit)


def pack_coarse(quads, unit):
    turn = iota((4, 128), 1) % 4
    for half in range(2):
        v = quads[half, 0, pl.ds(0, 4, stride=4), :]
        for c in range(1, 4):
            v = jnp.where(turn == c, quads[half, c, pl.ds(0, 4, stride=4), :], v)
        unit[4 * half:4 * half + 4] = v


def down_sweep(body, upper, lower, weight0, weight1, x0, x1, unit, r, r1, quads):
    for i in range(SLABS):
        v = assemble_fine(body, upper, lower, i)
        r[i] = v
        x0[i] = weight0[i] * v
    for m in range(MIDS):
        i = 2 * m + 1
        two = x0[i] + x0[i + 1]
        left = KEEP * (r[i] + r[i + 1]) + ((x0[i - 1] + x0[i + 2]) + two) + around(two, 1, 1)
        v = pair_mean(left, 1)
        r1[m] = v
        x1[m] = weight1[m] * v
    for c in range(4):
        m = 2 + 2 * c
        two = x1[m] + x1[m + 1]
        left = KEEP * (r1[m] + r1[m + 1]) + 0.25 * (((x1[m - 1] + x1[m + 2]) + two) + around(two, 2, 2))
        v = pair_mean(left, 2)[:16]
        quads[0, c], quads[1, c] = v[:, :128], v[:, 128:]
    pack_coarse(quads, unit)


def first_down_kernel(body, upper, lower, weight0, weight1, x0, x1, unit, r, r1, quads):
    fine_weights(body.at[1], upper.at[1], lower.at[1], weight0, weight1, r1, quads, unit.at[1])
    down_sweep(body.at[0], upper.at[0], lower.at[0], weight0, weight1, x0, x1, unit.at[0], r, r1, quads)


def down_kernel(body, upper, lower, weight0, weight1, x0, x1, unit, r, r1, quads):
    down_sweep(body, upper, lower, weight0, weight1, x0, x1, unit, r, r1, quads)


def assemble_coarse(gather, t, out, change):
    gy, ny = place()[1], sizes()[1]
    turn = iota((16, 256), 1) % 4
    for k in range(4):
        own, up1, up2, down2, down1 = [ny * k + lax.rem(gy + d + ny, ny) for d in (0, 1, 2, -2, -1)]
        v = jnp.concatenate(
            [
                jnp.concatenate([
                    gather[own, t, s:s + 4], gather[up1, t, s:s + 4], gather[up2, t, s:s + 2],
                    gather[down2, t, s + 2:s + 4], gather[down1, t, s:s + 4],
                ], axis=0)
                for s in (0, 4)
            ],
            axis=1,
        )
        moved = {d: roll(v, d, 1) for d in range(-3, 4)}
        for c in range(4):
            slab = moved[-c]
            for j in range(1, 4):
                slab = jnp.where(turn == j, moved[j - c], slab)
            out[4 * k + c + 1] = change(4 * k + c + 1, slab)


def up_sweep(gather, weight2, weight1, weight0, x0, x1, kap, u, w, a, b, rhs2, spread, middle, t1, t0):
    zero = jnp.zeros((16, 256), F32)
    for ref in (a, b):
        ref[0] = zero
        ref[17] = zero
    assemble_coarse(gather, 0, rhs2, lambda s, v: weight2[s] * v)
    for s in range(1, 17):
        a[s] = rhs2[s]
    for sweep in range(COARSE_SWEEPS - 1):
        old, new = (a, b) if sweep % 2 == 0 else (b, a)

        def step(s, carry, old=old, new=new):
            v = old[s]
            beside = (old[s - 1] + old[s + 1]) + around(v, 1, 4)
            new[s] = (KEEP * v + rhs2[s]) + weight2[s] * (0.0625 * beside)
            return carry

        lax.fori_loop(1, 17, step, 0, unroll=4)
    last = b if COARSE_SWEEPS % 2 == 0 else a
    half = iota((8, 256), 0) < 4
    for c in range(6):
        v = last[4 * place()[0] + c]
        spread[c] = jnp.concatenate(
            [
                jnp.where(half, jnp.broadcast_to(v[j:j + 1], (8, 256)), jnp.broadcast_to(v[j + 1:j + 2], (8, 256)))
                for j in (0, 2, 4, 14)
            ],
            axis=0,
        )
    for m in range(MIDS):
        t1[m] = x1[m] + spread[m // 2]
    for m in range(1, MIDS - 1):
        v = t1[m]
        beside = (t1[m - 1] + t1[m + 1]) + around(v, 2, 2)
        middle[m] = (KEEP * v + x1[m]) + weight1[m] * (0.25 * beside)
    for i in range(3, SLABS - 3):
        t0[i] = x0[i] + middle[(i - 1) // 2]
    for i in range(4, SLABS - 4):
        v = t0[i]
        beside = (t0[i - 1] + t0[i + 1]) + around(v, 1, 1)
        u[i] = (KEEP * v + x0[i]) + weight0[i] * beside
    for i in range(5, SLABS - 5):
        v = u[i]
        beside = (u[i - 1] + u[i + 1]) + around(v, 1, 1)
        w[i - 5] = (kap[i - 5] + 6.0) * v[:16, :128] - beside[:16, :128]


def lanes_of(values):
    lane = iota((8, 128), 1)
    out = jnp.zeros((8, 128), F32)
    for k, v in enumerate(values):
        out = jnp.where(lane == MARK + k, jnp.sum(v), out)
    return out


def first_up_kernel(gather, weight1, weight0, x0, x1, both, weight2, u, w, low, high, dots, *scratch):
    (*scratch, full) = scratch
    row, lane = iota((16, 256), 0), iota((16, 256), 1)
    y = jnp.where(row < 10, row, row - 16) + 4 * place()[1]
    inside = inside_lanes(lane) & (y >= 0) & (y < 4 * sizes()[1])
    assemble_coarse(gather, 1, weight2, lambda s, v: jnp.where(inside, v, 0.0))
    up_sweep(gather, weight2, weight1, weight0, x0, x1, both.at[1], full, w, *scratch)
    rz = curve = jnp.zeros((16, 128), F32)
    for k in range(16):
        v = full[k + 5][:16, :128]
        u[k] = v
        rz = rz + both[0, k] * v
        curve = curve + w[k] * v
    dots[...] = lanes_of([rz, curve])
    pack_fine(lambda k: w[k], low, high)


def second_up_kernel(gather, weight2, weight1, weight0, x0, x1, both, u0, w0,
                     m0, n0, r1, u1, w1, low, high, first, *scratch):
    (*scratch, full) = scratch
    sums = gather[0, 0]
    for k in range(1, gather.shape[0]):
        sums = sums + gather[k, 0]
    first[...] = sums
    alpha = sums[4:5, MARK:MARK + 1] / sums[4:5, MARK + 1:MARK + 2]
    up_sweep(gather, weight2, weight1, weight0, x0, x1, both.at[1], full, n0, *scratch)
    for k in range(16):
        v = full[k + 5][:16, :128]
        m0[k] = v
        r1[k] = both[0, k] - alpha * w0[k]
        u1[k] = u0[k] - alpha * v
        w1[k] = w0[k] - alpha * n0[k]
    pack_fine(lambda k: w1[k], low, high)


def third_up_kernel(gather, weight2, weight1, weight0, x0, x1, both, w0, m0, n0, r1, u1, w1, m1, n1, dots, *scratch):
    (*scratch, full) = scratch
    up_sweep(gather, weight2, weight1, weight0, x0, x1, both.at[1], full, n1, *scratch)
    sums = [jnp.zeros((16, 128), F32)] * 12
    for k in range(16):
        vm1 = full[k + 5][:16, :128]
        m1[k] = vm1
        vw0, vm0, vn0, vr1, vu1, vw1, vn1 = w0[k], m0[k], n0[k], r1[k], u1[k], w1[k], n1[k]
        terms = [vr1 * vu1, vr1 * vm1, vr1 * vm0, vw1 * vu1, vw1 * vm1, vw1 * vm0,
                 vw0 * vu1, vw0 * vm1, vw0 * vm0, vn1 * vm1, vn1 * vm0, vn0 * vm0]
        sums = [s + t for s, t in zip(sums, terms)]
    dots[...] = lanes_of(sums)


def finish_kernel(first, second, u0, w0, m0, n0, r1, u1, w1, m1, n1, field, residual):
    g0, d0 = first[4:5, MARK:MARK + 1], first[4:5, MARK + 1:MARK + 2]
    (r1u1, r1m1, r1m0, w1u1, w1m1, w1m0, w0u1, w0m1, w0m0, n1m1, n1m0, n0m0) = [
        second[0:1, MARK + k:MARK + k + 1] for k in range(12)
    ]
    alpha0 = g0 / d0
    beta1 = r1u1 / g0
    curve1 = w1u1 + 2.0 * beta1 * w0u1 + beta1 * beta1 * d0
    alpha1 = r1u1 / curve1
    ab = alpha1 * beta1
    su = w1u1 + beta1 * w0u1 - alpha1 * (w1m1 + beta1 * w0m1) - ab * (w1m0 + beta1 * w0m0)
    g2 = (r1u1 - alpha1 * r1m1 - ab * r1m0) - alpha1 * su
    beta2 = g2 / r1u1
    uw = (w1u1 - 2.0 * alpha1 * w1m1 - 2.0 * ab * w1m0) + (alpha1 * alpha1 * n1m1 + 2.0 * alpha1 * ab * n1m0 + ab * ab * n0m0)
    curve2 = uw + 2.0 * beta2 * su + beta2 * beta2 * curve1
    alpha2 = g2 / curve2
    mix = alpha1 + alpha2 * beta2
    cu0, cu1, cm1, cm0 = alpha0 + mix * beta1, mix + alpha2, alpha2 * alpha1, alpha2 * ab
    cw0 = mix * beta1
    for k in range(16):
        field[k] = (cu0 * u0[k] + cu1 * u1[k]) - (cm1 * m1[k] + cm0 * m0[k])
        residual[k] = r1[k] - (cw0 * w0[k] + cu1 * w1[k]) + (cm1 * n1[k] + cm0 * n0[k])


def shape(*dims):
    return jax.ShapeDtypeStruct(dims, F32)


def call(kernel, outs, scratch=(), specs=None, count=0):
    return pl.pallas_call(
        kernel,
        out_shape=outs,
        in_specs=specs or [VMEM] * count,
        out_specs=[VMEM] * len(outs),
        scratch_shapes=list(scratch),
        compiler_params=pltpu.CompilerParams(vmem_limit_bytes=40 * 1024 * 1024),
    )


def shift(v, axis, distance):
    count = lax.axis_size(axis)
    return lax.ppermute(v, axis, [((i + distance) % count, i) for i in range(count)])


def fine_exchange(own, low, high, scalars=None):
    if scalars is None:
        above, below = shift(low, "gz", 1), shift(high, "gz", -1)
    else:
        above = shift(jnp.concatenate([low.reshape(8, 8, 128), scalars[None]]), "gz", 1)
        below = shift(high, "gz", -1)
        scalars = scalars + above[8]
        above = above[:8].reshape(4, 16, 128)
    first = jnp.concatenate([own[..., :5, :, :], above[..., :2, :, :], below[..., :2, :, :]], axis=-3)
    last = jnp.concatenate([own[..., 11:, :, :], above[..., 2:, :, :], below[..., 2:, :, :]], axis=-3)
    if scalars is not None:
        first, last, scalars = lax.optimization_barrier((first, last, scalars))
        scalars = scalars + shift(scalars, "gz", 2)
    before, after = shift(last, "gx", -1), shift(first, "gx", 1)
    body = jnp.concatenate([own, above, below, before, after], axis=-3)
    if scalars is not None:
        body, scalars = lax.optimization_barrier((body, scalars))
        scalars = scalars + shift(scalars, "gz", 4)
    upper, lower = shift(body[..., :8, :], "gy", 1), shift(body[..., 8:, :], "gy", -1)
    return (body, upper, lower), scalars


def gather(unit):
    count = lax.axis_size("gx") * lax.axis_size("gy")
    return lax.all_to_all(jnp.broadcast_to(unit[None], (count,) + unit.shape), ("gx", "gy"), 0, 0, tiled=True)


def total(v):
    axes = ("gx", "gy", "gz")
    count = lax.axis_size("gx") * lax.axis_size("gy") * lax.axis_size("gz")
    parts = lax.all_to_all(jnp.broadcast_to(v[None, :1], (count, 1, 128)), axes, 0, 0, tiled=True)
    return jnp.broadcast_to(parts.sum(0), (8, 128))


def local(right_side, classes, table):
    def scratch(*shapes):
        return [pltpu.VMEM(s, F32) for s in shapes]

    block, halo, mids = shape(*BLOCK), shape(*HALO), shape(*MID)
    packs, tile = shape(4, 16, 128), shape(8, 128)
    down_scratch = scratch(HALO, MID, (2, 4, 16, 128))
    up_scratch = scratch((18, 16, 256), (18, 16, 256), (18, 16, 256), (6, 32, 256), MID, MID, HALO, HALO)

    both, low, high = call(
        prepare_kernel, [shape(2, *BLOCK), shape(2, 4, 16, 128), shape(2, 4, 16, 128)],
        [pltpu.VMEM(BLOCK, jnp.int32), pltpu.SMEM((CLASSES,), F32), pltpu.SemaphoreType.DMA((3,))], specs=[ANY] * 3,
    )(right_side, classes, table)
    halos, _ = fine_exchange(both, low, high)
    weight0, weight1, x0, x1, unit = call(
        first_down_kernel, [halo, mids, halo, mids, shape(2, 8, 128)], down_scratch, count=3
    )(*halos)
    weight2, u0, w0, low, high, dots = call(
        first_up_kernel, [shape(18, 16, 256), block, block, packs, packs, tile], up_scratch, count=6
    )(gather(unit), weight1, weight0, x0, x1, both)

    down = call(down_kernel, [halo, mids, tile], down_scratch, count=5)
    halos, scalars = fine_exchange(w0, low, high, dots)
    x0, x1, unit = down(*halos, weight0, weight1)
    free = (iota((8, 128), 0) >= 4) & (iota((8, 128), 1) >= 32) & (iota((8, 128), 1) < 96)
    unit = jnp.where(free, scalars, unit)
    m0, n0, r1, u1, w1, low, high, first = call(
        second_up_kernel, [block] * 5 + [packs, packs, tile], up_scratch, count=9
    )(gather(unit[None]), weight2, weight1, weight0, x0, x1, both, u0, w0)

    halos, _ = fine_exchange(w1, low, high)
    x0, x1, unit = down(*halos, weight0, weight1)
    m1, n1, dots = call(third_up_kernel, [block] * 2 + [tile], up_scratch, count=13)(
        gather(unit[None]), weight2, weight1, weight0, x0, x1, both, w0, m0, n0, r1, u1, w1
    )
    field, residual = call(finish_kernel, [block] * 2, count=11)(
        first, total(dots), u0, w0, m0, n0, r1, u1, w1, m1, n1
    )
    return field, residual


def solution(mesh):
    in_specs = (P("gx", "gy", "gz"), P("gx", "gy", "gz"), P())
    out_specs = (P("gx", "gy", "gz"), P("gx", "gy", "gz"))
    return jax.shard_map(local, mesh=mesh, in_specs=in_specs, out_specs=out_specs, check_vma=False)
```

time: 196 us -> 159 us (0.81)
  starting transfers between devices: 74.1 us -> 39 us
  blocking collectives: 46.2 us -> 73.4 us
  waiting for transfers between devices: 47.5 us -> 24 us
  Pallas kernels: 21.3 us -> 18.5 us
  local copies, waits for them, and re-layouts: 5.18 us -> 2.85 us
    ppermute x45 -> x20, starting transfers between devices: 74.1 us -> 39 us  [shift(): lax.ppermute(v, axis, [((i + distance) % count, i) for i in range(count)])]
    all_to_all x4, blocking collectives: 46.2 us -> 73.4 us  [the longest x3 48 us: gather(): lax.all_to_all(jnp.broadcast_to(unit[None], (count,) + unit.shape), ('gx'...]
    ppermute x45 -> x20, waiting for transfers between devices: 47.5 us -> 24 us  [shift(): lax.ppermute(v, axis, [((i + distance) % count, i) for i in range(count)])]
    pallas_call x9 -> x8, Pallas kernels: 21.3 us -> 18.5 us  [the longest x2 3.43 us: local(): x0, x1, unit = down(*halos, weight0, weight1)]
    unnamed x25 -> x18, local copies, waits for them, and re-layouts: 4.92 us -> 2.55 us
  transfers between devices with their start and end apart: 45 -> 20, of which waited for: 29 -> 14; matrix products, arithmetic and copies ran while one was open for 0% -> 0% of each run, Pallas kernels for 0% -> 1%
where the time goes in v2:
time: 159 us
  blocking collectives  73.4 us (46%)
  starting transfers between devices  39 us (25%)
  waiting for transfers between devices  24 us (15%)
  Pallas kernels  18.5 us (12%)
  local copies, waits for them, and re-layouts  2.85 us (2%)
    all_to_all x3, blocking collectives, gather(): lax.all_to_all(jnp.broadcast_to(unit[None], (count,) + unit.shape), ('gx'...  48 us
    ppermute x20, starting transfers between devices, shift(): lax.ppermute(v, axis, [((i + distance) % count, i) for i in range(count)])  39 us
    all_to_all x1, blocking collectives, total(): lax.all_to_all(jnp.broadcast_to(v[None, :1], (count, 1, 128)), axes, 0, 0...  25.4 us
    ppermute x20, waiting for transfers between devices, shift(): lax.ppermute(v, axis, [((i + distance) % count, i) for i in range(count)])  24 us
    pallas_call x2, Pallas kernels, local(): x0, x1, unit = down(*halos, weight0, weight1)  3.43 us
    pallas_call x1, Pallas kernels, local(): call(first_up_kernel, [shape(18, 16, 256), block, block, packs, packs, ti...  3.32 us
    pallas_call x1, Pallas kernels, local(): call(third_up_kernel, [block] * 2 + [tile], up_scratch, count=13)  3.28 us
    pallas_call x1, Pallas kernels, local(): call(second_up_kernel, [block] * 5 + [packs, packs, tile], up_scratch, co...  3.19 us
  transfers between devices with their start and end apart: 20, of which 14 were waited for; matrix products, arithmetic and copies ran while one was open for 0% of the time, Pallas kernels for 1%

profile of v2, /device:TPU:1, one launch (start us, length us, event | category | flops | bytes accessed | tf_op | source)
XLA Modules:
  0.0 158.8 jit_solution(13933271083976391474)
XLA Ops:
  3.1 1.1 shard_map.50
  4.2 3.3 %collective-permute-start = (f32[2,4,16,128]{3,2,1,0:T(8,128)S(1)}, f32[2,4,16,128]{3,2,1,0:T(8,128)S(1)}, u32[]{:S(2)}, u32[]{:S(2)}) collective-permute-start(f32[2,4,16,128]{3,2,1,0:T(8,128)S(1)} %get-tuple-element.39), channel_id=1, source_target_pairs={{1,0},{2,1},{3,2},{4,3},{5,4},{6,5},{7,6},{0,7},{9,8},{10,9},{11,1... | collective-permute-start | bytes 196616 | tf_op jit(solution)/shard_map/ppermute | solution.py:348
  7.5 1.4 collective-permute-done
  8.9 1.3 collective-permute-start.2
  10.2 1.5 collective-permute-start.3
  11.8 2.4 %collective-permute-done.2 = f32[2,9,16,128]{3,2,1,0:T(8,128)S(1)} collective-permute-done((f32[2,9,16,128]{3,2,1,0:T(8,128)S(1)}, f32[2,9,16,128]{3,2,1,0:T(8,128)S(1)}, u32[]{:S(2)}, u32[]{:S(2)}) %collective-permute-start.2) | collective-permute-done | bytes 147488 | tf_op jit(solution)/shard_map/ppermute | solution.py:348
  14.4 1.7 %collective-permute-start.5 = (f32[2,42,8,128]{3,2,1,0:T(8,128)S(1)}, f32[2,42,8,128]{3,2,1,0:T(8,128)S(1)}, u32[]{:S(2)}, u32[]{:S(2)}) collective-permute-start(f32[2,42,8,128]{3,2,1,0:T(8,128)S(1)} %get-tuple-element.74), channel_id=1, source_target_pairs={{56,0},{0,8},{8,16},{16,24},{24,32},{32,40},{40,48},{48,56},{57,1}... | collective-permute-start | bytes 1032200 | tf_op jit(solution)/shard_map/ppermute | solution.py:348
  16.1 4.0 %collective-permute-start.4 = (f32[2,42,8,128]{3,2,1,0:T(8,128)S(1)}, f32[2,42,8,128]{3,2,1,0:T(8,128)S(1)}, u32[]{:S(2)}, u32[]{:S(2)}) collective-permute-start(f32[2,42,8,128]{3,2,1,0:T(8,128)S(1)} %get-tuple-element.75), channel_id=1, source_target_pairs={{8,0},{16,8},{24,16},{32,24},{40,32},{48,40},{56,48},{0,56},{9,1},... | collective-permute-start | bytes 1032200 | tf_op jit(solution)/shard_map/ppermute | solution.py:348
  20.1 4.5 %collective-permute-done.5.lower = f32[2,42,8,128]{3,2,1,0:T(8,128)S(1)} collective-permute-done((f32[2,42,8,128]{3,2,1,0:T(8,128)S(1)}, f32[2,42,8,128]{3,2,1,0:T(8,128)S(1)}, u32[]{:S(2)}, u32[]{:S(2)}) %collective-permute-start.5) | collective-permute-done | bytes 344096 | tf_op jit(solution)/shard_map/ppermute | solution.py:348
  24.7 2.9 %shard_map.51 = (f32[26,32,256]{2,1,0:T(8,128)S(1)}, f32[12,32,256]{2,1,0:T(8,128)S(1)}, f32[26,32,256]{2,1,0:T(8,128)S(1)}, f32[12,32,256]{2,1,0:T(8,128)S(1)}, f32[2,8,128]{2,1,0:T(8,128)S(1)}) custom-call(f32[2,42,16,128]{3,2,1,0:T(8,128)S(1)} %constant_dynamic-update-slice_fusion.body, f32[2,42,8,128]{3,2,1,0:T(8,128)S(1)} %collective-permute-done.4.upper, ...), custom_call_target="tpu_custom_call" | custom-call | tf_op jit(solution)/shard_map/pallas_call | solution.py:399
  27.6 17.8 %all_to_all.20.gather = f32[32,2,8,128]{3,2,1,0:T(8,128)S(1)} all-to-all(f32[32,2,8,128]{3,2,1,0:T(8,128)S(1)} %broadcast_in_dim.14), channel_id=1, replica_groups=mesh['gx'=4,'gy'=8,'gz'=8] {'gx','gy'}, dimensions={0} | all-to-all | bytes 524288 | tf_op jit(solution)/shard_map/all_to_all | solution.py:375
  45.4 3.3 %shard_map.52 = (f32[18,16,256]{2,1,0:T(8,128)S(1)}, f32[16,16,128]{2,1,0:T(8,128)S(1)}, f32[16,16,128]{2,1,0:T(8,128)S(1)}, f32[4,16,128]{2,1,0:T(8,128)S(1)}, ...) custom-call(f32[32,2,8,128]{3,2,1,0:T(8,128)S(1)} %all_to_all.20.gather, f32[12,32,256]{2,1,0:T(8,128)S(1)} %get-tuple-element.42.weight1, ...), custom_call_target="tpu_custom_call" | custom-call | tf_op jit(solution)/shard_map/pallas_call | solution.py:402
  48.7 8.1 %collective-permute-start.7 = (f32[4,16,128]{2,1,0:T(8,128)S(1)}, f32[4,16,128]{2,1,0:T(8,128)S(1)}, u32[]{:S(2)}, u32[]{:S(2)}) collective-permute-start(f32[4,16,128]{2,1,0:T(8,128)S(1)} %get-tuple-element.49), channel_id=1, source_target_pairs={{7,0},{0,1},{1,2},{2,3},{3,4},{4,5},{5,6},{6,7},{15,8},{8,9},{9,10... | collective-permute-start | bytes 98312 | tf_op jit(solution)/shard_map/ppermute | solution.py:348
  57.9 2.3 %collective-permute-done.6 = f32[9,8,128]{2,1,0:T(8,128)S(1)} collective-permute-done((f32[9,8,128]{2,1,0:T(8,128)S(1)}, f32[9,8,128]{2,1,0:T(8,128)S(1)}, u32[]{:S(2)}, u32[]{:S(2)}) %collective-permute-start.6) | collective-permute-done | bytes 36896 | tf_op jit(solution)/shard_map/ppermute | solution.py:348
  60.2 4.2 %collective-permute-start.10 = (f32[8,128]{1,0:T(8,128)S(1)}, f32[8,128]{1,0:T(8,128)S(1)}, u32[]{:S(2)}, u32[]{:S(2)}) collective-permute-start(f32[8,128]{1,0:T(8,128)S(1)} %fusion), channel_id=1, source_target_pairs={{2,0},{3,1},{4,2},{5,3},{6,4},{7,5},{0,6},{1,7},{10,8},{11,9},{12,... | collective-permute-start | bytes 12296 | tf_op jit(solution)/shard_map/ppermute | solution.py:348
  64.8 2.3 %collective-permute-start.9 = (f32[9,16,128]{2,1,0:T(8,128)S(1)}, f32[9,16,128]{2,1,0:T(8,128)S(1)}, u32[]{:S(2)}, u32[]{:S(2)}) collective-permute-start(f32[9,16,128]{2,1,0:T(8,128)S(1)} %get-tuple-element.51), channel_id=1, source_target_pairs={{64,0},{128,64},{192,128},{0,192},{65,1},{129,65},{193,129},{1,193... | collective-permute-start | bytes 221192 | tf_op jit(solution)/shard_map/ppermute | solution.py:348
  67.2 2.6 %collective-permute-done.8 = f32[9,16,128]{2,1,0:T(8,128)S(1)} collective-permute-done((f32[9,16,128]{2,1,0:T(8,128)S(1)}, f32[9,16,128]{2,1,0:T(8,128)S(1)}, u32[]{:S(2)}, u32[]{:S(2)}) %collective-permute-start.8) | collective-permute-done | bytes 73760 | tf_op jit(solution)/shard_map/ppermute | solution.py:348
  69.8 1.8 %collective-permute-start.13 = (f32[42,8,128]{2,1,0:T(8,128)S(1)}, f32[42,8,128]{2,1,0:T(8,128)S(1)}, u32[]{:S(2)}, u32[]{:S(2)}) collective-permute-start(f32[42,8,128]{2,1,0:T(8,128)S(1)} %get-tuple-element.78), channel_id=1, source_target_pairs={{56,0},{0,8},{8,16},{16,24},{24,32},{32,40},{40,48},{48,56},{57,1}... | collective-permute-start | bytes 516104 | tf_op jit(solution)/shard_map/ppermute | solution.py:348
  72.6 3.9 %collective-permute-done.13.lower = f32[42,8,128]{2,1,0:T(8,128)S(1)} collective-permute-done((f32[42,8,128]{2,1,0:T(8,128)S(1)}, f32[42,8,128]{2,1,0:T(8,128)S(1)}, u32[]{:S(2)}, u32[]{:S(2)}) %collective-permute-start.13) | collective-permute-done | bytes 172064 | tf_op jit(solution)/shard_map/ppermute | solution.py:348
  76.8 1.7 %shard_map.53 = (f32[26,32,256]{2,1,0:T(8,128)S(1)}, f32[12,32,256]{2,1,0:T(8,128)S(1)}, f32[8,128]{1,0:T(8,128)S(1)}) custom-call(f32[42,16,128]{2,1,0:T(8,128)S(1)} %constant_dynamic-update-slice_fusion.5.body, f32[42,8,128]{2,1,0:T(8,128)S(1)} %collective-permute-done.12.upper, f32[42,8,128]{2,1,0:T(8,128)S(1)} %collective-permute-done.13.lower, ...), custom_call_target="tpu_custom_call" | custom-call | tf_op jit(solution)/shard_map/pallas_call | solution.py:408
  78.7 14.6 %all_to_all.21.gather = f32[32,1,8,128]{3,2,1,0:T(8,128)S(1)} all-to-all(f32[32,1,8,128]{3,2,1,0:T(8,128)S(1)} %broadcast_in_dim.16), channel_id=1, replica_groups=mesh['gx'=4,'gy'=8,'gz'=8] {'gx','gy'}, dimensions={0} | all-to-all | bytes 262144 | tf_op jit(solution)/shard_map/all_to_all | solution.py:375
  93.2 3.2 %shard_map.54 = (f32[16,16,128]{2,1,0:T(8,128)S(1)}, f32[16,16,128]{2,1,0:T(8,128)S(1)}, f32[16,16,128]{2,1,0:T(8,128)S(1)}, f32[16,16,128]{2,1,0:T(8,128)S(1)},...) custom-call(f32[32,1,8,128]{3,2,1,0:T(8,128)S(1)} %all_to_all.21.gath, ...), custom_call_target="tpu_custom_call" | custom-call | tf_op jit(solution)/shard_map/pallas_call | solution.py:411
  96.4 3.5 %collective-permute-start.14 = (f32[4,16,128]{2,1,0:T(8,128)S(1)}, f32[4,16,128]{2,1,0:T(8,128)S(1)}, u32[]{:S(2)}, u32[]{:S(2)}) collective-permute-start(f32[4,16,128]{2,1,0:T(8,128)S(1)} %get-tuple-element.62), channel_id=1, source_target_pairs={{1,0},{2,1},{3,2},{4,3},{5,4},{6,5},{7,6},{0,7},{9,8},{10,9},{11,1... | collective-permute-start | bytes 98312 | tf_op jit(solution)/shard_map/ppermute | solution.py:348
  101.6 2.3 %collective-permute-start.17 = (f32[9,16,128]{2,1,0:T(8,128)S(1)}, f32[9,16,128]{2,1,0:T(8,128)S(1)}, u32[]{:S(2)}, u32[]{:S(2)}) collective-permute-start(f32[9,16,128]{2,1,0:T(8,128)S(1)} %pad_maximum_fusion.5), channel_id=1, source_target_pairs={{64,0},{128,64},{192,128},{0,192},{65,1},{129,65},{193,129},{1,193... | collective-permute-start | bytes 221192 | tf_op jit(solution)/shard_map/ppermute | solution.py:348
  103.9 1.7 %collective-permute-done.16 = f32[9,16,128]{2,1,0:T(8,128)S(1)} collective-permute-done((f32[9,16,128]{2,1,0:T(8,128)S(1)}, f32[9,16,128]{2,1,0:T(8,128)S(1)}, u32[]{:S(2)}, u32[]{:S(2)}) %collective-permute-start.16) | collective-permute-done | bytes 73760 | tf_op jit(solution)/shard_map/ppermute | solution.py:348
  106.6 1.9 %collective-permute-start.18 = (f32[42,8,128]{2,1,0:T(8,128)S(1)}, f32[42,8,128]{2,1,0:T(8,128)S(1)}, u32[]{:S(2)}, u32[]{:S(2)}) collective-permute-start(f32[42,8,128]{2,1,0:T(8,128)S(1)} %get-tuple-element.77), channel_id=1, source_target_pairs={{8,0},{16,8},{24,16},{32,24},{40,32},{48,40},{56,48},{0,56},{9,1},... | collective-permute-start | bytes 516104 | tf_op jit(solution)/shard_map/ppermute | solution.py:348
  108.5 2.8 %collective-permute-done.19.lower = f32[42,8,128]{2,1,0:T(8,128)S(1)} collective-permute-done((f32[42,8,128]{2,1,0:T(8,128)S(1)}, f32[42,8,128]{2,1,0:T(8,128)S(1)}, u32[]{:S(2)}, u32[]{:S(2)}) %collective-permute-start.19) | collective-permute-done | bytes 172064 | tf_op jit(solution)/shard_map/ppermute | solution.py:348
  111.3 1.7 %shard_map.55 = (f32[26,32,256]{2,1,0:T(8,128)S(1)}, f32[12,32,256]{2,1,0:T(8,128)S(1)}, f32[8,128]{1,0:T(8,128)S(1)}) custom-call(f32[42,16,128]{2,1,0:T(8,128)S(1)} %constant_dynamic-update-slice_fusion.10.body, f32[42,8,128]{2,1,0:T(8,128)S(1)} %collective-permute-done.18.upper, f32[42,8,128]{2,1,0:T(8,128)S(1)} %collective-permute-done.19.lower, ...), custom_call_target="tpu_custom_call" | custom-call | tf_op jit(solution)/shard_map/pallas_call | solution.py:416
  113.0 15.7 %all_to_all.22.gather = f32[32,1,8,128]{3,2,1,0:T(8,128)S(1)} all-to-all(f32[32,1,8,128]{3,2,1,0:T(8,128)S(1)} %broadcast_in_dim.17), channel_id=1, replica_groups=mesh['gx'=4,'gy'=8,'gz'=8] {'gx','gy'}, dimensions={0} | all-to-all | bytes 262144 | tf_op jit(solution)/shard_map/all_to_all | solution.py:375
  128.7 3.3 %shard_map.56 = (f32[16,16,128]{2,1,0:T(8,128)S(1)}, f32[16,16,128]{2,1,0:T(8,128)S(1)}, f32[8,128]{1,0:T(8,128)S(1)}) custom-call(f32[32,1,8,128]{3,2,1,0:T(8,128)S(1)} %all_to_all.22.gather, f32[18,16,256]{2,1,0:T(8,128)S(1)} %get-tuple-element.56.weight2, f32[12,32,256]{2,1,0:T(8,128)S(1)} %get-tuple-element.42.weight1, ...), custom_call_target="tpu_custom_call" | custom-call | tf_op jit(solution)/shard_map/pallas_call | solution.py:417
  132.0 25.4 %all_to_all.23 = f32[256,1,128]{2,1,0:T(1,128)S(1)} all-to-all(f32[256,1,128]{2,1,0:T(1,128)S(1)} %broadcast_in_dim.37), channel_id=1, replica_groups=mesh['gx'=4,'gy'=8,'gz'=8] {'gx','gy','gz'}, dimensions={0} | all-to-all | bytes 262144 | tf_op jit(solution)/shard_map/all_to_all | solution.py:381
  157.4 1.3 shard_map.57
  (72 shorter events, 8.5 us)
Async XLA Ops:
  0.6 0.9 copy-start
  1.5 0.9 copy-start.1
  2.4 0.7 copy-start.2
  4.2 4.6 %collective-permute-start = (f32[2,4,16,128]{3,2,1,0:T(8,128)S(1)}, f32[2,4,16,128]{3,2,1,0:T(8,128)S(1)}, u32[]{:S(2)}, u32[]{:S(2)}) collective-permute-start(f32[2,4,16,128]{3,2,1,0:T(8,128)S(1)} %get-tuple-element.39), channel_id=1, source_target_pairs={{1,0},{2,1},{3,2},{4,3},{5,4},{6,5},{7,6},{0,7},{9,8},{10,9},{11,1... | collective-permute-start | bytes 196616 | tf_op jit(solution)/shard_map/ppermute | solution.py:348
  7.5 1.5 collective-permute-start.1
  8.9 5.3 %collective-permute-start.2 = (f32[2,9,16,128]{3,2,1,0:T(8,128)S(1)}, f32[2,9,16,128]{3,2,1,0:T(8,128)S(1)}, u32[]{:S(2)}, u32[]{:S(2)}) collective-permute-start(f32[2,9,16,128]{3,2,1,0:T(8,128)S(1)} %pad_maximum_fusion), channel_id=1, source_target_pairs={{192,0},{0,64},{64,128},{128,192},{193,1},{1,65},{65,129},{129,193... | collective-permute-start | bytes 442376 | tf_op jit(solution)/shard_map/ppermute | solution.py:348
  10.2 4.1 %collective-permute-start.3 = (f32[2,9,16,128]{3,2,1,0:T(8,128)S(1)}, f32[2,9,16,128]{3,2,1,0:T(8,128)S(1)}, u32[]{:S(2)}, u32[]{:S(2)}) collective-permute-start(f32[2,9,16,128]{3,2,1,0:T(8,128)S(1)} %pad_maximum_fusion.1), channel_id=1, source_target_pairs={{64,0},{128,64},{192,128},{0,192},{65,1},{129,65},{193,129},{1,193... | collective-permute-start | bytes 442376 | tf_op jit(solution)/shard_map/ppermute | solution.py:348
  14.4 10.3 %collective-permute-start.5 = (f32[2,42,8,128]{3,2,1,0:T(8,128)S(1)}, f32[2,42,8,128]{3,2,1,0:T(8,128)S(1)}, u32[]{:S(2)}, u32[]{:S(2)}) collective-permute-start(f32[2,42,8,128]{3,2,1,0:T(8,128)S(1)} %get-tuple-element.74), channel_id=1, source_target_pairs={{56,0},{0,8},{8,16},{16,24},{24,32},{32,40},{40,48},{48,56},{57,1}... | collective-permute-start | bytes 1032200 | tf_op jit(solution)/shard_map/ppermute | solution.py:348
  16.1 8.6 %collective-permute-start.4 = (f32[2,42,8,128]{3,2,1,0:T(8,128)S(1)}, f32[2,42,8,128]{3,2,1,0:T(8,128)S(1)}, u32[]{:S(2)}, u32[]{:S(2)}) collective-permute-start(f32[2,42,8,128]{3,2,1,0:T(8,128)S(1)} %get-tuple-element.75), channel_id=1, source_target_pairs={{8,0},{16,8},{24,16},{32,24},{40,32},{48,40},{56,48},{0,56},{9,1},... | collective-permute-start | bytes 1032200 | tf_op jit(solution)/shard_map/ppermute | solution.py:348
  48.7 9.2 %collective-permute-start.7 = (f32[4,16,128]{2,1,0:T(8,128)S(1)}, f32[4,16,128]{2,1,0:T(8,128)S(1)}, u32[]{:S(2)}, u32[]{:S(2)}) collective-permute-start(f32[4,16,128]{2,1,0:T(8,128)S(1)} %get-tuple-element.49), channel_id=1, source_target_pairs={{7,0},{0,1},{1,2},{2,3},{3,4},{4,5},{5,6},{6,7},{15,8},{8,9},{9,10... | collective-permute-start | bytes 98312 | tf_op jit(solution)/shard_map/ppermute | solution.py:348
  56.8 3.4 %collective-permute-start.6 = (f32[9,8,128]{2,1,0:T(8,128)S(1)}, f32[9,8,128]{2,1,0:T(8,128)S(1)}, u32[]{:S(2)}, u32[]{:S(2)}) collective-permute-start(f32[9,8,128]{2,1,0:T(8,128)S(1)} %pad_maximum_fusion.6), channel_id=1, source_target_pairs={{1,0},{2,1},{3,2},{4,3},{5,4},{6,5},{7,6},{0,7},{9,8},{10,9},{11,1... | collective-permute-start | bytes 110600 | tf_op jit(solution)/shard_map/ppermute | solution.py:348
  60.2 6.9 %collective-permute-start.10 = (f32[8,128]{1,0:T(8,128)S(1)}, f32[8,128]{1,0:T(8,128)S(1)}, u32[]{:S(2)}, u32[]{:S(2)}) collective-permute-start(f32[8,128]{1,0:T(8,128)S(1)} %fusion), channel_id=1, source_target_pairs={{2,0},{3,1},{4,2},{5,3},{6,4},{7,5},{0,6},{1,7},{10,8},{11,9},{12,... | collective-permute-start | bytes 12296 | tf_op jit(solution)/shard_map/ppermute | solution.py:348
  64.5 5.3 %collective-permute-start.8 = (f32[9,16,128]{2,1,0:T(8,128)S(1)}, f32[9,16,128]{2,1,0:T(8,128)S(1)}, u32[]{:S(2)}, u32[]{:S(2)}) collective-permute-start(f32[9,16,128]{2,1,0:T(8,128)S(1)} %get-tuple-element.50), channel_id=1, source_target_pairs={{192,0},{0,64},{64,128},{128,192},{193,1},{1,65},{65,129},{129,193... | collective-permute-start | bytes 221192 | tf_op jit(solution)/shard_map/ppermute | solution.py:348
  64.8 5.0 %collective-permute-start.9 = (f32[9,16,128]{2,1,0:T(8,128)S(1)}, f32[9,16,128]{2,1,0:T(8,128)S(1)}, u32[]{:S(2)}, u32[]{:S(2)}) collective-permute-start(f32[9,16,128]{2,1,0:T(8,128)S(1)} %get-tuple-element.51), channel_id=1, source_target_pairs={{64,0},{128,64},{192,128},{0,192},{65,1},{129,65},{193,129},{1,193... | collective-permute-start | bytes 221192 | tf_op jit(solution)/shard_map/ppermute | solution.py:348
  69.8 6.6 %collective-permute-start.13 = (f32[42,8,128]{2,1,0:T(8,128)S(1)}, f32[42,8,128]{2,1,0:T(8,128)S(1)}, u32[]{:S(2)}, u32[]{:S(2)}) collective-permute-start(f32[42,8,128]{2,1,0:T(8,128)S(1)} %get-tuple-element.78), channel_id=1, source_target_pairs={{56,0},{0,8},{8,16},{16,24},{24,32},{32,40},{40,48},{48,56},{57,1}... | collective-permute-start | bytes 516104 | tf_op jit(solution)/shard_map/ppermute | solution.py:348
  71.6 5.2 %collective-permute-start.12 = (f32[42,8,128]{2,1,0:T(8,128)S(1)}, f32[42,8,128]{2,1,0:T(8,128)S(1)}, u32[]{:S(2)}, u32[]{:S(2)}) collective-permute-start(f32[42,8,128]{2,1,0:T(8,128)S(1)} %get-tuple-element.79), channel_id=1, source_target_pairs={{8,0},{16,8},{24,16},{32,24},{40,32},{48,40},{56,48},{0,56},{9,1},... | collective-permute-start | bytes 516104 | tf_op jit(solution)/shard_map/ppermute | solution.py:348
  72.6 6.0 %collective-permute-start.11 = (f32[8,128]{1,0:T(8,128)S(1)}, f32[8,128]{1,0:T(8,128)S(1)}, u32[]{:S(2)}, u32[]{:S(2)}) collective-permute-start(f32[8,128]{1,0:T(8,128)S(1)} %add.10), channel_id=1, source_target_pairs={{4,0},{5,1},{6,2},{7,3},{0,4},{1,5},{2,6},{3,7},{12,8},{13,9},{14,... | collective-permute-start | bytes 12296 | tf_op jit(solution)/shard_map/ppermute | solution.py:348
  96.4 4.3 %collective-permute-start.14 = (f32[4,16,128]{2,1,0:T(8,128)S(1)}, f32[4,16,128]{2,1,0:T(8,128)S(1)}, u32[]{:S(2)}, u32[]{:S(2)}) collective-permute-start(f32[4,16,128]{2,1,0:T(8,128)S(1)} %get-tuple-element.62), channel_id=1, source_target_pairs={{1,0},{2,1},{3,2},{4,3},{5,4},{6,5},{7,6},{0,7},{9,8},{10,9},{11,1... | collective-permute-start | bytes 98312 | tf_op jit(solution)/shard_map/ppermute | solution.py:348
  99.9 1.2 collective-permute-start.15
  101.2 4.5 %collective-permute-start.16 = (f32[9,16,128]{2,1,0:T(8,128)S(1)}, f32[9,16,128]{2,1,0:T(8,128)S(1)}, u32[]{:S(2)}, u32[]{:S(2)}) collective-permute-start(f32[9,16,128]{2,1,0:T(8,128)S(1)} %pad_maximum_fusion.4), channel_id=1, source_target_pairs={{192,0},{0,64},{64,128},{128,192},{193,1},{1,65},{65,129},{129,193... | collective-permute-start | bytes 221192 | tf_op jit(solution)/shard_map/ppermute | solution.py:348
  101.6 4.0 %collective-permute-start.17 = (f32[9,16,128]{2,1,0:T(8,128)S(1)}, f32[9,16,128]{2,1,0:T(8,128)S(1)}, u32[]{:S(2)}, u32[]{:S(2)}) collective-permute-start(f32[9,16,128]{2,1,0:T(8,128)S(1)} %pad_maximum_fusion.5), channel_id=1, source_target_pairs={{64,0},{128,64},{192,128},{0,192},{65,1},{129,65},{193,129},{1,193... | collective-permute-start | bytes 221192 | tf_op jit(solution)/shard_map/ppermute | solution.py:348
  105.7 5.5 %collective-permute-start.19 = (f32[42,8,128]{2,1,0:T(8,128)S(1)}, f32[42,8,128]{2,1,0:T(8,128)S(1)}, u32[]{:S(2)}, u32[]{:S(2)}) collective-permute-start(f32[42,8,128]{2,1,0:T(8,128)S(1)} %get-tuple-element.76), channel_id=1, source_target_pairs={{56,0},{0,8},{8,16},{16,24},{24,32},{32,40},{40,48},{48,56},{57,1}... | collective-permute-start | bytes 516104 | tf_op jit(solution)/shard_map/ppermute | solution.py:348
  106.6 4.7 %collective-permute-start.18 = (f32[42,8,128]{2,1,0:T(8,128)S(1)}, f32[42,8,128]{2,1,0:T(8,128)S(1)}, u32[]{:S(2)}, u32[]{:S(2)}) collective-permute-start(f32[42,8,128]{2,1,0:T(8,128)S(1)} %get-tuple-element.77), channel_id=1, source_target_pairs={{8,0},{16,8},{24,16},{32,24},{40,32},{48,40},{56,48},{0,56},{9,1},... | collective-permute-start | bytes 516104 | tf_op jit(solution)/shard_map/ppermute | solution.py:348

commit v3 on v2

--- a/solution.py
+++ b/solution.py
@@ -10,7 +10,7 @@
 OMEGA = 0.8
 KEEP = 1.0 - OMEGA
 F32 = jnp.float32
-SLABS, MIDS = 26, 12
+SLABS, MIDS, UNITS = 26, 12, 40
 MARK = 64
 BLOCK, HALO, MID = (16, 16, 128), (SLABS, 32, 256), (MIDS, 32, 256)
 VMEM = pl.BlockSpec(memory_space=pltpu.VMEM)
@@ -47,7 +47,8 @@
 
 
 def pack_fine(read, low_ref, high_ref):
-    chunk = iota((16, 128), 1) // 32
+    lane = iota((16, 128), 1)
+    chunk = lane // 32
     for g in range(4):
         low = high = None
         for j in range(4):
@@ -55,6 +56,14 @@
             first, last = roll(v, 32 * j, 1), roll(v, 32 * j + 32, 1)
             low = first if j == 0 else jnp.where(chunk == j, first, low)
             high = last if j == 0 else jnp.where(chunk == j, last, high)
+        low_ref[g] = low
+        high_ref[g] = high
+    for g, slabs in ((4, (0, 1, 2, 3, 4)), (5, (15, 14, 13, 12, 11))):
+        low, high = read(slabs[0]), roll(read(slabs[0]), 32, 1)
+        for j in range(1, 5):
+            v, here = read(slabs[j]), (lane >= 112 if j == 4 else chunk == j)
+            low = jnp.where(here, roll(v, 112 if j == 4 else 32 * j, 1), low)
+            high = jnp.where(here, roll(v, (32, 64, 96, 112, 0)[j], 1), high)
         low_ref[g] = low
         high_ref[g] = high
 
@@ -81,23 +90,36 @@
 
 def slab_sources(i):
     x = i - 5
-    if x < 0:
-        k = 16 + x
-        return 24 + x + 5, 29 + k // 4 - 2, 31 + k // 4 - 2, k % 4
-    if x < 16:
-        return x, 16 + x // 4, 20 + x // 4, x % 4
-    k = x - 16
-    return 33 + k, 38 + k // 4, 40 + k // 4, k % 4
-
-
-def assemble_fine(body, upper, lower, i):
+    if 0 <= x < 16:
+        return x, 16 + x // 4, 20 + x // 4, -32 * (x % 4), 96 - 32 * (x % 4)
+    base, far = (24, -1 - x) if x < 0 else (31, x - 16)
+    return base + (x + 5 if x < 0 else far), base + 5, base + 6, (0, -32, -64, -96, -112)[far], (96, 64, 32, 16, 0)[far]
+
+
+def assemble_fine(body, sides, i):
     def unit(u):
-        return jnp.concatenate([body[u], upper[u], lower[u]], axis=0)
-
-    main, above, below, j = slab_sources(i)
+        return jnp.concatenate([body[u][...], sides[u][...]], axis=0)
+
+    main, above, below, up, down = slab_sources(i)
     lane = iota((32, 128), 1)
-    side = jnp.where(lane < 64, roll(unit(above), -32 * j, 1), roll(unit(below), 96 - 32 * j, 1))
+    side = jnp.where(lane < 64, roll(unit(above), up, 1), roll(unit(below), down, 1))
     return jnp.concatenate([unit(main), side], axis=1)
+
+
+def pack_rows_kernel(body, upper, lower):
+    for g in range(body.shape[0] // 128):
+        for t in range(5):
+            upper[5 * g + t] = body[pl.ds(128 * g + t, 8, stride=16), :]
+            lower[5 * g + t] = body[pl.ds(128 * g + 11 + t, 8, stride=16), :]
+
+
+def unpack_rows(upper, lower, first, sides):
+    sides[...] = jnp.zeros(sides.shape, F32)
+    for g in range(UNITS // 8):
+        for t in range(5):
+            sides[pl.ds(128 * g + t, 8, stride=16), :] = upper[first + 5 * g + t]
+            sides[pl.ds(128 * g + 11 + t, 8, stride=16), :] = lower[first + 5 * g + t]
+    return [sides.at[pl.ds(16 * u, 16)] for u in range(UNITS)]
 
 
 def near(lane):
@@ -115,11 +137,11 @@
     return inside_lanes(lane) & (y >= 0) & (y < 16 * sizes()[1])
 
 
-def fine_weights(body, upper, lower, weight0, weight1, middle, quads, unit):
+def fine_weights(body, sides, weight0, weight1, middle, quads, unit):
     inside, gx, nx = inside_fine(), place()[0], sizes()[0]
 
     def weigh(i):
-        kap = assemble_fine(body, upper, lower, i)
+        kap = assemble_fine(body, sides, i)
         x = 16 * gx + (i - 5)
         weight0[i] = jnp.where(inside & (x >= 0) & (x < 16 * nx), OMEGA / (kap + 6.0), 0.0)
         return kap
@@ -147,9 +169,9 @@
         unit[4 * half:4 * half + 4] = v
 
 
-def down_sweep(body, upper, lower, weight0, weight1, x0, x1, unit, r, r1, quads):
+def down_sweep(body, sides, weight0, weight1, x0, x1, unit, r, r1, quads):
     for i in range(SLABS):
-        v = assemble_fine(body, upper, lower, i)
+        v = assemble_fine(body, sides, i)
         r[i] = v
         x0[i] = weight0[i] * v
     for m in range(MIDS):
@@ -168,13 +190,20 @@
     pack_coarse(quads, unit)
 
 
-def first_down_kernel(body, upper, lower, weight0, weight1, x0, x1, unit, r, r1, quads):
-    fine_weights(body.at[1], upper.at[1], lower.at[1], weight0, weight1, r1, quads, unit.at[1])
-    down_sweep(body.at[0], upper.at[0], lower.at[0], weight0, weight1, x0, x1, unit.at[0], r, r1, quads)
-
-
-def down_kernel(body, upper, lower, weight0, weight1, x0, x1, unit, r, r1, quads):
-    down_sweep(body, upper, lower, weight0, weight1, x0, x1, unit, r, r1, quads)
+def units(body, first):
+    return [body.at[pl.ds(first + 16 * u, 16)] for u in range(UNITS)]
+
+
+def first_down_kernel(body, upper, lower, weight0, weight1, x0, x1, unit, r, r1, quads, sides, more):
+    kap_sides = unpack_rows(upper, lower, 5 * UNITS // 8, more)
+    fine_weights(units(body, 16 * UNITS), kap_sides, weight0, weight1, r1, quads, unit.at[1])
+    r_sides = unpack_rows(upper, lower, 0, sides)
+    down_sweep(units(body, 0), r_sides, weight0, weight1, x0, x1, unit.at[0], r, r1, quads)
+
+
+def down_kernel(body, upper, lower, weight0, weight1, x0, x1, unit, r, r1, quads, sides):
+    r_sides = unpack_rows(upper, lower, 0, sides)
+    down_sweep(units(body, 0), r_sides, weight0, weight1, x0, x1, unit, r, r1, quads)
 
 
 def assemble_coarse(gather, t, out, change):
@@ -211,13 +240,10 @@
     for sweep in range(COARSE_SWEEPS - 1):
         old, new = (a, b) if sweep % 2 == 0 else (b, a)
 
-        def step(s, carry, old=old, new=new):
+        for s in range(1, 17):
             v = old[s]
             beside = (old[s - 1] + old[s + 1]) + around(v, 1, 4)
             new[s] = (KEEP * v + rhs2[s]) + weight2[s] * (0.0625 * beside)
-            return carry
-
-        lax.fori_loop(1, 17, step, 0, unroll=4)
     last = b if COARSE_SWEEPS % 2 == 0 else a
     half = iota((8, 256), 0) < 4
     for c in range(6):
@@ -332,14 +358,14 @@
     return jax.ShapeDtypeStruct(dims, F32)
 
 
-def call(kernel, outs, scratch=(), specs=None, count=0):
+def call(kernel, outs, scratch=(), specs=None, count=0, grant=40):
     return pl.pallas_call(
         kernel,
         out_shape=outs,
         in_specs=specs or [VMEM] * count,
         out_specs=[VMEM] * len(outs),
         scratch_shapes=list(scratch),
-        compiler_params=pltpu.CompilerParams(vmem_limit_bytes=40 * 1024 * 1024),
+        compiler_params=pltpu.CompilerParams(vmem_limit_bytes=grant * 1024 * 1024),
     )
 
 
@@ -352,21 +378,23 @@
     if scalars is None:
         above, below = shift(low, "gz", 1), shift(high, "gz", -1)
     else:
-        above = shift(jnp.concatenate([low.reshape(8, 8, 128), scalars[None]]), "gz", 1)
-        below = shift(high, "gz", -1)
-        scalars = scalars + above[8]
-        above = above[:8].reshape(4, 16, 128)
-    first = jnp.concatenate([own[..., :5, :, :], above[..., :2, :, :], below[..., :2, :, :]], axis=-3)
-    last = jnp.concatenate([own[..., 11:, :, :], above[..., 2:, :, :], below[..., 2:, :, :]], axis=-3)
+        above = shift(jnp.concatenate([low.reshape(12, 8, 128), scalars[None]]), "gz", 1)
+        below = shift(jnp.concatenate([high.reshape(12, 8, 128), scalars[None]]), "gz", -1)
+        two = scalars + below[12]
+        three = two + above[12]
+        above, below = above[:12].reshape(6, 16, 128), below[:12].reshape(6, 16, 128)
+    first = jnp.concatenate([own[..., :5, :, :], above[..., 4:5, :, :], below[..., 4:5, :, :]], axis=-3)
+    last = jnp.concatenate([own[..., 11:, :, :], above[..., 5:6, :, :], below[..., 5:6, :, :]], axis=-3)
+    before, after = shift(last, "gx", -1), shift(first, "gx", 1)
+    parts = [own, above[..., :4, :, :], below[..., :4, :, :], before, after, own[..., :2, :, :]]
+    body = jnp.concatenate(parts, axis=-3).reshape(-1, 128)
+    tiles = body.shape[0] // 16 // 8 * 5
+    upper, lower = call(pack_rows_kernel, [shape(tiles, 8, 128)] * 2, count=1)(body)
     if scalars is not None:
-        first, last, scalars = lax.optimization_barrier((first, last, scalars))
-        scalars = scalars + shift(scalars, "gz", 2)
-    before, after = shift(last, "gx", -1), shift(first, "gx", 1)
-    body = jnp.concatenate([own, above, below, before, after], axis=-3)
+        upper, lower, two, three = lax.optimization_barrier((upper, lower, two, three))
+    upper, lower = shift(upper, "gy", 1), shift(lower, "gy", -1)
     if scalars is not None:
-        body, scalars = lax.optimization_barrier((body, scalars))
-        scalars = scalars + shift(scalars, "gz", 4)
-    upper, lower = shift(body[..., :8, :], "gy", 1), shift(body[..., 8:, :], "gy", -1)
+        scalars = (three + shift(three, "gz", 3)) + shift(two, "gz", -2)
     return (body, upper, lower), scalars
 
 
@@ -387,17 +415,17 @@
         return [pltpu.VMEM(s, F32) for s in shapes]
 
     block, halo, mids = shape(*BLOCK), shape(*HALO), shape(*MID)
-    packs, tile = shape(4, 16, 128), shape(8, 128)
-    down_scratch = scratch(HALO, MID, (2, 4, 16, 128))
+    packs, tile = shape(6, 16, 128), shape(8, 128)
+    down_scratch = scratch(HALO, MID, (2, 4, 16, 128), (16 * UNITS, 128))
     up_scratch = scratch((18, 16, 256), (18, 16, 256), (18, 16, 256), (6, 32, 256), MID, MID, HALO, HALO)
 
     both, low, high = call(
-        prepare_kernel, [shape(2, *BLOCK), shape(2, 4, 16, 128), shape(2, 4, 16, 128)],
-        [pltpu.VMEM(BLOCK, jnp.int32), pltpu.SMEM((CLASSES,), F32), pltpu.SemaphoreType.DMA((3,))], specs=[ANY] * 3,
+        prepare_kernel, [shape(2, *BLOCK), shape(2, 6, 16, 128), shape(2, 6, 16, 128)],
+        [pltpu.VMEM(BLOCK, jnp.int32), pltpu.SMEM((CLASSES,), F32), pltpu.SemaphoreType.DMA((3,))], specs=[ANY] * 3, grant=60,
     )(right_side, classes, table)
     halos, _ = fine_exchange(both, low, high)
     weight0, weight1, x0, x1, unit = call(
-        first_down_kernel, [halo, mids, halo, mids, shape(2, 8, 128)], down_scratch, count=3
+        first_down_kernel, [halo, mids, halo, mids, shape(2, 8, 128)], down_scratch + scratch((16 * UNITS, 128)), count=3
     )(*halos)
     weight2, u0, w0, low, high, dots = call(
         first_up_kernel, [shape(18, 16, 256), block, block, packs, packs, tile], up_scratch, count=6

time: 159 us -> 154 us (0.969)
  blocking collectives: 73.4 us -> 59.6 us
  waiting for transfers between devices: 24 us -> 31.6 us
  starting transfers between devices: 39 us -> 43.7 us
  Pallas kernels: 18.5 us -> 15.4 us
    all_to_all x3 -> x2, blocking collectives: 48 us -> 34.1 us  [gather(): lax.all_to_all(jnp.broadcast_to(unit[None], (count,) + unit.shape), ('gx'...]
    all_to_all x0 -> x1, waiting for transfers between devices: none -> 9.64 us  [gather(): lax.all_to_all(jnp.broadcast_to(unit[None], (count,) + unit.shape), ('gx'...]
    all_to_all x0 -> x1, starting transfers between devices: none -> 5.49 us  [gather(): lax.all_to_all(jnp.broadcast_to(unit[None], (count,) + unit.shape), ('gx'...]
    unnamed x18 -> x17, local copies, waits for them, and re-layouts: 2.55 us -> 0.11 us
    ppermute x20, waiting for transfers between devices: 24 us -> 21.9 us  [shift(): lax.ppermute(v, axis, [((i + distance) % count, i) for i in range(count)])]
  transfers between devices with their start and end apart: 20 -> 21, of which waited for: 14 -> 16; matrix products, arithmetic and copies ran while one was open for 0% -> 1% of each run, Pallas kernels for 1% -> 1%
where the time goes in v3:
time: 154 us; the launch traced here: 153 us
  blocking collectives  59.6 us (39%)
  starting transfers between devices  43.7 us (28%)
  waiting for transfers between devices  31.6 us (21%)
  Pallas kernels  15.4 us (10%)
  local copies, waits for them, and re-layouts  1.92 us (1%)
    ppermute x20, starting transfers between devices, shift(): lax.ppermute(v, axis, [((i + distance) % count, i) for i in range(count)])  38.2 us
    all_to_all x2, blocking collectives, gather(): lax.all_to_all(jnp.broadcast_to(unit[None], (count,) + unit.shape), ('gx'...  34.1 us
    all_to_all x1, blocking collectives, total(): lax.all_to_all(jnp.broadcast_to(v[None, :1], (count, 1, 128)), axes, 0, 0...  25.5 us
    ppermute x20, waiting for transfers between devices, shift(): lax.ppermute(v, axis, [((i + distance) % count, i) for i in range(count)])  21.9 us
    all_to_all x1, waiting for transfers between devices, gather(): lax.all_to_all(jnp.broadcast_to(unit[None], (count,) + unit.shape), ('gx'...  9.64 us
    all_to_all x1, starting transfers between devices, gather(): lax.all_to_all(jnp.broadcast_to(unit[None], (count,) + unit.shape), ('gx'...  5.49 us
    pallas_call x2, Pallas kernels, local(): x0, x1, unit = down(*halos, weight0, weight1)  3.55 us
  transfers between devices with their start and end apart: 21, of which 16 were waited for; matrix products, arithmetic and copies ran while one was open for 1% of the time, Pallas kernels for 1%

profile of v3, /device:TPU:1, one launch (start us, length us, event | category | flops | bytes accessed | tf_op | source)
XLA Modules:
  0.0 153.3 jit_solution(2065629230661598396)
XLA Ops:
  0.6 1.9 %shard_map.50 = (f32[2,16,16,128]{3,2,1,0:T(8,128)}, f32[2,6,16,128]{3,2,1,0:T(8,128)}, f32[2,6,16,128]{3,2,1,0:T(8,128)}) custom-call(f32[16,16,128]{2,1,0:T(8,128)} %rhs_in.1, s32[16,16,128]{2,1,0:T(8,128)} %classes_in.1, f32[16]{0:T(128)} %table_in.1), custom_call_target="tpu_custom_call" | custom-call | tf_op jit(solution)/shard_map/pallas_call | solution.py:422
  2.6 3.3 %collective-permute-start = (f32[2,6,16,128]{3,2,1,0:T(8,128)}, f32[2,6,16,128]{3,2,1,0:T(8,128)S(1)}, u32[]{:S(2)}, u32[]{:S(2)}) collective-permute-start(f32[2,6,16,128]{3,2,1,0:T(8,128)} %get-tuple-element.44), channel_id=1, source_target_pairs={{1,0},{2,1},{3,2},{4,3},{5,4},{6,5},{7,6},{0,7},{9,8},{10,9},{11,1... | collective-permute-start | bytes 294920 | tf_op jit(solution)/shard_map/ppermute | solution.py:374
  9.1 1.5 %collective-permute-start.3 = (f32[2,7,16,128]{3,2,1,0:T(8,128)S(1)}, f32[2,7,16,128]{3,2,1,0:T(8,128)S(1)}, u32[]{:S(2)}, u32[]{:S(2)}) collective-permute-start(f32[2,7,16,128]{3,2,1,0:T(8,128)S(1)} %pad_maximum_fusion.1), channel_id=1, source_target_pairs={{64,0},{128,64},{192,128},{0,192},{65,1},{129,65},{193,129},{1,193... | collective-permute-start | bytes 344072 | tf_op jit(solution)/shard_map/ppermute | solution.py:374
  10.7 2.1 %collective-permute-done.2 = f32[2,7,16,128]{3,2,1,0:T(8,128)S(1)} collective-permute-done((f32[2,7,16,128]{3,2,1,0:T(8,128)S(1)}, f32[2,7,16,128]{3,2,1,0:T(8,128)S(1)}, u32[]{:S(2)}, u32[]{:S(2)}) %collective-permute-start.2) | collective-permute-done | bytes 114720 | tf_op jit(solution)/shard_map/ppermute | solution.py:374
  13.0 5.7 %collective-permute-start.4 = (f32[50,8,128]{2,1,0:T(8,128)S(1)}, f32[50,8,128]{2,1,0:T(8,128)S(1)}, u32[]{:S(2)}, u32[]{:S(2)}) collective-permute-start(f32[50,8,128]{2,1,0:T(8,128)S(1)} %get-tuple-element.46), channel_id=1, source_target_pairs={{8,0},{16,8},{24,16},{32,24},{40,32},{48,40},{56,48},{0,56},{9,1},... | collective-permute-start | bytes 614408 | tf_op jit(solution)/shard_map/ppermute | solution.py:374
  18.7 2.7 %collective-permute-done.4.upper = f32[50,8,128]{2,1,0:T(8,128)S(1)} collective-permute-done((f32[50,8,128]{2,1,0:T(8,128)S(1)}, f32[50,8,128]{2,1,0:T(8,128)S(1)}, u32[]{:S(2)}, u32[]{:S(2)}) %collective-permute-start.4) | collective-permute-done | bytes 204832 | tf_op jit(solution)/shard_map/ppermute | solution.py:374
  21.4 3.1 %collective-permute-done.5.lower = f32[50,8,128]{2,1,0:T(8,128)S(1)} collective-permute-done((f32[50,8,128]{2,1,0:T(8,128)S(1)}, f32[50,8,128]{2,1,0:T(8,128)S(1)}, u32[]{:S(2)}, u32[]{:S(2)}) %collective-permute-start.5) | collective-permute-done | bytes 204832 | tf_op jit(solution)/shard_map/ppermute | solution.py:374
  24.5 2.9 %shard_map.52 = (f32[26,32,256]{2,1,0:T(8,128)S(1)}, f32[12,32,256]{2,1,0:T(8,128)S(1)}, f32[26,32,256]{2,1,0:T(8,128)S(1)}, f32[12,32,256]{2,1,0:T(8,128)S(1)}, f32[2,8,128]{2,1,0:T(8,128)S(1)}) custom-call(f32[1280,128]{1,0:T(8,128)S(1)} %bitcast.33, f32[50,8,128]{2,1,0:T(8,128)S(1)} %collective-permute-done.4.upper, ...), custom_call_target="tpu_custom_call" | custom-call | tf_op jit(solution)/shard_map/pallas_call | solution.py:427
  28.1 5.5 %all-to-all-start = ((f32[32,2,8,128]{3,2,1,0:T(8,128)}), f32[32,2,8,128]{3,2,1,0:T(8,128)S(1)}, u32[]{:S(2)}, u32[]{:S(2)}) async-start(f32[32,2,8,128]{3,2,1,0:T(8,128)} %broadcast_in_dim.14), calls=%async_computation | async-start | bytes 524288 | tf_op jit(solution)/shard_map/all_to_all | solution.py:403
  33.6 9.6 %all-to-all-done.gather = f32[32,2,8,128]{3,2,1,0:T(8,128)S(1)} async-done(((f32[32,2,8,128]{3,2,1,0:T(8,128)}), f32[32,2,8,128]{3,2,1,0:T(8,128)S(1)}, u32[]{:S(2)}, u32[]{:S(2)}) %all-to-all-start) | async-done | bytes 262176 | tf_op jit(solution)/shard_map/all_to_all | solution.py:403
  43.3 1.8 %shard_map.53 = (f32[18,16,256]{2,1,0:T(8,128)S(1)}, f32[16,16,128]{2,1,0:T(8,128)S(1)}, f32[16,16,128]{2,1,0:T(8,128)S(1)}, f32[6,16,128]{2,1,0:T(8,128)S(1)}, ...) custom-call(f32[32,2,8,128]{3,2,1,0:T(8,128)S(1)} %all-to-all-done.gather, f32[12,32,256]{2,1,0:T(8,128)S(1)} %get-tuple-element.49.weight1, ...), custom_call_target="tpu_custom_call" | custom-call | tf_op jit(solution)/shard_map/pallas_call | solution.py:430
  45.1 6.4 %collective-permute-start.7 = (f32[13,8,128]{2,1,0:T(8,128)S(1)}, f32[13,8,128]{2,1,0:T(8,128)S(1)}, u32[]{:S(2)}, u32[]{:S(2)}) collective-permute-start(f32[13,8,128]{2,1,0:T(8,128)S(1)} %get-tuple-element.104), channel_id=1, source_target_pairs={{7,0},{0,1},{1,2},{2,3},{3,4},{4,5},{5,6},{6,7},{15,8},{8,9},{9,10... | collective-permute-start | bytes 159752 | tf_op jit(solution)/shard_map/ppermute | solution.py:374
  51.6 1.9 %collective-permute-start.6 = (f32[13,8,128]{2,1,0:T(8,128)S(1)}, f32[13,8,128]{2,1,0:T(8,128)S(1)}, u32[]{:S(2)}, u32[]{:S(2)}) collective-permute-start(f32[13,8,128]{2,1,0:T(8,128)S(1)} %get-tuple-element.105), channel_id=1, source_target_pairs={{1,0},{2,1},{3,2},{4,3},{5,4},{6,5},{7,6},{0,7},{9,8},{10,9},{11,1... | collective-permute-start | bytes 159752 | tf_op jit(solution)/shard_map/ppermute | solution.py:374
  55.6 2.3 %collective-permute-start.9 = (f32[7,16,128]{2,1,0:T(8,128)S(1)}, f32[7,16,128]{2,1,0:T(8,128)S(1)}, u32[]{:S(2)}, u32[]{:S(2)}) collective-permute-start(f32[7,16,128]{2,1,0:T(8,128)S(1)} %pad_maximum_fusion.5), channel_id=1, source_target_pairs={{64,0},{128,64},{192,128},{0,192},{65,1},{129,65},{193,129},{1,193... | collective-permute-start | bytes 172040 | tf_op jit(solution)/shard_map/ppermute | solution.py:374
  58.0 1.5 collective-permute-done.8
  59.6 1.3 collective-permute-start.11
  60.9 5.7 %collective-permute-start.10 = (f32[8,128]{1,0:T(8,128)S(1)}, f32[8,128]{1,0:T(8,128)S(1)}, u32[]{:S(2)}, u32[]{:S(2)}) collective-permute-start(f32[8,128]{1,0:T(8,128)S(1)} %get-tuple-element.59), channel_id=1, source_target_pairs={{3,0},{4,1},{5,2},{6,3},{7,4},{0,5},{1,6},{2,7},{11,8},{12,9},{13,... | collective-permute-start | bytes 12296 | tf_op jit(solution)/shard_map/ppermute | solution.py:374
  66.7 1.6 %collective-permute-start.13 = (f32[25,8,128]{2,1,0:T(8,128)S(1)}, f32[25,8,128]{2,1,0:T(8,128)S(1)}, u32[]{:S(2)}, u32[]{:S(2)}) collective-permute-start(f32[25,8,128]{2,1,0:T(8,128)S(1)} %get-tuple-element.62), channel_id=1, source_target_pairs={{56,0},{0,8},{8,16},{16,24},{24,32},{32,40},{40,48},{48,56},{57,1}... | collective-permute-start | bytes 307208 | tf_op jit(solution)/shard_map/ppermute | solution.py:374
  68.4 3.1 %collective-permute-done.12.upper = f32[25,8,128]{2,1,0:T(8,128)S(1)} collective-permute-done((f32[25,8,128]{2,1,0:T(8,128)S(1)}, f32[25,8,128]{2,1,0:T(8,128)S(1)}, u32[]{:S(2)}, u32[]{:S(2)}) %collective-permute-start.12) | collective-permute-done | bytes 102432 | tf_op jit(solution)/shard_map/ppermute | solution.py:374
  72.0 1.8 %shard_map.55 = (f32[26,32,256]{2,1,0:T(8,128)S(1)}, f32[12,32,256]{2,1,0:T(8,128)S(1)}, f32[8,128]{1,0:T(8,128)S(1)}) custom-call(f32[640,128]{1,0:T(8,128)S(1)} %bitcast.35, f32[25,8,128]{2,1,0:T(8,128)S(1)} %collective-permute-done.12.upper, f32[25,8,128]{2,1,0:T(8,128)S(1)} %collective-permute-done.13.lower, ...), custom_call_target="tpu_custom_call" | custom-call | tf_op jit(solution)/shard_map/pallas_call | solution.py:436
  73.9 17.9 %all_to_all.20.gather = f32[32,1,8,128]{3,2,1,0:T(8,128)S(1)} all-to-all(f32[32,1,8,128]{3,2,1,0:T(8,128)S(1)} %broadcast_in_dim.16), channel_id=1, replica_groups=mesh['gx'=4,'gy'=8,'gz'=8] {'gx','gy'}, dimensions={0} | all-to-all | bytes 262144 | tf_op jit(solution)/shard_map/all_to_all | solution.py:403
  91.7 1.8 %shard_map.56 = (f32[16,16,128]{2,1,0:T(8,128)S(1)}, f32[16,16,128]{2,1,0:T(8,128)S(1)}, f32[16,16,128]{2,1,0:T(8,128)S(1)}, f32[16,16,128]{2,1,0:T(8,128)S(1)},...) custom-call(f32[32,1,8,128]{3,2,1,0:T(8,128)S(1)} %all_to_all.20.gath, ...), custom_call_target="tpu_custom_call" | custom-call | tf_op jit(solution)/shard_map/pallas_call | solution.py:439
  93.5 2.4 %collective-permute-start.14 = (f32[6,16,128]{2,1,0:T(8,128)S(1)}, f32[6,16,128]{2,1,0:T(8,128)S(1)}, u32[]{:S(2)}, u32[]{:S(2)}) collective-permute-start(f32[6,16,128]{2,1,0:T(8,128)S(1)} %get-tuple-element.70), channel_id=1, source_target_pairs={{1,0},{2,1},{3,2},{4,3},{5,4},{6,5},{7,6},{0,7},{9,8},{10,9},{11,1... | collective-permute-start | bytes 147464 | tf_op jit(solution)/shard_map/ppermute | solution.py:374
  97.6 2.3 %collective-permute-start.17 = (f32[7,16,128]{2,1,0:T(8,128)S(1)}, f32[7,16,128]{2,1,0:T(8,128)S(1)}, u32[]{:S(2)}, u32[]{:S(2)}) collective-permute-start(f32[7,16,128]{2,1,0:T(8,128)S(1)} %pad_maximum_fusion.7), channel_id=1, source_target_pairs={{64,0},{128,64},{192,128},{0,192},{65,1},{129,65},{193,129},{1,193... | collective-permute-start | bytes 172040 | tf_op jit(solution)/shard_map/ppermute | solution.py:374
  99.9 1.5 %collective-permute-done.16 = f32[7,16,128]{2,1,0:T(8,128)S(1)} collective-permute-done((f32[7,16,128]{2,1,0:T(8,128)S(1)}, f32[7,16,128]{2,1,0:T(8,128)S(1)}, u32[]{:S(2)}, u32[]{:S(2)}) %collective-permute-start.16) | collective-permute-done | bytes 57376 | tf_op jit(solution)/shard_map/ppermute | solution.py:374
  101.8 1.3 collective-permute-start.19
  103.1 2.3 %collective-permute-done.18.upper = f32[25,8,128]{2,1,0:T(8,128)S(1)} collective-permute-done((f32[25,8,128]{2,1,0:T(8,128)S(1)}, f32[25,8,128]{2,1,0:T(8,128)S(1)}, u32[]{:S(2)}, u32[]{:S(2)}) %collective-permute-start.18) | collective-permute-done | bytes 102432 | tf_op jit(solution)/shard_map/ppermute | solution.py:374
  106.5 1.8 %shard_map.58 = (f32[26,32,256]{2,1,0:T(8,128)S(1)}, f32[12,32,256]{2,1,0:T(8,128)S(1)}, f32[8,128]{1,0:T(8,128)S(1)}) custom-call(f32[640,128]{1,0:T(8,128)S(1)} %bitcast.37, f32[25,8,128]{2,1,0:T(8,128)S(1)} %collective-permute-done.18.upper, f32[25,8,128]{2,1,0:T(8,128)S(1)} %collective-permute-done.19.lower, ...), custom_call_target="tpu_custom_call" | custom-call | tf_op jit(solution)/shard_map/pallas_call | solution.py:444
  108.3 16.2 %all_to_all.21.gather = f32[32,1,8,128]{3,2,1,0:T(8,128)S(1)} all-to-all(f32[32,1,8,128]{3,2,1,0:T(8,128)S(1)} %broadcast_in_dim.17), channel_id=1, replica_groups=mesh['gx'=4,'gy'=8,'gz'=8] {'gx','gy'}, dimensions={0} | all-to-all | bytes 262144 | tf_op jit(solution)/shard_map/all_to_all | solution.py:403
  124.5 1.8 %shard_map.59 = (f32[16,16,128]{2,1,0:T(8,128)S(1)}, f32[16,16,128]{2,1,0:T(8,128)S(1)}, f32[8,128]{1,0:T(8,128)S(1)}) custom-call(f32[32,1,8,128]{3,2,1,0:T(8,128)S(1)} %all_to_all.21.gather, f32[18,16,256]{2,1,0:T(8,128)S(1)} %get-tuple-element.64.weight2, f32[12,32,256]{2,1,0:T(8,128)S(1)} %get-tuple-element.49.weight1, ...), custom_call_target="tpu_custom_call" | custom-call | tf_op jit(solution)/shard_map/pallas_call | solution.py:445
  126.4 25.5 %all_to_all.22 = f32[256,1,128]{2,1,0:T(1,128)S(1)} all-to-all(f32[256,1,128]{2,1,0:T(1,128)S(1)} %broadcast_in_dim.38), channel_id=1, replica_groups=mesh['gx'=4,'gy'=8,'gz'=8] {'gx','gy','gz'}, dimensions={0} | all-to-all | bytes 262144 | tf_op jit(solution)/shard_map/all_to_all | solution.py:409
  152.0 1.3 shard_map.60
  (73 shorter events, 10.4 us)
Async XLA Ops:
  2.6 4.2 %copy-start = (f32[2,16,16,128]{3,2,1,0:T(8,128)S(1)}, f32[2,16,16,128]{3,2,1,0:T(8,128)}, u32[]{:S(2)}) copy-start(f32[2,16,16,128]{3,2,1,0:T(8,128)} %get-tuple-element.43.both) | copy-start | bytes 786436
  2.6 5.2 %collective-permute-start = (f32[2,6,16,128]{3,2,1,0:T(8,128)}, f32[2,6,16,128]{3,2,1,0:T(8,128)S(1)}, u32[]{:S(2)}, u32[]{:S(2)}) collective-permute-start(f32[2,6,16,128]{3,2,1,0:T(8,128)} %get-tuple-element.44), channel_id=1, source_target_pairs={{1,0},{2,1},{3,2},{4,3},{5,4},{6,5},{7,6},{0,7},{9,8},{10,9},{11,1... | collective-permute-start | bytes 294920 | tf_op jit(solution)/shard_map/ppermute | solution.py:374
  5.8 2.0 %collective-permute-start.1 = (f32[2,6,16,128]{3,2,1,0:T(8,128)}, f32[2,6,16,128]{3,2,1,0:T(8,128)S(1)}, u32[]{:S(2)}, u32[]{:S(2)}) collective-permute-start(f32[2,6,16,128]{3,2,1,0:T(8,128)} %get-tuple-element.45), channel_id=1, source_target_pairs={{7,0},{0,1},{1,2},{2,3},{3,4},{4,5},{5,6},{6,7},{15,8},{8,9},{9,10... | collective-permute-start | bytes 294920 | tf_op jit(solution)/shard_map/ppermute | solution.py:374
  7.8 4.9 %collective-permute-start.2 = (f32[2,7,16,128]{3,2,1,0:T(8,128)S(1)}, f32[2,7,16,128]{3,2,1,0:T(8,128)S(1)}, u32[]{:S(2)}, u32[]{:S(2)}) collective-permute-start(f32[2,7,16,128]{3,2,1,0:T(8,128)S(1)} %pad_maximum_fusion), channel_id=1, source_target_pairs={{192,0},{0,64},{64,128},{128,192},{193,1},{1,65},{65,129},{129,193... | collective-permute-start | bytes 344072 | tf_op jit(solution)/shard_map/ppermute | solution.py:374
  9.1 3.7 %collective-permute-start.3 = (f32[2,7,16,128]{3,2,1,0:T(8,128)S(1)}, f32[2,7,16,128]{3,2,1,0:T(8,128)S(1)}, u32[]{:S(2)}, u32[]{:S(2)}) collective-permute-start(f32[2,7,16,128]{3,2,1,0:T(8,128)S(1)} %pad_maximum_fusion.1), channel_id=1, source_target_pairs={{64,0},{128,64},{192,128},{0,192},{65,1},{129,65},{193,129},{1,193... | collective-permute-start | bytes 344072 | tf_op jit(solution)/shard_map/ppermute | solution.py:374
  13.0 8.4 %collective-permute-start.4 = (f32[50,8,128]{2,1,0:T(8,128)S(1)}, f32[50,8,128]{2,1,0:T(8,128)S(1)}, u32[]{:S(2)}, u32[]{:S(2)}) collective-permute-start(f32[50,8,128]{2,1,0:T(8,128)S(1)} %get-tuple-element.46), channel_id=1, source_target_pairs={{8,0},{16,8},{24,16},{32,24},{40,32},{48,40},{56,48},{0,56},{9,1},... | collective-permute-start | bytes 614408 | tf_op jit(solution)/shard_map/ppermute | solution.py:374
  18.7 5.8 %collective-permute-start.5 = (f32[50,8,128]{2,1,0:T(8,128)S(1)}, f32[50,8,128]{2,1,0:T(8,128)S(1)}, u32[]{:S(2)}, u32[]{:S(2)}) collective-permute-start(f32[50,8,128]{2,1,0:T(8,128)S(1)} %get-tuple-element.47), channel_id=1, source_target_pairs={{56,0},{0,8},{8,16},{16,24},{24,32},{32,40},{40,48},{48,56},{57,1}... | collective-permute-start | bytes 614408 | tf_op jit(solution)/shard_map/ppermute | solution.py:374
  28.1 15.1 %all-to-all-start = ((f32[32,2,8,128]{3,2,1,0:T(8,128)}), f32[32,2,8,128]{3,2,1,0:T(8,128)S(1)}, u32[]{:S(2)}, u32[]{:S(2)}) async-start(f32[32,2,8,128]{3,2,1,0:T(8,128)} %broadcast_in_dim.14), calls=%async_computation | async-start | bytes 524288 | tf_op jit(solution)/shard_map/all_to_all | solution.py:403
  45.1 9.0 %collective-permute-start.7 = (f32[13,8,128]{2,1,0:T(8,128)S(1)}, f32[13,8,128]{2,1,0:T(8,128)S(1)}, u32[]{:S(2)}, u32[]{:S(2)}) collective-permute-start(f32[13,8,128]{2,1,0:T(8,128)S(1)} %get-tuple-element.104), channel_id=1, source_target_pairs={{7,0},{0,1},{1,2},{2,3},{3,4},{4,5},{5,6},{6,7},{15,8},{8,9},{9,10... | collective-permute-start | bytes 159752 | tf_op jit(solution)/shard_map/ppermute | solution.py:374
  51.6 3.6 %collective-permute-start.6 = (f32[13,8,128]{2,1,0:T(8,128)S(1)}, f32[13,8,128]{2,1,0:T(8,128)S(1)}, u32[]{:S(2)}, u32[]{:S(2)}) collective-permute-start(f32[13,8,128]{2,1,0:T(8,128)S(1)} %get-tuple-element.105), channel_id=1, source_target_pairs={{1,0},{2,1},{3,2},{4,3},{5,4},{6,5},{7,6},{0,7},{9,8},{10,9},{11,1... | collective-permute-start | bytes 159752 | tf_op jit(solution)/shard_map/ppermute | solution.py:374
  55.2 4.3 %collective-permute-start.8 = (f32[7,16,128]{2,1,0:T(8,128)S(1)}, f32[7,16,128]{2,1,0:T(8,128)S(1)}, u32[]{:S(2)}, u32[]{:S(2)}) collective-permute-start(f32[7,16,128]{2,1,0:T(8,128)S(1)} %pad_maximum_fusion.4), channel_id=1, source_target_pairs={{192,0},{0,64},{64,128},{128,192},{193,1},{1,65},{65,129},{129,193... | collective-permute-start | bytes 172040 | tf_op jit(solution)/shard_map/ppermute | solution.py:374
  55.6 3.9 %collective-permute-start.9 = (f32[7,16,128]{2,1,0:T(8,128)S(1)}, f32[7,16,128]{2,1,0:T(8,128)S(1)}, u32[]{:S(2)}, u32[]{:S(2)}) collective-permute-start(f32[7,16,128]{2,1,0:T(8,128)S(1)} %pad_maximum_fusion.5), channel_id=1, source_target_pairs={{64,0},{128,64},{192,128},{0,192},{65,1},{129,65},{193,129},{1,193... | collective-permute-start | bytes 172040 | tf_op jit(solution)/shard_map/ppermute | solution.py:374
  59.6 14.2 %collective-permute-start.11 = (f32[8,128]{1,0:T(8,128)S(1)}, f32[8,128]{1,0:T(8,128)S(1)}, u32[]{:S(2)}, u32[]{:S(2)}) collective-permute-start(f32[8,128]{1,0:T(8,128)S(1)} %get-tuple-element.60), channel_id=1, source_target_pairs={{6,0},{7,1},{0,2},{1,3},{2,4},{3,5},{4,6},{5,7},{14,8},{15,9},{8,1... | collective-permute-start | bytes 12296 | tf_op jit(solution)/shard_map/ppermute | solution.py:374
  60.9 12.8 %collective-permute-start.10 = (f32[8,128]{1,0:T(8,128)S(1)}, f32[8,128]{1,0:T(8,128)S(1)}, u32[]{:S(2)}, u32[]{:S(2)}) collective-permute-start(f32[8,128]{1,0:T(8,128)S(1)} %get-tuple-element.59), channel_id=1, source_target_pairs={{3,0},{4,1},{5,2},{6,3},{7,4},{0,5},{1,6},{2,7},{11,8},{12,9},{13,... | collective-permute-start | bytes 12296 | tf_op jit(solution)/shard_map/ppermute | solution.py:374
  66.7 4.8 %collective-permute-start.12 = (f32[25,8,128]{2,1,0:T(8,128)S(1)}, f32[25,8,128]{2,1,0:T(8,128)S(1)}, u32[]{:S(2)}, u32[]{:S(2)}) collective-permute-start(f32[25,8,128]{2,1,0:T(8,128)S(1)} %get-tuple-element.61), channel_id=1, source_target_pairs={{8,0},{16,8},{24,16},{32,24},{40,32},{48,40},{56,48},{0,56},{9,1},... | collective-permute-start | bytes 307208 | tf_op jit(solution)/shard_map/ppermute | solution.py:374
  66.7 5.2 %collective-permute-start.13 = (f32[25,8,128]{2,1,0:T(8,128)S(1)}, f32[25,8,128]{2,1,0:T(8,128)S(1)}, u32[]{:S(2)}, u32[]{:S(2)}) collective-permute-start(f32[25,8,128]{2,1,0:T(8,128)S(1)} %get-tuple-element.62), channel_id=1, source_target_pairs={{56,0},{0,8},{8,16},{16,24},{24,32},{32,40},{40,48},{48,56},{57,1}... | collective-permute-start | bytes 307208 | tf_op jit(solution)/shard_map/ppermute | solution.py:374
  93.5 3.5 %collective-permute-start.14 = (f32[6,16,128]{2,1,0:T(8,128)S(1)}, f32[6,16,128]{2,1,0:T(8,128)S(1)}, u32[]{:S(2)}, u32[]{:S(2)}) collective-permute-start(f32[6,16,128]{2,1,0:T(8,128)S(1)} %get-tuple-element.70), channel_id=1, source_target_pairs={{1,0},{2,1},{3,2},{4,3},{5,4},{6,5},{7,6},{0,7},{9,8},{10,9},{11,1... | collective-permute-start | bytes 147464 | tf_op jit(solution)/shard_map/ppermute | solution.py:374
  95.9 1.2 collective-permute-start.15
  97.2 4.3 %collective-permute-start.16 = (f32[7,16,128]{2,1,0:T(8,128)S(1)}, f32[7,16,128]{2,1,0:T(8,128)S(1)}, u32[]{:S(2)}, u32[]{:S(2)}) collective-permute-start(f32[7,16,128]{2,1,0:T(8,128)S(1)} %pad_maximum_fusion.6), channel_id=1, source_target_pairs={{192,0},{0,64},{64,128},{128,192},{193,1},{1,65},{65,129},{129,193... | collective-permute-start | bytes 172040 | tf_op jit(solution)/shard_map/ppermute | solution.py:374
  97.6 3.9 %collective-permute-start.17 = (f32[7,16,128]{2,1,0:T(8,128)S(1)}, f32[7,16,128]{2,1,0:T(8,128)S(1)}, u32[]{:S(2)}, u32[]{:S(2)}) collective-permute-start(f32[7,16,128]{2,1,0:T(8,128)S(1)} %pad_maximum_fusion.7), channel_id=1, source_target_pairs={{64,0},{128,64},{192,128},{0,192},{65,1},{129,65},{193,129},{1,193... | collective-permute-start | bytes 172040 | tf_op jit(solution)/shard_map/ppermute | solution.py:374
  101.6 3.9 %collective-permute-start.18 = (f32[25,8,128]{2,1,0:T(8,128)S(1)}, f32[25,8,128]{2,1,0:T(8,128)S(1)}, u32[]{:S(2)}, u32[]{:S(2)}) collective-permute-start(f32[25,8,128]{2,1,0:T(8,128)S(1)} %get-tuple-element.72), channel_id=1, source_target_pairs={{8,0},{16,8},{24,16},{32,24},{40,32},{48,40},{56,48},{0,56},{9,1},... | collective-permute-start | bytes 307208 | tf_op jit(solution)/shard_map/ppermute | solution.py:374
  101.8 4.7 %collective-permute-start.19 = (f32[25,8,128]{2,1,0:T(8,128)S(1)}, f32[25,8,128]{2,1,0:T(8,128)S(1)}, u32[]{:S(2)}, u32[]{:S(2)}) collective-permute-start(f32[25,8,128]{2,1,0:T(8,128)S(1)} %get-tuple-element.73), channel_id=1, source_target_pairs={{56,0},{0,8},{8,16},{16,24},{24,32},{32,40},{40,48},{48,56},{57,1}... | collective-permute-start | bytes 307208 | tf_op jit(solution)/shard_map/ppermute | solution.py:374

commit v4 on v3

--- a/solution.py
+++ b/solution.py
@@ -68,6 +68,26 @@
         high_ref[g] = high
 
 
+def pack_near(read, low_ref, high_ref):
+    lane = iota((16, 128), 1)
+    near_low = near_high = None
+    for g in range(4):
+        low = high = None
+        for j in range(4):
+            k = 4 * g + j
+            v = read(k)
+            first, last = roll(v, 32 * j, 1), roll(v, 32 * j + 32, 1)
+            low = first if j == 0 else jnp.where(lane // 32 == j, first, low)
+            high = last if j == 0 else jnp.where(lane // 32 == j, last, high)
+            first, last = roll(v, 8 * k, 1), roll(v, 8 * k + 8, 1)
+            near_low = first if k == 0 else jnp.where(lane // 8 == k, first, near_low)
+            near_high = last if k == 0 else jnp.where(lane // 8 == k, last, near_high)
+        low_ref[g] = low
+        high_ref[g] = high
+    low_ref[4] = near_low
+    high_ref[4] = near_high
+
+
 def prepare_kernel(rhs_in, classes_in, table_in, both, low, high, classes, table, sems):
     copies = [
         pltpu.make_async_copy(rhs_in, both.at[0], sems.at[0]),
@@ -96,11 +116,17 @@
     return base + (x + 5 if x < 0 else far), base + 5, base + 6, (0, -32, -64, -96, -112)[far], (96, 64, 32, 16, 0)[far]
 
 
-def assemble_fine(body, sides, i):
+def near_sources(i):
+    x = i - 5
+    base, above, k = (x, 16, x) if 0 <= x < 16 else ((23 + x, 23, 16 + x) if x < 0 else (x + 9, 30, x - 16))
+    return base, above, above + 1, -8 * k, 120 - 8 * k
+
+
+def assemble_fine(body, sides, i, sources=slab_sources):
     def unit(u):
         return jnp.concatenate([body[u][...], sides[u][...]], axis=0)
 
-    main, above, below, up, down = slab_sources(i)
+    main, above, below, up, down = sources(i)
     lane = iota((32, 128), 1)
     side = jnp.where(lane < 64, roll(unit(above), up, 1), roll(unit(below), down, 1))
     return jnp.concatenate([unit(main), side], axis=1)
@@ -113,13 +139,17 @@
             lower[5 * g + t] = body[pl.ds(128 * g + 11 + t, 8, stride=16), :]
 
 
+def units(body, first, count):
+    return [body.at[pl.ds(first + 16 * u, 16)] for u in range(count)]
+
+
 def unpack_rows(upper, lower, first, sides):
     sides[...] = jnp.zeros(sides.shape, F32)
-    for g in range(UNITS // 8):
+    for g in range(sides.shape[0] // 128):
         for t in range(5):
             sides[pl.ds(128 * g + t, 8, stride=16), :] = upper[first + 5 * g + t]
             sides[pl.ds(128 * g + 11 + t, 8, stride=16), :] = lower[first + 5 * g + t]
-    return [sides.at[pl.ds(16 * u, 16)] for u in range(UNITS)]
+    return units(sides, 0, sides.shape[0] // 16)
 
 
 def near(lane):
@@ -190,25 +220,124 @@
     pack_coarse(quads, unit)
 
 
-def units(body, first):
-    return [body.at[pl.ds(first + 16 * u, 16)] for u in range(UNITS)]
-
-
 def first_down_kernel(body, upper, lower, weight0, weight1, x0, x1, unit, r, r1, quads, sides, more):
     kap_sides = unpack_rows(upper, lower, 5 * UNITS // 8, more)
-    fine_weights(units(body, 16 * UNITS), kap_sides, weight0, weight1, r1, quads, unit.at[1])
+    fine_weights(units(body, 16 * UNITS, UNITS), kap_sides, weight0, weight1, r1, quads, unit.at[1])
     r_sides = unpack_rows(upper, lower, 0, sides)
-    down_sweep(units(body, 0), r_sides, weight0, weight1, x0, x1, unit.at[0], r, r1, quads)
-
-
-def down_kernel(body, upper, lower, weight0, weight1, x0, x1, unit, r, r1, quads, sides):
-    r_sides = unpack_rows(upper, lower, 0, sides)
-    down_sweep(units(body, 0), r_sides, weight0, weight1, x0, x1, unit, r, r1, quads)
+    down_sweep(units(body, 0, UNITS), r_sides, weight0, weight1, x0, x1, unit.at[0], r, r1, quads)
+
+
+def share_kernel(own, above, below, weight0, weight1, share, r, x0, r1, x1, quads):
+    lane = iota((16, 128), 1)
+    for k in range(16):
+        up, down = above[k // 4], below[k // 4]
+        side = jnp.where(lane < 64, roll(up, -32 * (k % 4), 1), roll(down, 96 - 32 * (k % 4), 1))
+        v = jnp.concatenate([own[k], side], axis=1)
+        r[k] = v
+        x0[k] = weight0[k + 5, :16] * v
+    zero = jnp.zeros((16, 256), F32)
+
+    def tall(v):
+        return jnp.concatenate([v, zero], axis=0)
+
+    for m in range(10):
+        x = 2 * (m - 1)
+        if m == 0:
+            left = tall(x0[0])
+        elif m == 9:
+            left = tall(x0[15])
+        else:
+            two = x0[x] + x0[x + 1]
+            flat = KEEP * (r[x] + r[x + 1]) + two
+            flat = flat + x0[x - 1] if x > 0 else flat
+            flat = flat + x0[x + 2] if x < 14 else flat
+            left = tall(flat) + around(tall(two), 1, 1)
+        v = pair_mean(left, 1)
+        r1[m] = v
+        x1[m] = weight1[m + 1] * v
+    for c in range(6):
+        pair = [m for m in (2 * c - 1, 2 * c) if 0 <= m < 10]
+        two = sum(x1[m] for m in pair)
+        left = KEEP * sum(r1[m] for m in pair)
+        beside = two + around(two, 2, 2)
+        for m in (2 * c - 2, 2 * c + 1):
+            beside = beside + x1[m] if 0 <= m < 10 else beside
+        v = pair_mean(left + 0.25 * beside, 2)
+        quads[0, c], quads[1, c] = v[:, :128], v[:, 128:]
+    gy = place()[1]
+    for half in range(2):
+        for start, count, first in ((28, 1, 0), (0, 5, 1)):
+            turn = iota((count, 128), 1) % 4
+            inside = gy > 0 if count == 1 else (iota((count, 128), 0) < 4) | (gy < sizes()[1] - 1)
+
+            def rows(c):
+                v = quads[half, c, pl.ds(start, count, stride=4), :] if count > 1 else quads[half, c, pl.ds(start, 1), :]
+                return jnp.where(inside, v, 0.0)
+
+            v = rows(1)
+            for c in range(1, 4):
+                v = jnp.where(turn == c, rows(c + 1), v)
+            share[pl.ds(6 * half + first, count)] = v
+            v = jnp.where(turn == 3, rows(0), jnp.where(turn == 0, rows(5), 0.0))
+            share[pl.ds(12 + 6 * half + first, count)] = v
+
+
+def pack_both_kernel(body, own, next1, next2, next3, upper, lower, coarse, stage):
+    pack_rows_kernel(body, upper, lower)
+    gx = place()[0]
+    for k, share in enumerate((own, next1, next2, next3)):
+        stage[lax.rem(gx + k, 4)] = share[...]
+    turn = iota((12, 128), 1) % 4
+    for b in range(4):
+        v = stage[b, :12]
+        if b < 3:
+            v = v + jnp.where(turn == 3, stage[b + 1, 12:], 0.0)
+        if b > 0:
+            v = v + jnp.where(turn == 0, stage[b - 1, 12:], 0.0)
+        coarse[pl.ds(12 * b, 12)] = v
+
+
+def near_sweep(body, upper, lower, weight0, weight1, x0, x1, r, sides):
+    here, there = units(body, 0, 32), unpack_rows(upper, lower, 0, sides)
+    for i in range(SLABS):
+        v = assemble_fine(here, there, i, near_sources)
+        r[i] = v
+        x0[i] = weight0[i] * v
+    for m in range(MIDS):
+        i = 2 * m + 1
+        two = x0[i] + x0[i + 1]
+        left = KEEP * (r[i] + r[i + 1]) + ((x0[i - 1] + x0[i + 2]) + two) + around(two, 1, 1)
+        x1[m] = weight1[m] * pair_mean(left, 1)
+
+
+def unfold(v, k, out, change):
+    turn = iota((16, 256), 1) % 4
+    moved = {d: roll(v, d, 1) for d in range(-3, 4)}
+    for c in range(4):
+        slab = moved[-c]
+        for j in range(1, 4):
+            slab = jnp.where(turn == j, moved[j - c], slab)
+        out[4 * k + c + 1] = change(4 * k + c + 1, slab)
+
+
+def assemble_shares(own, up1, down1, up2, down2, out, change):
+    def zeros(n):
+        return jnp.zeros((n, 128), F32)
+
+    for k in range(4):
+        halves = []
+        for s in (12 * k, 12 * k + 6):
+            v = jnp.concatenate([own[s + 1:s + 6], zeros(10), own[s:s + 1]], axis=0)
+            v = v + jnp.concatenate([zeros(3), up1[s:s + 6], zeros(7)], axis=0)
+            v = v + jnp.concatenate([zeros(7), up2[s:s + 3], zeros(6)], axis=0)
+            v = v + jnp.concatenate([down1[s + 5:s + 6], zeros(10), down1[s:s + 5]], axis=0)
+            v = v + jnp.concatenate([zeros(10), down2[s + 3:s + 6], zeros(3)], axis=0)
+            halves.append(v)
+        unfold(jnp.concatenate(halves, axis=1), k, out, change)
 
 
 def assemble_coarse(gather, t, out, change):
     gy, ny = place()[1], sizes()[1]
-    turn = iota((16, 256), 1) % 4
     for k in range(4):
         own, up1, up2, down2, down1 = [ny * k + lax.rem(gy + d + ny, ny) for d in (0, 1, 2, -2, -1)]
         v = jnp.concatenate(
@@ -221,20 +350,15 @@
             ],
             axis=1,
         )
-        moved = {d: roll(v, d, 1) for d in range(-3, 4)}
-        for c in range(4):
-            slab = moved[-c]
-            for j in range(1, 4):
-                slab = jnp.where(turn == j, moved[j - c], slab)
-            out[4 * k + c + 1] = change(4 * k + c + 1, slab)
-
-
-def up_sweep(gather, weight2, weight1, weight0, x0, x1, kap, u, w, a, b, rhs2, spread, middle, t1, t0):
+        unfold(v, k, out, change)
+
+
+def up_sweep(assemble, weight2, weight1, weight0, x0, x1, kap, u, w, a, b, rhs2, spread, middle, t1, t0):
     zero = jnp.zeros((16, 256), F32)
     for ref in (a, b):
         ref[0] = zero
         ref[17] = zero
-    assemble_coarse(gather, 0, rhs2, lambda s, v: weight2[s] * v)
+    assemble(rhs2, lambda s, v: weight2[s] * v)
     for s in range(1, 17):
         a[s] = rhs2[s]
     for sweep in range(COARSE_SWEEPS - 1):
@@ -287,7 +411,7 @@
     y = jnp.where(row < 10, row, row - 16) + 4 * place()[1]
     inside = inside_lanes(lane) & (y >= 0) & (y < 4 * sizes()[1])
     assemble_coarse(gather, 1, weight2, lambda s, v: jnp.where(inside, v, 0.0))
-    up_sweep(gather, weight2, weight1, weight0, x0, x1, both.at[1], full, w, *scratch)
+    up_sweep(lambda *a: assemble_coarse(gather, 0, *a), weight2, weight1, weight0, x0, x1, both.at[1], full, w, *scratch)
     rz = curve = jnp.zeros((16, 128), F32)
     for k in range(16):
         v = full[k + 5][:16, :128]
@@ -295,35 +419,36 @@
         rz = rz + both[0, k] * v
         curve = curve + w[k] * v
     dots[...] = lanes_of([rz, curve])
-    pack_fine(lambda k: w[k], low, high)
-
-
-def second_up_kernel(gather, weight2, weight1, weight0, x0, x1, both, u0, w0,
-                     m0, n0, r1, u1, w1, low, high, first, *scratch):
-    (*scratch, full) = scratch
-    sums = gather[0, 0]
-    for k in range(1, gather.shape[0]):
-        sums = sums + gather[k, 0]
-    first[...] = sums
-    alpha = sums[4:5, MARK:MARK + 1] / sums[4:5, MARK + 1:MARK + 2]
-    up_sweep(gather, weight2, weight1, weight0, x0, x1, both.at[1], full, n0, *scratch)
+    pack_near(lambda k: w[k], low, high)
+
+
+def whole_sweep(body, upper, lower, shares, weight2, weight1, weight0, kap, full, w, x0, x1, r, sides, *scratch):
+    near_sweep(body, upper, lower, weight0, weight1, x0, x1, r, sides)
+    up_sweep(lambda *a: assemble_shares(*shares, *a), weight2, weight1, weight0, x0, x1, kap, full, w, *scratch)
+
+
+def second_kernel(body, upper, lower, own, up1, down1, up2, down2, weight2, weight1, weight0, both, m0, n0, low, high, full, *scratch):
+    shares = (own, up1, down1, up2, down2)
+    whole_sweep(body, upper, lower, shares, weight2, weight1, weight0, both.at[1], full, n0, *scratch)
     for k in range(16):
-        v = full[k + 5][:16, :128]
-        m0[k] = v
-        r1[k] = both[0, k] - alpha * w0[k]
-        u1[k] = u0[k] - alpha * v
-        w1[k] = w0[k] - alpha * n0[k]
-    pack_fine(lambda k: w1[k], low, high)
-
-
-def third_up_kernel(gather, weight2, weight1, weight0, x0, x1, both, w0, m0, n0, r1, u1, w1, m1, n1, dots, *scratch):
-    (*scratch, full) = scratch
-    up_sweep(gather, weight2, weight1, weight0, x0, x1, both.at[1], full, n1, *scratch)
+        m0[k] = full[k + 5, :16, :128]
+    pack_near(lambda k: n0[k], low, high)
+
+
+def third_kernel(body, upper, lower, own, up1, down1, up2, down2, weight2, weight1, weight0, both, first, u0, w0, m0, n0,
+                 r1, u1, w1, m1, n1, dots, full, last, *scratch):
+    shares = (own, up1, down1, up2, down2)
+    whole_sweep(body, upper, lower, shares, weight2, weight1, weight0, both.at[1], full, last, *scratch)
+    alpha = first[0:1, MARK:MARK + 1] / first[0:1, MARK + 1:MARK + 2]
     sums = [jnp.zeros((16, 128), F32)] * 12
     for k in range(16):
-        vm1 = full[k + 5][:16, :128]
-        m1[k] = vm1
-        vw0, vm0, vn0, vr1, vu1, vw1, vn1 = w0[k], m0[k], n0[k], r1[k], u1[k], w1[k], n1[k]
+        vw0, vm0, vn0 = w0[k], m0[k], n0[k]
+        vr1 = both[0, k] - alpha * vw0
+        vu1 = u0[k] - alpha * vm0
+        vw1 = vw0 - alpha * vn0
+        vm1 = vm0 - alpha * full[k + 5, :16, :128]
+        vn1 = vn0 - alpha * last[k]
+        r1[k], u1[k], w1[k], m1[k], n1[k] = vr1, vu1, vw1, vm1, vn1
         terms = [vr1 * vu1, vr1 * vm1, vr1 * vm0, vw1 * vu1, vw1 * vm1, vw1 * vm0,
                  vw0 * vu1, vw0 * vm1, vw0 * vm0, vn1 * vm1, vn1 * vm0, vn0 * vm0]
         sums = [s + t for s, t in zip(sums, terms)]
@@ -331,7 +456,7 @@
 
 
 def finish_kernel(first, second, u0, w0, m0, n0, r1, u1, w1, m1, n1, field, residual):
-    g0, d0 = first[4:5, MARK:MARK + 1], first[4:5, MARK + 1:MARK + 2]
+    g0, d0 = first[0:1, MARK:MARK + 1], first[0:1, MARK + 1:MARK + 2]
     (r1u1, r1m1, r1m0, w1u1, w1m1, w1m0, w0u1, w0m1, w0m0, n1m1, n1m0, n0m0) = [
         second[0:1, MARK + k:MARK + k + 1] for k in range(12)
     ]
@@ -374,28 +499,57 @@
     return lax.ppermute(v, axis, [((i + distance) % count, i) for i in range(count)])
 
 
-def fine_exchange(own, low, high, scalars=None):
-    if scalars is None:
-        above, below = shift(low, "gz", 1), shift(high, "gz", -1)
+def fine_exchange(own, low, high):
+    above, below = shift(low, "gz", 1), shift(high, "gz", -1)
+    first = jnp.concatenate([own[:, :5], above[:, 4:5], below[:, 4:5]], axis=1)
+    last = jnp.concatenate([own[:, 11:], above[:, 5:6], below[:, 5:6]], axis=1)
+    before, after = shift(last, "gx", -1), shift(first, "gx", 1)
+    body = jnp.concatenate([own, above[:, :4], below[:, :4], before, after, own[:, :2]], axis=1).reshape(-1, 128)
+    upper, lower = call(pack_rows_kernel, [shape(10 * UNITS // 8, 8, 128)] * 2, count=1)(body)
+    return body, shift(upper, "gy", 1), shift(lower, "gy", -1)
+
+
+def stack(*parts):
+    return jnp.concatenate([part.reshape(-1, 8, 128) for part in parts])
+
+
+def spread_rows(*rows):
+    rows = jnp.concatenate(rows)
+    return jnp.concatenate([rows, jnp.zeros((8 - rows.shape[0], 128), F32)])
+
+
+def joint_exchange(own, low, high, weight0, weight1, state, final):
+    above, below = shift(stack(low, state), "gz", 1), shift(stack(high, state), "gz", -1)
+    packs_above, packs_below = above[:10].reshape(5, 16, 128), below[:10].reshape(5, 16, 128)
+    if final:
+        state = spread_rows(*[state[j:j + 1] + state[j + 1:j + 2] + above[10, j + 1:j + 2] + below[10, j:j + 1] for j in (0, 2, 4)])
     else:
-        above = shift(jnp.concatenate([low.reshape(12, 8, 128), scalars[None]]), "gz", 1)
-        below = shift(jnp.concatenate([high.reshape(12, 8, 128), scalars[None]]), "gz", -1)
-        two = scalars + below[12]
-        three = two + above[12]
-        above, below = above[:12].reshape(6, 16, 128), below[:12].reshape(6, 16, 128)
-    first = jnp.concatenate([own[..., :5, :, :], above[..., 4:5, :, :], below[..., 4:5, :, :]], axis=-3)
-    last = jnp.concatenate([own[..., 11:, :, :], above[..., 5:6, :, :], below[..., 5:6, :, :]], axis=-3)
-    before, after = shift(last, "gx", -1), shift(first, "gx", 1)
-    parts = [own, above[..., :4, :, :], below[..., :4, :, :], before, after, own[..., :2, :, :]]
-    body = jnp.concatenate(parts, axis=-3).reshape(-1, 128)
-    tiles = body.shape[0] // 16 // 8 * 5
-    upper, lower = call(pack_rows_kernel, [shape(tiles, 8, 128)] * 2, count=1)(body)
-    if scalars is not None:
-        upper, lower, two, three = lax.optimization_barrier((upper, lower, two, three))
-    upper, lower = shift(upper, "gy", 1), shift(lower, "gy", -1)
-    if scalars is not None:
-        scalars = (three + shift(three, "gz", 3)) + shift(two, "gz", -2)
-    return (body, upper, lower), scalars
+        state = spread_rows(state[:1], above[10, :1])
+    share_scratch = [pltpu.VMEM(s, F32) for s in ((16, 16, 256), (16, 16, 256), (10, 32, 256), (10, 32, 256), (2, 6, 32, 128))]
+    (share,) = call(share_kernel, [shape(24, 128)], share_scratch, count=5)(own, packs_above, packs_below, weight0, weight1)
+    ends = [packs_above[4:], packs_below[4:]]
+    small = stack(share, state)
+    before, after = shift(stack(own[11:], *ends, small), "gx", -1), shift(stack(own[:5], *ends, small), "gx", 1)
+    across = shift(small, "gx", 2)
+    if final:
+        state = (state + before[17]) + (after[17] + across[3])
+    else:
+        state = state + shift(state, "gz", 4)
+    shares = [v.reshape(24, 128) for v in (share, after[14:17], across[:3], before[14:17])]
+    body = stack(own, *ends, before[:14], after[:14]).reshape(512, 128)
+    upper, lower, coarse = call(
+        pack_both_kernel, [shape(20, 8, 128), shape(20, 8, 128), shape(48, 128)], [pltpu.VMEM((4, 24, 128), F32)], count=5
+    )(body, *shares)
+    small = stack(coarse, state)
+    upper, lower = shift(stack(upper, small), "gy", 1), shift(stack(lower, small), "gy", -1)
+    up2, down2 = shift(small, "gy", 2), shift(small, "gy", -2)
+    if final:
+        state = jnp.broadcast_to(state[:1] + up2[6, 1:2] + down2[6, 2:3], (8, 128))
+    else:
+        ahead, behind = upper[26, :2] + up2[6, :2], lower[26, :2] + state[:2]
+        state = spread_rows(ahead + behind, ahead, behind)
+    groups = [coarse] + [v.reshape(48, 128) for v in (upper[20:26], lower[20:26], up2[:6], down2[:6])]
+    return [body, upper, lower] + groups, state
 
 
 def gather(unit):
@@ -415,7 +569,7 @@
         return [pltpu.VMEM(s, F32) for s in shapes]
 
     block, halo, mids = shape(*BLOCK), shape(*HALO), shape(*MID)
-    packs, tile = shape(6, 16, 128), shape(8, 128)
+    packs, tile = shape(5, 16, 128), shape(8, 128)
     down_scratch = scratch(HALO, MID, (2, 4, 16, 128), (16 * UNITS, 128))
     up_scratch = scratch((18, 16, 256), (18, 16, 256), (18, 16, 256), (6, 32, 256), MID, MID, HALO, HALO)
 
@@ -423,7 +577,7 @@
         prepare_kernel, [shape(2, *BLOCK), shape(2, 6, 16, 128), shape(2, 6, 16, 128)],
         [pltpu.VMEM(BLOCK, jnp.int32), pltpu.SMEM((CLASSES,), F32), pltpu.SemaphoreType.DMA((3,))], specs=[ANY] * 3, grant=60,
     )(right_side, classes, table)
-    halos, _ = fine_exchange(both, low, high)
+    halos = fine_exchange(both, low, high)
     weight0, weight1, x0, x1, unit = call(
         first_down_kernel, [halo, mids, halo, mids, shape(2, 8, 128)], down_scratch + scratch((16 * UNITS, 128)), count=3
     )(*halos)
@@ -431,20 +585,15 @@
         first_up_kernel, [shape(18, 16, 256), block, block, packs, packs, tile], up_scratch, count=6
     )(gather(unit), weight1, weight0, x0, x1, both)
 
-    down = call(down_kernel, [halo, mids, tile], down_scratch, count=5)
-    halos, scalars = fine_exchange(w0, low, high, dots)
-    x0, x1, unit = down(*halos, weight0, weight1)
-    free = (iota((8, 128), 0) >= 4) & (iota((8, 128), 1) >= 32) & (iota((8, 128), 1) < 96)
-    unit = jnp.where(free, scalars, unit)
-    m0, n0, r1, u1, w1, low, high, first = call(
-        second_up_kernel, [block] * 5 + [packs, packs, tile], up_scratch, count=9
-    )(gather(unit[None]), weight2, weight1, weight0, x0, x1, both, u0, w0)
-
-    halos, _ = fine_exchange(w1, low, high)
-    x0, x1, unit = down(*halos, weight0, weight1)
-    m1, n1, dots = call(third_up_kernel, [block] * 2 + [tile], up_scratch, count=13)(
-        gather(unit[None]), weight2, weight1, weight0, x0, x1, both, w0, m0, n0, r1, u1, w1
+    whole_scratch = scratch(HALO, MID, HALO, (512, 128)) + up_scratch[:-1]
+    halos, state = joint_exchange(w0, low, high, weight0, weight1, dots, False)
+    m0, n0, low, high = call(second_kernel, [block, block, packs, packs], scratch(HALO) + whole_scratch, count=12)(
+        *halos, weight2, weight1, weight0, both
     )
+    halos, first = joint_exchange(n0, low, high, weight0, weight1, state, True)
+    r1, u1, w1, m1, n1, dots = call(
+        third_kernel, [block] * 5 + [tile], scratch(HALO, BLOCK) + whole_scratch, count=17
+    )(*halos, weight2, weight1, weight0, both, first, u0, w0, m0, n0)
     field, residual = call(finish_kernel, [block] * 2, count=11)(
         first, total(dots), u0, w0, m0, n0, r1, u1, w1, m1, n1
     )

time: 154 us -> 132 us (0.86)
  blocking collectives: 59.6 us -> 26.4 us
  starting transfers between devices: 43.7 us -> 54.7 us
  waiting for transfers between devices: 31.6 us -> 29.1 us
  Pallas kernels: 15.4 us -> 17.7 us
    all_to_all x2 -> x0, blocking collectives: 34.1 us -> none  [gather(): lax.all_to_all(jnp.broadcast_to(unit[None], (count,) + unit.shape), ('gx'...]
    ppermute x20 -> x25, starting transfers between devices: 38.2 us -> 49.2 us  [shift(): lax.ppermute(v, axis, [((i + distance) % count, i) for i in range(count)])]
    ppermute x20 -> x25, waiting for transfers between devices: 21.9 us -> 19.7 us  [shift(): lax.ppermute(v, axis, [((i + distance) % count, i) for i in range(count)])]
    pallas_call x7, Pallas kernels: 7.39 us -> 9.57 us  [the longest x1 3.45 us: local(): call(third_kernel, [block] * 5 + [tile], scratch(HALO, BLOCK) + whole_scr...]
  transfers between devices with their start and end apart: 21 -> 26, of which waited for: 16 -> 14; matrix products, arithmetic and copies ran while one was open for 1% -> 1% of each run, Pallas kernels for 1% -> 1%
where the time goes in v4:
time: 132 us
  starting transfers between devices  54.7 us (41%)
  waiting for transfers between devices  29.1 us (22%)
  blocking collectives  26.4 us (20%)
  Pallas kernels  17.7 us (13%)
  local copies, waits for them, and re-layouts  2.19 us (2%)
    ppermute x25, starting transfers between devices, shift(): lax.ppermute(v, axis, [((i + distance) % count, i) for i in range(count)])  49.2 us
    all_to_all x1, blocking collectives, total(): lax.all_to_all(jnp.broadcast_to(v[None, :1], (count, 1, 128)), axes, 0, 0...  26.4 us
    ppermute x25, waiting for transfers between devices, shift(): lax.ppermute(v, axis, [((i + distance) % count, i) for i in range(count)])  19.7 us
    all_to_all x1, waiting for transfers between devices, gather(): lax.all_to_all(jnp.broadcast_to(unit[None], (count,) + unit.shape), ('gx'...  9.41 us
    all_to_all x1, starting transfers between devices, gather(): lax.all_to_all(jnp.broadcast_to(unit[None], (count,) + unit.shape), ('gx'...  5.49 us
    pallas_call x1, Pallas kernels, local(): call(third_kernel, [block] * 5 + [tile], scratch(HALO, BLOCK) + whole_scr...  3.45 us
    pallas_call x1, Pallas kernels, local(): call(second_kernel, [block, block, packs, packs], scratch(HALO) + whole_s...  3.24 us
    pallas_call x1, Pallas kernels, local(): call(first_down_kernel, [halo, mids, halo, mids, shape(2, 8, 128)], down_...  2.92 us
  transfers between devices with their start and end apart: 26, of which 14 were waited for; matrix products, arithmetic and copies ran while one was open for 1% of the time, Pallas kernels for 1%

profile of v4, /device:TPU:1, one launch (start us, length us, event | category | flops | bytes accessed | tf_op | source)
XLA Modules:
  0.0 131.8 jit_solution(8626533862132323477)
XLA Ops:
  0.6 1.9 %shard_map.50 = (f32[2,16,16,128]{3,2,1,0:T(8,128)}, f32[2,6,16,128]{3,2,1,0:T(8,128)}, f32[2,6,16,128]{3,2,1,0:T(8,128)}) custom-call(f32[16,16,128]{2,1,0:T(8,128)} %rhs_in.1, s32[16,16,128]{2,1,0:T(8,128)} %classes_in.1, f32[16]{0:T(128)} %table_in.1), custom_call_target="tpu_custom_call" | custom-call | tf_op jit(solution)/shard_map/pallas_call | solution.py:576
  2.6 3.3 %collective-permute-start = (f32[2,6,16,128]{3,2,1,0:T(8,128)}, f32[2,6,16,128]{3,2,1,0:T(8,128)S(1)}, u32[]{:S(2)}, u32[]{:S(2)}) collective-permute-start(f32[2,6,16,128]{3,2,1,0:T(8,128)} %get-tuple-element.35), channel_id=1, source_target_pairs={{1,0},{2,1},{3,2},{4,3},{5,4},{6,5},{7,6},{0,7},{9,8},{10,9},{11,1... | collective-permute-start | bytes 294920 | tf_op jit(solution)/shard_map/ppermute | solution.py:499
  9.1 1.5 %collective-permute-start.3 = (f32[2,7,16,128]{3,2,1,0:T(8,128)S(1)}, f32[2,7,16,128]{3,2,1,0:T(8,128)S(1)}, u32[]{:S(2)}, u32[]{:S(2)}) collective-permute-start(f32[2,7,16,128]{3,2,1,0:T(8,128)S(1)} %pad_maximum_fusion.9), channel_id=1, source_target_pairs={{64,0},{128,64},{192,128},{0,192},{65,1},{129,65},{193,129},{1,193... | collective-permute-start | bytes 344072 | tf_op jit(solution)/shard_map/ppermute | solution.py:499
  10.7 2.1 %collective-permute-done.2 = f32[2,7,16,128]{3,2,1,0:T(8,128)S(1)} collective-permute-done((f32[2,7,16,128]{3,2,1,0:T(8,128)S(1)}, f32[2,7,16,128]{3,2,1,0:T(8,128)S(1)}, u32[]{:S(2)}, u32[]{:S(2)}) %collective-permute-start.2) | collective-permute-done | bytes 114720 | tf_op jit(solution)/shard_map/ppermute | solution.py:499
  13.0 5.7 %collective-permute-start.4 = (f32[50,8,128]{2,1,0:T(8,128)S(1)}, f32[50,8,128]{2,1,0:T(8,128)S(1)}, u32[]{:S(2)}, u32[]{:S(2)}) collective-permute-start(f32[50,8,128]{2,1,0:T(8,128)S(1)} %get-tuple-element.37), channel_id=1, source_target_pairs={{8,0},{16,8},{24,16},{32,24},{40,32},{48,40},{56,48},{0,56},{9,1},... | collective-permute-start | bytes 614408 | tf_op jit(solution)/shard_map/ppermute | solution.py:499
  18.7 2.7 %collective-permute-done.4.upper = f32[50,8,128]{2,1,0:T(8,128)S(1)} collective-permute-done((f32[50,8,128]{2,1,0:T(8,128)S(1)}, f32[50,8,128]{2,1,0:T(8,128)S(1)}, u32[]{:S(2)}, u32[]{:S(2)}) %collective-permute-start.4) | collective-permute-done | bytes 204832 | tf_op jit(solution)/shard_map/ppermute | solution.py:499
  21.4 3.1 %collective-permute-done.5.lower = f32[50,8,128]{2,1,0:T(8,128)S(1)} collective-permute-done((f32[50,8,128]{2,1,0:T(8,128)S(1)}, f32[50,8,128]{2,1,0:T(8,128)S(1)}, u32[]{:S(2)}, u32[]{:S(2)}) %collective-permute-start.5) | collective-permute-done | bytes 204832 | tf_op jit(solution)/shard_map/ppermute | solution.py:499
  24.5 2.9 %shard_map.52 = (f32[26,32,256]{2,1,0:T(8,128)S(1)}, f32[12,32,256]{2,1,0:T(8,128)S(1)}, f32[26,32,256]{2,1,0:T(8,128)S(1)}, f32[12,32,256]{2,1,0:T(8,128)S(1)}, f32[2,8,128]{2,1,0:T(8,128)S(1)}) custom-call(f32[1280,128]{1,0:T(8,128)S(1)} %bitcast.123, f32[50,8,128]{2,1,0:T(8,128)S(1)} %collective-permute-done.4.upper, ...), custom_call_target="tpu_custom_call" | custom-call | tf_op jit(solution)/shard_map/pallas_call | solution.py:581
  28.1 5.5 %all-to-all-start = ((f32[32,2,8,128]{3,2,1,0:T(8,128)}), f32[32,2,8,128]{3,2,1,0:T(8,128)S(1)}, u32[]{:S(2)}, u32[]{:S(2)}) async-start(f32[32,2,8,128]{3,2,1,0:T(8,128)} %broadcast_in_dim.37), calls=%async_computation | async-start | bytes 524288 | tf_op jit(solution)/shard_map/all_to_all | solution.py:557
  33.9 9.4 %all-to-all-done.gather = f32[32,2,8,128]{3,2,1,0:T(8,128)S(1)} async-done(((f32[32,2,8,128]{3,2,1,0:T(8,128)}), f32[32,2,8,128]{3,2,1,0:T(8,128)S(1)}, u32[]{:S(2)}, u32[]{:S(2)}) %all-to-all-start) | async-done | bytes 262176 | tf_op jit(solution)/shard_map/all_to_all | solution.py:557
  43.3 1.9 %shard_map.53 = (f32[18,16,256]{2,1,0:T(8,128)S(1)}, f32[16,16,128]{2,1,0:T(8,128)S(1)}, f32[16,16,128]{2,1,0:T(8,128)S(1)}, f32[5,16,128]{2,1,0:T(8,128)S(1)}, ...) custom-call(f32[32,2,8,128]{3,2,1,0:T(8,128)S(1)} %all-to-all-done.gather, f32[12,32,256]{2,1,0:T(8,128)S(1)} %get-tuple-element.40.weight1, ...), custom_call_target="tpu_custom_call" | custom-call | tf_op jit(solution)/shard_map/pallas_call | solution.py:584
  45.2 8.2 %collective-permute-start.6 = (f32[11,8,128]{2,1,0:T(8,128)S(1)}, f32[11,8,128]{2,1,0:T(8,128)S(1)}, u32[]{:S(2)}, u32[]{:S(2)}) collective-permute-start(f32[11,8,128]{2,1,0:T(8,128)S(1)} %get-tuple-element.104), channel_id=1, source_target_pairs={{1,0},{2,1},{3,2},{4,3},{5,4},{6,5},{7,6},{0,7},{9,8},{10,9},{11,1... | collective-permute-start | bytes 135176 | tf_op jit(solution)/shard_map/ppermute | solution.py:499
  54.4 3.7 %collective-permute-start.11 = (f32[8,128]{1,0:T(8,128)S(1)}, f32[8,128]{1,0:T(8,128)S(1)}, u32[]{:S(2)}, u32[]{:S(2)}) collective-permute-start(f32[8,128]{1,0:T(8,128)S(1)} %maximum_maximum_fusion), channel_id=1, source_target_pairs={{4,0},{5,1},{6,2},{7,3},{0,4},{1,5},{2,6},{3,7},{12,8},{13,9},{14,... | collective-permute-start | bytes 12296 | tf_op jit(solution)/shard_map/ppermute | solution.py:499
  59.5 1.3 %collective-permute-start.10 = (f32[4,8,128]{2,1,0:T(8,128)S(1)}, f32[4,8,128]{2,1,0:T(8,128)S(1)}, u32[]{:S(2)}, u32[]{:S(2)}) collective-permute-start(f32[4,8,128]{2,1,0:T(8,128)S(1)} %pad_maximum_fusion.16), channel_id=1, source_target_pairs={{128,0},{192,64},{0,128},{64,192},{129,1},{193,65},{1,129},{65,193... | collective-permute-start | bytes 49160 | tf_op jit(solution)/shard_map/ppermute | solution.py:499
  61.3 2.4 %collective-permute-start.9 = (f32[18,8,128]{2,1,0:T(8,128)S(1)}, f32[18,8,128]{2,1,0:T(8,128)S(1)}, u32[]{:S(2)}, u32[]{:S(2)}) collective-permute-start(f32[18,8,128]{2,1,0:T(8,128)S(1)} %get-tuple-element.109), channel_id=1, source_target_pairs={{64,0},{128,64},{192,128},{0,192},{65,1},{129,65},{193,129},{1,193... | collective-permute-start | bytes 221192 | tf_op jit(solution)/shard_map/ppermute | solution.py:499
  63.7 1.9 %collective-permute-done.8 = f32[18,8,128]{2,1,0:T(8,128)S(1)} collective-permute-done((f32[18,8,128]{2,1,0:T(8,128)S(1)}, f32[18,8,128]{2,1,0:T(8,128)S(1)}, u32[]{:S(2)}, u32[]{:S(2)}) %collective-permute-start.8) | collective-permute-done | bytes 73760 | tf_op jit(solution)/shard_map/ppermute | solution.py:499
  65.7 1.9 %collective-permute-start.15 = (f32[7,8,128]{2,1,0:T(8,128)S(1)}, f32[7,8,128]{2,1,0:T(8,128)S(1)}, u32[]{:S(2)}, u32[]{:S(2)}) collective-permute-start(f32[7,8,128]{2,1,0:T(8,128)S(1)} %pad_maximum_fusion.14), channel_id=1, source_target_pairs={{48,0},{56,8},{0,16},{8,24},{16,32},{24,40},{32,48},{40,56},{49,1}... | collective-permute-start | bytes 86024 | tf_op jit(solution)/shard_map/ppermute | solution.py:499
  67.6 2.0 %collective-permute-start.13 = (f32[7,8,128]{2,1,0:T(8,128)S(1)}, f32[7,8,128]{2,1,0:T(8,128)S(1)}, u32[]{:S(2)}, u32[]{:S(2)}) collective-permute-start(f32[7,8,128]{2,1,0:T(8,128)S(1)} %pad_maximum_fusion.14), channel_id=1, source_target_pairs={{16,0},{24,8},{32,16},{40,24},{48,32},{56,40},{0,48},{8,56},{17,1}... | collective-permute-start | bytes 86024 | tf_op jit(solution)/shard_map/ppermute | solution.py:499
  69.6 1.4 %collective-permute-start.14 = (f32[27,8,128]{2,1,0:T(8,128)S(1)}, f32[27,8,128]{2,1,0:T(8,128)S(1)}, u32[]{:S(2)}, u32[]{:S(2)}) collective-permute-start(f32[27,8,128]{2,1,0:T(8,128)S(1)} %get-tuple-element.95), channel_id=1, source_target_pairs={{56,0},{0,8},{8,16},{16,24},{24,32},{32,40},{40,48},{48,56},{57,1}... | collective-permute-start | bytes 331784 | tf_op jit(solution)/shard_map/ppermute | solution.py:499
  72.3 2.7 %collective-permute-done.14.lower = f32[27,8,128]{2,1,0:T(8,128)S(1)} collective-permute-done((f32[27,8,128]{2,1,0:T(8,128)S(1)}, f32[27,8,128]{2,1,0:T(8,128)S(1)}, u32[]{:S(2)}, u32[]{:S(2)}) %collective-permute-start.14) | collective-permute-done | bytes 110624 | tf_op jit(solution)/shard_map/ppermute | solution.py:499
  75.1 3.2 %shard_map.56 = (f32[16,16,128]{2,1,0:T(8,128)S(1)}, f32[16,16,128]{2,1,0:T(8,128)S(1)}, f32[5,16,128]{2,1,0:T(8,128)S(1)}, f32[5,16,128]{2,1,0:T(8,128)S(1)}) custom-call(f32[512,128]{1,0:T(8,128)S(1)} %bitcast.129, f32[27,8,128]{2,1,0:T(8,128)S(1)} %collective-permute-done.12.upper, f32[27,8,128]{2,1,0:T(8,128)S(1)} %collective-permute-done.14.lower, ...), custom_call_target="tpu_custom_call" | custom-call | tf_op jit(solution)/shard_map/pallas_call | solution.py:590
  78.4 3.8 %collective-permute-start.16 = (f32[11,8,128]{2,1,0:T(8,128)S(1)}, f32[11,8,128]{2,1,0:T(8,128)S(1)}, u32[]{:S(2)}, u32[]{:S(2)}) collective-permute-start(f32[11,8,128]{2,1,0:T(8,128)S(1)} %get-tuple-element.101), channel_id=1, source_target_pairs={{1,0},{2,1},{3,2},{4,3},{5,4},{6,5},{7,6},{0,7},{9,8},{10,9},{11,1... | collective-permute-start | bytes 135176 | tf_op jit(solution)/shard_map/ppermute | solution.py:499
  84.9 1.9 %collective-permute-start.20 = (f32[4,8,128]{2,1,0:T(8,128)S(1)}, f32[4,8,128]{2,1,0:T(8,128)S(1)}, u32[]{:S(2)}, u32[]{:S(2)}) collective-permute-start(f32[4,8,128]{2,1,0:T(8,128)S(1)} %pad_maximum_fusion.17), channel_id=1, source_target_pairs={{128,0},{192,64},{0,128},{64,192},{129,1},{193,65},{1,129},{65,193... | collective-permute-start | bytes 49160 | tf_op jit(solution)/shard_map/ppermute | solution.py:499
  86.8 1.7 %collective-permute-start.18 = (f32[18,8,128]{2,1,0:T(8,128)S(1)}, f32[18,8,128]{2,1,0:T(8,128)S(1)}, u32[]{:S(2)}, u32[]{:S(2)}) collective-permute-start(f32[18,8,128]{2,1,0:T(8,128)S(1)} %get-tuple-element.106), channel_id=1, source_target_pairs={{192,0},{0,64},{64,128},{128,192},{193,1},{1,65},{65,129},{129,193... | collective-permute-start | bytes 221192 | tf_op jit(solution)/shard_map/ppermute | solution.py:499
  89.5 1.7 %collective-permute-done.18 = f32[18,8,128]{2,1,0:T(8,128)S(1)} collective-permute-done((f32[18,8,128]{2,1,0:T(8,128)S(1)}, f32[18,8,128]{2,1,0:T(8,128)S(1)}, u32[]{:S(2)}, u32[]{:S(2)}) %collective-permute-start.18) | collective-permute-done | bytes 73760 | tf_op jit(solution)/shard_map/ppermute | solution.py:499
  92.6 1.6 %collective-permute-start.22 = (f32[7,8,128]{2,1,0:T(8,128)S(1)}, f32[7,8,128]{2,1,0:T(8,128)S(1)}, u32[]{:S(2)}, u32[]{:S(2)}) collective-permute-start(f32[7,8,128]{2,1,0:T(8,128)S(1)} %pad_maximum_fusion.15), channel_id=1, source_target_pairs={{48,0},{56,8},{0,16},{8,24},{16,32},{24,40},{32,48},{40,56},{49,1}... | collective-permute-start | bytes 86024 | tf_op jit(solution)/shard_map/ppermute | solution.py:499
  94.3 1.4 %collective-permute-start.24 = (f32[27,8,128]{2,1,0:T(8,128)S(1)}, f32[27,8,128]{2,1,0:T(8,128)S(1)}, u32[]{:S(2)}, u32[]{:S(2)}) collective-permute-start(f32[27,8,128]{2,1,0:T(8,128)S(1)} %get-tuple-element.93), channel_id=1, source_target_pairs={{56,0},{0,8},{8,16},{16,24},{24,32},{32,40},{40,48},{48,56},{57,1}... | collective-permute-start | bytes 331784 | tf_op jit(solution)/shard_map/ppermute | solution.py:499
  95.7 2.7 %collective-permute-start.23 = (f32[27,8,128]{2,1,0:T(8,128)S(1)}, f32[27,8,128]{2,1,0:T(8,128)S(1)}, u32[]{:S(2)}, u32[]{:S(2)}) collective-permute-start(f32[27,8,128]{2,1,0:T(8,128)S(1)} %get-tuple-element.94), channel_id=1, source_target_pairs={{8,0},{16,8},{24,16},{32,24},{40,32},{48,40},{56,48},{0,56},{9,1},... | collective-permute-start | bytes 331784 | tf_op jit(solution)/shard_map/ppermute | solution.py:499
  98.5 1.9 %collective-permute-done.24.lower = f32[27,8,128]{2,1,0:T(8,128)S(1)} collective-permute-done((f32[27,8,128]{2,1,0:T(8,128)S(1)}, f32[27,8,128]{2,1,0:T(8,128)S(1)}, u32[]{:S(2)}, u32[]{:S(2)}) %collective-permute-start.24) | collective-permute-done | bytes 110624 | tf_op jit(solution)/shard_map/ppermute | solution.py:499
  100.4 3.5 %shard_map.59 = (f32[16,16,128]{2,1,0:T(8,128)S(1)}, f32[16,16,128]{2,1,0:T(8,128)S(1)}, f32[16,16,128]{2,1,0:T(8,128)S(1)}, f32[16,16,128]{2,1,0:T(8,128)S(1)},...) custom-call(f32[512,128]{1,0:T(8,128)S(1)} %bitcast.127, f32[27,8,128]{2,1,0:T(8,128)S(1)} %collective-permute-done.23.upper, ...), custom_call_target="tpu_custom_call" | custom-call | tf_op jit(solution)/shard_map/pallas_call | solution.py:594
  104.0 26.4 %all_to_all.10 = f32[256,1,128]{2,1,0:T(1,128)S(1)} all-to-all(f32[256,1,128]{2,1,0:T(1,128)S(1)} %broadcast_in_dim.45), channel_id=1, replica_groups=mesh['gx'=4,'gy'=8,'gz'=8] {'gx','gy','gz'}, dimensions={0} | all-to-all | bytes 262144 | tf_op jit(solution)/shard_map/all_to_all | solution.py:563
  130.5 1.3 %shard_map.60 = (f32[16,16,128]{2,1,0:T(8,128)}, f32[16,16,128]{2,1,0:T(8,128)}) custom-call(f32[8,128]{1,0:T(8,128)S(1)} %broadcast_in_dim.43.first, f32[8,128]{1,0:T(8,128)S(1)} %broadcast_in_dim.46.second, f32[16,16,128]{2,1,0:T(8,128)S(1)} %get-tuple-element.58.u0, f32[16,16,128]{2,1,0:T(8,128)S(1)} %get-tuple-element.44.own.w0, ...), custom_call_target="tpu_custom_call" | custom-call | tf_op jit(solution)/shard_map/pallas_call | solution.py:597
  (114 shorter events, 14.1 us)
Async XLA Ops:
  2.6 4.2 %copy-start = (f32[2,16,16,128]{3,2,1,0:T(8,128)S(1)}, f32[2,16,16,128]{3,2,1,0:T(8,128)}, u32[]{:S(2)}) copy-start(f32[2,16,16,128]{3,2,1,0:T(8,128)} %get-tuple-element.34.both) | copy-start | bytes 786436
  2.6 5.2 %collective-permute-start = (f32[2,6,16,128]{3,2,1,0:T(8,128)}, f32[2,6,16,128]{3,2,1,0:T(8,128)S(1)}, u32[]{:S(2)}, u32[]{:S(2)}) collective-permute-start(f32[2,6,16,128]{3,2,1,0:T(8,128)} %get-tuple-element.35), channel_id=1, source_target_pairs={{1,0},{2,1},{3,2},{4,3},{5,4},{6,5},{7,6},{0,7},{9,8},{10,9},{11,1... | collective-permute-start | bytes 294920 | tf_op jit(solution)/shard_map/ppermute | solution.py:499
  5.8 2.0 %collective-permute-start.1 = (f32[2,6,16,128]{3,2,1,0:T(8,128)}, f32[2,6,16,128]{3,2,1,0:T(8,128)S(1)}, u32[]{:S(2)}, u32[]{:S(2)}) collective-permute-start(f32[2,6,16,128]{3,2,1,0:T(8,128)} %get-tuple-element.36), channel_id=1, source_target_pairs={{7,0},{0,1},{1,2},{2,3},{3,4},{4,5},{5,6},{6,7},{15,8},{8,9},{9,10... | collective-permute-start | bytes 294920 | tf_op jit(solution)/shard_map/ppermute | solution.py:499
  7.8 4.9 %collective-permute-start.2 = (f32[2,7,16,128]{3,2,1,0:T(8,128)S(1)}, f32[2,7,16,128]{3,2,1,0:T(8,128)S(1)}, u32[]{:S(2)}, u32[]{:S(2)}) collective-permute-start(f32[2,7,16,128]{3,2,1,0:T(8,128)S(1)} %pad_maximum_fusion.8), channel_id=1, source_target_pairs={{192,0},{0,64},{64,128},{128,192},{193,1},{1,65},{65,129},{129,193... | collective-permute-start | bytes 344072 | tf_op jit(solution)/shard_map/ppermute | solution.py:499
  9.1 3.7 %collective-permute-start.3 = (f32[2,7,16,128]{3,2,1,0:T(8,128)S(1)}, f32[2,7,16,128]{3,2,1,0:T(8,128)S(1)}, u32[]{:S(2)}, u32[]{:S(2)}) collective-permute-start(f32[2,7,16,128]{3,2,1,0:T(8,128)S(1)} %pad_maximum_fusion.9), channel_id=1, source_target_pairs={{64,0},{128,64},{192,128},{0,192},{65,1},{129,65},{193,129},{1,193... | collective-permute-start | bytes 344072 | tf_op jit(solution)/shard_map/ppermute | solution.py:499
  13.0 8.4 %collective-permute-start.4 = (f32[50,8,128]{2,1,0:T(8,128)S(1)}, f32[50,8,128]{2,1,0:T(8,128)S(1)}, u32[]{:S(2)}, u32[]{:S(2)}) collective-permute-start(f32[50,8,128]{2,1,0:T(8,128)S(1)} %get-tuple-element.37), channel_id=1, source_target_pairs={{8,0},{16,8},{24,16},{32,24},{40,32},{48,40},{56,48},{0,56},{9,1},... | collective-permute-start | bytes 614408 | tf_op jit(solution)/shard_map/ppermute | solution.py:499
  18.7 5.8 %collective-permute-start.5 = (f32[50,8,128]{2,1,0:T(8,128)S(1)}, f32[50,8,128]{2,1,0:T(8,128)S(1)}, u32[]{:S(2)}, u32[]{:S(2)}) collective-permute-start(f32[50,8,128]{2,1,0:T(8,128)S(1)} %get-tuple-element.38), channel_id=1, source_target_pairs={{56,0},{0,8},{8,16},{16,24},{24,32},{32,40},{40,48},{48,56},{57,1}... | collective-permute-start | bytes 614408 | tf_op jit(solution)/shard_map/ppermute | solution.py:499
  28.1 15.1 %all-to-all-start = ((f32[32,2,8,128]{3,2,1,0:T(8,128)}), f32[32,2,8,128]{3,2,1,0:T(8,128)S(1)}, u32[]{:S(2)}, u32[]{:S(2)}) async-start(f32[32,2,8,128]{3,2,1,0:T(8,128)} %broadcast_in_dim.37), calls=%async_computation | async-start | bytes 524288 | tf_op jit(solution)/shard_map/all_to_all | solution.py:557
  45.2 9.1 %collective-permute-start.6 = (f32[11,8,128]{2,1,0:T(8,128)S(1)}, f32[11,8,128]{2,1,0:T(8,128)S(1)}, u32[]{:S(2)}, u32[]{:S(2)}) collective-permute-start(f32[11,8,128]{2,1,0:T(8,128)S(1)} %get-tuple-element.104), channel_id=1, source_target_pairs={{1,0},{2,1},{3,2},{4,3},{5,4},{6,5},{7,6},{0,7},{9,8},{10,9},{11,1... | collective-permute-start | bytes 135176 | tf_op jit(solution)/shard_map/ppermute | solution.py:499
  53.4 4.7 %collective-permute-start.7 = (f32[11,8,128]{2,1,0:T(8,128)S(1)}, f32[11,8,128]{2,1,0:T(8,128)S(1)}, u32[]{:S(2)}, u32[]{:S(2)}) collective-permute-start(f32[11,8,128]{2,1,0:T(8,128)S(1)} %get-tuple-element.103), channel_id=1, source_target_pairs={{7,0},{0,1},{1,2},{2,3},{3,4},{4,5},{5,6},{6,7},{15,8},{8,9},{9,10... | collective-permute-start | bytes 135176 | tf_op jit(solution)/shard_map/ppermute | solution.py:499
  54.4 5.1 %collective-permute-start.11 = (f32[8,128]{1,0:T(8,128)S(1)}, f32[8,128]{1,0:T(8,128)S(1)}, u32[]{:S(2)}, u32[]{:S(2)}) collective-permute-start(f32[8,128]{1,0:T(8,128)S(1)} %maximum_maximum_fusion), channel_id=1, source_target_pairs={{4,0},{5,1},{6,2},{7,3},{0,4},{1,5},{2,6},{3,7},{12,8},{13,9},{14,... | collective-permute-start | bytes 12296 | tf_op jit(solution)/shard_map/ppermute | solution.py:499
  59.5 4.1 %collective-permute-start.10 = (f32[4,8,128]{2,1,0:T(8,128)S(1)}, f32[4,8,128]{2,1,0:T(8,128)S(1)}, u32[]{:S(2)}, u32[]{:S(2)}) collective-permute-start(f32[4,8,128]{2,1,0:T(8,128)S(1)} %pad_maximum_fusion.16), channel_id=1, source_target_pairs={{128,0},{192,64},{0,128},{64,192},{129,1},{193,65},{1,129},{65,193... | collective-permute-start | bytes 49160 | tf_op jit(solution)/shard_map/ppermute | solution.py:499
  61.0 4.6 %collective-permute-start.8 = (f32[18,8,128]{2,1,0:T(8,128)S(1)}, f32[18,8,128]{2,1,0:T(8,128)S(1)}, u32[]{:S(2)}, u32[]{:S(2)}) collective-permute-start(f32[18,8,128]{2,1,0:T(8,128)S(1)} %get-tuple-element.110), channel_id=1, source_target_pairs={{192,0},{0,64},{64,128},{128,192},{193,1},{1,65},{65,129},{129,193... | collective-permute-start | bytes 221192 | tf_op jit(solution)/shard_map/ppermute | solution.py:499
  61.3 4.3 %collective-permute-start.9 = (f32[18,8,128]{2,1,0:T(8,128)S(1)}, f32[18,8,128]{2,1,0:T(8,128)S(1)}, u32[]{:S(2)}, u32[]{:S(2)}) collective-permute-start(f32[18,8,128]{2,1,0:T(8,128)S(1)} %get-tuple-element.109), channel_id=1, source_target_pairs={{64,0},{128,64},{192,128},{0,192},{65,1},{129,65},{193,129},{1,193... | collective-permute-start | bytes 221192 | tf_op jit(solution)/shard_map/ppermute | solution.py:499
  65.7 6.6 %collective-permute-start.15 = (f32[7,8,128]{2,1,0:T(8,128)S(1)}, f32[7,8,128]{2,1,0:T(8,128)S(1)}, u32[]{:S(2)}, u32[]{:S(2)}) collective-permute-start(f32[7,8,128]{2,1,0:T(8,128)S(1)} %pad_maximum_fusion.14), channel_id=1, source_target_pairs={{48,0},{56,8},{0,16},{8,24},{16,32},{24,40},{32,48},{40,56},{49,1}... | collective-permute-start | bytes 86024 | tf_op jit(solution)/shard_map/ppermute | solution.py:499
  67.6 4.7 %collective-permute-start.13 = (f32[7,8,128]{2,1,0:T(8,128)S(1)}, f32[7,8,128]{2,1,0:T(8,128)S(1)}, u32[]{:S(2)}, u32[]{:S(2)}) collective-permute-start(f32[7,8,128]{2,1,0:T(8,128)S(1)} %pad_maximum_fusion.14), channel_id=1, source_target_pairs={{16,0},{24,8},{32,16},{40,24},{48,32},{56,40},{0,48},{8,56},{17,1}... | collective-permute-start | bytes 86024 | tf_op jit(solution)/shard_map/ppermute | solution.py:499
  69.6 5.5 %collective-permute-start.14 = (f32[27,8,128]{2,1,0:T(8,128)S(1)}, f32[27,8,128]{2,1,0:T(8,128)S(1)}, u32[]{:S(2)}, u32[]{:S(2)}) collective-permute-start(f32[27,8,128]{2,1,0:T(8,128)S(1)} %get-tuple-element.95), channel_id=1, source_target_pairs={{56,0},{0,8},{8,16},{16,24},{24,32},{32,40},{40,48},{48,56},{57,1}... | collective-permute-start | bytes 331784 | tf_op jit(solution)/shard_map/ppermute | solution.py:499
  71.0 4.1 %collective-permute-start.12 = (f32[27,8,128]{2,1,0:T(8,128)S(1)}, f32[27,8,128]{2,1,0:T(8,128)S(1)}, u32[]{:S(2)}, u32[]{:S(2)}) collective-permute-start(f32[27,8,128]{2,1,0:T(8,128)S(1)} %get-tuple-element.96), channel_id=1, source_target_pairs={{8,0},{16,8},{24,16},{32,24},{40,32},{48,40},{56,48},{0,56},{9,1},... | collective-permute-start | bytes 331784 | tf_op jit(solution)/shard_map/ppermute | solution.py:499
  78.4 4.9 %collective-permute-start.16 = (f32[11,8,128]{2,1,0:T(8,128)S(1)}, f32[11,8,128]{2,1,0:T(8,128)S(1)}, u32[]{:S(2)}, u32[]{:S(2)}) collective-permute-start(f32[11,8,128]{2,1,0:T(8,128)S(1)} %get-tuple-element.101), channel_id=1, source_target_pairs={{1,0},{2,1},{3,2},{4,3},{5,4},{6,5},{7,6},{0,7},{9,8},{10,9},{11,1... | collective-permute-start | bytes 135176 | tf_op jit(solution)/shard_map/ppermute | solution.py:499
  82.2 1.2 collective-permute-start.17
  84.9 4.7 %collective-permute-start.20 = (f32[4,8,128]{2,1,0:T(8,128)S(1)}, f32[4,8,128]{2,1,0:T(8,128)S(1)}, u32[]{:S(2)}, u32[]{:S(2)}) collective-permute-start(f32[4,8,128]{2,1,0:T(8,128)S(1)} %pad_maximum_fusion.17), channel_id=1, source_target_pairs={{128,0},{192,64},{0,128},{64,192},{129,1},{193,65},{1,129},{65,193... | collective-permute-start | bytes 49160 | tf_op jit(solution)/shard_map/ppermute | solution.py:499
  86.8 4.4 %collective-permute-start.18 = (f32[18,8,128]{2,1,0:T(8,128)S(1)}, f32[18,8,128]{2,1,0:T(8,128)S(1)}, u32[]{:S(2)}, u32[]{:S(2)}) collective-permute-start(f32[18,8,128]{2,1,0:T(8,128)S(1)} %get-tuple-element.106), channel_id=1, source_target_pairs={{192,0},{0,64},{64,128},{128,192},{193,1},{1,65},{65,129},{129,193... | collective-permute-start | bytes 221192 | tf_op jit(solution)/shard_map/ppermute | solution.py:499
  88.5 3.2 %collective-permute-start.19 = (f32[18,8,128]{2,1,0:T(8,128)S(1)}, f32[18,8,128]{2,1,0:T(8,128)S(1)}, u32[]{:S(2)}, u32[]{:S(2)}) collective-permute-start(f32[18,8,128]{2,1,0:T(8,128)S(1)} %get-tuple-element.105), channel_id=1, source_target_pairs={{64,0},{128,64},{192,128},{0,192},{65,1},{129,65},{193,129},{1,193... | collective-permute-start | bytes 221192 | tf_op jit(solution)/shard_map/ppermute | solution.py:499
  91.9 6.6 %collective-permute-start.21 = (f32[7,8,128]{2,1,0:T(8,128)S(1)}, f32[7,8,128]{2,1,0:T(8,128)S(1)}, u32[]{:S(2)}, u32[]{:S(2)}) collective-permute-start(f32[7,8,128]{2,1,0:T(8,128)S(1)} %pad_maximum_fusion.15), channel_id=1, source_target_pairs={{16,0},{24,8},{32,16},{40,24},{48,32},{56,40},{0,48},{8,56},{17,1}... | collective-permute-start | bytes 86024 | tf_op jit(solution)/shard_map/ppermute | solution.py:499
  92.6 5.8 %collective-permute-start.22 = (f32[7,8,128]{2,1,0:T(8,128)S(1)}, f32[7,8,128]{2,1,0:T(8,128)S(1)}, u32[]{:S(2)}, u32[]{:S(2)}) collective-permute-start(f32[7,8,128]{2,1,0:T(8,128)S(1)} %pad_maximum_fusion.15), channel_id=1, source_target_pairs={{48,0},{56,8},{0,16},{8,24},{16,32},{24,40},{32,48},{40,56},{49,1}... | collective-permute-start | bytes 86024 | tf_op jit(solution)/shard_map/ppermute | solution.py:499
  94.3 6.1 %collective-permute-start.24 = (f32[27,8,128]{2,1,0:T(8,128)S(1)}, f32[27,8,128]{2,1,0:T(8,128)S(1)}, u32[]{:S(2)}, u32[]{:S(2)}) collective-permute-start(f32[27,8,128]{2,1,0:T(8,128)S(1)} %get-tuple-element.93), channel_id=1, source_target_pairs={{56,0},{0,8},{8,16},{16,24},{24,32},{32,40},{40,48},{48,56},{57,1}... | collective-permute-start | bytes 331784 | tf_op jit(solution)/shard_map/ppermute | solution.py:499
  95.7 4.7 %collective-permute-start.23 = (f32[27,8,128]{2,1,0:T(8,128)S(1)}, f32[27,8,128]{2,1,0:T(8,128)S(1)}, u32[]{:S(2)}, u32[]{:S(2)}) collective-permute-start(f32[27,8,128]{2,1,0:T(8,128)S(1)} %get-tuple-element.94), channel_id=1, source_target_pairs={{8,0},{16,8},{24,16},{32,24},{40,32},{48,40},{56,48},{0,56},{9,1},... | collective-permute-start | bytes 331784 | tf_op jit(solution)/shard_map/ppermute | solution.py:499

commit v5 on v4

--- a/solution.py
+++ b/solution.py
@@ -1,3 +1,5 @@
+import functools
+
 import jax
 import jax.numpy as jnp
 from jax import lax
@@ -69,23 +71,15 @@
 
 
 def pack_near(read, low_ref, high_ref):
-    lane = iota((16, 128), 1)
-    near_low = near_high = None
-    for g in range(4):
-        low = high = None
-        for j in range(4):
-            k = 4 * g + j
-            v = read(k)
-            first, last = roll(v, 32 * j, 1), roll(v, 32 * j + 32, 1)
-            low = first if j == 0 else jnp.where(lane // 32 == j, first, low)
-            high = last if j == 0 else jnp.where(lane // 32 == j, last, high)
-            first, last = roll(v, 8 * k, 1), roll(v, 8 * k + 8, 1)
-            near_low = first if k == 0 else jnp.where(lane // 8 == k, first, near_low)
-            near_high = last if k == 0 else jnp.where(lane // 8 == k, last, near_high)
-        low_ref[g] = low
-        high_ref[g] = high
-    low_ref[4] = near_low
-    high_ref[4] = near_high
+    chunk = iota((16, 128), 1) // 8
+    low = high = None
+    for k in range(16):
+        v = read(k)
+        first, last = roll(v, 8 * k, 1), roll(v, 8 * k + 8, 1)
+        low = first if k == 0 else jnp.where(chunk == k, first, low)
+        high = last if k == 0 else jnp.where(chunk == k, last, high)
+    low_ref[...] = low
+    high_ref[...] = high
 
 
 def prepare_kernel(rhs_in, classes_in, table_in, both, low, high, classes, table, sems):
@@ -135,8 +129,9 @@
 def pack_rows_kernel(body, upper, lower):
     for g in range(body.shape[0] // 128):
         for t in range(5):
-            upper[5 * g + t] = body[pl.ds(128 * g + t, 8, stride=16), :]
-            lower[5 * g + t] = body[pl.ds(128 * g + 11 + t, 8, stride=16), :]
+            here = pl.ds(8 * (5 * g + t), 8)
+            upper[here] = body[pl.ds(128 * g + t, 8, stride=16), :]
+            lower[here] = body[pl.ds(128 * g + 11 + t, 8, stride=16), :]
 
 
 def units(body, first, count):
@@ -147,8 +142,9 @@
     sides[...] = jnp.zeros(sides.shape, F32)
     for g in range(sides.shape[0] // 128):
         for t in range(5):
-            sides[pl.ds(128 * g + t, 8, stride=16), :] = upper[first + 5 * g + t]
-            sides[pl.ds(128 * g + 11 + t, 8, stride=16), :] = lower[first + 5 * g + t]
+            here = pl.ds(8 * (first + 5 * g + t), 8)
+            sides[pl.ds(128 * g + t, 8, stride=16), :] = upper[here]
+            sides[pl.ds(128 * g + 11 + t, 8, stride=16), :] = lower[here]
     return units(sides, 0, sides.shape[0] // 16)
 
 
@@ -227,18 +223,13 @@
     down_sweep(units(body, 0, UNITS), r_sides, weight0, weight1, x0, x1, unit.at[0], r, r1, quads)
 
 
-def share_kernel(own, above, below, weight0, weight1, share, r, x0, r1, x1, quads):
-    lane = iota((16, 128), 1)
-    for k in range(16):
-        up, down = above[k // 4], below[k // 4]
-        side = jnp.where(lane < 64, roll(up, -32 * (k % 4), 1), roll(down, 96 - 32 * (k % 4), 1))
-        v = jnp.concatenate([own[k], side], axis=1)
-        r[k] = v
-        x0[k] = weight0[k + 5, :16] * v
-    zero = jnp.zeros((16, 256), F32)
+def share_sweep(block, weight0, weight1, share, x0, r1, x1, quads):
+    for k in range(16):
+        x0[k] = weight0[k + 5, :16, :128] * block[k]
+    zero, low = jnp.zeros((16, 128), F32), jnp.zeros((16, 256), F32)
 
     def tall(v):
-        return jnp.concatenate([v, zero], axis=0)
+        return jnp.concatenate([jnp.concatenate([v, zero], axis=1), low], axis=0)
 
     for m in range(10):
         x = 2 * (m - 1)
@@ -248,7 +239,7 @@
             left = tall(x0[15])
         else:
             two = x0[x] + x0[x + 1]
-            flat = KEEP * (r[x] + r[x + 1]) + two
+            flat = KEEP * (block[x] + block[x + 1]) + two
             flat = flat + x0[x - 1] if x > 0 else flat
             flat = flat + x0[x + 2] if x < 14 else flat
             left = tall(flat) + around(tall(two), 1, 1)
@@ -264,16 +255,22 @@
             beside = beside + x1[m] if 0 <= m < 10 else beside
         v = pair_mean(left + 0.25 * beside, 2)
         quads[0, c], quads[1, c] = v[:, :128], v[:, 128:]
-    gy = place()[1]
+    gy, gz = place()[1:]
+    ny, nz = sizes()[1:]
     for half in range(2):
         for start, count, first in ((28, 1, 0), (0, 5, 1)):
-            turn = iota((count, 128), 1) % 4
-            inside = gy > 0 if count == 1 else (iota((count, 128), 0) < 4) | (gy < sizes()[1] - 1)
+            row, lane = iota((count, 128), 0), iota((count, 128), 1)
+            y = row // 4 + gy - (1 if count == 1 else 0)
+            inside = (y >= 0) & (y < ny)
+            if half == 1:
+                z = jnp.where(lane < 64, gz + 1, gz - 1)
+                inside = inside & (z >= 0) & (z < nz)
 
             def rows(c):
                 v = quads[half, c, pl.ds(start, count, stride=4), :] if count > 1 else quads[half, c, pl.ds(start, 1), :]
                 return jnp.where(inside, v, 0.0)
 
+            turn = lane % 4
             v = rows(1)
             for c in range(1, 4):
                 v = jnp.where(turn == c, rows(c + 1), v)
@@ -282,11 +279,43 @@
             share[pl.ds(12 + 6 * half + first, count)] = v
 
 
-def pack_both_kernel(body, own, next1, next2, next3, upper, lower, coarse, stage):
+def join_z_kernel(final, own, share, state, above, below, first, last, small):
+    lane = iota((6, 128), 1)
+    for s in (0, 12):
+        main, side = pl.ds(16 + s, 6), pl.ds(22 + s, 6)
+        v = share[s:s + 6] + jnp.where(lane >= 124, above[side], 0.0) + jnp.where(lane < 4, below[side], 0.0)
+        small[pl.ds(s, 6)] = v
+        v = share[s + 6:s + 12] + jnp.where(lane < 32, above[main], jnp.where(lane >= 96, below[main], 0.0))
+        small[pl.ds(s + 6, 6)] = v
+    row = iota((8, 128), 0)
+    if final:
+        sums = [state[j:j + 1] + state[j + 1:j + 2] + above[41 + j:42 + j] + below[40 + j:41 + j] for j in (0, 2, 4)]
+    else:
+        sums = [state[0:1], above[40:41]]
+    v = jnp.zeros((8, 128), F32)
+    for j, part in enumerate(sums):
+        v = jnp.where(row == j, part, v)
+    small[24:32] = v
+    for k in range(5):
+        first[pl.ds(16 * k, 16)] = own[k]
+        last[pl.ds(16 * k, 16)] = own[11 + k]
+    for ref in (first, last):
+        ref[80:96] = above[:16]
+        ref[96:112] = below[:16]
+        ref[112:144] = small[...]
+
+
+def join_x_kernel(final, own, above, below, small, before, after, across, body, upper, lower, ahead, behind, stage):
+    for k in range(16):
+        body[pl.ds(16 * k, 16)] = own[k]
+    body[256:272] = above[:16]
+    body[272:288] = below[:16]
+    body[288:400] = before[:112]
+    body[400:512] = after[:112]
     pack_rows_kernel(body, upper, lower)
     gx = place()[0]
-    for k, share in enumerate((own, next1, next2, next3)):
-        stage[lax.rem(gx + k, 4)] = share[...]
+    for k, rows in enumerate((small[:24], after[112:136], across[:24], before[112:136])):
+        stage[lax.rem(gx + k, 4)] = rows
     turn = iota((12, 128), 1) % 4
     for b in range(4):
         v = stage[b, :12]
@@ -294,7 +323,16 @@
             v = v + jnp.where(turn == 3, stage[b + 1, 12:], 0.0)
         if b > 0:
             v = v + jnp.where(turn == 0, stage[b - 1, 12:], 0.0)
-        coarse[pl.ds(12 * b, 12)] = v
+        for ref in (upper, lower):
+            ref[pl.ds(160 + 12 * b, 12)] = v
+        for half in range(2):
+            ahead[pl.ds(6 * b + 3 * half, 3)] = v[6 * half:6 * half + 3]
+            behind[pl.ds(6 * b + 3 * half, 3)] = v[6 * half + 3:6 * half + 6]
+    state = small[24:32]
+    if not final:
+        state = (state + before[136:144]) + (after[136:144] + across[24:32])
+    for ref, start in ((upper, 208), (lower, 208), (ahead, 24), (behind, 24)):
+        ref[pl.ds(start, 8)] = state
 
 
 def near_sweep(body, upper, lower, weight0, weight1, x0, x1, r, sides):
@@ -326,12 +364,13 @@
 
     for k in range(4):
         halves = []
-        for s in (12 * k, 12 * k + 6):
+        for half in range(2):
+            s, t = 160 + 12 * k + 6 * half, 6 * k + 3 * half
             v = jnp.concatenate([own[s + 1:s + 6], zeros(10), own[s:s + 1]], axis=0)
             v = v + jnp.concatenate([zeros(3), up1[s:s + 6], zeros(7)], axis=0)
-            v = v + jnp.concatenate([zeros(7), up2[s:s + 3], zeros(6)], axis=0)
+            v = v + jnp.concatenate([zeros(7), up2[t:t + 3], zeros(6)], axis=0)
             v = v + jnp.concatenate([down1[s + 5:s + 6], zeros(10), down1[s:s + 5]], axis=0)
-            v = v + jnp.concatenate([zeros(10), down2[s + 3:s + 6], zeros(3)], axis=0)
+            v = v + jnp.concatenate([zeros(10), down2[t:t + 3], zeros(3)], axis=0)
             halves.append(v)
         unfold(jnp.concatenate(halves, axis=1), k, out, change)
 
@@ -405,8 +444,8 @@
     return out
 
 
-def first_up_kernel(gather, weight1, weight0, x0, x1, both, weight2, u, w, low, high, dots, *scratch):
-    (*scratch, full) = scratch
+def first_up_kernel(gather, weight1, weight0, x0, x1, both, weight2, u, w, share, low, high, dots, *scratch):
+    (*scratch, full, y0, y1, z1, quads) = scratch
     row, lane = iota((16, 256), 0), iota((16, 256), 1)
     y = jnp.where(row < 10, row, row - 16) + 4 * place()[1]
     inside = inside_lanes(lane) & (y >= 0) & (y < 4 * sizes()[1])
@@ -420,26 +459,31 @@
         curve = curve + w[k] * v
     dots[...] = lanes_of([rz, curve])
     pack_near(lambda k: w[k], low, high)
-
-
-def whole_sweep(body, upper, lower, shares, weight2, weight1, weight0, kap, full, w, x0, x1, r, sides, *scratch):
-    near_sweep(body, upper, lower, weight0, weight1, x0, x1, r, sides)
+    share_sweep(w, weight0, weight1, share, y0, y1, z1, quads)
+
+
+def whole_sweep(body, shares, weight2, weight1, weight0, kap, full, w, x0, x1, r, sides, *scratch):
+    near_sweep(body, shares[1], shares[2], weight0, weight1, x0, x1, r, sides)
     up_sweep(lambda *a: assemble_shares(*shares, *a), weight2, weight1, weight0, x0, x1, kap, full, w, *scratch)
 
 
-def second_kernel(body, upper, lower, own, up1, down1, up2, down2, weight2, weight1, weight0, both, m0, n0, low, high, full, *scratch):
+def second_kernel(body, own, up1, down1, up2, down2, weight2, weight1, weight0, both, m0, n0, share, low, high, *scratch):
+    (full, *scratch, y0, y1, z1, quads) = scratch
     shares = (own, up1, down1, up2, down2)
-    whole_sweep(body, upper, lower, shares, weight2, weight1, weight0, both.at[1], full, n0, *scratch)
+    whole_sweep(body, shares, weight2, weight1, weight0, both.at[1], full, n0, *scratch)
     for k in range(16):
         m0[k] = full[k + 5, :16, :128]
     pack_near(lambda k: n0[k], low, high)
-
-
-def third_kernel(body, upper, lower, own, up1, down1, up2, down2, weight2, weight1, weight0, both, first, u0, w0, m0, n0,
-                 r1, u1, w1, m1, n1, dots, full, last, *scratch):
+    share_sweep(n0, weight0, weight1, share, y0, y1, z1, quads)
+
+
+def third_kernel(body, own, up1, down1, up2, down2, weight2, weight1, weight0, both, u0, w0, m0, n0,
+                 r1, u1, w1, m1, n1, first, dots, full, last, *scratch):
     shares = (own, up1, down1, up2, down2)
-    whole_sweep(body, upper, lower, shares, weight2, weight1, weight0, both.at[1], full, last, *scratch)
-    alpha = first[0:1, MARK:MARK + 1] / first[0:1, MARK + 1:MARK + 2]
+    whole_sweep(body, shares, weight2, weight1, weight0, both.at[1], full, last, *scratch)
+    total0 = own[208:209] + up2[25:26] + down2[26:27]
+    first[...] = jnp.broadcast_to(total0, (8, 128))
+    alpha = total0[:, MARK:MARK + 1] / total0[:, MARK + 1:MARK + 2]
     sums = [jnp.zeros((16, 128), F32)] * 12
     for k in range(16):
         vw0, vm0, vn0 = w0[k], m0[k], n0[k]
@@ -505,51 +549,22 @@
     last = jnp.concatenate([own[:, 11:], above[:, 5:6], below[:, 5:6]], axis=1)
     before, after = shift(last, "gx", -1), shift(first, "gx", 1)
     body = jnp.concatenate([own, above[:, :4], below[:, :4], before, after, own[:, :2]], axis=1).reshape(-1, 128)
-    upper, lower = call(pack_rows_kernel, [shape(10 * UNITS // 8, 8, 128)] * 2, count=1)(body)
+    upper, lower = call(pack_rows_kernel, [shape(10 * UNITS, 128)] * 2, count=1)(body)
     return body, shift(upper, "gy", 1), shift(lower, "gy", -1)
 
 
-def stack(*parts):
-    return jnp.concatenate([part.reshape(-1, 8, 128) for part in parts])
-
-
-def spread_rows(*rows):
-    rows = jnp.concatenate(rows)
-    return jnp.concatenate([rows, jnp.zeros((8 - rows.shape[0], 128), F32)])
-
-
-def joint_exchange(own, low, high, weight0, weight1, state, final):
-    above, below = shift(stack(low, state), "gz", 1), shift(stack(high, state), "gz", -1)
-    packs_above, packs_below = above[:10].reshape(5, 16, 128), below[:10].reshape(5, 16, 128)
-    if final:
-        state = spread_rows(*[state[j:j + 1] + state[j + 1:j + 2] + above[10, j + 1:j + 2] + below[10, j:j + 1] for j in (0, 2, 4)])
-    else:
-        state = spread_rows(state[:1], above[10, :1])
-    share_scratch = [pltpu.VMEM(s, F32) for s in ((16, 16, 256), (16, 16, 256), (10, 32, 256), (10, 32, 256), (2, 6, 32, 128))]
-    (share,) = call(share_kernel, [shape(24, 128)], share_scratch, count=5)(own, packs_above, packs_below, weight0, weight1)
-    ends = [packs_above[4:], packs_below[4:]]
-    small = stack(share, state)
-    before, after = shift(stack(own[11:], *ends, small), "gx", -1), shift(stack(own[:5], *ends, small), "gx", 1)
-    across = shift(small, "gx", 2)
-    if final:
-        state = (state + before[17]) + (after[17] + across[3])
-    else:
-        state = state + shift(state, "gz", 4)
-    shares = [v.reshape(24, 128) for v in (share, after[14:17], across[:3], before[14:17])]
-    body = stack(own, *ends, before[:14], after[:14]).reshape(512, 128)
-    upper, lower, coarse = call(
-        pack_both_kernel, [shape(20, 8, 128), shape(20, 8, 128), shape(48, 128)], [pltpu.VMEM((4, 24, 128), F32)], count=5
-    )(body, *shares)
-    small = stack(coarse, state)
-    upper, lower = shift(stack(upper, small), "gy", 1), shift(stack(lower, small), "gy", -1)
-    up2, down2 = shift(small, "gy", 2), shift(small, "gy", -2)
-    if final:
-        state = jnp.broadcast_to(state[:1] + up2[6, 1:2] + down2[6, 2:3], (8, 128))
-    else:
-        ahead, behind = upper[26, :2] + up2[6, :2], lower[26, :2] + state[:2]
-        state = spread_rows(ahead + behind, ahead, behind)
-    groups = [coarse] + [v.reshape(48, 128) for v in (upper[20:26], lower[20:26], up2[:6], down2[:6])]
-    return [body, upper, lower] + groups, state
+def joint_exchange(own, share, low, high, state, final):
+    above = shift(jnp.concatenate([low, share, state]), "gz", 1)
+    below = shift(jnp.concatenate([high, share, state]), "gz", -1)
+    first, last, small = call(
+        functools.partial(join_z_kernel, final), [shape(144, 128), shape(144, 128), shape(32, 128)], count=5
+    )(own, share, state, above, below)
+    before, after, across = shift(last, "gx", -1), shift(first, "gx", 1), shift(small, "gx", 2)
+    body, upper, lower, ahead, behind = call(
+        functools.partial(join_x_kernel, final), [shape(512, 128), shape(216, 128), shape(216, 128), shape(32, 128), shape(32, 128)],
+        [pltpu.VMEM((4, 24, 128), F32)], count=7,
+    )(own, above, below, small, before, after, across)
+    return body, upper, shift(upper, "gy", 1), shift(lower, "gy", -1), shift(ahead, "gy", 2), shift(behind, "gy", -2)
 
 
 def gather(unit):
@@ -568,8 +583,7 @@
     def scratch(*shapes):
         return [pltpu.VMEM(s, F32) for s in shapes]
 
-    block, halo, mids = shape(*BLOCK), shape(*HALO), shape(*MID)
-    packs, tile = shape(5, 16, 128), shape(8, 128)
+    block, halo, mids, tile = shape(*BLOCK), shape(*HALO), shape(*MID), shape(8, 128)
     down_scratch = scratch(HALO, MID, (2, 4, 16, 128), (16 * UNITS, 128))
     up_scratch = scratch((18, 16, 256), (18, 16, 256), (18, 16, 256), (6, 32, 256), MID, MID, HALO, HALO)
 
@@ -581,19 +595,25 @@
     weight0, weight1, x0, x1, unit = call(
         first_down_kernel, [halo, mids, halo, mids, shape(2, 8, 128)], down_scratch + scratch((16 * UNITS, 128)), count=3
     )(*halos)
-    weight2, u0, w0, low, high, dots = call(
-        first_up_kernel, [shape(18, 16, 256), block, block, packs, packs, tile], up_scratch, count=6
+    share_outs = [shape(24, 128), shape(16, 128), shape(16, 128)]
+    share_scratch = scratch(BLOCK, (10, 32, 256), (10, 32, 256), (2, 6, 32, 128))
+    weight2, u0, w0, share, low, high, dots = call(
+        first_up_kernel, [shape(18, 16, 256), block, block, *share_outs, tile], up_scratch + share_scratch, count=6
     )(gather(unit), weight1, weight0, x0, x1, both)
 
     whole_scratch = scratch(HALO, MID, HALO, (512, 128)) + up_scratch[:-1]
-    halos, state = joint_exchange(w0, low, high, weight0, weight1, dots, False)
-    m0, n0, low, high = call(second_kernel, [block, block, packs, packs], scratch(HALO) + whole_scratch, count=12)(
-        *halos, weight2, weight1, weight0, both
-    )
-    halos, first = joint_exchange(n0, low, high, weight0, weight1, state, True)
-    r1, u1, w1, m1, n1, dots = call(
-        third_kernel, [block] * 5 + [tile], scratch(HALO, BLOCK) + whole_scratch, count=17
-    )(*halos, weight2, weight1, weight0, both, first, u0, w0, m0, n0)
+    halos = joint_exchange(w0, share, low, high, dots, False)
+    _, own, up1, down1, up2, _ = halos
+    ahead, behind = up1[208:210] + up2[24:26], down1[208:210] + own[208:210]
+    state = jnp.concatenate([ahead + behind, ahead, behind, jnp.zeros((2, 128), F32)])
+    state = state + shift(state, "gz", 4)
+    m0, n0, share, low, high = call(
+        second_kernel, [block, block, *share_outs], scratch(HALO) + whole_scratch + share_scratch, count=10
+    )(*halos, weight2, weight1, weight0, both)
+    halos = joint_exchange(n0, share, low, high, state, True)
+    r1, u1, w1, m1, n1, first, dots = call(
+        third_kernel, [block] * 5 + [tile, tile], scratch(HALO, BLOCK) + whole_scratch, count=14
+    )(*halos, weight2, weight1, weight0, both, u0, w0, m0, n0)
     field, residual = call(finish_kernel, [block] * 2, count=11)(
         first, total(dots), u0, w0, m0, n0, r1, u1, w1, m1, n1
     )

time: 132 us -> 130 us (0.985)
  starting transfers between devices: 54.7 us -> 39.9 us
  blocking collectives: 26.4 us -> 40.3 us
    all_to_all x0 -> x1, blocking collectives: none -> 14.7 us  [gather(): lax.all_to_all(jnp.broadcast_to(unit[None], (count,) + unit.shape), ('gx'...]
    all_to_all x1 -> x0, waiting for transfers between devices: 9.41 us -> none  [gather(): lax.all_to_all(jnp.broadcast_to(unit[None], (count,) + unit.shape), ('gx'...]
    ppermute x25, waiting for transfers between devices: 19.7 us -> 29 us  [shift(): lax.ppermute(v, axis, [((i + distance) % count, i) for i in range(count)])]
    ppermute x25, starting transfers between devices: 49.2 us -> 39.9 us  [shift(): lax.ppermute(v, axis, [((i + distance) % count, i) for i in range(count)])]
    all_to_all x1 -> x0, starting transfers between devices: 5.49 us -> none  [gather(): lax.all_to_all(jnp.broadcast_to(unit[None], (count,) + unit.shape), ('gx'...]
  transfers between devices with their start and end apart: 26 -> 25, of which waited for: 14 -> 14; matrix products, arithmetic and copies ran while one was open for 1% -> 1% of each run, Pallas kernels for 1% -> 4%
where the time goes in v5:
time: 130 us; the launch traced here: 129 us
  blocking collectives  40.3 us (31%)
  starting transfers between devices  39.9 us (31%)
  waiting for transfers between devices  29 us (22%)
  Pallas kernels  17.8 us (14%)
    ppermute x25, starting transfers between devices, shift(): lax.ppermute(v, axis, [((i + distance) % count, i) for i in range(count)])  39.9 us
    ppermute x25, waiting for transfers between devices, shift(): lax.ppermute(v, axis, [((i + distance) % count, i) for i in range(count)])  29 us
    all_to_all x1, blocking collectives, total(): lax.all_to_all(jnp.broadcast_to(v[None, :1], (count, 1, 128)), axes, 0, 0...  25.7 us
    all_to_all x1, blocking collectives, gather(): lax.all_to_all(jnp.broadcast_to(unit[None], (count,) + unit.shape), ('gx'...  14.7 us
    pallas_call x1, Pallas kernels, local(): call(second_kernel, [block, block, *share_outs], scratch(HALO) + whole_sc...  4.56 us
    pallas_call x1, Pallas kernels, local(): call(third_kernel, [block] * 5 + [tile, tile], scratch(HALO, BLOCK) + who...  3.5 us
    pallas_call x1, Pallas kernels, local(): call(first_up_kernel, [shape(18, 16, 256), block, block, *share_outs, til...  3.2 us
    pallas_call x1, Pallas kernels, local(): call(first_down_kernel, [halo, mids, halo, mids, shape(2, 8, 128)], down_...  2.94 us
  transfers between devices with their start and end apart: 25, of which 14 were waited for; matrix products, arithmetic and copies ran while one was open for 1% of the time, Pallas kernels for 4%

profile of v5, /device:TPU:1, one launch (start us, length us, event | category | flops | bytes accessed | tf_op | source)
XLA Modules:
  0.0 129.3 jit_solution(9280272680535200534)
XLA Ops:
  0.6 1.9 %shard_map.50 = (f32[2,16,16,128]{3,2,1,0:T(8,128)}, f32[2,6,16,128]{3,2,1,0:T(8,128)}, f32[2,6,16,128]{3,2,1,0:T(8,128)}) custom-call(f32[16,16,128]{2,1,0:T(8,128)} %rhs_in.1, s32[16,16,128]{2,1,0:T(8,128)} %classes_in.1, f32[16]{0:T(128)} %table_in.1), custom_call_target="tpu_custom_call" | custom-call | tf_op jit(solution)/shard_map/pallas_call | solution.py:590
  2.6 2.7 %collective-permute-start.1 = (f32[2,6,16,128]{3,2,1,0:T(8,128)}, f32[2,6,16,128]{3,2,1,0:T(8,128)S(1)}, u32[]{:S(2)}, u32[]{:S(2)}) collective-permute-start(f32[2,6,16,128]{3,2,1,0:T(8,128)} %get-tuple-element.49), channel_id=1, source_target_pairs={{7,0},{0,1},{1,2},{2,3},{3,4},{4,5},{5,6},{6,7},{15,8},{8,9},{9,10... | collective-permute-start | bytes 294920 | tf_op jit(solution)/shard_map/ppermute | solution.py:543
  7.2 2.3 %collective-permute-done = f32[2,6,16,128]{3,2,1,0:T(8,128)S(1)} collective-permute-done((f32[2,6,16,128]{3,2,1,0:T(8,128)}, f32[2,6,16,128]{3,2,1,0:T(8,128)S(1)}, u32[]{:S(2)}, u32[]{:S(2)}) %collective-permute-start) | collective-permute-done | bytes 98336 | tf_op jit(solution)/shard_map/ppermute | solution.py:543
  9.5 1.3 collective-permute-start.2
  10.8 1.5 %collective-permute-start.3 = (f32[2,7,16,128]{3,2,1,0:T(8,128)S(1)}, f32[2,7,16,128]{3,2,1,0:T(8,128)S(1)}, u32[]{:S(2)}, u32[]{:S(2)}) collective-permute-start(f32[2,7,16,128]{3,2,1,0:T(8,128)S(1)} %pad_maximum_fusion.1), channel_id=1, source_target_pairs={{64,0},{128,64},{192,128},{0,192},{65,1},{129,65},{193,129},{1,193... | collective-permute-start | bytes 344072 | tf_op jit(solution)/shard_map/ppermute | solution.py:543
  12.4 2.1 %collective-permute-done.2 = f32[2,7,16,128]{3,2,1,0:T(8,128)S(1)} collective-permute-done((f32[2,7,16,128]{3,2,1,0:T(8,128)S(1)}, f32[2,7,16,128]{3,2,1,0:T(8,128)S(1)}, u32[]{:S(2)}, u32[]{:S(2)}) %collective-permute-start.2) | collective-permute-done | bytes 114720 | tf_op jit(solution)/shard_map/ppermute | solution.py:543
  15.2 6.2 %collective-permute-start.4 = (f32[400,128]{1,0:T(8,128)S(1)}, f32[400,128]{1,0:T(8,128)S(1)}, u32[]{:S(2)}, u32[]{:S(2)}) collective-permute-start(f32[400,128]{1,0:T(8,128)S(1)} %get-tuple-element.50), channel_id=1, source_target_pairs={{8,0},{16,8},{24,16},{32,24},{40,32},{48,40},{56,48},{0,56},{9,1},... | collective-permute-start | bytes 614408 | tf_op jit(solution)/shard_map/ppermute | solution.py:543
  21.4 3.5 %collective-permute-done.4.upper = f32[400,128]{1,0:T(8,128)S(1)} collective-permute-done((f32[400,128]{1,0:T(8,128)S(1)}, f32[400,128]{1,0:T(8,128)S(1)}, u32[]{:S(2)}, u32[]{:S(2)}) %collective-permute-start.4) | collective-permute-done | bytes 204832 | tf_op jit(solution)/shard_map/ppermute | solution.py:543
  24.9 3.1 %collective-permute-done.5.lower = f32[400,128]{1,0:T(8,128)S(1)} collective-permute-done((f32[400,128]{1,0:T(8,128)S(1)}, f32[400,128]{1,0:T(8,128)S(1)}, u32[]{:S(2)}, u32[]{:S(2)}) %collective-permute-start.5) | collective-permute-done | bytes 204832 | tf_op jit(solution)/shard_map/ppermute | solution.py:543
  28.0 2.9 %shard_map.52 = (f32[26,32,256]{2,1,0:T(8,128)S(1)}, f32[12,32,256]{2,1,0:T(8,128)S(1)}, f32[26,32,256]{2,1,0:T(8,128)S(1)}, f32[12,32,256]{2,1,0:T(8,128)S(1)}, f32[2,8,128]{2,1,0:T(8,128)S(1)}) custom-call(f32[1280,128]{1,0:T(8,128)S(1)} %bitcast.5, f32[400,128]{1,0:T(8,128)S(1)} %collective-permute-done.4.upper, f32[400,128]{1,0:T(8,128)S(1)} %collective-permute-done.5.lower), custom_call_target="tpu_custom_call" | custom-call | tf_op jit(solution)/shard_map/pallas_call | solution.py:595
  31.0 14.7 %all_to_all.10.gather = f32[32,2,8,128]{3,2,1,0:T(8,128)S(1)} all-to-all(f32[32,2,8,128]{3,2,1,0:T(8,128)S(1)} %broadcast_in_dim.10), channel_id=1, replica_groups=mesh['gx'=4,'gy'=8,'gz'=8] {'gx','gy'}, dimensions={0} | all-to-all | bytes 524288 | tf_op jit(solution)/shard_map/all_to_all | solution.py:572
  45.7 3.2 %shard_map.53 = (f32[18,16,256]{2,1,0:T(8,128)S(1)}, f32[16,16,128]{2,1,0:T(8,128)S(1)}, f32[16,16,128]{2,1,0:T(8,128)S(1)}, f32[24,128]{1,0:T(8,128)S(1)}, f32[...) custom-call(f32[32,2,8,128]{3,2,1,0:T(8,128)S(1)} %all_to_all.10.gather, ...), custom_call_target="tpu_custom_call" | custom-call | tf_op jit(solution)/shard_map/pallas_call | solution.py:600
  48.9 4.1 %collective-permute-start.6 = (f32[48,128]{1,0:T(8,128)S(1)}, f32[48,128]{1,0:T(8,128)S(1)}, u32[]{:S(2)}, u32[]{:S(2)}) collective-permute-start(f32[48,128]{1,0:T(8,128)S(1)} %get-tuple-element.104), channel_id=1, source_target_pairs={{1,0},{2,1},{3,2},{4,3},{5,4},{6,5},{7,6},{0,7},{9,8},{10,9},{11,1... | collective-permute-start | bytes 73736 | tf_op jit(solution)/shard_map/ppermute | solution.py:543
  53.0 1.7 %collective-permute-start.7 = (f32[48,128]{1,0:T(8,128)S(1)}, f32[48,128]{1,0:T(8,128)S(1)}, u32[]{:S(2)}, u32[]{:S(2)}) collective-permute-start(f32[48,128]{1,0:T(8,128)S(1)} %get-tuple-element.103), channel_id=1, source_target_pairs={{7,0},{0,1},{1,2},{2,3},{3,4},{4,5},{5,6},{6,7},{15,8},{8,9},{9,10... | collective-permute-start | bytes 73736 | tf_op jit(solution)/shard_map/ppermute | solution.py:543
  54.7 1.5 %collective-permute-done.6.above = f32[48,128]{1,0:T(8,128)S(1)} collective-permute-done((f32[48,128]{1,0:T(8,128)S(1)}, f32[48,128]{1,0:T(8,128)S(1)}, u32[]{:S(2)}, u32[]{:S(2)}) %collective-permute-start.6) | collective-permute-done | bytes 24608 | tf_op jit(solution)/shard_map/ppermute | solution.py:543
  56.6 2.3 %collective-permute-start.9 = (f32[144,128]{1,0:T(8,128)S(1)}, f32[144,128]{1,0:T(8,128)S(1)}, u32[]{:S(2)}, u32[]{:S(2)}) collective-permute-start(f32[144,128]{1,0:T(8,128)S(1)} %get-tuple-element.64), channel_id=1, source_target_pairs={{64,0},{128,64},{192,128},{0,192},{65,1},{129,65},{193,129},{1,193... | collective-permute-start | bytes 221192 | tf_op jit(solution)/shard_map/ppermute | solution.py:543
  58.9 4.2 %collective-permute-done.10.across = f32[32,128]{1,0:T(8,128)S(1)} collective-permute-done((f32[32,128]{1,0:T(8,128)S(1)}, f32[32,128]{1,0:T(8,128)S(1)}, u32[]{:S(2)}, u32[]{:S(2)}) %collective-permute-start.10) | collective-permute-done | bytes 16416 | tf_op jit(solution)/shard_map/ppermute | solution.py:543
  63.3 1.8 %collective-permute-start.12 = (f32[216,128]{1,0:T(8,128)S(1)}, f32[216,128]{1,0:T(8,128)S(1)}, u32[]{:S(2)}, u32[]{:S(2)}) collective-permute-start(f32[216,128]{1,0:T(8,128)S(1)} %get-tuple-element.67), channel_id=1, source_target_pairs={{56,0},{0,8},{8,16},{16,24},{24,32},{32,40},{40,48},{48,56},{57,1}... | collective-permute-start | bytes 331784 | tf_op jit(solution)/shard_map/ppermute | solution.py:543
  65.1 1.3 %collective-permute-start.13 = (f32[32,128]{1,0:T(8,128)S(1)}, f32[32,128]{1,0:T(8,128)S(1)}, u32[]{:S(2)}, u32[]{:S(2)}) collective-permute-start(f32[32,128]{1,0:T(8,128)S(1)} %get-tuple-element.68), channel_id=1, source_target_pairs={{16,0},{24,8},{32,16},{40,24},{48,32},{56,40},{0,48},{8,56},{17,1}... | collective-permute-start | bytes 49160 | tf_op jit(solution)/shard_map/ppermute | solution.py:543
  67.6 1.1 collective-permute-done.13.up2
  68.8 2.4 %collective-permute-start.15 = (f32[8,128]{1,0:T(8,128)S(1)}, f32[8,128]{1,0:T(8,128)S(1)}, u32[]{:S(2)}, u32[]{:S(2)}) collective-permute-start(f32[8,128]{1,0:T(8,128)S(1)} %maximum_maximum_fusion), channel_id=1, source_target_pairs={{4,0},{5,1},{6,2},{7,3},{0,4},{1,5},{2,6},{3,7},{12,8},{13,9},{14,... | collective-permute-start | bytes 12296 | tf_op jit(solution)/shard_map/ppermute | solution.py:543
  71.2 4.6 %shard_map.56 = (f32[16,16,128]{2,1,0:T(8,128)S(1)}, f32[16,16,128]{2,1,0:T(8,128)S(1)}, f32[24,128]{1,0:T(8,128)S(1)}, f32[16,128]{1,0:T(8,128)S(1)}, f32[16,128]{1,0:T(8,128)S(1)}) custom-call(f32[512,128]{1,0:T(8,128)S(1)} %get-tuple-element.65.body, f32[216,128]{1,0:T(8,128)S(1)} %get-tuple-element.66.own, f32[216,128]{1,0:T(8,128)S(1)} %collective-permute-done.11.up1, ...), custom_call_target="tpu_custom_call" | custom-call | tf_op jit(solution)/shard_map/pallas_call | solution.py:610
  75.9 5.6 %collective-permute-start.16 = (f32[48,128]{1,0:T(8,128)S(1)}, f32[48,128]{1,0:T(8,128)S(1)}, u32[]{:S(2)}, u32[]{:S(2)}) collective-permute-start(f32[48,128]{1,0:T(8,128)S(1)} %get-tuple-element.102), channel_id=1, source_target_pairs={{1,0},{2,1},{3,2},{4,3},{5,4},{6,5},{7,6},{0,7},{9,8},{10,9},{11,1... | collective-permute-start | bytes 73736 | tf_op jit(solution)/shard_map/ppermute | solution.py:543
  81.5 1.4 %collective-permute-done.16.above = f32[48,128]{1,0:T(8,128)S(1)} collective-permute-done((f32[48,128]{1,0:T(8,128)S(1)}, f32[48,128]{1,0:T(8,128)S(1)}, u32[]{:S(2)}, u32[]{:S(2)}) %collective-permute-start.16) | collective-permute-done | bytes 24608 | tf_op jit(solution)/shard_map/ppermute | solution.py:543
  83.0 2.7 %collective-permute-start.19 = (f32[144,128]{1,0:T(8,128)S(1)}, f32[144,128]{1,0:T(8,128)S(1)}, u32[]{:S(2)}, u32[]{:S(2)}) collective-permute-start(f32[144,128]{1,0:T(8,128)S(1)} %get-tuple-element.77), channel_id=1, source_target_pairs={{64,0},{128,64},{192,128},{0,192},{65,1},{129,65},{193,129},{1,193... | collective-permute-start | bytes 221192 | tf_op jit(solution)/shard_map/ppermute | solution.py:543
  85.6 4.2 %collective-permute-done.20.across = f32[32,128]{1,0:T(8,128)S(1)} collective-permute-done((f32[32,128]{1,0:T(8,128)S(1)}, f32[32,128]{1,0:T(8,128)S(1)}, u32[]{:S(2)}, u32[]{:S(2)}) %collective-permute-start.20) | collective-permute-done | bytes 16416 | tf_op jit(solution)/shard_map/ppermute | solution.py:543
  89.9 1.7 %collective-permute-start.21 = (f32[216,128]{1,0:T(8,128)S(1)}, f32[216,128]{1,0:T(8,128)S(1)}, u32[]{:S(2)}, u32[]{:S(2)}) collective-permute-start(f32[216,128]{1,0:T(8,128)S(1)} %get-tuple-element.79.own), channel_id=1, source_target_pairs={{8,0},{16,8},{24,16},{32,24},{40,32},{48,40},{56,48},{0,56},{9,1},... | collective-permute-start | bytes 331784 | tf_op jit(solution)/shard_map/ppermute | solution.py:543
  91.7 2.3 %collective-permute-start.23 = (f32[32,128]{1,0:T(8,128)S(1)}, f32[32,128]{1,0:T(8,128)S(1)}, u32[]{:S(2)}, u32[]{:S(2)}) collective-permute-start(f32[32,128]{1,0:T(8,128)S(1)} %get-tuple-element.81), channel_id=1, source_target_pairs={{16,0},{24,8},{32,16},{40,24},{48,32},{56,40},{0,48},{8,56},{17,1}... | collective-permute-start | bytes 49160 | tf_op jit(solution)/shard_map/ppermute | solution.py:543
  95.1 3.5 %collective-permute-done.24.down2 = f32[32,128]{1,0:T(8,128)S(1)} collective-permute-done((f32[32,128]{1,0:T(8,128)S(1)}, f32[32,128]{1,0:T(8,128)S(1)}, u32[]{:S(2)}, u32[]{:S(2)}) %collective-permute-start.24) | collective-permute-done | bytes 16416 | tf_op jit(solution)/shard_map/ppermute | solution.py:543
  98.7 3.5 %shard_map.59 = (f32[16,16,128]{2,1,0:T(8,128)S(1)}, f32[16,16,128]{2,1,0:T(8,128)S(1)}, f32[16,16,128]{2,1,0:T(8,128)S(1)}, f32[16,16,128]{2,1,0:T(8,128)S(1)},...) custom-call(f32[512,128]{1,0:T(8,128)S(1)} %get-tuple-element.78.body, ...), custom_call_target="tpu_custom_call" | custom-call | tf_op jit(solution)/shard_map/pallas_call | solution.py:614
  102.3 25.7 %all_to_all.11 = f32[256,1,128]{2,1,0:T(1,128)S(1)} all-to-all(f32[256,1,128]{2,1,0:T(1,128)S(1)} %broadcast_in_dim.25), channel_id=1, replica_groups=mesh['gx'=4,'gy'=8,'gz'=8] {'gx','gy','gz'}, dimensions={0} | all-to-all | bytes 262144 | tf_op jit(solution)/shard_map/all_to_all | solution.py:578
  128.0 1.3 %shard_map.60 = (f32[16,16,128]{2,1,0:T(8,128)}, f32[16,16,128]{2,1,0:T(8,128)}) custom-call(f32[8,128]{1,0:T(8,128)S(1)} %get-tuple-element.85.first, f32[8,128]{1,0:T(8,128)S(1)} %broadcast_in_dim.26.second, f32[16,16,128]{2,1,0:T(8,128)S(1)} %get-tuple-element.83.u0, f32[16,16,128]{2,1,0:T(8,128)S(1)} %get-tuple-element.57.own.w0, ...), custom_call_target="tpu_custom_call" | custom-call | tf_op jit(solution)/shard_map/pallas_call | solution.py:617
  (56 shorter events, 6.1 us)
Async XLA Ops:
  2.6 4.2 %copy-start = (f32[2,16,16,128]{3,2,1,0:T(8,128)S(1)}, f32[2,16,16,128]{3,2,1,0:T(8,128)}, u32[]{:S(2)}) copy-start(f32[2,16,16,128]{3,2,1,0:T(8,128)} %get-tuple-element.47.both) | copy-start | bytes 786436
  2.6 4.7 %collective-permute-start.1 = (f32[2,6,16,128]{3,2,1,0:T(8,128)}, f32[2,6,16,128]{3,2,1,0:T(8,128)S(1)}, u32[]{:S(2)}, u32[]{:S(2)}) collective-permute-start(f32[2,6,16,128]{3,2,1,0:T(8,128)} %get-tuple-element.49), channel_id=1, source_target_pairs={{7,0},{0,1},{1,2},{2,3},{3,4},{4,5},{5,6},{6,7},{15,8},{8,9},{9,10... | collective-permute-start | bytes 294920 | tf_op jit(solution)/shard_map/ppermute | solution.py:543
  5.3 4.3 %collective-permute-start = (f32[2,6,16,128]{3,2,1,0:T(8,128)}, f32[2,6,16,128]{3,2,1,0:T(8,128)S(1)}, u32[]{:S(2)}, u32[]{:S(2)}) collective-permute-start(f32[2,6,16,128]{3,2,1,0:T(8,128)} %get-tuple-element.48), channel_id=1, source_target_pairs={{1,0},{2,1},{3,2},{4,3},{5,4},{6,5},{7,6},{0,7},{9,8},{10,9},{11,1... | collective-permute-start | bytes 294920 | tf_op jit(solution)/shard_map/ppermute | solution.py:543
  9.5 4.9 %collective-permute-start.2 = (f32[2,7,16,128]{3,2,1,0:T(8,128)S(1)}, f32[2,7,16,128]{3,2,1,0:T(8,128)S(1)}, u32[]{:S(2)}, u32[]{:S(2)}) collective-permute-start(f32[2,7,16,128]{3,2,1,0:T(8,128)S(1)} %pad_maximum_fusion), channel_id=1, source_target_pairs={{192,0},{0,64},{64,128},{128,192},{193,1},{1,65},{65,129},{129,193... | collective-permute-start | bytes 344072 | tf_op jit(solution)/shard_map/ppermute | solution.py:543
  10.8 4.2 %collective-permute-start.3 = (f32[2,7,16,128]{3,2,1,0:T(8,128)S(1)}, f32[2,7,16,128]{3,2,1,0:T(8,128)S(1)}, u32[]{:S(2)}, u32[]{:S(2)}) collective-permute-start(f32[2,7,16,128]{3,2,1,0:T(8,128)S(1)} %pad_maximum_fusion.1), channel_id=1, source_target_pairs={{64,0},{128,64},{192,128},{0,192},{65,1},{129,65},{193,129},{1,193... | collective-permute-start | bytes 344072 | tf_op jit(solution)/shard_map/ppermute | solution.py:543
  15.2 9.7 %collective-permute-start.4 = (f32[400,128]{1,0:T(8,128)S(1)}, f32[400,128]{1,0:T(8,128)S(1)}, u32[]{:S(2)}, u32[]{:S(2)}) collective-permute-start(f32[400,128]{1,0:T(8,128)S(1)} %get-tuple-element.50), channel_id=1, source_target_pairs={{8,0},{16,8},{24,16},{32,24},{40,32},{48,40},{56,48},{0,56},{9,1},... | collective-permute-start | bytes 614408 | tf_op jit(solution)/shard_map/ppermute | solution.py:543
  21.4 6.6 %collective-permute-start.5 = (f32[400,128]{1,0:T(8,128)S(1)}, f32[400,128]{1,0:T(8,128)S(1)}, u32[]{:S(2)}, u32[]{:S(2)}) collective-permute-start(f32[400,128]{1,0:T(8,128)S(1)} %get-tuple-element.51), channel_id=1, source_target_pairs={{56,0},{0,8},{8,16},{16,24},{24,32},{32,40},{40,48},{48,56},{57,1}... | collective-permute-start | bytes 614408 | tf_op jit(solution)/shard_map/ppermute | solution.py:543
  48.9 7.2 %collective-permute-start.6 = (f32[48,128]{1,0:T(8,128)S(1)}, f32[48,128]{1,0:T(8,128)S(1)}, u32[]{:S(2)}, u32[]{:S(2)}) collective-permute-start(f32[48,128]{1,0:T(8,128)S(1)} %get-tuple-element.104), channel_id=1, source_target_pairs={{1,0},{2,1},{3,2},{4,3},{5,4},{6,5},{7,6},{0,7},{9,8},{10,9},{11,1... | collective-permute-start | bytes 73736 | tf_op jit(solution)/shard_map/ppermute | solution.py:543
  53.0 3.2 %collective-permute-start.7 = (f32[48,128]{1,0:T(8,128)S(1)}, f32[48,128]{1,0:T(8,128)S(1)}, u32[]{:S(2)}, u32[]{:S(2)}) collective-permute-start(f32[48,128]{1,0:T(8,128)S(1)} %get-tuple-element.103), channel_id=1, source_target_pairs={{7,0},{0,1},{1,2},{2,3},{3,4},{4,5},{5,6},{6,7},{15,8},{8,9},{9,10... | collective-permute-start | bytes 73736 | tf_op jit(solution)/shard_map/ppermute | solution.py:543
  56.2 7.0 %collective-permute-start.8 = (f32[144,128]{1,0:T(8,128)S(1)}, f32[144,128]{1,0:T(8,128)S(1)}, u32[]{:S(2)}, u32[]{:S(2)}) collective-permute-start(f32[144,128]{1,0:T(8,128)S(1)} %get-tuple-element.63), channel_id=1, source_target_pairs={{192,0},{0,64},{64,128},{128,192},{193,1},{1,65},{65,129},{129,193... | collective-permute-start | bytes 221192 | tf_op jit(solution)/shard_map/ppermute | solution.py:543
  56.6 6.6 %collective-permute-start.9 = (f32[144,128]{1,0:T(8,128)S(1)}, f32[144,128]{1,0:T(8,128)S(1)}, u32[]{:S(2)}, u32[]{:S(2)}) collective-permute-start(f32[144,128]{1,0:T(8,128)S(1)} %get-tuple-element.64), channel_id=1, source_target_pairs={{64,0},{128,64},{192,128},{0,192},{65,1},{129,65},{193,129},{1,193... | collective-permute-start | bytes 221192 | tf_op jit(solution)/shard_map/ppermute | solution.py:543
  58.9 4.2 %collective-permute-start.10 = (f32[32,128]{1,0:T(8,128)S(1)}, f32[32,128]{1,0:T(8,128)S(1)}, u32[]{:S(2)}, u32[]{:S(2)}) collective-permute-start(f32[32,128]{1,0:T(8,128)S(1)} %get-tuple-element.62.small), channel_id=1, source_target_pairs={{128,0},{192,64},{0,128},{64,192},{129,1},{193,65},{1,129},{65,193... | collective-permute-start | bytes 49160 | tf_op jit(solution)/shard_map/ppermute | solution.py:543
  63.2 5.5 %collective-permute-start.11 = (f32[216,128]{1,0:T(8,128)S(1)}, f32[216,128]{1,0:T(8,128)S(1)}, u32[]{:S(2)}, u32[]{:S(2)}) collective-permute-start(f32[216,128]{1,0:T(8,128)S(1)} %get-tuple-element.66.own), channel_id=1, source_target_pairs={{8,0},{16,8},{24,16},{32,24},{40,32},{48,40},{56,48},{0,56},{9,1},... | collective-permute-start | bytes 331784 | tf_op jit(solution)/shard_map/ppermute | solution.py:543
  63.3 5.4 %collective-permute-start.12 = (f32[216,128]{1,0:T(8,128)S(1)}, f32[216,128]{1,0:T(8,128)S(1)}, u32[]{:S(2)}, u32[]{:S(2)}) collective-permute-start(f32[216,128]{1,0:T(8,128)S(1)} %get-tuple-element.67), channel_id=1, source_target_pairs={{56,0},{0,8},{8,16},{16,24},{24,32},{32,40},{40,48},{48,56},{57,1}... | collective-permute-start | bytes 331784 | tf_op jit(solution)/shard_map/ppermute | solution.py:543
  65.1 3.6 %collective-permute-start.13 = (f32[32,128]{1,0:T(8,128)S(1)}, f32[32,128]{1,0:T(8,128)S(1)}, u32[]{:S(2)}, u32[]{:S(2)}) collective-permute-start(f32[32,128]{1,0:T(8,128)S(1)} %get-tuple-element.68), channel_id=1, source_target_pairs={{16,0},{24,8},{32,16},{40,24},{48,32},{56,40},{0,48},{8,56},{17,1}... | collective-permute-start | bytes 49160 | tf_op jit(solution)/shard_map/ppermute | solution.py:543
  66.5 4.7 %collective-permute-start.14 = (f32[32,128]{1,0:T(8,128)S(1)}, f32[32,128]{1,0:T(8,128)S(1)}, u32[]{:S(2)}, u32[]{:S(2)}) collective-permute-start(f32[32,128]{1,0:T(8,128)S(1)} %get-tuple-element.69), channel_id=1, source_target_pairs={{48,0},{56,8},{0,16},{8,24},{16,32},{24,40},{32,48},{40,56},{49,1}... | collective-permute-start | bytes 49160 | tf_op jit(solution)/shard_map/ppermute | solution.py:543
  68.8 7.0 %collective-permute-start.15 = (f32[8,128]{1,0:T(8,128)S(1)}, f32[8,128]{1,0:T(8,128)S(1)}, u32[]{:S(2)}, u32[]{:S(2)}) collective-permute-start(f32[8,128]{1,0:T(8,128)S(1)} %maximum_maximum_fusion), channel_id=1, source_target_pairs={{4,0},{5,1},{6,2},{7,3},{0,4},{1,5},{2,6},{3,7},{12,8},{13,9},{14,... | collective-permute-start | bytes 12296 | tf_op jit(solution)/shard_map/ppermute | solution.py:543
  75.9 7.0 %collective-permute-start.16 = (f32[48,128]{1,0:T(8,128)S(1)}, f32[48,128]{1,0:T(8,128)S(1)}, u32[]{:S(2)}, u32[]{:S(2)}) collective-permute-start(f32[48,128]{1,0:T(8,128)S(1)} %get-tuple-element.102), channel_id=1, source_target_pairs={{1,0},{2,1},{3,2},{4,3},{5,4},{6,5},{7,6},{0,7},{9,8},{10,9},{11,1... | collective-permute-start | bytes 73736 | tf_op jit(solution)/shard_map/ppermute | solution.py:543
  81.5 1.4 %collective-permute-start.17 = (f32[48,128]{1,0:T(8,128)S(1)}, f32[48,128]{1,0:T(8,128)S(1)}, u32[]{:S(2)}, u32[]{:S(2)}) collective-permute-start(f32[48,128]{1,0:T(8,128)S(1)} %get-tuple-element.101), channel_id=1, source_target_pairs={{7,0},{0,1},{1,2},{2,3},{3,4},{4,5},{5,6},{6,7},{15,8},{8,9},{9,10... | collective-permute-start | bytes 73736 | tf_op jit(solution)/shard_map/ppermute | solution.py:543
  82.9 7.0 %collective-permute-start.18 = (f32[144,128]{1,0:T(8,128)S(1)}, f32[144,128]{1,0:T(8,128)S(1)}, u32[]{:S(2)}, u32[]{:S(2)}) collective-permute-start(f32[144,128]{1,0:T(8,128)S(1)} %get-tuple-element.76), channel_id=1, source_target_pairs={{192,0},{0,64},{64,128},{128,192},{193,1},{1,65},{65,129},{129,193... | collective-permute-start | bytes 221192 | tf_op jit(solution)/shard_map/ppermute | solution.py:543
  83.0 6.9 %collective-permute-start.19 = (f32[144,128]{1,0:T(8,128)S(1)}, f32[144,128]{1,0:T(8,128)S(1)}, u32[]{:S(2)}, u32[]{:S(2)}) collective-permute-start(f32[144,128]{1,0:T(8,128)S(1)} %get-tuple-element.77), channel_id=1, source_target_pairs={{64,0},{128,64},{192,128},{0,192},{65,1},{129,65},{193,129},{1,193... | collective-permute-start | bytes 221192 | tf_op jit(solution)/shard_map/ppermute | solution.py:543
  85.6 4.2 %collective-permute-start.20 = (f32[32,128]{1,0:T(8,128)S(1)}, f32[32,128]{1,0:T(8,128)S(1)}, u32[]{:S(2)}, u32[]{:S(2)}) collective-permute-start(f32[32,128]{1,0:T(8,128)S(1)} %get-tuple-element.75.small), channel_id=1, source_target_pairs={{128,0},{192,64},{0,128},{64,192},{129,1},{193,65},{1,129},{65,193... | collective-permute-start | bytes 49160 | tf_op jit(solution)/shard_map/ppermute | solution.py:543
  89.9 8.7 %collective-permute-start.21 = (f32[216,128]{1,0:T(8,128)S(1)}, f32[216,128]{1,0:T(8,128)S(1)}, u32[]{:S(2)}, u32[]{:S(2)}) collective-permute-start(f32[216,128]{1,0:T(8,128)S(1)} %get-tuple-element.79.own), channel_id=1, source_target_pairs={{8,0},{16,8},{24,16},{32,24},{40,32},{48,40},{56,48},{0,56},{9,1},... | collective-permute-start | bytes 331784 | tf_op jit(solution)/shard_map/ppermute | solution.py:543
  91.6 7.0 %collective-permute-start.22 = (f32[216,128]{1,0:T(8,128)S(1)}, f32[216,128]{1,0:T(8,128)S(1)}, u32[]{:S(2)}, u32[]{:S(2)}) collective-permute-start(f32[216,128]{1,0:T(8,128)S(1)} %get-tuple-element.80), channel_id=1, source_target_pairs={{56,0},{0,8},{8,16},{16,24},{24,32},{32,40},{40,48},{48,56},{57,1}... | collective-permute-start | bytes 331784 | tf_op jit(solution)/shard_map/ppermute | solution.py:543
  91.7 3.5 %collective-permute-start.23 = (f32[32,128]{1,0:T(8,128)S(1)}, f32[32,128]{1,0:T(8,128)S(1)}, u32[]{:S(2)}, u32[]{:S(2)}) collective-permute-start(f32[32,128]{1,0:T(8,128)S(1)} %get-tuple-element.81), channel_id=1, source_target_pairs={{16,0},{24,8},{32,16},{40,24},{48,32},{56,40},{0,48},{8,56},{17,1}... | collective-permute-start | bytes 49160 | tf_op jit(solution)/shard_map/ppermute | solution.py:543
  94.0 4.7 %collective-permute-start.24 = (f32[32,128]{1,0:T(8,128)S(1)}, f32[32,128]{1,0:T(8,128)S(1)}, u32[]{:S(2)}, u32[]{:S(2)}) collective-permute-start(f32[32,128]{1,0:T(8,128)S(1)} %get-tuple-element.82), channel_id=1, source_target_pairs={{48,0},{56,8},{0,16},{8,24},{16,32},{24,40},{32,48},{40,56},{49,1}... | collective-permute-start | bytes 49160 | tf_op jit(solution)/shard_map/ppermute | solution.py:543

commit v6 on v5

--- a/solution.py
+++ b/solution.py
@@ -14,7 +14,7 @@
 F32 = jnp.float32
 SLABS, MIDS, UNITS = 26, 12, 40
 MARK = 64
-BLOCK, HALO, MID = (16, 16, 128), (SLABS, 32, 256), (MIDS, 32, 256)
+BLOCK, HALO, SHORT, MID = (16, 16, 128), (SLABS, 32, 256), (SLABS, 24, 256), (MIDS, 24, 256)
 VMEM = pl.BlockSpec(memory_space=pltpu.VMEM)
 ANY = pl.BlockSpec(memory_space=pl.ANY)
 
@@ -148,6 +148,10 @@
     return units(sides, 0, sides.shape[0] // 16)
 
 
+def squeeze(v):
+    return jnp.concatenate([v[:16], jnp.where(iota((8, v.shape[1]), 0) < 4, v[16:24], v[24:])], axis=0)
+
+
 def near(lane):
     return (lane < 160) | (lane >= 224)
 
@@ -157,20 +161,23 @@
     return near(lane) & (z >= 0) & (z < 128 * sizes()[2])
 
 
-def inside_fine():
-    row, lane = iota((32, 256), 0), iota((32, 256), 1)
-    y = jnp.where(row < 24, row, row - 32) + 16 * place()[1]
+def inside_fine(rows):
+    row, lane = iota((rows, 256), 0), iota((rows, 256), 1)
+    y = jnp.where(row < rows // 2 + 8, row, row - rows) + 16 * place()[1]
     return inside_lanes(lane) & (y >= 0) & (y < 16 * sizes()[1])
 
 
-def fine_weights(body, sides, weight0, weight1, middle, quads, unit):
-    inside, gx, nx = inside_fine(), place()[0], sizes()[0]
+def fine_weights(body, sides, weight0, weight0s, weight1, middle, quads, unit):
+    gx, nx = place()[0], sizes()[0]
+    inside, insides = inside_fine(32), inside_fine(24)
 
     def weigh(i):
         kap = assemble_fine(body, sides, i)
         x = 16 * gx + (i - 5)
-        weight0[i] = jnp.where(inside & (x >= 0) & (x < 16 * nx), OMEGA / (kap + 6.0), 0.0)
-        return kap
+        v = jnp.where(inside & (x >= 0) & (x < 16 * nx), OMEGA / (kap + 6.0), 0.0)
+        weight0[i] = v
+        weight0s[i] = squeeze(v)
+        return squeeze(kap)
 
     weigh(0)
     weigh(SLABS - 1)
@@ -178,7 +185,7 @@
         kap1 = pair_mean(weigh(2 * m + 1) + weigh(2 * m + 2), 1)
         middle[m] = kap1
         x = 8 * gx + (m - 2)
-        weight1[m] = jnp.where(inside & (x >= 0) & (x < 8 * nx), OMEGA / (kap1 + 1.5), 0.0)
+        weight1[m] = jnp.where(insides & (x >= 0) & (x < 8 * nx), OMEGA / (kap1 + 1.5), 0.0)
     for c in range(4):
         kap2 = pair_mean(middle[2 + 2 * c] + middle[3 + 2 * c], 2)[:16]
         weight2 = OMEGA / (kap2 + 0.375)
@@ -195,38 +202,43 @@
         unit[4 * half:4 * half + 4] = v
 
 
-def down_sweep(body, sides, weight0, weight1, x0, x1, unit, r, r1, quads):
+def near_sweep(read, weight0, weight1, x0, x1, r1, r, tall):
     for i in range(SLABS):
-        v = assemble_fine(body, sides, i)
-        r[i] = v
-        x0[i] = weight0[i] * v
+        v = read(i)
+        r[i] = squeeze(v)
+        v = weight0[i] * v
+        tall[i] = v
+        x0[i] = squeeze(v)
     for m in range(MIDS):
         i = 2 * m + 1
+        two = tall[i] + tall[i + 1]
+        rows = squeeze(roll(two, 1, 0) + roll(two, -1, 0))
         two = x0[i] + x0[i + 1]
-        left = KEEP * (r[i] + r[i + 1]) + ((x0[i - 1] + x0[i + 2]) + two) + around(two, 1, 1)
-        v = pair_mean(left, 1)
-        r1[m] = v
+        lanes = roll(two, 1, 1) + roll(two, -1, 1)
+        v = pair_mean(KEEP * (r[i] + r[i + 1]) + ((x0[i - 1] + x0[i + 2]) + two) + (rows + lanes), 1)
+        if r1 is not None:
+            r1[m] = v
         x1[m] = weight1[m] * v
+
+
+def first_down_kernel(body, upper, lower, weight0, weight0s, weight1, x0, x1, unit, r, tall, r1, quads, sides):
+    there = unpack_rows(upper, lower, 5 * UNITS // 8, sides)
+    fine_weights(units(body, 16 * UNITS, UNITS), there, weight0, weight0s, weight1, r1, quads, unit.at[1])
+    here, there = units(body, 0, UNITS), unpack_rows(upper, lower, 0, sides)
+    near_sweep(lambda i: assemble_fine(here, there, i), weight0, weight1, x0, x1, r1, r, tall)
     for c in range(4):
         m = 2 + 2 * c
         two = x1[m] + x1[m + 1]
         left = KEEP * (r1[m] + r1[m + 1]) + 0.25 * (((x1[m - 1] + x1[m + 2]) + two) + around(two, 2, 2))
         v = pair_mean(left, 2)[:16]
         quads[0, c], quads[1, c] = v[:, :128], v[:, 128:]
-    pack_coarse(quads, unit)
-
-
-def first_down_kernel(body, upper, lower, weight0, weight1, x0, x1, unit, r, r1, quads, sides, more):
-    kap_sides = unpack_rows(upper, lower, 5 * UNITS // 8, more)
-    fine_weights(units(body, 16 * UNITS, UNITS), kap_sides, weight0, weight1, r1, quads, unit.at[1])
-    r_sides = unpack_rows(upper, lower, 0, sides)
-    down_sweep(units(body, 0, UNITS), r_sides, weight0, weight1, x0, x1, unit.at[0], r, r1, quads)
+    pack_coarse(quads, unit.at[0])
 
 
 def share_sweep(block, weight0, weight1, share, x0, r1, x1, quads):
     for k in range(16):
         x0[k] = weight0[k + 5, :16, :128] * block[k]
-    zero, low = jnp.zeros((16, 128), F32), jnp.zeros((16, 256), F32)
+    zero, low = jnp.zeros((16, 128), F32), jnp.zeros((8, 256), F32)
 
     def tall(v):
         return jnp.concatenate([jnp.concatenate([v, zero], axis=1), low], axis=0)
@@ -258,7 +270,7 @@
     gy, gz = place()[1:]
     ny, nz = sizes()[1:]
     for half in range(2):
-        for start, count, first in ((28, 1, 0), (0, 5, 1)):
+        for start, count, first in ((20, 1, 0), (0, 5, 1)):
             row, lane = iota((count, 128), 0), iota((count, 128), 1)
             y = row // 4 + gy - (1 if count == 1 else 0)
             inside = (y >= 0) & (y < ny)
@@ -335,27 +347,12 @@
         ref[pl.ds(start, 8)] = state
 
 
-def near_sweep(body, upper, lower, weight0, weight1, x0, x1, r, sides):
-    here, there = units(body, 0, 32), unpack_rows(upper, lower, 0, sides)
-    for i in range(SLABS):
-        v = assemble_fine(here, there, i, near_sources)
-        r[i] = v
-        x0[i] = weight0[i] * v
-    for m in range(MIDS):
-        i = 2 * m + 1
-        two = x0[i] + x0[i + 1]
-        left = KEEP * (r[i] + r[i + 1]) + ((x0[i - 1] + x0[i + 2]) + two) + around(two, 1, 1)
-        x1[m] = weight1[m] * pair_mean(left, 1)
-
-
-def unfold(v, k, out, change):
-    turn = iota((16, 256), 1) % 4
-    moved = {d: roll(v, d, 1) for d in range(-3, 4)}
-    for c in range(4):
-        slab = moved[-c]
-        for j in range(1, 4):
-            slab = jnp.where(turn == j, moved[j - c], slab)
-        out[4 * k + c + 1] = change(4 * k + c + 1, slab)
+def unfold(v, c):
+    turn = iota(v.shape, 1) % 4
+    slab = roll(v, -c, 1)
+    for j in range(1, 4):
+        slab = jnp.where(turn == j, roll(v, j - c, 1), slab)
+    return slab
 
 
 def assemble_shares(own, up1, down1, up2, down2, out, change):
@@ -372,7 +369,7 @@
             v = v + jnp.concatenate([down1[s + 5:s + 6], zeros(10), down1[s:s + 5]], axis=0)
             v = v + jnp.concatenate([zeros(10), down2[t:t + 3], zeros(3)], axis=0)
             halves.append(v)
-        unfold(jnp.concatenate(halves, axis=1), k, out, change)
+        out[k] = change(k, jnp.concatenate(halves, axis=1))
 
 
 def assemble_coarse(gather, t, out, change):
@@ -389,32 +386,38 @@
             ],
             axis=1,
         )
-        unfold(v, k, out, change)
+        out[k] = change(k, v)
 
 
 def up_sweep(assemble, weight2, weight1, weight0, x0, x1, kap, u, w, a, b, rhs2, spread, middle, t1, t0):
     zero = jnp.zeros((16, 256), F32)
     for ref in (a, b):
         ref[0] = zero
-        ref[17] = zero
-    assemble(rhs2, lambda s, v: weight2[s] * v)
-    for s in range(1, 17):
-        a[s] = rhs2[s]
+        ref[5] = zero
+    assemble(rhs2, lambda g, v: weight2[g] * v)
+    for g in range(4):
+        a[g + 1] = rhs2[g]
+    turn = iota((16, 256), 1) % 4
     for sweep in range(COARSE_SWEEPS - 1):
         old, new = (a, b) if sweep % 2 == 0 else (b, a)
-
-        for s in range(1, 17):
-            v = old[s]
-            beside = (old[s - 1] + old[s + 1]) + around(v, 1, 4)
-            new[s] = (KEEP * v + rhs2[s]) + weight2[s] * (0.0625 * beside)
+        ahead = [None] + [roll(old[g], -4, 1) for g in range(1, 5)] + [None]
+        back = [None] + [roll(old[g], 4, 1) for g in range(1, 5)] + [None]
+        for g in range(1, 5):
+            v = old[g]
+            up = roll(jnp.where(turn == 3, zero if g == 1 else ahead[g - 1], v), 1, 1)
+            down = roll(jnp.where(turn == 0, zero if g == 4 else back[g + 1], v), -1, 1)
+            beside = (up + down) + (ahead[g] + back[g]) + (roll(v, 1, 0) + roll(v, -1, 0))
+            new[g] = (KEEP * v + rhs2[g - 1]) + weight2[g - 1] * (0.0625 * beside)
     last = b if COARSE_SWEEPS % 2 == 0 else a
+    gx = place()[0]
     half = iota((8, 256), 0) < 4
     for c in range(6):
-        v = last[4 * place()[0] + c]
+        g, t = (gx, 3) if c == 0 else ((gx + 2, 0) if c == 5 else (gx + 1, c - 1))
+        v = unfold(last[g], t)
         spread[c] = jnp.concatenate(
             [
-                jnp.where(half, jnp.broadcast_to(v[j:j + 1], (8, 256)), jnp.broadcast_to(v[j + 1:j + 2], (8, 256)))
-                for j in (0, 2, 4, 14)
+                jnp.where(half, jnp.broadcast_to(v[j:j + 1], (8, 256)), jnp.broadcast_to(v[k:k + 1], (8, 256)))
+                for j, k in ((0, 1), (2, 3), (4, 15))
             ],
             axis=0,
         )
@@ -462,25 +465,26 @@
     share_sweep(w, weight0, weight1, share, y0, y1, z1, quads)
 
 
-def whole_sweep(body, shares, weight2, weight1, weight0, kap, full, w, x0, x1, r, sides, *scratch):
-    near_sweep(body, shares[1], shares[2], weight0, weight1, x0, x1, r, sides)
-    up_sweep(lambda *a: assemble_shares(*shares, *a), weight2, weight1, weight0, x0, x1, kap, full, w, *scratch)
-
-
-def second_kernel(body, own, up1, down1, up2, down2, weight2, weight1, weight0, both, m0, n0, share, low, high, *scratch):
+def whole_sweep(body, shares, weight2, weight1, weight0, weight0s, kap, full, w, x0, x1, r, tall, sides, *scratch):
+    here, there = units(body, 0, 32), unpack_rows(shares[1], shares[2], 0, sides)
+    near_sweep(lambda i: assemble_fine(here, there, i, near_sources), weight0, weight1, x0, x1, None, r, tall)
+    up_sweep(lambda *a: assemble_shares(*shares, *a), weight2, weight1, weight0s, x0, x1, kap, full, w, *scratch)
+
+
+def second_kernel(body, own, up1, down1, up2, down2, weight2, weight1, weight0, weight0s, both, m0, n0, share, low, high, *scratch):
     (full, *scratch, y0, y1, z1, quads) = scratch
     shares = (own, up1, down1, up2, down2)
-    whole_sweep(body, shares, weight2, weight1, weight0, both.at[1], full, n0, *scratch)
+    whole_sweep(body, shares, weight2, weight1, weight0, weight0s, both.at[1], full, n0, *scratch)
     for k in range(16):
         m0[k] = full[k + 5, :16, :128]
     pack_near(lambda k: n0[k], low, high)
     share_sweep(n0, weight0, weight1, share, y0, y1, z1, quads)
 
 
-def third_kernel(body, own, up1, down1, up2, down2, weight2, weight1, weight0, both, u0, w0, m0, n0,
+def third_kernel(body, own, up1, down1, up2, down2, weight2, weight1, weight0, weight0s, both, u0, w0, m0, n0,
                  r1, u1, w1, m1, n1, first, dots, full, last, *scratch):
     shares = (own, up1, down1, up2, down2)
-    whole_sweep(body, shares, weight2, weight1, weight0, both.at[1], full, last, *scratch)
+    whole_sweep(body, shares, weight2, weight1, weight0, weight0s, both.at[1], full, last, *scratch)
     total0 = own[208:209] + up2[25:26] + down2[26:27]
     first[...] = jnp.broadcast_to(total0, (8, 128))
     alpha = total0[:, MARK:MARK + 1] / total0[:, MARK + 1:MARK + 2]
@@ -583,37 +587,37 @@
     def scratch(*shapes):
         return [pltpu.VMEM(s, F32) for s in shapes]
 
-    block, halo, mids, tile = shape(*BLOCK), shape(*HALO), shape(*MID), shape(8, 128)
-    down_scratch = scratch(HALO, MID, (2, 4, 16, 128), (16 * UNITS, 128))
-    up_scratch = scratch((18, 16, 256), (18, 16, 256), (18, 16, 256), (6, 32, 256), MID, MID, HALO, HALO)
+    block, short, mids, tile = shape(*BLOCK), shape(*SHORT), shape(*MID), shape(8, 128)
+    up_scratch = scratch((6, 16, 256), (6, 16, 256), (4, 16, 256), (6, 24, 256), MID, MID, SHORT, SHORT)
 
     both, low, high = call(
         prepare_kernel, [shape(2, *BLOCK), shape(2, 6, 16, 128), shape(2, 6, 16, 128)],
         [pltpu.VMEM(BLOCK, jnp.int32), pltpu.SMEM((CLASSES,), F32), pltpu.SemaphoreType.DMA((3,))], specs=[ANY] * 3, grant=60,
     )(right_side, classes, table)
     halos = fine_exchange(both, low, high)
-    weight0, weight1, x0, x1, unit = call(
-        first_down_kernel, [halo, mids, halo, mids, shape(2, 8, 128)], down_scratch + scratch((16 * UNITS, 128)), count=3
+    weight0, weight0s, weight1, x0, x1, unit = call(
+        first_down_kernel, [shape(*HALO), short, mids, short, mids, shape(2, 8, 128)],
+        scratch(SHORT, HALO, MID, (2, 4, 16, 128), (16 * UNITS, 128)), count=3,
     )(*halos)
     share_outs = [shape(24, 128), shape(16, 128), shape(16, 128)]
-    share_scratch = scratch(BLOCK, (10, 32, 256), (10, 32, 256), (2, 6, 32, 128))
+    share_scratch = scratch(BLOCK, (10, 24, 256), (10, 24, 256), (2, 6, 24, 128))
     weight2, u0, w0, share, low, high, dots = call(
-        first_up_kernel, [shape(18, 16, 256), block, block, *share_outs, tile], up_scratch + share_scratch, count=6
-    )(gather(unit), weight1, weight0, x0, x1, both)
-
-    whole_scratch = scratch(HALO, MID, HALO, (512, 128)) + up_scratch[:-1]
+        first_up_kernel, [shape(4, 16, 256), block, block, *share_outs, tile], up_scratch + share_scratch, count=6
+    )(gather(unit), weight1, weight0s, x0, x1, both)
+
+    whole_scratch = scratch(SHORT, MID, SHORT, HALO, (512, 128)) + up_scratch[:-1]
     halos = joint_exchange(w0, share, low, high, dots, False)
     _, own, up1, down1, up2, _ = halos
     ahead, behind = up1[208:210] + up2[24:26], down1[208:210] + own[208:210]
     state = jnp.concatenate([ahead + behind, ahead, behind, jnp.zeros((2, 128), F32)])
     state = state + shift(state, "gz", 4)
     m0, n0, share, low, high = call(
-        second_kernel, [block, block, *share_outs], scratch(HALO) + whole_scratch + share_scratch, count=10
-    )(*halos, weight2, weight1, weight0, both)
+        second_kernel, [block, block, *share_outs], scratch(SHORT) + whole_scratch + share_scratch, count=11
+    )(*halos, weight2, weight1, weight0, weight0s, both)
     halos = joint_exchange(n0, share, low, high, state, True)
     r1, u1, w1, m1, n1, first, dots = call(
-        third_kernel, [block] * 5 + [tile, tile], scratch(HALO, BLOCK) + whole_scratch, count=14
-    )(*halos, weight2, weight1, weight0, both, u0, w0, m0, n0)
+        third_kernel, [block] * 5 + [tile, tile], scratch(SHORT, BLOCK) + whole_scratch, count=15
+    )(*halos, weight2, weight1, weight0, weight0s, both, u0, w0, m0, n0)
     field, residual = call(finish_kernel, [block] * 2, count=11)(
         first, total(dots), u0, w0, m0, n0, r1, u1, w1, m1, n1
     )

time: 130 us -> 128 us (0.985)
  starting transfers between devices: 39.9 us -> 44.1 us
  waiting for transfers between devices: 29 us -> 25.2 us
  Pallas kernels: 17.8 us -> 16.1 us
    ppermute x25, starting transfers between devices: 39.9 us -> 44.1 us  [shift(): lax.ppermute(v, axis, [((i + distance) % count, i) for i in range(count)])]
    ppermute x25, waiting for transfers between devices: 29 us -> 25.2 us  [shift(): lax.ppermute(v, axis, [((i + distance) % count, i) for i in range(count)])]
    pallas_call x4, Pallas kernels: 14.2 us -> 12.4 us  [the longest x1 4.22 us: local(): call(second_kernel, [block, block, *share_outs], scratch(SHORT) + whole_s...]
  transfers between devices with their start and end apart: 25 -> 25, of which waited for: 14 -> 14; matrix products, arithmetic and copies ran while one was open for 1% -> 1% of each run, Pallas kernels for 4% -> 3%
where the time goes in v6:
time: 128 us
  starting transfers between devices  44.1 us (34%)
  blocking collectives  40.2 us (31%)
  waiting for transfers between devices  25.2 us (20%)
  Pallas kernels  16.1 us (13%)
    ppermute x25, starting transfers between devices, shift(): lax.ppermute(v, axis, [((i + distance) % count, i) for i in range(count)])  44.1 us
    all_to_all x1, blocking collectives, total(): lax.all_to_all(jnp.broadcast_to(v[None, :1], (count, 1, 128)), axes, 0, 0...  25.3 us
    ppermute x25, waiting for transfers between devices, shift(): lax.ppermute(v, axis, [((i + distance) % count, i) for i in range(count)])  25.2 us
    all_to_all x1, blocking collectives, gather(): lax.all_to_all(jnp.broadcast_to(unit[None], (count,) + unit.shape), ('gx'...  14.9 us
    pallas_call x1, Pallas kernels, local(): call(second_kernel, [block, block, *share_outs], scratch(SHORT) + whole_s...  4.22 us
    pallas_call x1, Pallas kernels, local(): call(third_kernel, [block] * 5 + [tile, tile], scratch(SHORT, BLOCK) + wh...  3.32 us
    pallas_call x1, Pallas kernels, local(): call(first_down_kernel, [shape(*HALO), short, mids, short, mids, shape(2,...  2.72 us
  transfers between devices with their start and end apart: 25, of which 14 were waited for; matrix products, arithmetic and copies ran while one was open for 1% of the time, Pallas kernels for 3%

profile of v6, /device:TPU:1, one launch (start us, length us, event | category | flops | bytes accessed | tf_op | source)
XLA Modules:
  0.0 127.7 jit_solution(14181543176660874488)
XLA Ops:
  0.6 1.9 %shard_map.50 = (f32[2,16,16,128]{3,2,1,0:T(8,128)}, f32[2,6,16,128]{3,2,1,0:T(8,128)}, f32[2,6,16,128]{3,2,1,0:T(8,128)}) custom-call(f32[16,16,128]{2,1,0:T(8,128)} %rhs_in.1, s32[16,16,128]{2,1,0:T(8,128)} %classes_in.1, f32[16]{0:T(128)} %table_in.1), custom_call_target="tpu_custom_call" | custom-call | tf_op jit(solution)/shard_map/pallas_call | solution.py:593
  2.6 3.3 %collective-permute-start = (f32[2,6,16,128]{3,2,1,0:T(8,128)}, f32[2,6,16,128]{3,2,1,0:T(8,128)S(1)}, u32[]{:S(2)}, u32[]{:S(2)}) collective-permute-start(f32[2,6,16,128]{3,2,1,0:T(8,128)} %get-tuple-element.49), channel_id=1, source_target_pairs={{1,0},{2,1},{3,2},{4,3},{5,4},{6,5},{7,6},{0,7},{9,8},{10,9},{11,1... | collective-permute-start | bytes 294920 | tf_op jit(solution)/shard_map/ppermute | solution.py:547
  5.8 0.9 fusion.2
  6.8 1.0 collective-permute-done
  7.8 1.3 %collective-permute-start.2 = (f32[2,7,16,128]{3,2,1,0:T(8,128)S(1)}, f32[2,7,16,128]{3,2,1,0:T(8,128)S(1)}, u32[]{:S(2)}, u32[]{:S(2)}) collective-permute-start(f32[2,7,16,128]{3,2,1,0:T(8,128)S(1)} %pad_maximum_fusion), channel_id=1, source_target_pairs={{192,0},{0,64},{64,128},{128,192},{193,1},{1,65},{65,129},{129,193... | collective-permute-start | bytes 344072 | tf_op jit(solution)/shard_map/ppermute | solution.py:547
  9.1 1.5 %collective-permute-start.3 = (f32[2,7,16,128]{3,2,1,0:T(8,128)S(1)}, f32[2,7,16,128]{3,2,1,0:T(8,128)S(1)}, u32[]{:S(2)}, u32[]{:S(2)}) collective-permute-start(f32[2,7,16,128]{3,2,1,0:T(8,128)S(1)} %pad_maximum_fusion.1), channel_id=1, source_target_pairs={{64,0},{128,64},{192,128},{0,192},{65,1},{129,65},{193,129},{1,193... | collective-permute-start | bytes 344072 | tf_op jit(solution)/shard_map/ppermute | solution.py:547
  10.7 2.1 %collective-permute-done.2 = f32[2,7,16,128]{3,2,1,0:T(8,128)S(1)} collective-permute-done((f32[2,7,16,128]{3,2,1,0:T(8,128)S(1)}, f32[2,7,16,128]{3,2,1,0:T(8,128)S(1)}, u32[]{:S(2)}, u32[]{:S(2)}) %collective-permute-start.2) | collective-permute-done | bytes 114720 | tf_op jit(solution)/shard_map/ppermute | solution.py:547
  13.0 5.7 %collective-permute-start.4 = (f32[400,128]{1,0:T(8,128)S(1)}, f32[400,128]{1,0:T(8,128)S(1)}, u32[]{:S(2)}, u32[]{:S(2)}) collective-permute-start(f32[400,128]{1,0:T(8,128)S(1)} %get-tuple-element.51), channel_id=1, source_target_pairs={{8,0},{16,8},{24,16},{32,24},{40,32},{48,40},{56,48},{0,56},{9,1},... | collective-permute-start | bytes 614408 | tf_op jit(solution)/shard_map/ppermute | solution.py:547
  18.7 2.7 %collective-permute-done.4.upper = f32[400,128]{1,0:T(8,128)S(1)} collective-permute-done((f32[400,128]{1,0:T(8,128)S(1)}, f32[400,128]{1,0:T(8,128)S(1)}, u32[]{:S(2)}, u32[]{:S(2)}) %collective-permute-start.4) | collective-permute-done | bytes 204832 | tf_op jit(solution)/shard_map/ppermute | solution.py:547
  21.4 3.1 %collective-permute-done.5.lower = f32[400,128]{1,0:T(8,128)S(1)} collective-permute-done((f32[400,128]{1,0:T(8,128)S(1)}, f32[400,128]{1,0:T(8,128)S(1)}, u32[]{:S(2)}, u32[]{:S(2)}) %collective-permute-start.5) | collective-permute-done | bytes 204832 | tf_op jit(solution)/shard_map/ppermute | solution.py:547
  24.5 2.7 %shard_map.52 = (f32[26,32,256]{2,1,0:T(8,128)S(1)}, f32[26,24,256]{2,1,0:T(8,128)S(1)}, f32[12,24,256]{2,1,0:T(8,128)S(1)}, f32[26,24,256]{2,1,0:T(8,128)S(1)},...) custom-call(f32[1280,128]{1,0:T(8,128)S(1)} %bitcast.5, f32[400,128]{1,0:T(8,128)S(1)} %collective-permute-done.4.upper, ...), custom_call_target="tpu_custom_call" | custom-call | tf_op jit(solution)/shard_map/pallas_call | solution.py:598
  27.2 14.9 %all_to_all.10.gather = f32[32,2,8,128]{3,2,1,0:T(8,128)S(1)} all-to-all(f32[32,2,8,128]{3,2,1,0:T(8,128)S(1)} %broadcast_in_dim.10), channel_id=1, replica_groups=mesh['gx'=4,'gy'=8,'gz'=8] {'gx','gy'}, dimensions={0} | all-to-all | bytes 524288 | tf_op jit(solution)/shard_map/all_to_all | solution.py:576
  42.2 2.2 %shard_map.53 = (f32[4,16,256]{2,1,0:T(8,128)S(1)}, f32[16,16,128]{2,1,0:T(8,128)S(1)}, f32[16,16,128]{2,1,0:T(8,128)S(1)}, f32[24,128]{1,0:T(8,128)S(1)}, f32[1...) custom-call(f32[32,2,8,128]{3,2,1,0:T(8,128)S(1)} %all_to_all.10.gather, ...), custom_call_target="tpu_custom_call" | custom-call | tf_op jit(solution)/shard_map/pallas_call | solution.py:604
  44.4 8.2 %collective-permute-start.6 = (f32[48,128]{1,0:T(8,128)S(1)}, f32[48,128]{1,0:T(8,128)S(1)}, u32[]{:S(2)}, u32[]{:S(2)}) collective-permute-start(f32[48,128]{1,0:T(8,128)S(1)} %get-tuple-element.106), channel_id=1, source_target_pairs={{1,0},{2,1},{3,2},{4,3},{5,4},{6,5},{7,6},{0,7},{9,8},{10,9},{11,1... | collective-permute-start | bytes 73736 | tf_op jit(solution)/shard_map/ppermute | solution.py:547
  54.3 2.3 %collective-permute-start.9 = (f32[144,128]{1,0:T(8,128)S(1)}, f32[144,128]{1,0:T(8,128)S(1)}, u32[]{:S(2)}, u32[]{:S(2)}) collective-permute-start(f32[144,128]{1,0:T(8,128)S(1)} %get-tuple-element.65), channel_id=1, source_target_pairs={{64,0},{128,64},{192,128},{0,192},{65,1},{129,65},{193,129},{1,193... | collective-permute-start | bytes 221192 | tf_op jit(solution)/shard_map/ppermute | solution.py:547
  56.8 3.9 %collective-permute-done.10.across = f32[32,128]{1,0:T(8,128)S(1)} collective-permute-done((f32[32,128]{1,0:T(8,128)S(1)}, f32[32,128]{1,0:T(8,128)S(1)}, u32[]{:S(2)}, u32[]{:S(2)}) %collective-permute-start.10) | collective-permute-done | bytes 16416 | tf_op jit(solution)/shard_map/ppermute | solution.py:547
  60.9 1.7 %collective-permute-start.12 = (f32[216,128]{1,0:T(8,128)S(1)}, f32[216,128]{1,0:T(8,128)S(1)}, u32[]{:S(2)}, u32[]{:S(2)}) collective-permute-start(f32[216,128]{1,0:T(8,128)S(1)} %get-tuple-element.68), channel_id=1, source_target_pairs={{56,0},{0,8},{8,16},{16,24},{24,32},{32,40},{40,48},{48,56},{57,1}... | collective-permute-start | bytes 331784 | tf_op jit(solution)/shard_map/ppermute | solution.py:547
  62.6 1.5 %collective-permute-start.13 = (f32[32,128]{1,0:T(8,128)S(1)}, f32[32,128]{1,0:T(8,128)S(1)}, u32[]{:S(2)}, u32[]{:S(2)}) collective-permute-start(f32[32,128]{1,0:T(8,128)S(1)} %get-tuple-element.69), channel_id=1, source_target_pairs={{16,0},{24,8},{32,16},{40,24},{48,32},{56,40},{0,48},{8,56},{17,1}... | collective-permute-start | bytes 49160 | tf_op jit(solution)/shard_map/ppermute | solution.py:547
  64.2 1.1 collective-permute-start.14
  65.3 0.9 collective-permute-done.13.up2
  66.2 3.8 %collective-permute-start.15 = (f32[8,128]{1,0:T(8,128)S(1)}, f32[8,128]{1,0:T(8,128)S(1)}, u32[]{:S(2)}, u32[]{:S(2)}) collective-permute-start(f32[8,128]{1,0:T(8,128)S(1)} %maximum_maximum_fusion), channel_id=1, source_target_pairs={{4,0},{5,1},{6,2},{7,3},{0,4},{1,5},{2,6},{3,7},{12,8},{13,9},{14,... | collective-permute-start | bytes 12296 | tf_op jit(solution)/shard_map/ppermute | solution.py:547
  70.0 4.2 %shard_map.56 = (f32[16,16,128]{2,1,0:T(8,128)S(1)}, f32[16,16,128]{2,1,0:T(8,128)S(1)}, f32[24,128]{1,0:T(8,128)S(1)}, f32[16,128]{1,0:T(8,128)S(1)}, f32[16,128]{1,0:T(8,128)S(1)}) custom-call(f32[512,128]{1,0:T(8,128)S(1)} %get-tuple-element.66.body, f32[216,128]{1,0:T(8,128)S(1)} %get-tuple-element.67.own, f32[216,128]{1,0:T(8,128)S(1)} %collective-permute-done.11.up1, ...), custom_call_target="tpu_custom_call" | custom-call | tf_op jit(solution)/shard_map/pallas_call | solution.py:614
  74.3 6.1 %collective-permute-start.16 = (f32[48,128]{1,0:T(8,128)S(1)}, f32[48,128]{1,0:T(8,128)S(1)}, u32[]{:S(2)}, u32[]{:S(2)}) collective-permute-start(f32[48,128]{1,0:T(8,128)S(1)} %get-tuple-element.104), channel_id=1, source_target_pairs={{1,0},{2,1},{3,2},{4,3},{5,4},{6,5},{7,6},{0,7},{9,8},{10,9},{11,1... | collective-permute-start | bytes 73736 | tf_op jit(solution)/shard_map/ppermute | solution.py:547
  81.8 2.7 %collective-permute-start.19 = (f32[144,128]{1,0:T(8,128)S(1)}, f32[144,128]{1,0:T(8,128)S(1)}, u32[]{:S(2)}, u32[]{:S(2)}) collective-permute-start(f32[144,128]{1,0:T(8,128)S(1)} %get-tuple-element.79), channel_id=1, source_target_pairs={{64,0},{128,64},{192,128},{0,192},{65,1},{129,65},{193,129},{1,193... | collective-permute-start | bytes 221192 | tf_op jit(solution)/shard_map/ppermute | solution.py:547
  84.5 4.2 %collective-permute-done.20.across = f32[32,128]{1,0:T(8,128)S(1)} collective-permute-done((f32[32,128]{1,0:T(8,128)S(1)}, f32[32,128]{1,0:T(8,128)S(1)}, u32[]{:S(2)}, u32[]{:S(2)}) %collective-permute-start.20) | collective-permute-done | bytes 16416 | tf_op jit(solution)/shard_map/ppermute | solution.py:547
  89.4 0.9 collective-permute-start.22
  90.3 2.5 %collective-permute-start.23 = (f32[32,128]{1,0:T(8,128)S(1)}, f32[32,128]{1,0:T(8,128)S(1)}, u32[]{:S(2)}, u32[]{:S(2)}) collective-permute-start(f32[32,128]{1,0:T(8,128)S(1)} %get-tuple-element.83), channel_id=1, source_target_pairs={{16,0},{24,8},{32,16},{40,24},{48,32},{56,40},{0,48},{8,56},{17,1}... | collective-permute-start | bytes 49160 | tf_op jit(solution)/shard_map/ppermute | solution.py:547
  92.8 1.0 collective-permute-done.23.up2
  93.8 3.9 %collective-permute-done.24.down2 = f32[32,128]{1,0:T(8,128)S(1)} collective-permute-done((f32[32,128]{1,0:T(8,128)S(1)}, f32[32,128]{1,0:T(8,128)S(1)}, u32[]{:S(2)}, u32[]{:S(2)}) %collective-permute-start.24) | collective-permute-done | bytes 16416 | tf_op jit(solution)/shard_map/ppermute | solution.py:547
  97.6 3.3 %shard_map.59 = (f32[16,16,128]{2,1,0:T(8,128)S(1)}, f32[16,16,128]{2,1,0:T(8,128)S(1)}, f32[16,16,128]{2,1,0:T(8,128)S(1)}, f32[16,16,128]{2,1,0:T(8,128)S(1)},...) custom-call(f32[512,128]{1,0:T(8,128)S(1)} %get-tuple-element.80.body, ...), custom_call_target="tpu_custom_call" | custom-call | tf_op jit(solution)/shard_map/pallas_call | solution.py:618
  101.1 25.3 %all_to_all.11 = f32[256,1,128]{2,1,0:T(1,128)S(1)} all-to-all(f32[256,1,128]{2,1,0:T(1,128)S(1)} %broadcast_in_dim.25), channel_id=1, replica_groups=mesh['gx'=4,'gy'=8,'gz'=8] {'gx','gy','gz'}, dimensions={0} | all-to-all | bytes 262144 | tf_op jit(solution)/shard_map/all_to_all | solution.py:582
  126.4 1.3 %shard_map.60 = (f32[16,16,128]{2,1,0:T(8,128)}, f32[16,16,128]{2,1,0:T(8,128)}) custom-call(f32[8,128]{1,0:T(8,128)S(1)} %get-tuple-element.87.first, f32[8,128]{1,0:T(8,128)S(1)} %broadcast_in_dim.26.second, f32[16,16,128]{2,1,0:T(8,128)S(1)} %get-tuple-element.85.u0, f32[16,16,128]{2,1,0:T(8,128)S(1)} %get-tuple-element.58.own.w0, ...), custom_call_target="tpu_custom_call" | custom-call | tf_op jit(solution)/shard_map/pallas_call | solution.py:621
  (56 shorter events, 4.8 us)
Async XLA Ops:
  2.6 4.2 %copy-start = (f32[2,16,16,128]{3,2,1,0:T(8,128)S(1)}, f32[2,16,16,128]{3,2,1,0:T(8,128)}, u32[]{:S(2)}) copy-start(f32[2,16,16,128]{3,2,1,0:T(8,128)} %get-tuple-element.48.both) | copy-start | bytes 786436
  2.6 5.2 %collective-permute-start = (f32[2,6,16,128]{3,2,1,0:T(8,128)}, f32[2,6,16,128]{3,2,1,0:T(8,128)S(1)}, u32[]{:S(2)}, u32[]{:S(2)}) collective-permute-start(f32[2,6,16,128]{3,2,1,0:T(8,128)} %get-tuple-element.49), channel_id=1, source_target_pairs={{1,0},{2,1},{3,2},{4,3},{5,4},{6,5},{7,6},{0,7},{9,8},{10,9},{11,1... | collective-permute-start | bytes 294920 | tf_op jit(solution)/shard_map/ppermute | solution.py:547
  5.8 2.0 %collective-permute-start.1 = (f32[2,6,16,128]{3,2,1,0:T(8,128)}, f32[2,6,16,128]{3,2,1,0:T(8,128)S(1)}, u32[]{:S(2)}, u32[]{:S(2)}) collective-permute-start(f32[2,6,16,128]{3,2,1,0:T(8,128)} %get-tuple-element.50), channel_id=1, source_target_pairs={{7,0},{0,1},{1,2},{2,3},{3,4},{4,5},{5,6},{6,7},{15,8},{8,9},{9,10... | collective-permute-start | bytes 294920 | tf_op jit(solution)/shard_map/ppermute | solution.py:547
  7.8 4.9 %collective-permute-start.2 = (f32[2,7,16,128]{3,2,1,0:T(8,128)S(1)}, f32[2,7,16,128]{3,2,1,0:T(8,128)S(1)}, u32[]{:S(2)}, u32[]{:S(2)}) collective-permute-start(f32[2,7,16,128]{3,2,1,0:T(8,128)S(1)} %pad_maximum_fusion), channel_id=1, source_target_pairs={{192,0},{0,64},{64,128},{128,192},{193,1},{1,65},{65,129},{129,193... | collective-permute-start | bytes 344072 | tf_op jit(solution)/shard_map/ppermute | solution.py:547
  9.1 3.7 %collective-permute-start.3 = (f32[2,7,16,128]{3,2,1,0:T(8,128)S(1)}, f32[2,7,16,128]{3,2,1,0:T(8,128)S(1)}, u32[]{:S(2)}, u32[]{:S(2)}) collective-permute-start(f32[2,7,16,128]{3,2,1,0:T(8,128)S(1)} %pad_maximum_fusion.1), channel_id=1, source_target_pairs={{64,0},{128,64},{192,128},{0,192},{65,1},{129,65},{193,129},{1,193... | collective-permute-start | bytes 344072 | tf_op jit(solution)/shard_map/ppermute | solution.py:547
  13.0 8.4 %collective-permute-start.4 = (f32[400,128]{1,0:T(8,128)S(1)}, f32[400,128]{1,0:T(8,128)S(1)}, u32[]{:S(2)}, u32[]{:S(2)}) collective-permute-start(f32[400,128]{1,0:T(8,128)S(1)} %get-tuple-element.51), channel_id=1, source_target_pairs={{8,0},{16,8},{24,16},{32,24},{40,32},{48,40},{56,48},{0,56},{9,1},... | collective-permute-start | bytes 614408 | tf_op jit(solution)/shard_map/ppermute | solution.py:547
  18.7 5.8 %collective-permute-start.5 = (f32[400,128]{1,0:T(8,128)S(1)}, f32[400,128]{1,0:T(8,128)S(1)}, u32[]{:S(2)}, u32[]{:S(2)}) collective-permute-start(f32[400,128]{1,0:T(8,128)S(1)} %get-tuple-element.52), channel_id=1, source_target_pairs={{56,0},{0,8},{8,16},{16,24},{24,32},{32,40},{40,48},{48,56},{57,1}... | collective-permute-start | bytes 614408 | tf_op jit(solution)/shard_map/ppermute | solution.py:547
  44.4 9.1 %collective-permute-start.6 = (f32[48,128]{1,0:T(8,128)S(1)}, f32[48,128]{1,0:T(8,128)S(1)}, u32[]{:S(2)}, u32[]{:S(2)}) collective-permute-start(f32[48,128]{1,0:T(8,128)S(1)} %get-tuple-element.106), channel_id=1, source_target_pairs={{1,0},{2,1},{3,2},{4,3},{5,4},{6,5},{7,6},{0,7},{9,8},{10,9},{11,1... | collective-permute-start | bytes 73736 | tf_op jit(solution)/shard_map/ppermute | solution.py:547
  52.6 1.2 collective-permute-start.7
  53.8 6.9 %collective-permute-start.8 = (f32[144,128]{1,0:T(8,128)S(1)}, f32[144,128]{1,0:T(8,128)S(1)}, u32[]{:S(2)}, u32[]{:S(2)}) collective-permute-start(f32[144,128]{1,0:T(8,128)S(1)} %get-tuple-element.64), channel_id=1, source_target_pairs={{192,0},{0,64},{64,128},{128,192},{193,1},{1,65},{65,129},{129,193... | collective-permute-start | bytes 221192 | tf_op jit(solution)/shard_map/ppermute | solution.py:547
  54.3 6.4 %collective-permute-start.9 = (f32[144,128]{1,0:T(8,128)S(1)}, f32[144,128]{1,0:T(8,128)S(1)}, u32[]{:S(2)}, u32[]{:S(2)}) collective-permute-start(f32[144,128]{1,0:T(8,128)S(1)} %get-tuple-element.65), channel_id=1, source_target_pairs={{64,0},{128,64},{192,128},{0,192},{65,1},{129,65},{193,129},{1,193... | collective-permute-start | bytes 221192 | tf_op jit(solution)/shard_map/ppermute | solution.py:547
  56.6 4.1 %collective-permute-start.10 = (f32[32,128]{1,0:T(8,128)S(1)}, f32[32,128]{1,0:T(8,128)S(1)}, u32[]{:S(2)}, u32[]{:S(2)}) collective-permute-start(f32[32,128]{1,0:T(8,128)S(1)} %get-tuple-element.63.small), channel_id=1, source_target_pairs={{128,0},{192,64},{0,128},{64,192},{129,1},{193,65},{1,129},{65,193... | collective-permute-start | bytes 49160 | tf_op jit(solution)/shard_map/ppermute | solution.py:547
  60.8 5.3 %collective-permute-start.11 = (f32[216,128]{1,0:T(8,128)S(1)}, f32[216,128]{1,0:T(8,128)S(1)}, u32[]{:S(2)}, u32[]{:S(2)}) collective-permute-start(f32[216,128]{1,0:T(8,128)S(1)} %get-tuple-element.67.own), channel_id=1, source_target_pairs={{8,0},{16,8},{24,16},{32,24},{40,32},{48,40},{56,48},{0,56},{9,1},... | collective-permute-start | bytes 331784 | tf_op jit(solution)/shard_map/ppermute | solution.py:547
  60.9 5.2 %collective-permute-start.12 = (f32[216,128]{1,0:T(8,128)S(1)}, f32[216,128]{1,0:T(8,128)S(1)}, u32[]{:S(2)}, u32[]{:S(2)}) collective-permute-start(f32[216,128]{1,0:T(8,128)S(1)} %get-tuple-element.68), channel_id=1, source_target_pairs={{56,0},{0,8},{8,16},{16,24},{24,32},{32,40},{40,48},{48,56},{57,1}... | collective-permute-start | bytes 331784 | tf_op jit(solution)/shard_map/ppermute | solution.py:547
  62.6 3.5 %collective-permute-start.13 = (f32[32,128]{1,0:T(8,128)S(1)}, f32[32,128]{1,0:T(8,128)S(1)}, u32[]{:S(2)}, u32[]{:S(2)}) collective-permute-start(f32[32,128]{1,0:T(8,128)S(1)} %get-tuple-element.69), channel_id=1, source_target_pairs={{16,0},{24,8},{32,16},{40,24},{48,32},{56,40},{0,48},{8,56},{17,1}... | collective-permute-start | bytes 49160 | tf_op jit(solution)/shard_map/ppermute | solution.py:547
  64.2 5.8 %collective-permute-start.14 = (f32[32,128]{1,0:T(8,128)S(1)}, f32[32,128]{1,0:T(8,128)S(1)}, u32[]{:S(2)}, u32[]{:S(2)}) collective-permute-start(f32[32,128]{1,0:T(8,128)S(1)} %get-tuple-element.70), channel_id=1, source_target_pairs={{48,0},{56,8},{0,16},{8,24},{16,32},{24,40},{32,48},{40,56},{49,1}... | collective-permute-start | bytes 49160 | tf_op jit(solution)/shard_map/ppermute | solution.py:547
  66.2 8.0 %collective-permute-start.15 = (f32[8,128]{1,0:T(8,128)S(1)}, f32[8,128]{1,0:T(8,128)S(1)}, u32[]{:S(2)}, u32[]{:S(2)}) collective-permute-start(f32[8,128]{1,0:T(8,128)S(1)} %maximum_maximum_fusion), channel_id=1, source_target_pairs={{4,0},{5,1},{6,2},{7,3},{0,4},{1,5},{2,6},{3,7},{12,8},{13,9},{14,... | collective-permute-start | bytes 12296 | tf_op jit(solution)/shard_map/ppermute | solution.py:547
  74.3 7.0 %collective-permute-start.16 = (f32[48,128]{1,0:T(8,128)S(1)}, f32[48,128]{1,0:T(8,128)S(1)}, u32[]{:S(2)}, u32[]{:S(2)}) collective-permute-start(f32[48,128]{1,0:T(8,128)S(1)} %get-tuple-element.104), channel_id=1, source_target_pairs={{1,0},{2,1},{3,2},{4,3},{5,4},{6,5},{7,6},{0,7},{9,8},{10,9},{11,1... | collective-permute-start | bytes 73736 | tf_op jit(solution)/shard_map/ppermute | solution.py:547
  80.5 1.2 collective-permute-start.17
  81.7 6.9 %collective-permute-start.18 = (f32[144,128]{1,0:T(8,128)S(1)}, f32[144,128]{1,0:T(8,128)S(1)}, u32[]{:S(2)}, u32[]{:S(2)}) collective-permute-start(f32[144,128]{1,0:T(8,128)S(1)} %get-tuple-element.78), channel_id=1, source_target_pairs={{192,0},{0,64},{64,128},{128,192},{193,1},{1,65},{65,129},{129,193... | collective-permute-start | bytes 221192 | tf_op jit(solution)/shard_map/ppermute | solution.py:547
  81.8 6.9 %collective-permute-start.19 = (f32[144,128]{1,0:T(8,128)S(1)}, f32[144,128]{1,0:T(8,128)S(1)}, u32[]{:S(2)}, u32[]{:S(2)}) collective-permute-start(f32[144,128]{1,0:T(8,128)S(1)} %get-tuple-element.79), channel_id=1, source_target_pairs={{64,0},{128,64},{192,128},{0,192},{65,1},{129,65},{193,129},{1,193... | collective-permute-start | bytes 221192 | tf_op jit(solution)/shard_map/ppermute | solution.py:547
  84.5 4.2 %collective-permute-start.20 = (f32[32,128]{1,0:T(8,128)S(1)}, f32[32,128]{1,0:T(8,128)S(1)}, u32[]{:S(2)}, u32[]{:S(2)}) collective-permute-start(f32[32,128]{1,0:T(8,128)S(1)} %get-tuple-element.77.small), channel_id=1, source_target_pairs={{128,0},{192,64},{0,128},{64,192},{129,1},{193,65},{1,129},{65,193... | collective-permute-start | bytes 49160 | tf_op jit(solution)/shard_map/ppermute | solution.py:547
  88.7 8.9 %collective-permute-start.21 = (f32[216,128]{1,0:T(8,128)S(1)}, f32[216,128]{1,0:T(8,128)S(1)}, u32[]{:S(2)}, u32[]{:S(2)}) collective-permute-start(f32[216,128]{1,0:T(8,128)S(1)} %get-tuple-element.81.own), channel_id=1, source_target_pairs={{8,0},{16,8},{24,16},{32,24},{40,32},{48,40},{56,48},{0,56},{9,1},... | collective-permute-start | bytes 331784 | tf_op jit(solution)/shard_map/ppermute | solution.py:547
  89.4 8.2 %collective-permute-start.22 = (f32[216,128]{1,0:T(8,128)S(1)}, f32[216,128]{1,0:T(8,128)S(1)}, u32[]{:S(2)}, u32[]{:S(2)}) collective-permute-start(f32[216,128]{1,0:T(8,128)S(1)} %get-tuple-element.82), channel_id=1, source_target_pairs={{56,0},{0,8},{8,16},{16,24},{24,32},{32,40},{40,48},{48,56},{57,1}... | collective-permute-start | bytes 331784 | tf_op jit(solution)/shard_map/ppermute | solution.py:547
  90.3 3.5 %collective-permute-start.23 = (f32[32,128]{1,0:T(8,128)S(1)}, f32[32,128]{1,0:T(8,128)S(1)}, u32[]{:S(2)}, u32[]{:S(2)}) collective-permute-start(f32[32,128]{1,0:T(8,128)S(1)} %get-tuple-element.83), channel_id=1, source_target_pairs={{16,0},{24,8},{32,16},{40,24},{48,32},{56,40},{0,48},{8,56},{17,1}... | collective-permute-start | bytes 49160 | tf_op jit(solution)/shard_map/ppermute | solution.py:547
  92.8 4.8 %collective-permute-start.24 = (f32[32,128]{1,0:T(8,128)S(1)}, f32[32,128]{1,0:T(8,128)S(1)}, u32[]{:S(2)}, u32[]{:S(2)}) collective-permute-start(f32[32,128]{1,0:T(8,128)S(1)} %get-tuple-element.84), channel_id=1, source_target_pairs={{48,0},{56,8},{0,16},{8,24},{16,32},{24,40},{32,48},{40,56},{49,1}... | collective-permute-start | bytes 49160 | tf_op jit(solution)/shard_map/ppermute | solution.py:547

commit v7 on v6

--- a/solution.py
+++ b/solution.py
@@ -209,7 +209,7 @@
         v = weight0[i] * v
         tall[i] = v
         x0[i] = squeeze(v)
-    for m in range(MIDS):
+    def middle_slab(m, carry):
         i = 2 * m + 1
         two = tall[i] + tall[i + 1]
         rows = squeeze(roll(two, 1, 0) + roll(two, -1, 0))
@@ -219,6 +219,9 @@
         if r1 is not None:
             r1[m] = v
         x1[m] = weight1[m] * v
+        return carry
+
+    lax.fori_loop(0, MIDS, middle_slab, 0, unroll=4)
 
 
 def first_down_kernel(body, upper, lower, weight0, weight0s, weight1, x0, x1, unit, r, tall, r1, quads, sides):

time: 128 us -> 126 us (0.984)
  Pallas kernels: 16.1 us -> 14 us
where the time goes in v7:
time: 126 us
  starting transfers between devices  44.1 us (35%)
  blocking collectives  40.5 us (32%)
  waiting for transfers between devices  25 us (20%)
  Pallas kernels  14 us (11%)
    ppermute x25, starting transfers between devices, shift(): lax.ppermute(v, axis, [((i + distance) % count, i) for i in range(count)])  44.1 us
    all_to_all x1, blocking collectives, total(): lax.all_to_all(jnp.broadcast_to(v[None, :1], (count, 1, 128)), axes, 0, 0...  25.6 us
    ppermute x25, waiting for transfers between devices, shift(): lax.ppermute(v, axis, [((i + distance) % count, i) for i in range(count)])  25 us
    all_to_all x1, blocking collectives, gather(): lax.all_to_all(jnp.broadcast_to(unit[None], (count,) + unit.shape), ('gx'...  14.9 us
    pallas_call x1, Pallas kernels, local(): call(second_kernel, [block, block, *share_outs], scratch(SHORT) + whole_s...  3.17 us
    pallas_call x1, Pallas kernels, local(): call(third_kernel, [block] * 5 + [tile, tile], scratch(SHORT, BLOCK) + wh...  2.78 us
  transfers between devices with their start and end apart: 25, of which 14 were waited for; matrix products, arithmetic and copies ran while one was open for 1% of the time, Pallas kernels for 3%

profile of v7, /device:TPU:1, one launch (start us, length us, event | category | flops | bytes accessed | tf_op | source)
XLA Modules:
  0.0 125.8 jit_solution(3951974129617654928)
XLA Ops:
  0.6 1.9 %shard_map.50 = (f32[2,16,16,128]{3,2,1,0:T(8,128)}, f32[2,6,16,128]{3,2,1,0:T(8,128)}, f32[2,6,16,128]{3,2,1,0:T(8,128)}) custom-call(f32[16,16,128]{2,1,0:T(8,128)} %rhs_in.1, s32[16,16,128]{2,1,0:T(8,128)} %classes_in.1, f32[16]{0:T(128)} %table_in.1), custom_call_target="tpu_custom_call" | custom-call | tf_op jit(solution)/shard_map/pallas_call | solution.py:596
  2.6 3.3 %collective-permute-start = (f32[2,6,16,128]{3,2,1,0:T(8,128)}, f32[2,6,16,128]{3,2,1,0:T(8,128)S(1)}, u32[]{:S(2)}, u32[]{:S(2)}) collective-permute-start(f32[2,6,16,128]{3,2,1,0:T(8,128)} %get-tuple-element.49), channel_id=1, source_target_pairs={{1,0},{2,1},{3,2},{4,3},{5,4},{6,5},{7,6},{0,7},{9,8},{10,9},{11,1... | collective-permute-start | bytes 294920 | tf_op jit(solution)/shard_map/ppermute | solution.py:550
  5.8 0.9 fusion.2
  6.8 1.0 collective-permute-done
  7.8 1.3 %collective-permute-start.2 = (f32[2,7,16,128]{3,2,1,0:T(8,128)S(1)}, f32[2,7,16,128]{3,2,1,0:T(8,128)S(1)}, u32[]{:S(2)}, u32[]{:S(2)}) collective-permute-start(f32[2,7,16,128]{3,2,1,0:T(8,128)S(1)} %pad_maximum_fusion), channel_id=1, source_target_pairs={{192,0},{0,64},{64,128},{128,192},{193,1},{1,65},{65,129},{129,193... | collective-permute-start | bytes 344072 | tf_op jit(solution)/shard_map/ppermute | solution.py:550
  9.1 1.5 %collective-permute-start.3 = (f32[2,7,16,128]{3,2,1,0:T(8,128)S(1)}, f32[2,7,16,128]{3,2,1,0:T(8,128)S(1)}, u32[]{:S(2)}, u32[]{:S(2)}) collective-permute-start(f32[2,7,16,128]{3,2,1,0:T(8,128)S(1)} %pad_maximum_fusion.1), channel_id=1, source_target_pairs={{64,0},{128,64},{192,128},{0,192},{65,1},{129,65},{193,129},{1,193... | collective-permute-start | bytes 344072 | tf_op jit(solution)/shard_map/ppermute | solution.py:550
  10.7 2.1 %collective-permute-done.2 = f32[2,7,16,128]{3,2,1,0:T(8,128)S(1)} collective-permute-done((f32[2,7,16,128]{3,2,1,0:T(8,128)S(1)}, f32[2,7,16,128]{3,2,1,0:T(8,128)S(1)}, u32[]{:S(2)}, u32[]{:S(2)}) %collective-permute-start.2) | collective-permute-done | bytes 114720 | tf_op jit(solution)/shard_map/ppermute | solution.py:550
  13.0 5.7 %collective-permute-start.4 = (f32[400,128]{1,0:T(8,128)S(1)}, f32[400,128]{1,0:T(8,128)S(1)}, u32[]{:S(2)}, u32[]{:S(2)}) collective-permute-start(f32[400,128]{1,0:T(8,128)S(1)} %get-tuple-element.51), channel_id=1, source_target_pairs={{8,0},{16,8},{24,16},{32,24},{40,32},{48,40},{56,48},{0,56},{9,1},... | collective-permute-start | bytes 614408 | tf_op jit(solution)/shard_map/ppermute | solution.py:550
  18.7 2.7 %collective-permute-done.4.upper = f32[400,128]{1,0:T(8,128)S(1)} collective-permute-done((f32[400,128]{1,0:T(8,128)S(1)}, f32[400,128]{1,0:T(8,128)S(1)}, u32[]{:S(2)}, u32[]{:S(2)}) %collective-permute-start.4) | collective-permute-done | bytes 204832 | tf_op jit(solution)/shard_map/ppermute | solution.py:550
  21.4 3.1 %collective-permute-done.5.lower = f32[400,128]{1,0:T(8,128)S(1)} collective-permute-done((f32[400,128]{1,0:T(8,128)S(1)}, f32[400,128]{1,0:T(8,128)S(1)}, u32[]{:S(2)}, u32[]{:S(2)}) %collective-permute-start.5) | collective-permute-done | bytes 204832 | tf_op jit(solution)/shard_map/ppermute | solution.py:550
  24.5 2.2 %shard_map.52 = (f32[26,32,256]{2,1,0:T(8,128)S(1)}, f32[26,24,256]{2,1,0:T(8,128)S(1)}, f32[12,24,256]{2,1,0:T(8,128)S(1)}, f32[26,24,256]{2,1,0:T(8,128)S(1)},...) custom-call(f32[1280,128]{1,0:T(8,128)S(1)} %bitcast.5, f32[400,128]{1,0:T(8,128)S(1)} %collective-permute-done.4.upper, ...), custom_call_target="tpu_custom_call" | custom-call | tf_op jit(solution)/shard_map/pallas_call | solution.py:601
  26.8 14.9 %all_to_all.10.gather = f32[32,2,8,128]{3,2,1,0:T(8,128)S(1)} all-to-all(f32[32,2,8,128]{3,2,1,0:T(8,128)S(1)} %broadcast_in_dim.10), channel_id=1, replica_groups=mesh['gx'=4,'gy'=8,'gz'=8] {'gx','gy'}, dimensions={0} | all-to-all | bytes 524288 | tf_op jit(solution)/shard_map/all_to_all | solution.py:579
  41.7 2.2 %shard_map.53 = (f32[4,16,256]{2,1,0:T(8,128)S(1)}, f32[16,16,128]{2,1,0:T(8,128)S(1)}, f32[16,16,128]{2,1,0:T(8,128)S(1)}, f32[24,128]{1,0:T(8,128)S(1)}, f32[1...) custom-call(f32[32,2,8,128]{3,2,1,0:T(8,128)S(1)} %all_to_all.10.gather, ...), custom_call_target="tpu_custom_call" | custom-call | tf_op jit(solution)/shard_map/pallas_call | solution.py:607
  43.9 8.2 %collective-permute-start.6 = (f32[48,128]{1,0:T(8,128)S(1)}, f32[48,128]{1,0:T(8,128)S(1)}, u32[]{:S(2)}, u32[]{:S(2)}) collective-permute-start(f32[48,128]{1,0:T(8,128)S(1)} %get-tuple-element.106), channel_id=1, source_target_pairs={{1,0},{2,1},{3,2},{4,3},{5,4},{6,5},{7,6},{0,7},{9,8},{10,9},{11,1... | collective-permute-start | bytes 73736 | tf_op jit(solution)/shard_map/ppermute | solution.py:550
  53.8 2.3 %collective-permute-start.9 = (f32[144,128]{1,0:T(8,128)S(1)}, f32[144,128]{1,0:T(8,128)S(1)}, u32[]{:S(2)}, u32[]{:S(2)}) collective-permute-start(f32[144,128]{1,0:T(8,128)S(1)} %get-tuple-element.65), channel_id=1, source_target_pairs={{64,0},{128,64},{192,128},{0,192},{65,1},{129,65},{193,129},{1,193... | collective-permute-start | bytes 221192 | tf_op jit(solution)/shard_map/ppermute | solution.py:550
  56.3 3.9 %collective-permute-done.10.across = f32[32,128]{1,0:T(8,128)S(1)} collective-permute-done((f32[32,128]{1,0:T(8,128)S(1)}, f32[32,128]{1,0:T(8,128)S(1)}, u32[]{:S(2)}, u32[]{:S(2)}) %collective-permute-start.10) | collective-permute-done | bytes 16416 | tf_op jit(solution)/shard_map/ppermute | solution.py:550
  60.5 1.7 %collective-permute-start.12 = (f32[216,128]{1,0:T(8,128)S(1)}, f32[216,128]{1,0:T(8,128)S(1)}, u32[]{:S(2)}, u32[]{:S(2)}) collective-permute-start(f32[216,128]{1,0:T(8,128)S(1)} %get-tuple-element.68), channel_id=1, source_target_pairs={{56,0},{0,8},{8,16},{16,24},{24,32},{32,40},{40,48},{48,56},{57,1}... | collective-permute-start | bytes 331784 | tf_op jit(solution)/shard_map/ppermute | solution.py:550
  62.2 1.5 %collective-permute-start.13 = (f32[32,128]{1,0:T(8,128)S(1)}, f32[32,128]{1,0:T(8,128)S(1)}, u32[]{:S(2)}, u32[]{:S(2)}) collective-permute-start(f32[32,128]{1,0:T(8,128)S(1)} %get-tuple-element.69), channel_id=1, source_target_pairs={{16,0},{24,8},{32,16},{40,24},{48,32},{56,40},{0,48},{8,56},{17,1}... | collective-permute-start | bytes 49160 | tf_op jit(solution)/shard_map/ppermute | solution.py:550
  63.7 1.1 collective-permute-start.14
  64.8 0.9 collective-permute-done.13.up2
  65.8 3.8 %collective-permute-start.15 = (f32[8,128]{1,0:T(8,128)S(1)}, f32[8,128]{1,0:T(8,128)S(1)}, u32[]{:S(2)}, u32[]{:S(2)}) collective-permute-start(f32[8,128]{1,0:T(8,128)S(1)} %maximum_maximum_fusion), channel_id=1, source_target_pairs={{4,0},{5,1},{6,2},{7,3},{0,4},{1,5},{2,6},{3,7},{12,8},{13,9},{14,... | collective-permute-start | bytes 12296 | tf_op jit(solution)/shard_map/ppermute | solution.py:550
  69.6 3.2 %shard_map.56 = (f32[16,16,128]{2,1,0:T(8,128)S(1)}, f32[16,16,128]{2,1,0:T(8,128)S(1)}, f32[24,128]{1,0:T(8,128)S(1)}, f32[16,128]{1,0:T(8,128)S(1)}, f32[16,128]{1,0:T(8,128)S(1)}) custom-call(f32[512,128]{1,0:T(8,128)S(1)} %get-tuple-element.66.body, f32[216,128]{1,0:T(8,128)S(1)} %get-tuple-element.67.own, f32[216,128]{1,0:T(8,128)S(1)} %collective-permute-done.11.up1, ...), custom_call_target="tpu_custom_call" | custom-call | tf_op jit(solution)/shard_map/pallas_call | solution.py:617
  72.8 6.1 %collective-permute-start.16 = (f32[48,128]{1,0:T(8,128)S(1)}, f32[48,128]{1,0:T(8,128)S(1)}, u32[]{:S(2)}, u32[]{:S(2)}) collective-permute-start(f32[48,128]{1,0:T(8,128)S(1)} %get-tuple-element.104), channel_id=1, source_target_pairs={{1,0},{2,1},{3,2},{4,3},{5,4},{6,5},{7,6},{0,7},{9,8},{10,9},{11,1... | collective-permute-start | bytes 73736 | tf_op jit(solution)/shard_map/ppermute | solution.py:550
  80.3 2.7 %collective-permute-start.19 = (f32[144,128]{1,0:T(8,128)S(1)}, f32[144,128]{1,0:T(8,128)S(1)}, u32[]{:S(2)}, u32[]{:S(2)}) collective-permute-start(f32[144,128]{1,0:T(8,128)S(1)} %get-tuple-element.79), channel_id=1, source_target_pairs={{64,0},{128,64},{192,128},{0,192},{65,1},{129,65},{193,129},{1,193... | collective-permute-start | bytes 221192 | tf_op jit(solution)/shard_map/ppermute | solution.py:550
  82.9 4.2 %collective-permute-done.20.across = f32[32,128]{1,0:T(8,128)S(1)} collective-permute-done((f32[32,128]{1,0:T(8,128)S(1)}, f32[32,128]{1,0:T(8,128)S(1)}, u32[]{:S(2)}, u32[]{:S(2)}) %collective-permute-start.20) | collective-permute-done | bytes 16416 | tf_op jit(solution)/shard_map/ppermute | solution.py:550
  87.2 1.2 collective-permute-start.21
  88.8 2.5 %collective-permute-start.23 = (f32[32,128]{1,0:T(8,128)S(1)}, f32[32,128]{1,0:T(8,128)S(1)}, u32[]{:S(2)}, u32[]{:S(2)}) collective-permute-start(f32[32,128]{1,0:T(8,128)S(1)} %get-tuple-element.83), channel_id=1, source_target_pairs={{16,0},{24,8},{32,16},{40,24},{48,32},{56,40},{0,48},{8,56},{17,1}... | collective-permute-start | bytes 49160 | tf_op jit(solution)/shard_map/ppermute | solution.py:550
  91.3 1.0 collective-permute-done.23.up2
  92.3 3.7 %collective-permute-done.24.down2 = f32[32,128]{1,0:T(8,128)S(1)} collective-permute-done((f32[32,128]{1,0:T(8,128)S(1)}, f32[32,128]{1,0:T(8,128)S(1)}, u32[]{:S(2)}, u32[]{:S(2)}) %collective-permute-start.24) | collective-permute-done | bytes 16416 | tf_op jit(solution)/shard_map/ppermute | solution.py:550
  96.0 2.8 %shard_map.59 = (f32[16,16,128]{2,1,0:T(8,128)S(1)}, f32[16,16,128]{2,1,0:T(8,128)S(1)}, f32[16,16,128]{2,1,0:T(8,128)S(1)}, f32[16,16,128]{2,1,0:T(8,128)S(1)},...) custom-call(f32[512,128]{1,0:T(8,128)S(1)} %get-tuple-element.80.body, ...), custom_call_target="tpu_custom_call" | custom-call | tf_op jit(solution)/shard_map/pallas_call | solution.py:621
  98.9 25.6 %all_to_all.11 = f32[256,1,128]{2,1,0:T(1,128)S(1)} all-to-all(f32[256,1,128]{2,1,0:T(1,128)S(1)} %broadcast_in_dim.25), channel_id=1, replica_groups=mesh['gx'=4,'gy'=8,'gz'=8] {'gx','gy','gz'}, dimensions={0} | all-to-all | bytes 262144 | tf_op jit(solution)/shard_map/all_to_all | solution.py:585
  124.5 1.3 %shard_map.60 = (f32[16,16,128]{2,1,0:T(8,128)}, f32[16,16,128]{2,1,0:T(8,128)}) custom-call(f32[8,128]{1,0:T(8,128)S(1)} %get-tuple-element.87.first, f32[8,128]{1,0:T(8,128)S(1)} %broadcast_in_dim.26.second, f32[16,16,128]{2,1,0:T(8,128)S(1)} %get-tuple-element.85.u0, f32[16,16,128]{2,1,0:T(8,128)S(1)} %get-tuple-element.58.own.w0, ...), custom_call_target="tpu_custom_call" | custom-call | tf_op jit(solution)/shard_map/pallas_call | solution.py:624
  (56 shorter events, 4.5 us)
Async XLA Ops:
  2.6 4.2 %copy-start = (f32[2,16,16,128]{3,2,1,0:T(8,128)S(1)}, f32[2,16,16,128]{3,2,1,0:T(8,128)}, u32[]{:S(2)}) copy-start(f32[2,16,16,128]{3,2,1,0:T(8,128)} %get-tuple-element.48.both) | copy-start | bytes 786436
  2.6 5.2 %collective-permute-start = (f32[2,6,16,128]{3,2,1,0:T(8,128)}, f32[2,6,16,128]{3,2,1,0:T(8,128)S(1)}, u32[]{:S(2)}, u32[]{:S(2)}) collective-permute-start(f32[2,6,16,128]{3,2,1,0:T(8,128)} %get-tuple-element.49), channel_id=1, source_target_pairs={{1,0},{2,1},{3,2},{4,3},{5,4},{6,5},{7,6},{0,7},{9,8},{10,9},{11,1... | collective-permute-start | bytes 294920 | tf_op jit(solution)/shard_map/ppermute | solution.py:550
  5.8 2.0 %collective-permute-start.1 = (f32[2,6,16,128]{3,2,1,0:T(8,128)}, f32[2,6,16,128]{3,2,1,0:T(8,128)S(1)}, u32[]{:S(2)}, u32[]{:S(2)}) collective-permute-start(f32[2,6,16,128]{3,2,1,0:T(8,128)} %get-tuple-element.50), channel_id=1, source_target_pairs={{7,0},{0,1},{1,2},{2,3},{3,4},{4,5},{5,6},{6,7},{15,8},{8,9},{9,10... | collective-permute-start | bytes 294920 | tf_op jit(solution)/shard_map/ppermute | solution.py:550
  7.8 4.9 %collective-permute-start.2 = (f32[2,7,16,128]{3,2,1,0:T(8,128)S(1)}, f32[2,7,16,128]{3,2,1,0:T(8,128)S(1)}, u32[]{:S(2)}, u32[]{:S(2)}) collective-permute-start(f32[2,7,16,128]{3,2,1,0:T(8,128)S(1)} %pad_maximum_fusion), channel_id=1, source_target_pairs={{192,0},{0,64},{64,128},{128,192},{193,1},{1,65},{65,129},{129,193... | collective-permute-start | bytes 344072 | tf_op jit(solution)/shard_map/ppermute | solution.py:550
  9.1 3.7 %collective-permute-start.3 = (f32[2,7,16,128]{3,2,1,0:T(8,128)S(1)}, f32[2,7,16,128]{3,2,1,0:T(8,128)S(1)}, u32[]{:S(2)}, u32[]{:S(2)}) collective-permute-start(f32[2,7,16,128]{3,2,1,0:T(8,128)S(1)} %pad_maximum_fusion.1), channel_id=1, source_target_pairs={{64,0},{128,64},{192,128},{0,192},{65,1},{129,65},{193,129},{1,193... | collective-permute-start | bytes 344072 | tf_op jit(solution)/shard_map/ppermute | solution.py:550
  13.0 8.4 %collective-permute-start.4 = (f32[400,128]{1,0:T(8,128)S(1)}, f32[400,128]{1,0:T(8,128)S(1)}, u32[]{:S(2)}, u32[]{:S(2)}) collective-permute-start(f32[400,128]{1,0:T(8,128)S(1)} %get-tuple-element.51), channel_id=1, source_target_pairs={{8,0},{16,8},{24,16},{32,24},{40,32},{48,40},{56,48},{0,56},{9,1},... | collective-permute-start | bytes 614408 | tf_op jit(solution)/shard_map/ppermute | solution.py:550
  18.7 5.8 %collective-permute-start.5 = (f32[400,128]{1,0:T(8,128)S(1)}, f32[400,128]{1,0:T(8,128)S(1)}, u32[]{:S(2)}, u32[]{:S(2)}) collective-permute-start(f32[400,128]{1,0:T(8,128)S(1)} %get-tuple-element.52), channel_id=1, source_target_pairs={{56,0},{0,8},{8,16},{16,24},{24,32},{32,40},{40,48},{48,56},{57,1}... | collective-permute-start | bytes 614408 | tf_op jit(solution)/shard_map/ppermute | solution.py:550
  43.9 9.1 %collective-permute-start.6 = (f32[48,128]{1,0:T(8,128)S(1)}, f32[48,128]{1,0:T(8,128)S(1)}, u32[]{:S(2)}, u32[]{:S(2)}) collective-permute-start(f32[48,128]{1,0:T(8,128)S(1)} %get-tuple-element.106), channel_id=1, source_target_pairs={{1,0},{2,1},{3,2},{4,3},{5,4},{6,5},{7,6},{0,7},{9,8},{10,9},{11,1... | collective-permute-start | bytes 73736 | tf_op jit(solution)/shard_map/ppermute | solution.py:550
  52.2 1.2 collective-permute-start.7
  53.4 6.9 %collective-permute-start.8 = (f32[144,128]{1,0:T(8,128)S(1)}, f32[144,128]{1,0:T(8,128)S(1)}, u32[]{:S(2)}, u32[]{:S(2)}) collective-permute-start(f32[144,128]{1,0:T(8,128)S(1)} %get-tuple-element.64), channel_id=1, source_target_pairs={{192,0},{0,64},{64,128},{128,192},{193,1},{1,65},{65,129},{129,193... | collective-permute-start | bytes 221192 | tf_op jit(solution)/shard_map/ppermute | solution.py:550
  53.8 6.4 %collective-permute-start.9 = (f32[144,128]{1,0:T(8,128)S(1)}, f32[144,128]{1,0:T(8,128)S(1)}, u32[]{:S(2)}, u32[]{:S(2)}) collective-permute-start(f32[144,128]{1,0:T(8,128)S(1)} %get-tuple-element.65), channel_id=1, source_target_pairs={{64,0},{128,64},{192,128},{0,192},{65,1},{129,65},{193,129},{1,193... | collective-permute-start | bytes 221192 | tf_op jit(solution)/shard_map/ppermute | solution.py:550
  56.1 4.1 %collective-permute-start.10 = (f32[32,128]{1,0:T(8,128)S(1)}, f32[32,128]{1,0:T(8,128)S(1)}, u32[]{:S(2)}, u32[]{:S(2)}) collective-permute-start(f32[32,128]{1,0:T(8,128)S(1)} %get-tuple-element.63.small), channel_id=1, source_target_pairs={{128,0},{192,64},{0,128},{64,192},{129,1},{193,65},{1,129},{65,193... | collective-permute-start | bytes 49160 | tf_op jit(solution)/shard_map/ppermute | solution.py:550
  60.3 5.3 %collective-permute-start.11 = (f32[216,128]{1,0:T(8,128)S(1)}, f32[216,128]{1,0:T(8,128)S(1)}, u32[]{:S(2)}, u32[]{:S(2)}) collective-permute-start(f32[216,128]{1,0:T(8,128)S(1)} %get-tuple-element.67.own), channel_id=1, source_target_pairs={{8,0},{16,8},{24,16},{32,24},{40,32},{48,40},{56,48},{0,56},{9,1},... | collective-permute-start | bytes 331784 | tf_op jit(solution)/shard_map/ppermute | solution.py:550
  60.5 5.2 %collective-permute-start.12 = (f32[216,128]{1,0:T(8,128)S(1)}, f32[216,128]{1,0:T(8,128)S(1)}, u32[]{:S(2)}, u32[]{:S(2)}) collective-permute-start(f32[216,128]{1,0:T(8,128)S(1)} %get-tuple-element.68), channel_id=1, source_target_pairs={{56,0},{0,8},{8,16},{16,24},{24,32},{32,40},{40,48},{48,56},{57,1}... | collective-permute-start | bytes 331784 | tf_op jit(solution)/shard_map/ppermute | solution.py:550
  62.2 3.5 %collective-permute-start.13 = (f32[32,128]{1,0:T(8,128)S(1)}, f32[32,128]{1,0:T(8,128)S(1)}, u32[]{:S(2)}, u32[]{:S(2)}) collective-permute-start(f32[32,128]{1,0:T(8,128)S(1)} %get-tuple-element.69), channel_id=1, source_target_pairs={{16,0},{24,8},{32,16},{40,24},{48,32},{56,40},{0,48},{8,56},{17,1}... | collective-permute-start | bytes 49160 | tf_op jit(solution)/shard_map/ppermute | solution.py:550
  63.7 5.8 %collective-permute-start.14 = (f32[32,128]{1,0:T(8,128)S(1)}, f32[32,128]{1,0:T(8,128)S(1)}, u32[]{:S(2)}, u32[]{:S(2)}) collective-permute-start(f32[32,128]{1,0:T(8,128)S(1)} %get-tuple-element.70), channel_id=1, source_target_pairs={{48,0},{56,8},{0,16},{8,24},{16,32},{24,40},{32,48},{40,56},{49,1}... | collective-permute-start | bytes 49160 | tf_op jit(solution)/shard_map/ppermute | solution.py:550
  65.8 7.0 %collective-permute-start.15 = (f32[8,128]{1,0:T(8,128)S(1)}, f32[8,128]{1,0:T(8,128)S(1)}, u32[]{:S(2)}, u32[]{:S(2)}) collective-permute-start(f32[8,128]{1,0:T(8,128)S(1)} %maximum_maximum_fusion), channel_id=1, source_target_pairs={{4,0},{5,1},{6,2},{7,3},{0,4},{1,5},{2,6},{3,7},{12,8},{13,9},{14,... | collective-permute-start | bytes 12296 | tf_op jit(solution)/shard_map/ppermute | solution.py:550
  72.8 7.0 %collective-permute-start.16 = (f32[48,128]{1,0:T(8,128)S(1)}, f32[48,128]{1,0:T(8,128)S(1)}, u32[]{:S(2)}, u32[]{:S(2)}) collective-permute-start(f32[48,128]{1,0:T(8,128)S(1)} %get-tuple-element.104), channel_id=1, source_target_pairs={{1,0},{2,1},{3,2},{4,3},{5,4},{6,5},{7,6},{0,7},{9,8},{10,9},{11,1... | collective-permute-start | bytes 73736 | tf_op jit(solution)/shard_map/ppermute | solution.py:550
  79.0 1.2 collective-permute-start.17
  80.2 6.9 %collective-permute-start.18 = (f32[144,128]{1,0:T(8,128)S(1)}, f32[144,128]{1,0:T(8,128)S(1)}, u32[]{:S(2)}, u32[]{:S(2)}) collective-permute-start(f32[144,128]{1,0:T(8,128)S(1)} %get-tuple-element.78), channel_id=1, source_target_pairs={{192,0},{0,64},{64,128},{128,192},{193,1},{1,65},{65,129},{129,193... | collective-permute-start | bytes 221192 | tf_op jit(solution)/shard_map/ppermute | solution.py:550
  80.3 6.9 %collective-permute-start.19 = (f32[144,128]{1,0:T(8,128)S(1)}, f32[144,128]{1,0:T(8,128)S(1)}, u32[]{:S(2)}, u32[]{:S(2)}) collective-permute-start(f32[144,128]{1,0:T(8,128)S(1)} %get-tuple-element.79), channel_id=1, source_target_pairs={{64,0},{128,64},{192,128},{0,192},{65,1},{129,65},{193,129},{1,193... | collective-permute-start | bytes 221192 | tf_op jit(solution)/shard_map/ppermute | solution.py:550
  82.9 4.2 %collective-permute-start.20 = (f32[32,128]{1,0:T(8,128)S(1)}, f32[32,128]{1,0:T(8,128)S(1)}, u32[]{:S(2)}, u32[]{:S(2)}) collective-permute-start(f32[32,128]{1,0:T(8,128)S(1)} %get-tuple-element.77.small), channel_id=1, source_target_pairs={{128,0},{192,64},{0,128},{64,192},{129,1},{193,65},{1,129},{65,193... | collective-permute-start | bytes 49160 | tf_op jit(solution)/shard_map/ppermute | solution.py:550
  87.2 8.8 %collective-permute-start.21 = (f32[216,128]{1,0:T(8,128)S(1)}, f32[216,128]{1,0:T(8,128)S(1)}, u32[]{:S(2)}, u32[]{:S(2)}) collective-permute-start(f32[216,128]{1,0:T(8,128)S(1)} %get-tuple-element.81.own), channel_id=1, source_target_pairs={{8,0},{16,8},{24,16},{32,24},{40,32},{48,40},{56,48},{0,56},{9,1},... | collective-permute-start | bytes 331784 | tf_op jit(solution)/shard_map/ppermute | solution.py:550
  88.4 7.6 %collective-permute-start.22 = (f32[216,128]{1,0:T(8,128)S(1)}, f32[216,128]{1,0:T(8,128)S(1)}, u32[]{:S(2)}, u32[]{:S(2)}) collective-permute-start(f32[216,128]{1,0:T(8,128)S(1)} %get-tuple-element.82), channel_id=1, source_target_pairs={{56,0},{0,8},{8,16},{16,24},{24,32},{32,40},{40,48},{48,56},{57,1}... | collective-permute-start | bytes 331784 | tf_op jit(solution)/shard_map/ppermute | solution.py:550
  88.8 3.5 %collective-permute-start.23 = (f32[32,128]{1,0:T(8,128)S(1)}, f32[32,128]{1,0:T(8,128)S(1)}, u32[]{:S(2)}, u32[]{:S(2)}) collective-permute-start(f32[32,128]{1,0:T(8,128)S(1)} %get-tuple-element.83), channel_id=1, source_target_pairs={{16,0},{24,8},{32,16},{40,24},{48,32},{56,40},{0,48},{8,56},{17,1}... | collective-permute-start | bytes 49160 | tf_op jit(solution)/shard_map/ppermute | solution.py:550
  91.3 4.7 %collective-permute-start.24 = (f32[32,128]{1,0:T(8,128)S(1)}, f32[32,128]{1,0:T(8,128)S(1)}, u32[]{:S(2)}, u32[]{:S(2)}) collective-permute-start(f32[32,128]{1,0:T(8,128)S(1)} %get-tuple-element.84), channel_id=1, source_target_pairs={{48,0},{56,8},{0,16},{8,24},{16,32},{24,40},{32,48},{40,56},{49,1}... | collective-permute-start | bytes 49160 | tf_op jit(solution)/shard_map/ppermute | solution.py:550

commit v8 on v7

--- a/solution.py
+++ b/solution.py
@@ -320,7 +320,7 @@
         ref[112:144] = small[...]
 
 
-def join_x_kernel(final, own, above, below, small, before, after, across, body, upper, lower, ahead, behind, stage):
+def join_x_kernel(final, own, above, below, small, sums, before, after, across, body, upper, lower, ahead, behind, stage):
     for k in range(16):
         body[pl.ds(16 * k, 16)] = own[k]
     body[256:272] = above[:16]
@@ -343,8 +343,8 @@
         for half in range(2):
             ahead[pl.ds(6 * b + 3 * half, 3)] = v[6 * half:6 * half + 3]
             behind[pl.ds(6 * b + 3 * half, 3)] = v[6 * half + 3:6 * half + 6]
-    state = small[24:32]
-    if not final:
+    state = sums[...]
+    if final:
         state = (state + before[136:144]) + (after[136:144] + across[24:32])
     for ref, start in ((upper, 208), (lower, 208), (ahead, 24), (behind, 24)):
         ref[pl.ds(start, 8)] = state
@@ -443,11 +443,10 @@
 
 
 def lanes_of(values):
-    lane = iota((8, 128), 1)
-    out = jnp.zeros((8, 128), F32)
-    for k, v in enumerate(values):
-        out = jnp.where(lane == MARK + k, jnp.sum(v), out)
-    return out
+    rows = [jnp.sum(v, axis=0, keepdims=True) for v in values]
+    sums = jnp.sum(jnp.concatenate(rows + [jnp.zeros((16 - len(rows), 128), F32)], axis=0), axis=1, keepdims=True)
+    picked = jnp.where(iota((16, 128), 1) == MARK + iota((16, 128), 0), sums, 0.0)
+    return jnp.broadcast_to(jnp.sum(picked, axis=0, keepdims=True), (8, 128))
 
 
 def first_up_kernel(gather, weight1, weight0, x0, x1, both, weight2, u, w, share, low, high, dots, *scratch):
@@ -468,26 +467,25 @@
     share_sweep(w, weight0, weight1, share, y0, y1, z1, quads)
 
 
-def whole_sweep(body, shares, weight2, weight1, weight0, weight0s, kap, full, w, x0, x1, r, tall, sides, *scratch):
-    here, there = units(body, 0, 32), unpack_rows(shares[1], shares[2], 0, sides)
+def near_kernel(body, up1, down1, weight0, weight1, x0, x1, r, tall, sides):
+    here, there = units(body, 0, 32), unpack_rows(up1, down1, 0, sides)
     near_sweep(lambda i: assemble_fine(here, there, i, near_sources), weight0, weight1, x0, x1, None, r, tall)
-    up_sweep(lambda *a: assemble_shares(*shares, *a), weight2, weight1, weight0s, x0, x1, kap, full, w, *scratch)
-
-
-def second_kernel(body, own, up1, down1, up2, down2, weight2, weight1, weight0, weight0s, both, m0, n0, share, low, high, *scratch):
+
+
+def second_kernel(x0, x1, own, up1, down1, up2, down2, weight2, weight1, weight0s, both, m0, n0, share, low, high, *scratch):
     (full, *scratch, y0, y1, z1, quads) = scratch
     shares = (own, up1, down1, up2, down2)
-    whole_sweep(body, shares, weight2, weight1, weight0, weight0s, both.at[1], full, n0, *scratch)
+    up_sweep(lambda *a: assemble_shares(*shares, *a), weight2, weight1, weight0s, x0, x1, both.at[1], full, n0, *scratch)
     for k in range(16):
         m0[k] = full[k + 5, :16, :128]
     pack_near(lambda k: n0[k], low, high)
-    share_sweep(n0, weight0, weight1, share, y0, y1, z1, quads)
-
-
-def third_kernel(body, own, up1, down1, up2, down2, weight2, weight1, weight0, weight0s, both, u0, w0, m0, n0,
+    share_sweep(n0, weight0s, weight1, share, y0, y1, z1, quads)
+
+
+def third_kernel(x0, x1, own, up1, down1, up2, down2, weight2, weight1, weight0s, both, u0, w0, m0, n0,
                  r1, u1, w1, m1, n1, first, dots, full, last, *scratch):
     shares = (own, up1, down1, up2, down2)
-    whole_sweep(body, shares, weight2, weight1, weight0, weight0s, both.at[1], full, last, *scratch)
+    up_sweep(lambda *a: assemble_shares(*shares, *a), weight2, weight1, weight0s, x0, x1, both.at[1], full, last, *scratch)
     total0 = own[208:209] + up2[25:26] + down2[26:27]
     first[...] = jnp.broadcast_to(total0, (8, 128))
     alpha = total0[:, MARK:MARK + 1] / total0[:, MARK + 1:MARK + 2]
@@ -534,7 +532,7 @@
     return jax.ShapeDtypeStruct(dims, F32)
 
 
-def call(kernel, outs, scratch=(), specs=None, count=0, grant=40):
+def call(kernel, outs, scratch=(), specs=None, count=0, grant=40, flops=0):
     return pl.pallas_call(
         kernel,
         out_shape=outs,
@@ -542,6 +540,7 @@
         out_specs=[VMEM] * len(outs),
         scratch_shapes=list(scratch),
         compiler_params=pltpu.CompilerParams(vmem_limit_bytes=grant * 1024 * 1024),
+        cost_estimate=pl.CostEstimate(flops=flops, bytes_accessed=flops, transcendentals=0) if flops else None,
     )
 
 
@@ -567,10 +566,11 @@
         functools.partial(join_z_kernel, final), [shape(144, 128), shape(144, 128), shape(32, 128)], count=5
     )(own, share, state, above, below)
     before, after, across = shift(last, "gx", -1), shift(first, "gx", 1), shift(small, "gx", 2)
+    state = small[24:] if final else small[24:] + shift(small[24:], "gz", 4)
     body, upper, lower, ahead, behind = call(
         functools.partial(join_x_kernel, final), [shape(512, 128), shape(216, 128), shape(216, 128), shape(32, 128), shape(32, 128)],
-        [pltpu.VMEM((4, 24, 128), F32)], count=7,
-    )(own, above, below, small, before, after, across)
+        [pltpu.VMEM((4, 24, 128), F32)], count=8,
+    )(own, above, below, small, state, before, after, across)
     return body, upper, shift(upper, "gy", 1), shift(lower, "gy", -1), shift(ahead, "gy", 2), shift(behind, "gy", -2)
 
 
@@ -608,19 +608,23 @@
         first_up_kernel, [shape(4, 16, 256), block, block, *share_outs, tile], up_scratch + share_scratch, count=6
     )(gather(unit), weight1, weight0s, x0, x1, both)
 
-    whole_scratch = scratch(SHORT, MID, SHORT, HALO, (512, 128)) + up_scratch[:-1]
-    halos = joint_exchange(w0, share, low, high, dots, False)
-    _, own, up1, down1, up2, _ = halos
+    def near(body, up1, down1):
+        return call(near_kernel, [short, mids], scratch(SHORT, HALO, (512, 128)), count=5, flops=4_000_000)(
+            body, up1, down1, weight0, weight1
+        )
+
+    body, own, up1, down1, up2, down2 = joint_exchange(w0, share, low, high, dots, False)
+    x0, x1 = near(body, up1, down1)
     ahead, behind = up1[208:210] + up2[24:26], down1[208:210] + own[208:210]
     state = jnp.concatenate([ahead + behind, ahead, behind, jnp.zeros((2, 128), F32)])
-    state = state + shift(state, "gz", 4)
     m0, n0, share, low, high = call(
-        second_kernel, [block, block, *share_outs], scratch(SHORT) + whole_scratch + share_scratch, count=11
-    )(*halos, weight2, weight1, weight0, weight0s, both)
-    halos = joint_exchange(n0, share, low, high, state, True)
+        second_kernel, [block, block, *share_outs], scratch(SHORT) + up_scratch[:-1] + share_scratch, count=11
+    )(x0, x1, own, up1, down1, up2, down2, weight2, weight1, weight0s, both)
+    body, own, up1, down1, up2, down2 = joint_exchange(n0, share, low, high, state, True)
+    x0, x1 = near(body, up1, down1)
     r1, u1, w1, m1, n1, first, dots = call(
-        third_kernel, [block] * 5 + [tile, tile], scratch(SHORT, BLOCK) + whole_scratch, count=15
-    )(*halos, weight2, weight1, weight0, weight0s, both, u0, w0, m0, n0)
+        third_kernel, [block] * 5 + [tile, tile], scratch(SHORT, BLOCK) + up_scratch[:-1], count=15
+    )(x0, x1, own, up1, down1, up2, down2, weight2, weight1, weight0s, both, u0, w0, m0, n0)
     field, residual = call(finish_kernel, [block] * 2, count=11)(
         first, total(dots), u0, w0, m0, n0, r1, u1, w1, m1, n1
     )

time: 126 us -> 123 us (0.976)
  waiting for transfers between devices: 25 us -> 22.5 us
  starting transfers between devices: 44.1 us -> 46.3 us
  blocking collectives: 40.5 us -> 38.4 us
    ppermute x25, waiting for transfers between devices: 25 us -> 22.5 us  [shift(): lax.ppermute(v, axis, [((i + distance) % count, i) for i in range(count)])]
    ppermute x25, starting transfers between devices: 44.1 us -> 46.3 us  [shift(): lax.ppermute(v, axis, [((i + distance) % count, i) for i in range(count)])]
    all_to_all x1, blocking collectives: 25.6 us -> 23.4 us  [total(): lax.all_to_all(jnp.broadcast_to(v[None, :1], (count, 1, 128)), axes, 0, 0...]
    pallas_call x2 -> x4, Pallas kernels: 5.95 us -> 5.84 us  [the longest x1 2.12 us: local(): call(second_kernel, [block, block, *share_outs], scratch(SHORT) + up_scra...]
  transfers between devices with their start and end apart: 25 -> 25, of which waited for: 14 -> 16; matrix products, arithmetic and copies ran while one was open for 1% -> 1% of each run, Pallas kernels for 3% -> 2%
where the time goes in v8:
time: 123 us
  starting transfers between devices  46.3 us (38%)
  blocking collectives  38.4 us (31%)
  waiting for transfers between devices  22.5 us (18%)
  Pallas kernels  13.8 us (11%)
    ppermute x25, starting transfers between devices, shift(): lax.ppermute(v, axis, [((i + distance) % count, i) for i in range(count)])  46.3 us
    all_to_all x1, blocking collectives, total(): lax.all_to_all(jnp.broadcast_to(v[None, :1], (count, 1, 128)), axes, 0, 0...  23.4 us
    ppermute x25, waiting for transfers between devices, shift(): lax.ppermute(v, axis, [((i + distance) % count, i) for i in range(count)])  22.5 us
    all_to_all x1, blocking collectives, gather(): lax.all_to_all(jnp.broadcast_to(unit[None], (count,) + unit.shape), ('gx'...  14.9 us
  transfers between devices with their start and end apart: 25, of which 16 were waited for; matrix products, arithmetic and copies ran while one was open for 1% of the time, Pallas kernels for 2%

profile of v8, /device:TPU:1, one launch (start us, length us, event | category | flops | bytes accessed | tf_op | source)
XLA Modules:
  0.0 123.1 jit_solution(3978494279019774500)
XLA Ops:
  0.6 1.9 %shard_map.50 = (f32[2,16,16,128]{3,2,1,0:T(8,128)}, f32[2,6,16,128]{3,2,1,0:T(8,128)}, f32[2,6,16,128]{3,2,1,0:T(8,128)}) custom-call(f32[16,16,128]{2,1,0:T(8,128)} %rhs_in.1, s32[16,16,128]{2,1,0:T(8,128)} %classes_in.1, f32[16]{0:T(128)} %table_in.1), custom_call_target="tpu_custom_call" | custom-call | tf_op jit(solution)/shard_map/pallas_call | solution.py:596
  2.6 3.3 %collective-permute-start = (f32[2,6,16,128]{3,2,1,0:T(8,128)}, f32[2,6,16,128]{3,2,1,0:T(8,128)S(1)}, u32[]{:S(2)}, u32[]{:S(2)}) collective-permute-start(f32[2,6,16,128]{3,2,1,0:T(8,128)} %get-tuple-element.53), channel_id=1, source_target_pairs={{1,0},{2,1},{3,2},{4,3},{5,4},{6,5},{7,6},{0,7},{9,8},{10,9},{11,1... | collective-permute-start | bytes 294920 | tf_op jit(solution)/shard_map/ppermute | solution.py:549
  7.8 1.3 %collective-permute-start.2 = (f32[2,7,16,128]{3,2,1,0:T(8,128)S(1)}, f32[2,7,16,128]{3,2,1,0:T(8,128)S(1)}, u32[]{:S(2)}, u32[]{:S(2)}) collective-permute-start(f32[2,7,16,128]{3,2,1,0:T(8,128)S(1)} %pad_maximum_fusion), channel_id=1, source_target_pairs={{192,0},{0,64},{64,128},{128,192},{193,1},{1,65},{65,129},{129,193... | collective-permute-start | bytes 344072 | tf_op jit(solution)/shard_map/ppermute | solution.py:549
  9.1 1.5 %collective-permute-start.3 = (f32[2,7,16,128]{3,2,1,0:T(8,128)S(1)}, f32[2,7,16,128]{3,2,1,0:T(8,128)S(1)}, u32[]{:S(2)}, u32[]{:S(2)}) collective-permute-start(f32[2,7,16,128]{3,2,1,0:T(8,128)S(1)} %pad_maximum_fusion.1), channel_id=1, source_target_pairs={{64,0},{128,64},{192,128},{0,192},{65,1},{129,65},{193,129},{1,193... | collective-permute-start | bytes 344072 | tf_op jit(solution)/shard_map/ppermute | solution.py:549
  10.7 2.1 %collective-permute-done.2 = f32[2,7,16,128]{3,2,1,0:T(8,128)S(1)} collective-permute-done((f32[2,7,16,128]{3,2,1,0:T(8,128)S(1)}, f32[2,7,16,128]{3,2,1,0:T(8,128)S(1)}, u32[]{:S(2)}, u32[]{:S(2)}) %collective-permute-start.2) | collective-permute-done | bytes 114720 | tf_op jit(solution)/shard_map/ppermute | solution.py:549
  13.0 5.7 %collective-permute-start.4 = (f32[400,128]{1,0:T(8,128)S(1)}, f32[400,128]{1,0:T(8,128)S(1)}, u32[]{:S(2)}, u32[]{:S(2)}) collective-permute-start(f32[400,128]{1,0:T(8,128)S(1)} %get-tuple-element.55), channel_id=1, source_target_pairs={{8,0},{16,8},{24,16},{32,24},{40,32},{48,40},{56,48},{0,56},{9,1},... | collective-permute-start | bytes 614408 | tf_op jit(solution)/shard_map/ppermute | solution.py:549
  18.7 2.7 %collective-permute-done.4.upper = f32[400,128]{1,0:T(8,128)S(1)} collective-permute-done((f32[400,128]{1,0:T(8,128)S(1)}, f32[400,128]{1,0:T(8,128)S(1)}, u32[]{:S(2)}, u32[]{:S(2)}) %collective-permute-start.4) | collective-permute-done | bytes 204832 | tf_op jit(solution)/shard_map/ppermute | solution.py:549
  21.4 3.1 %collective-permute-done.5.lower = f32[400,128]{1,0:T(8,128)S(1)} collective-permute-done((f32[400,128]{1,0:T(8,128)S(1)}, f32[400,128]{1,0:T(8,128)S(1)}, u32[]{:S(2)}, u32[]{:S(2)}) %collective-permute-start.5) | collective-permute-done | bytes 204832 | tf_op jit(solution)/shard_map/ppermute | solution.py:549
  24.5 2.2 %shard_map.52 = (f32[26,32,256]{2,1,0:T(8,128)S(1)}, f32[26,24,256]{2,1,0:T(8,128)S(1)}, f32[12,24,256]{2,1,0:T(8,128)S(1)}, f32[26,24,256]{2,1,0:T(8,128)S(1)},...) custom-call(f32[1280,128]{1,0:T(8,128)S(1)} %bitcast.5, f32[400,128]{1,0:T(8,128)S(1)} %collective-permute-done.4.upper, ...), custom_call_target="tpu_custom_call" | custom-call | tf_op jit(solution)/shard_map/pallas_call | solution.py:601
  26.8 14.9 %all_to_all.10.gather = f32[32,2,8,128]{3,2,1,0:T(8,128)S(1)} all-to-all(f32[32,2,8,128]{3,2,1,0:T(8,128)S(1)} %broadcast_in_dim.10), channel_id=1, replica_groups=mesh['gx'=4,'gy'=8,'gz'=8] {'gx','gy'}, dimensions={0} | all-to-all | bytes 524288 | tf_op jit(solution)/shard_map/all_to_all | solution.py:579
  41.7 2.1 %shard_map.53 = (f32[4,16,256]{2,1,0:T(8,128)S(1)}, f32[16,16,128]{2,1,0:T(8,128)S(1)}, f32[16,16,128]{2,1,0:T(8,128)S(1)}, f32[24,128]{1,0:T(8,128)S(1)}, f32[1...) custom-call(f32[32,2,8,128]{3,2,1,0:T(8,128)S(1)} %all_to_all.10.gather, ...), custom_call_target="tpu_custom_call" | custom-call | tf_op jit(solution)/shard_map/pallas_call | solution.py:607
  43.9 6.4 %collective-permute-start.7 = (f32[48,128]{1,0:T(8,128)S(1)}, f32[48,128]{1,0:T(8,128)S(1)}, u32[]{:S(2)}, u32[]{:S(2)}) collective-permute-start(f32[48,128]{1,0:T(8,128)S(1)} %get-tuple-element.111), channel_id=1, source_target_pairs={{7,0},{0,1},{1,2},{2,3},{3,4},{4,5},{5,6},{6,7},{15,8},{8,9},{9,10... | collective-permute-start | bytes 73736 | tf_op jit(solution)/shard_map/ppermute | solution.py:549
  50.3 1.8 %collective-permute-start.6 = (f32[48,128]{1,0:T(8,128)S(1)}, f32[48,128]{1,0:T(8,128)S(1)}, u32[]{:S(2)}, u32[]{:S(2)}) collective-permute-start(f32[48,128]{1,0:T(8,128)S(1)} %get-tuple-element.112), channel_id=1, source_target_pairs={{1,0},{2,1},{3,2},{4,3},{5,4},{6,5},{7,6},{0,7},{9,8},{10,9},{11,1... | collective-permute-start | bytes 73736 | tf_op jit(solution)/shard_map/ppermute | solution.py:549
  53.6 4.7 %collective-permute-start.8 = (f32[8,128]{1,0:T(8,128)S(1)}, f32[8,128]{1,0:T(8,128)S(1)}, u32[]{:S(2)}, u32[]{:S(2)}) collective-permute-start(f32[8,128]{1,0:T(8,128)S(1)} %slice.58), channel_id=1, source_target_pairs={{4,0},{5,1},{6,2},{7,3},{0,4},{1,5},{2,6},{3,7},{12,8},{13,9},{14,... | collective-permute-start | bytes 12296 | tf_op jit(solution)/shard_map/ppermute | solution.py:549
  58.3 1.3 %collective-permute-start.11 = (f32[32,128]{1,0:T(8,128)S(1)}, f32[32,128]{1,0:T(8,128)S(1)}, u32[]{:S(2)}, u32[]{:S(2)}) collective-permute-start(f32[32,128]{1,0:T(8,128)S(1)} %get-tuple-element.67.small), channel_id=1, source_target_pairs={{128,0},{192,64},{0,128},{64,192},{129,1},{193,65},{1,129},{65,193... | collective-permute-start | bytes 49160 | tf_op jit(solution)/shard_map/ppermute | solution.py:549
  59.9 2.4 %collective-permute-start.10 = (f32[144,128]{1,0:T(8,128)S(1)}, f32[144,128]{1,0:T(8,128)S(1)}, u32[]{:S(2)}, u32[]{:S(2)}) collective-permute-start(f32[144,128]{1,0:T(8,128)S(1)} %get-tuple-element.69), channel_id=1, source_target_pairs={{64,0},{128,64},{192,128},{0,192},{65,1},{129,65},{193,129},{1,193... | collective-permute-start | bytes 221192 | tf_op jit(solution)/shard_map/ppermute | solution.py:549
  62.4 1.7 %collective-permute-done.9.before = f32[144,128]{1,0:T(8,128)S(1)} collective-permute-done((f32[144,128]{1,0:T(8,128)S(1)}, f32[144,128]{1,0:T(8,128)S(1)}, u32[]{:S(2)}, u32[]{:S(2)}) %collective-permute-start.9) | collective-permute-done | bytes 73760 | tf_op jit(solution)/shard_map/ppermute | solution.py:549
  64.2 1.5 %collective-permute-start.13 = (f32[216,128]{1,0:T(8,128)S(1)}, f32[216,128]{1,0:T(8,128)S(1)}, u32[]{:S(2)}, u32[]{:S(2)}) collective-permute-start(f32[216,128]{1,0:T(8,128)S(1)} %get-tuple-element.72), channel_id=1, source_target_pairs={{56,0},{0,8},{8,16},{16,24},{24,32},{32,40},{40,48},{48,56},{57,1}... | collective-permute-start | bytes 331784 | tf_op jit(solution)/shard_map/ppermute | solution.py:549
  65.7 1.3 %collective-permute-start.12 = (f32[216,128]{1,0:T(8,128)S(1)}, f32[216,128]{1,0:T(8,128)S(1)}, u32[]{:S(2)}, u32[]{:S(2)}) collective-permute-start(f32[216,128]{1,0:T(8,128)S(1)} %get-tuple-element.71.own), channel_id=1, source_target_pairs={{8,0},{16,8},{24,16},{32,24},{40,32},{48,40},{56,48},{0,56},{9,1},... | collective-permute-start | bytes 331784 | tf_op jit(solution)/shard_map/ppermute | solution.py:549
  67.3 2.1 %collective-permute-start.15 = (f32[32,128]{1,0:T(8,128)S(1)}, f32[32,128]{1,0:T(8,128)S(1)}, u32[]{:S(2)}, u32[]{:S(2)}) collective-permute-start(f32[32,128]{1,0:T(8,128)S(1)} %get-tuple-element.77), channel_id=1, source_target_pairs={{48,0},{56,8},{0,16},{8,24},{16,32},{24,40},{32,48},{40,56},{49,1}... | collective-permute-start | bytes 49160 | tf_op jit(solution)/shard_map/ppermute | solution.py:549
  69.3 1.5 %collective-permute-done.14.up2 = f32[32,128]{1,0:T(8,128)S(1)} collective-permute-done((f32[32,128]{1,0:T(8,128)S(1)}, f32[32,128]{1,0:T(8,128)S(1)}, u32[]{:S(2)}, u32[]{:S(2)}) %collective-permute-start.14) | collective-permute-done | bytes 16416 | tf_op jit(solution)/shard_map/ppermute | solution.py:549
  72.0 2.1 %shard_map.57 = (f32[16,16,128]{2,1,0:T(8,128)S(1)}, f32[16,16,128]{2,1,0:T(8,128)S(1)}, f32[24,128]{1,0:T(8,128)S(1)}, f32[16,128]{1,0:T(8,128)S(1)}, f32[16,128]{1,0:T(8,128)S(1)}) custom-call(f32[26,24,256]{2,1,0:T(8,128)S(1)} %get-tuple-element.74.x0, f32[12,24,256]{2,1,0:T(8,128)S(1)} %get-tuple-element.75.x1, f32[216,128]{1,0:T(8,128)S(1)} %get-tuple-element.71.own, ...), custom_call_target="tpu_custom_call" | custom-call | tf_op jit(solution)/shard_map/pallas_call | solution.py:620
  74.2 3.0 %collective-permute-start.17 = (f32[48,128]{1,0:T(8,128)S(1)}, f32[48,128]{1,0:T(8,128)S(1)}, u32[]{:S(2)}, u32[]{:S(2)}) collective-permute-start(f32[48,128]{1,0:T(8,128)S(1)} %concatenate.32), channel_id=1, source_target_pairs={{7,0},{0,1},{1,2},{2,3},{3,4},{4,5},{5,6},{6,7},{15,8},{8,9},{9,10... | collective-permute-start | bytes 73736 | tf_op jit(solution)/shard_map/ppermute | solution.py:549
  78.2 2.3 %collective-permute-done.16.above = f32[48,128]{1,0:T(8,128)S(1)} collective-permute-done((f32[48,128]{1,0:T(8,128)S(1)}, f32[48,128]{1,0:T(8,128)S(1)}, u32[]{:S(2)}, u32[]{:S(2)}) %collective-permute-start.16) | collective-permute-done | bytes 24608 | tf_op jit(solution)/shard_map/ppermute | solution.py:549
  81.4 2.3 %collective-permute-start.19 = (f32[144,128]{1,0:T(8,128)S(1)}, f32[144,128]{1,0:T(8,128)S(1)}, u32[]{:S(2)}, u32[]{:S(2)}) collective-permute-start(f32[144,128]{1,0:T(8,128)S(1)} %get-tuple-element.85), channel_id=1, source_target_pairs={{64,0},{128,64},{192,128},{0,192},{65,1},{129,65},{193,129},{1,193... | collective-permute-start | bytes 221192 | tf_op jit(solution)/shard_map/ppermute | solution.py:549
  84.8 3.0 %collective-permute-done.20.across = f32[32,128]{1,0:T(8,128)S(1)} collective-permute-done((f32[32,128]{1,0:T(8,128)S(1)}, f32[32,128]{1,0:T(8,128)S(1)}, u32[]{:S(2)}, u32[]{:S(2)}) %collective-permute-start.20) | collective-permute-done | bytes 16416 | tf_op jit(solution)/shard_map/ppermute | solution.py:549
  88.6 2.0 %collective-permute-start.21 = (f32[216,128]{1,0:T(8,128)S(1)}, f32[216,128]{1,0:T(8,128)S(1)}, u32[]{:S(2)}, u32[]{:S(2)}) collective-permute-start(f32[216,128]{1,0:T(8,128)S(1)} %get-tuple-element.87.own), channel_id=1, source_target_pairs={{8,0},{16,8},{24,16},{32,24},{40,32},{48,40},{56,48},{0,56},{9,1},... | collective-permute-start | bytes 331784 | tf_op jit(solution)/shard_map/ppermute | solution.py:549
  91.8 1.2 collective-permute-start.24
  94.7 1.8 %collective-permute-done.24.down2 = f32[32,128]{1,0:T(8,128)S(1)} collective-permute-done((f32[32,128]{1,0:T(8,128)S(1)}, f32[32,128]{1,0:T(8,128)S(1)}, u32[]{:S(2)}, u32[]{:S(2)}) %collective-permute-start.24) | collective-permute-done | bytes 16416 | tf_op jit(solution)/shard_map/ppermute | solution.py:549
  96.5 1.7 %shard_map.61 = (f32[16,16,128]{2,1,0:T(8,128)S(1)}, f32[16,16,128]{2,1,0:T(8,128)S(1)}, f32[16,16,128]{2,1,0:T(8,128)S(1)}, f32[16,16,128]{2,1,0:T(8,128)S(1)},...) custom-call(f32[26,24,256]{2,1,0:T(8,128)S(1)} %get-tuple-element.89.x0, ...), custom_call_target="tpu_custom_call" | custom-call | tf_op jit(solution)/shard_map/pallas_call | solution.py:625
  98.3 23.4 %all_to_all.11 = f32[256,1,128]{2,1,0:T(1,128)S(1)} all-to-all(f32[256,1,128]{2,1,0:T(1,128)S(1)} %broadcast_in_dim.25), channel_id=1, replica_groups=mesh['gx'=4,'gy'=8,'gz'=8] {'gx','gy','gz'}, dimensions={0} | all-to-all | bytes 262144 | tf_op jit(solution)/shard_map/all_to_all | solution.py:585
  121.7 1.3 %shard_map.62 = (f32[16,16,128]{2,1,0:T(8,128)}, f32[16,16,128]{2,1,0:T(8,128)}) custom-call(f32[8,128]{1,0:T(8,128)S(1)} %get-tuple-element.95.first, f32[8,128]{1,0:T(8,128)S(1)} %broadcast_in_dim.26.second, f32[16,16,128]{2,1,0:T(8,128)S(1)} %get-tuple-element.93.u0, f32[16,16,128]{2,1,0:T(8,128)S(1)} %get-tuple-element.62.own.w0, ...), custom_call_target="tpu_custom_call" | custom-call | tf_op jit(solution)/shard_map/pallas_call | solution.py:628
  (60 shorter events, 12.4 us)
Async XLA Ops:
  2.6 4.2 %copy-start = (f32[2,16,16,128]{3,2,1,0:T(8,128)S(1)}, f32[2,16,16,128]{3,2,1,0:T(8,128)}, u32[]{:S(2)}) copy-start(f32[2,16,16,128]{3,2,1,0:T(8,128)} %get-tuple-element.52.both) | copy-start | bytes 786436
  2.6 5.2 %collective-permute-start = (f32[2,6,16,128]{3,2,1,0:T(8,128)}, f32[2,6,16,128]{3,2,1,0:T(8,128)S(1)}, u32[]{:S(2)}, u32[]{:S(2)}) collective-permute-start(f32[2,6,16,128]{3,2,1,0:T(8,128)} %get-tuple-element.53), channel_id=1, source_target_pairs={{1,0},{2,1},{3,2},{4,3},{5,4},{6,5},{7,6},{0,7},{9,8},{10,9},{11,1... | collective-permute-start | bytes 294920 | tf_op jit(solution)/shard_map/ppermute | solution.py:549
  5.8 2.0 %collective-permute-start.1 = (f32[2,6,16,128]{3,2,1,0:T(8,128)}, f32[2,6,16,128]{3,2,1,0:T(8,128)S(1)}, u32[]{:S(2)}, u32[]{:S(2)}) collective-permute-start(f32[2,6,16,128]{3,2,1,0:T(8,128)} %get-tuple-element.54), channel_id=1, source_target_pairs={{7,0},{0,1},{1,2},{2,3},{3,4},{4,5},{5,6},{6,7},{15,8},{8,9},{9,10... | collective-permute-start | bytes 294920 | tf_op jit(solution)/shard_map/ppermute | solution.py:549
  7.8 4.9 %collective-permute-start.2 = (f32[2,7,16,128]{3,2,1,0:T(8,128)S(1)}, f32[2,7,16,128]{3,2,1,0:T(8,128)S(1)}, u32[]{:S(2)}, u32[]{:S(2)}) collective-permute-start(f32[2,7,16,128]{3,2,1,0:T(8,128)S(1)} %pad_maximum_fusion), channel_id=1, source_target_pairs={{192,0},{0,64},{64,128},{128,192},{193,1},{1,65},{65,129},{129,193... | collective-permute-start | bytes 344072 | tf_op jit(solution)/shard_map/ppermute | solution.py:549
  9.1 3.7 %collective-permute-start.3 = (f32[2,7,16,128]{3,2,1,0:T(8,128)S(1)}, f32[2,7,16,128]{3,2,1,0:T(8,128)S(1)}, u32[]{:S(2)}, u32[]{:S(2)}) collective-permute-start(f32[2,7,16,128]{3,2,1,0:T(8,128)S(1)} %pad_maximum_fusion.1), channel_id=1, source_target_pairs={{64,0},{128,64},{192,128},{0,192},{65,1},{129,65},{193,129},{1,193... | collective-permute-start | bytes 344072 | tf_op jit(solution)/shard_map/ppermute | solution.py:549
  13.0 8.4 %collective-permute-start.4 = (f32[400,128]{1,0:T(8,128)S(1)}, f32[400,128]{1,0:T(8,128)S(1)}, u32[]{:S(2)}, u32[]{:S(2)}) collective-permute-start(f32[400,128]{1,0:T(8,128)S(1)} %get-tuple-element.55), channel_id=1, source_target_pairs={{8,0},{16,8},{24,16},{32,24},{40,32},{48,40},{56,48},{0,56},{9,1},... | collective-permute-start | bytes 614408 | tf_op jit(solution)/shard_map/ppermute | solution.py:549
  18.7 5.8 %collective-permute-start.5 = (f32[400,128]{1,0:T(8,128)S(1)}, f32[400,128]{1,0:T(8,128)S(1)}, u32[]{:S(2)}, u32[]{:S(2)}) collective-permute-start(f32[400,128]{1,0:T(8,128)S(1)} %get-tuple-element.56), channel_id=1, source_target_pairs={{56,0},{0,8},{8,16},{16,24},{24,32},{32,40},{40,48},{48,56},{57,1}... | collective-permute-start | bytes 614408 | tf_op jit(solution)/shard_map/ppermute | solution.py:549
  43.9 8.9 %collective-permute-start.7 = (f32[48,128]{1,0:T(8,128)S(1)}, f32[48,128]{1,0:T(8,128)S(1)}, u32[]{:S(2)}, u32[]{:S(2)}) collective-permute-start(f32[48,128]{1,0:T(8,128)S(1)} %get-tuple-element.111), channel_id=1, source_target_pairs={{7,0},{0,1},{1,2},{2,3},{3,4},{4,5},{5,6},{6,7},{15,8},{8,9},{9,10... | collective-permute-start | bytes 73736 | tf_op jit(solution)/shard_map/ppermute | solution.py:549
  50.3 3.3 %collective-permute-start.6 = (f32[48,128]{1,0:T(8,128)S(1)}, f32[48,128]{1,0:T(8,128)S(1)}, u32[]{:S(2)}, u32[]{:S(2)}) collective-permute-start(f32[48,128]{1,0:T(8,128)S(1)} %get-tuple-element.112), channel_id=1, source_target_pairs={{1,0},{2,1},{3,2},{4,3},{5,4},{6,5},{7,6},{0,7},{9,8},{10,9},{11,1... | collective-permute-start | bytes 73736 | tf_op jit(solution)/shard_map/ppermute | solution.py:549
  53.6 8.7 %collective-permute-start.8 = (f32[8,128]{1,0:T(8,128)S(1)}, f32[8,128]{1,0:T(8,128)S(1)}, u32[]{:S(2)}, u32[]{:S(2)}) collective-permute-start(f32[8,128]{1,0:T(8,128)S(1)} %slice.58), channel_id=1, source_target_pairs={{4,0},{5,1},{6,2},{7,3},{0,4},{1,5},{2,6},{3,7},{12,8},{13,9},{14,... | collective-permute-start | bytes 12296 | tf_op jit(solution)/shard_map/ppermute | solution.py:549
  58.3 4.1 %collective-permute-start.11 = (f32[32,128]{1,0:T(8,128)S(1)}, f32[32,128]{1,0:T(8,128)S(1)}, u32[]{:S(2)}, u32[]{:S(2)}) collective-permute-start(f32[32,128]{1,0:T(8,128)S(1)} %get-tuple-element.67.small), channel_id=1, source_target_pairs={{128,0},{192,64},{0,128},{64,192},{129,1},{193,65},{1,129},{65,193... | collective-permute-start | bytes 49160 | tf_op jit(solution)/shard_map/ppermute | solution.py:549
  59.6 4.5 %collective-permute-start.9 = (f32[144,128]{1,0:T(8,128)S(1)}, f32[144,128]{1,0:T(8,128)S(1)}, u32[]{:S(2)}, u32[]{:S(2)}) collective-permute-start(f32[144,128]{1,0:T(8,128)S(1)} %get-tuple-element.68), channel_id=1, source_target_pairs={{192,0},{0,64},{64,128},{128,192},{193,1},{1,65},{65,129},{129,193... | collective-permute-start | bytes 221192 | tf_op jit(solution)/shard_map/ppermute | solution.py:549
  59.9 4.2 %collective-permute-start.10 = (f32[144,128]{1,0:T(8,128)S(1)}, f32[144,128]{1,0:T(8,128)S(1)}, u32[]{:S(2)}, u32[]{:S(2)}) collective-permute-start(f32[144,128]{1,0:T(8,128)S(1)} %get-tuple-element.69), channel_id=1, source_target_pairs={{64,0},{128,64},{192,128},{0,192},{65,1},{129,65},{193,129},{1,193... | collective-permute-start | bytes 221192 | tf_op jit(solution)/shard_map/ppermute | solution.py:549
  64.2 6.6 %collective-permute-start.13 = (f32[216,128]{1,0:T(8,128)S(1)}, f32[216,128]{1,0:T(8,128)S(1)}, u32[]{:S(2)}, u32[]{:S(2)}) collective-permute-start(f32[216,128]{1,0:T(8,128)S(1)} %get-tuple-element.72), channel_id=1, source_target_pairs={{56,0},{0,8},{8,16},{16,24},{24,32},{32,40},{40,48},{48,56},{57,1}... | collective-permute-start | bytes 331784 | tf_op jit(solution)/shard_map/ppermute | solution.py:549
  65.7 5.1 %collective-permute-start.12 = (f32[216,128]{1,0:T(8,128)S(1)}, f32[216,128]{1,0:T(8,128)S(1)}, u32[]{:S(2)}, u32[]{:S(2)}) collective-permute-start(f32[216,128]{1,0:T(8,128)S(1)} %get-tuple-element.71.own), channel_id=1, source_target_pairs={{8,0},{16,8},{24,16},{32,24},{40,32},{48,40},{56,48},{0,56},{9,1},... | collective-permute-start | bytes 331784 | tf_op jit(solution)/shard_map/ppermute | solution.py:549
  67.0 3.8 %collective-permute-start.14 = (f32[32,128]{1,0:T(8,128)S(1)}, f32[32,128]{1,0:T(8,128)S(1)}, u32[]{:S(2)}, u32[]{:S(2)}) collective-permute-start(f32[32,128]{1,0:T(8,128)S(1)} %get-tuple-element.76), channel_id=1, source_target_pairs={{16,0},{24,8},{32,16},{40,24},{48,32},{56,40},{0,48},{8,56},{17,1}... | collective-permute-start | bytes 49160 | tf_op jit(solution)/shard_map/ppermute | solution.py:549
  67.3 4.7 %collective-permute-start.15 = (f32[32,128]{1,0:T(8,128)S(1)}, f32[32,128]{1,0:T(8,128)S(1)}, u32[]{:S(2)}, u32[]{:S(2)}) collective-permute-start(f32[32,128]{1,0:T(8,128)S(1)} %get-tuple-element.77), channel_id=1, source_target_pairs={{48,0},{56,8},{0,16},{8,24},{16,32},{24,40},{32,48},{40,56},{49,1}... | collective-permute-start | bytes 49160 | tf_op jit(solution)/shard_map/ppermute | solution.py:549
  74.2 4.0 %collective-permute-start.17 = (f32[48,128]{1,0:T(8,128)S(1)}, f32[48,128]{1,0:T(8,128)S(1)}, u32[]{:S(2)}, u32[]{:S(2)}) collective-permute-start(f32[48,128]{1,0:T(8,128)S(1)} %concatenate.32), channel_id=1, source_target_pairs={{7,0},{0,1},{1,2},{2,3},{3,4},{4,5},{5,6},{6,7},{15,8},{8,9},{9,10... | collective-permute-start | bytes 73736 | tf_op jit(solution)/shard_map/ppermute | solution.py:549
  77.2 3.3 %collective-permute-start.16 = (f32[48,128]{1,0:T(8,128)S(1)}, f32[48,128]{1,0:T(8,128)S(1)}, u32[]{:S(2)}, u32[]{:S(2)}) collective-permute-start(f32[48,128]{1,0:T(8,128)S(1)} %concatenate.31), channel_id=1, source_target_pairs={{1,0},{2,1},{3,2},{4,3},{5,4},{6,5},{7,6},{0,7},{9,8},{10,9},{11,1... | collective-permute-start | bytes 73736 | tf_op jit(solution)/shard_map/ppermute | solution.py:549
  80.5 7.3 %collective-permute-start.18 = (f32[144,128]{1,0:T(8,128)S(1)}, f32[144,128]{1,0:T(8,128)S(1)}, u32[]{:S(2)}, u32[]{:S(2)}) collective-permute-start(f32[144,128]{1,0:T(8,128)S(1)} %get-tuple-element.84), channel_id=1, source_target_pairs={{192,0},{0,64},{64,128},{128,192},{193,1},{1,65},{65,129},{129,193... | collective-permute-start | bytes 221192 | tf_op jit(solution)/shard_map/ppermute | solution.py:549
  81.4 6.4 %collective-permute-start.19 = (f32[144,128]{1,0:T(8,128)S(1)}, f32[144,128]{1,0:T(8,128)S(1)}, u32[]{:S(2)}, u32[]{:S(2)}) collective-permute-start(f32[144,128]{1,0:T(8,128)S(1)} %get-tuple-element.85), channel_id=1, source_target_pairs={{64,0},{128,64},{192,128},{0,192},{65,1},{129,65},{193,129},{1,193... | collective-permute-start | bytes 221192 | tf_op jit(solution)/shard_map/ppermute | solution.py:549
  83.7 4.1 %collective-permute-start.20 = (f32[32,128]{1,0:T(8,128)S(1)}, f32[32,128]{1,0:T(8,128)S(1)}, u32[]{:S(2)}, u32[]{:S(2)}) collective-permute-start(f32[32,128]{1,0:T(8,128)S(1)} %get-tuple-element.83.small), channel_id=1, source_target_pairs={{128,0},{192,64},{0,128},{64,192},{129,1},{193,65},{1,129},{65,193... | collective-permute-start | bytes 49160 | tf_op jit(solution)/shard_map/ppermute | solution.py:549
  87.9 5.1 %collective-permute-start.22 = (f32[216,128]{1,0:T(8,128)S(1)}, f32[216,128]{1,0:T(8,128)S(1)}, u32[]{:S(2)}, u32[]{:S(2)}) collective-permute-start(f32[216,128]{1,0:T(8,128)S(1)} %get-tuple-element.88), channel_id=1, source_target_pairs={{56,0},{0,8},{8,16},{16,24},{24,32},{32,40},{40,48},{48,56},{57,1}... | collective-permute-start | bytes 331784 | tf_op jit(solution)/shard_map/ppermute | solution.py:549
  88.6 4.4 %collective-permute-start.21 = (f32[216,128]{1,0:T(8,128)S(1)}, f32[216,128]{1,0:T(8,128)S(1)}, u32[]{:S(2)}, u32[]{:S(2)}) collective-permute-start(f32[216,128]{1,0:T(8,128)S(1)} %get-tuple-element.87.own), channel_id=1, source_target_pairs={{8,0},{16,8},{24,16},{32,24},{40,32},{48,40},{56,48},{0,56},{9,1},... | collective-permute-start | bytes 331784 | tf_op jit(solution)/shard_map/ppermute | solution.py:549
  90.6 4.0 %collective-permute-start.23 = (f32[32,128]{1,0:T(8,128)S(1)}, f32[32,128]{1,0:T(8,128)S(1)}, u32[]{:S(2)}, u32[]{:S(2)}) collective-permute-start(f32[32,128]{1,0:T(8,128)S(1)} %get-tuple-element.91), channel_id=1, source_target_pairs={{16,0},{24,8},{32,16},{40,24},{48,32},{56,40},{0,48},{8,56},{17,1}... | collective-permute-start | bytes 49160 | tf_op jit(solution)/shard_map/ppermute | solution.py:549
  91.8 4.7 %collective-permute-start.24 = (f32[32,128]{1,0:T(8,128)S(1)}, f32[32,128]{1,0:T(8,128)S(1)}, u32[]{:S(2)}, u32[]{:S(2)}) collective-permute-start(f32[32,128]{1,0:T(8,128)S(1)} %get-tuple-element.92), channel_id=1, source_target_pairs={{48,0},{56,8},{0,16},{8,24},{16,32},{24,40},{32,48},{40,56},{49,1}... | collective-permute-start | bytes 49160 | tf_op jit(solution)/shard_map/ppermute | solution.py:549

commit v9 on v8

--- a/solution.py
+++ b/solution.py
@@ -116,14 +116,23 @@
     return base, above, above + 1, -8 * k, 120 - 8 * k
 
 
+def assemble_half(refs, i, sources):
+    main, above, below, up, down = sources(i)
+    lane = iota((16, 128), 1)
+    side = jnp.where(lane < 64, roll(refs[above][...], up, 1), roll(refs[below][...], down, 1))
+    return jnp.concatenate([refs[main][...], side], axis=1)
+
+
 def assemble_fine(body, sides, i, sources=slab_sources):
-    def unit(u):
-        return jnp.concatenate([body[u][...], sides[u][...]], axis=0)
-
-    main, above, below, up, down = sources(i)
-    lane = iota((32, 128), 1)
-    side = jnp.where(lane < 64, roll(unit(above), up, 1), roll(unit(below), down, 1))
-    return jnp.concatenate([unit(main), side], axis=1)
+    return jnp.concatenate([assemble_half(body, i, sources), assemble_half(sides, i, sources)], axis=0)
+
+
+class Joined:
+    def __init__(self, top, bottom):
+        self.top, self.bottom = top, bottom
+
+    def __getitem__(self, i):
+        return jnp.concatenate([self.top[i], self.bottom[i]], axis=0)
 
 
 def pack_rows_kernel(body, upper, lower):
@@ -161,36 +170,52 @@
     return near(lane) & (z >= 0) & (z < 128 * sizes()[2])
 
 
-def inside_fine(rows):
-    row, lane = iota((rows, 256), 0), iota((rows, 256), 1)
-    y = jnp.where(row < rows // 2 + 8, row, row - rows) + 16 * place()[1]
-    return inside_lanes(lane) & (y >= 0) & (y < 16 * sizes()[1])
-
-
-def fine_weights(body, sides, weight0, weight0s, weight1, middle, quads, unit):
-    gx, nx = place()[0], sizes()[0]
-    inside, insides = inside_fine(32), inside_fine(24)
-
-    def weigh(i):
-        kap = assemble_fine(body, sides, i)
-        x = 16 * gx + (i - 5)
-        v = jnp.where(inside & (x >= 0) & (x < 16 * nx), OMEGA / (kap + 6.0), 0.0)
-        weight0[i] = v
-        weight0s[i] = squeeze(v)
-        return squeeze(kap)
-
-    weigh(0)
-    weigh(SLABS - 1)
-    for m in range(MIDS):
-        kap1 = pair_mean(weigh(2 * m + 1) + weigh(2 * m + 2), 1)
-        middle[m] = kap1
-        x = 8 * gx + (m - 2)
-        weight1[m] = jnp.where(insides & (x >= 0) & (x < 8 * nx), OMEGA / (kap1 + 1.5), 0.0)
+def squeeze_half(v):
+    return jnp.where(iota((8, v.shape[1]), 0) < 4, v[:8], v[8:])
+
+
+def weigh(kap, extra, i, shift, cells, inside):
+    x = cells * place()[0] + (i - shift)
+    return jnp.where(inside & (x >= 0) & (x < cells * sizes()[0]), OMEGA / (kap + extra), 0.0)
+
+
+def own_weights_kernel(body, weight0, weight1, unit, middle, quads):
+    here = units(body, 16 * UNITS, UNITS)
+    inside = inside_lanes(iota((16, 256), 1))
+    for m in range(-1, MIDS + 1):
+        pair = []
+        for i in (2 * m + 1, 2 * m + 2):
+            if 0 <= i < SLABS:
+                kap = assemble_half(here, i, slab_sources)
+                weight0[i] = weigh(kap, 6.0, i, 5, 16, inside)
+                pair.append(kap)
+        if 0 <= m < MIDS:
+            kap1 = pair_mean(pair[0] + pair[1], 1)
+            middle[m] = kap1
+            weight1[m] = weigh(kap1, 1.5, m, 2, 8, inside)
     for c in range(4):
-        kap2 = pair_mean(middle[2 + 2 * c] + middle[3 + 2 * c], 2)[:16]
-        weight2 = OMEGA / (kap2 + 0.375)
+        weight2 = OMEGA / (pair_mean(middle[2 + 2 * c] + middle[3 + 2 * c], 2) + 0.375)
         quads[0, c], quads[1, c] = weight2[:, :128], weight2[:, 128:]
     pack_coarse(quads, unit)
+
+
+def halo_weights(there, weight0, weight0s, weight1):
+    row, lane = iota((16, 256), 0), iota((16, 256), 1)
+    y = jnp.where(row < 8, row + 16, row - 16) + 16 * place()[1]
+    inside = inside_lanes(lane) & (y >= 0) & (y < 16 * sizes()[1])
+    y = jnp.where(iota((8, 256), 0) < 4, 1, -1) + place()[1]
+    insides = inside_lanes(iota((8, 256), 1)) & (y >= 0) & (y < sizes()[1])
+    for m in range(-1, MIDS + 1):
+        pair = []
+        for i in (2 * m + 1, 2 * m + 2):
+            if 0 <= i < SLABS:
+                kap = assemble_half(there, i, slab_sources)
+                v = weigh(kap, 6.0, i, 5, 16, inside)
+                weight0[i] = v
+                weight0s[i] = squeeze_half(v)
+                pair.append(squeeze_half(kap))
+        if 0 <= m < MIDS:
+            weight1[m] = weigh(pair_mean(pair[0] + pair[1], 1), 1.5, m, 2, 8, insides)
 
 
 def pack_coarse(quads, unit):
@@ -224,10 +249,10 @@
     lax.fori_loop(0, MIDS, middle_slab, 0, unroll=4)
 
 
-def first_down_kernel(body, upper, lower, weight0, weight0s, weight1, x0, x1, unit, r, tall, r1, quads, sides):
-    there = unpack_rows(upper, lower, 5 * UNITS // 8, sides)
-    fine_weights(units(body, 16 * UNITS, UNITS), there, weight0, weight0s, weight1, r1, quads, unit.at[1])
+def first_down_kernel(body, upper, lower, own0, own1, halo0, halo0s, halo1, x0, x1, unit, r, tall, r1, quads, sides):
+    halo_weights(unpack_rows(upper, lower, 5 * UNITS // 8, sides), halo0, halo0s, halo1)
     here, there = units(body, 0, UNITS), unpack_rows(upper, lower, 0, sides)
+    weight0, weight1 = Joined(own0, halo0), Joined(own1, halo1)
     near_sweep(lambda i: assemble_fine(here, there, i), weight0, weight1, x0, x1, r1, r, tall)
     for c in range(4):
         m = 2 + 2 * c
@@ -235,12 +260,12 @@
         left = KEEP * (r1[m] + r1[m + 1]) + 0.25 * (((x1[m - 1] + x1[m + 2]) + two) + around(two, 2, 2))
         v = pair_mean(left, 2)[:16]
         quads[0, c], quads[1, c] = v[:, :128], v[:, 128:]
-    pack_coarse(quads, unit.at[0])
+    pack_coarse(quads, unit)
 
 
 def share_sweep(block, weight0, weight1, share, x0, r1, x1, quads):
     for k in range(16):
-        x0[k] = weight0[k + 5, :16, :128] * block[k]
+        x0[k] = weight0.top[k + 5, :, :128] * block[k]
     zero, low = jnp.zeros((16, 128), F32), jnp.zeros((8, 256), F32)
 
     def tall(v):
@@ -449,8 +474,13 @@
     return jnp.broadcast_to(jnp.sum(picked, axis=0, keepdims=True), (8, 128))
 
 
-def first_up_kernel(gather, weight1, weight0, x0, x1, both, weight2, u, w, share, low, high, dots, *scratch):
+def wide(row, k):
+    return jnp.broadcast_to(row[:, MARK + k:MARK + k + 1], (16, 128))
+
+
+def first_up_kernel(gather, own0, halo0s, own1, halo1, x0, x1, both, weight2, u, w, share, low, high, dots, *scratch):
     (*scratch, full, y0, y1, z1, quads) = scratch
+    weight0, weight1 = Joined(own0, halo0s), Joined(own1, halo1)
     row, lane = iota((16, 256), 0), iota((16, 256), 1)
     y = jnp.where(row < 10, row, row - 16) + 4 * place()[1]
     inside = inside_lanes(lane) & (y >= 0) & (y < 4 * sizes()[1])
@@ -467,12 +497,15 @@
     share_sweep(w, weight0, weight1, share, y0, y1, z1, quads)
 
 
-def near_kernel(body, up1, down1, weight0, weight1, x0, x1, r, tall, sides):
+def near_kernel(body, up1, down1, own0, halo0, own1, halo1, x0, x1, r, tall, sides):
+    weight0, weight1 = Joined(own0, halo0), Joined(own1, halo1)
     here, there = units(body, 0, 32), unpack_rows(up1, down1, 0, sides)
     near_sweep(lambda i: assemble_fine(here, there, i, near_sources), weight0, weight1, x0, x1, None, r, tall)
 
 
-def second_kernel(x0, x1, own, up1, down1, up2, down2, weight2, weight1, weight0s, both, m0, n0, share, low, high, *scratch):
+def second_kernel(x0, x1, own, up1, down1, up2, down2, weight2, own0, halo0s, own1, halo1, both,
+                  m0, n0, share, low, high, *scratch):
+    weight0s, weight1 = Joined(own0, halo0s), Joined(own1, halo1)
     (full, *scratch, y0, y1, z1, quads) = scratch
     shares = (own, up1, down1, up2, down2)
     up_sweep(lambda *a: assemble_shares(*shares, *a), weight2, weight1, weight0s, x0, x1, both.at[1], full, n0, *scratch)
@@ -482,13 +515,14 @@
     share_sweep(n0, weight0s, weight1, share, y0, y1, z1, quads)
 
 
-def third_kernel(x0, x1, own, up1, down1, up2, down2, weight2, weight1, weight0s, both, u0, w0, m0, n0,
+def third_kernel(x0, x1, own, up1, down1, up2, down2, weight2, own0, halo0s, own1, halo1, both, u0, w0, m0, n0,
                  r1, u1, w1, m1, n1, first, dots, full, last, *scratch):
+    weight0s, weight1 = Joined(own0, halo0s), Joined(own1, halo1)
     shares = (own, up1, down1, up2, down2)
     up_sweep(lambda *a: assemble_shares(*shares, *a), weight2, weight1, weight0s, x0, x1, both.at[1], full, last, *scratch)
     total0 = own[208:209] + up2[25:26] + down2[26:27]
     first[...] = jnp.broadcast_to(total0, (8, 128))
-    alpha = total0[:, MARK:MARK + 1] / total0[:, MARK + 1:MARK + 2]
+    alpha = wide(total0, 0) / wide(total0, 1)
     sums = [jnp.zeros((16, 128), F32)] * 12
     for k in range(16):
         vw0, vm0, vn0 = w0[k], m0[k], n0[k]
@@ -504,11 +538,9 @@
     dots[...] = lanes_of(sums)
 
 
-def finish_kernel(first, second, u0, w0, m0, n0, r1, u1, w1, m1, n1, field, residual):
-    g0, d0 = first[0:1, MARK:MARK + 1], first[0:1, MARK + 1:MARK + 2]
-    (r1u1, r1m1, r1m0, w1u1, w1m1, w1m0, w0u1, w0m1, w0m0, n1m1, n1m0, n0m0) = [
-        second[0:1, MARK + k:MARK + k + 1] for k in range(12)
-    ]
+def finish_kernel(first, second, u0, w0, m0, n0, r1, u1, w1, m1, n1, field_out, residual_out, field, residual, sems):
+    g0, d0 = [wide(first[0:1], k) for k in range(2)]
+    (r1u1, r1m1, r1m0, w1u1, w1m1, w1m0, w0u1, w0m1, w0m0, n1m1, n1m0, n0m0) = [wide(second[0:1], k) for k in range(12)]
     alpha0 = g0 / d0
     beta1 = r1u1 / g0
     curve1 = w1u1 + 2.0 * beta1 * w0u1 + beta1 * beta1 * d0
@@ -523,21 +555,30 @@
     mix = alpha1 + alpha2 * beta2
     cu0, cu1, cm1, cm0 = alpha0 + mix * beta1, mix + alpha2, alpha2 * alpha1, alpha2 * ab
     cw0 = mix * beta1
+    copies = []
     for k in range(16):
         field[k] = (cu0 * u0[k] + cu1 * u1[k]) - (cm1 * m1[k] + cm0 * m0[k])
         residual[k] = r1[k] - (cw0 * w0[k] + cu1 * w1[k]) + (cm1 * n1[k] + cm0 * n0[k])
+        if k % 4 == 3:
+            part = pl.ds(k - 3, 4)
+            copies.append(pltpu.make_async_copy(field.at[part], field_out.at[part], sems.at[0, k // 4]))
+            copies.append(pltpu.make_async_copy(residual.at[part], residual_out.at[part], sems.at[1, k // 4]))
+            copies[-2].start()
+            copies[-1].start()
+    for copy in copies:
+        copy.wait()
 
 
 def shape(*dims):
     return jax.ShapeDtypeStruct(dims, F32)
 
 
-def call(kernel, outs, scratch=(), specs=None, count=0, grant=40, flops=0):
+def call(kernel, outs, scratch=(), specs=None, count=0, grant=40, flops=0, out=VMEM):
     return pl.pallas_call(
         kernel,
         out_shape=outs,
         in_specs=specs or [VMEM] * count,
-        out_specs=[VMEM] * len(outs),
+        out_specs=[out] * len(outs),
         scratch_shapes=list(scratch),
         compiler_params=pltpu.CompilerParams(vmem_limit_bytes=grant * 1024 * 1024),
         cost_estimate=pl.CostEstimate(flops=flops, bytes_accessed=flops, transcendentals=0) if flops else None,
@@ -598,19 +639,23 @@
         [pltpu.VMEM(BLOCK, jnp.int32), pltpu.SMEM((CLASSES,), F32), pltpu.SemaphoreType.DMA((3,))], specs=[ANY] * 3, grant=60,
     )(right_side, classes, table)
     halos = fine_exchange(both, low, high)
-    weight0, weight0s, weight1, x0, x1, unit = call(
-        first_down_kernel, [shape(*HALO), short, mids, short, mids, shape(2, 8, 128)],
-        scratch(SHORT, HALO, MID, (2, 4, 16, 128), (16 * UNITS, 128)), count=3,
-    )(*halos)
+    own0, own1, unit2 = call(
+        own_weights_kernel, [shape(SLABS, 16, 256), shape(MIDS, 16, 256), tile],
+        scratch((MIDS, 16, 256), (2, 4, 16, 128)), count=1, flops=4_000_000,
+    )(halos[0])
+    halo0, halo0s, halo1, x0, x1, unit = call(
+        first_down_kernel, [shape(SLABS, 16, 256), shape(SLABS, 8, 256), shape(MIDS, 8, 256), short, mids, tile],
+        scratch(SHORT, HALO, MID, (2, 4, 16, 128), (16 * UNITS, 128)), count=5,
+    )(*halos, own0, own1)
     share_outs = [shape(24, 128), shape(16, 128), shape(16, 128)]
     share_scratch = scratch(BLOCK, (10, 24, 256), (10, 24, 256), (2, 6, 24, 128))
     weight2, u0, w0, share, low, high, dots = call(
-        first_up_kernel, [shape(4, 16, 256), block, block, *share_outs, tile], up_scratch + share_scratch, count=6
-    )(gather(unit), weight1, weight0s, x0, x1, both)
+        first_up_kernel, [shape(4, 16, 256), block, block, *share_outs, tile], up_scratch + share_scratch, count=8
+    )(gather(jnp.stack([unit, unit2])), own0, halo0s, own1, halo1, x0, x1, both)
 
     def near(body, up1, down1):
-        return call(near_kernel, [short, mids], scratch(SHORT, HALO, (512, 128)), count=5, flops=4_000_000)(
-            body, up1, down1, weight0, weight1
+        return call(near_kernel, [short, mids], scratch(SHORT, HALO, (512, 128)), count=7, flops=4_000_000)(
+            body, up1, down1, own0, halo0, own1, halo1
         )
 
     body, own, up1, down1, up2, down2 = joint_exchange(w0, share, low, high, dots, False)
@@ -618,14 +663,16 @@
     ahead, behind = up1[208:210] + up2[24:26], down1[208:210] + own[208:210]
     state = jnp.concatenate([ahead + behind, ahead, behind, jnp.zeros((2, 128), F32)])
     m0, n0, share, low, high = call(
-        second_kernel, [block, block, *share_outs], scratch(SHORT) + up_scratch[:-1] + share_scratch, count=11
-    )(x0, x1, own, up1, down1, up2, down2, weight2, weight1, weight0s, both)
+        second_kernel, [block, block, *share_outs], scratch(SHORT) + up_scratch[:-1] + share_scratch, count=13
+    )(x0, x1, own, up1, down1, up2, down2, weight2, own0, halo0s, own1, halo1, both)
     body, own, up1, down1, up2, down2 = joint_exchange(n0, share, low, high, state, True)
     x0, x1 = near(body, up1, down1)
     r1, u1, w1, m1, n1, first, dots = call(
-        third_kernel, [block] * 5 + [tile, tile], scratch(SHORT, BLOCK) + up_scratch[:-1], count=15
-    )(x0, x1, own, up1, down1, up2, down2, weight2, weight1, weight0s, both, u0, w0, m0, n0)
-    field, residual = call(finish_kernel, [block] * 2, count=11)(
+        third_kernel, [block] * 5 + [tile, tile], scratch(SHORT, BLOCK) + up_scratch[:-1], count=17
+    )(x0, x1, own, up1, down1, up2, down2, weight2, own0, halo0s, own1, halo1, both, u0, w0, m0, n0)
+    field, residual = call(
+        finish_kernel, [block] * 2, scratch(BLOCK, BLOCK) + [pltpu.SemaphoreType.DMA((2, 4))], count=11, out=ANY
+    )(
         first, total(dots), u0, w0, m0, n0, r1, u1, w1, m1, n1
     )
     return field, residual

time: 123 us -> 123 us (level)
    pallas_call x2 -> x3, Pallas kernels: 3.58 us -> 3.17 us  [the longest x1 1.76 us: local(): call(first_down_kernel, [shape(SLABS, 16, 256), shape(SLABS, 8, 256), sha...]
where the time goes in v9:
time: 123 us; the launch traced here: 122 us
  starting transfers between devices  46.3 us (38%)
  blocking collectives  38.4 us (31%)
  waiting for transfers between devices  22 us (18%)
  Pallas kernels  13.4 us (11%)
    ppermute x25, starting transfers between devices, shift(): lax.ppermute(v, axis, [((i + distance) % count, i) for i in range(count)])  46.3 us
    all_to_all x1, blocking collectives, total(): lax.all_to_all(jnp.broadcast_to(v[None, :1], (count, 1, 128)), axes, 0, 0...  23.4 us
    ppermute x25, waiting for transfers between devices, shift(): lax.ppermute(v, axis, [((i + distance) % count, i) for i in range(count)])  22 us
    all_to_all x1, blocking collectives, gather(): lax.all_to_all(jnp.broadcast_to(unit[None], (count,) + unit.shape), ('gx'...  14.9 us
  transfers between devices with their start and end apart: 25, of which 16 were waited for; matrix products, arithmetic and copies ran while one was open for 1% of the time, Pallas kernels for 2%

profile of v9, /device:TPU:1, one launch (start us, length us, event | category | flops | bytes accessed | tf_op | source)
XLA Modules:
  0.0 122.3 jit_solution(2963597025242002811)
XLA Ops:
  0.6 1.9 %shard_map.50 = (f32[2,16,16,128]{3,2,1,0:T(8,128)}, f32[2,6,16,128]{3,2,1,0:T(8,128)}, f32[2,6,16,128]{3,2,1,0:T(8,128)}) custom-call(f32[16,16,128]{2,1,0:T(8,128)} %rhs_in.1, s32[16,16,128]{2,1,0:T(8,128)} %classes_in.1, f32[16]{0:T(128)} %table_in.1), custom_call_target="tpu_custom_call" | custom-call | tf_op jit(solution)/shard_map/pallas_call | solution.py:637
  2.6 3.3 %collective-permute-start = (f32[2,6,16,128]{3,2,1,0:T(8,128)}, f32[2,6,16,128]{3,2,1,0:T(8,128)S(1)}, u32[]{:S(2)}, u32[]{:S(2)}) collective-permute-start(f32[2,6,16,128]{3,2,1,0:T(8,128)} %get-tuple-element.56), channel_id=1, source_target_pairs={{1,0},{2,1},{3,2},{4,3},{5,4},{6,5},{7,6},{0,7},{9,8},{10,9},{11,1... | collective-permute-start | bytes 294920 | tf_op jit(solution)/shard_map/ppermute | solution.py:590
  7.8 1.3 %collective-permute-start.2 = (f32[2,7,16,128]{3,2,1,0:T(8,128)S(1)}, f32[2,7,16,128]{3,2,1,0:T(8,128)S(1)}, u32[]{:S(2)}, u32[]{:S(2)}) collective-permute-start(f32[2,7,16,128]{3,2,1,0:T(8,128)S(1)} %pad_maximum_fusion), channel_id=1, source_target_pairs={{192,0},{0,64},{64,128},{128,192},{193,1},{1,65},{65,129},{129,193... | collective-permute-start | bytes 344072 | tf_op jit(solution)/shard_map/ppermute | solution.py:590
  9.1 1.5 %collective-permute-start.3 = (f32[2,7,16,128]{3,2,1,0:T(8,128)S(1)}, f32[2,7,16,128]{3,2,1,0:T(8,128)S(1)}, u32[]{:S(2)}, u32[]{:S(2)}) collective-permute-start(f32[2,7,16,128]{3,2,1,0:T(8,128)S(1)} %pad_maximum_fusion.1), channel_id=1, source_target_pairs={{64,0},{128,64},{192,128},{0,192},{65,1},{129,65},{193,129},{1,193... | collective-permute-start | bytes 344072 | tf_op jit(solution)/shard_map/ppermute | solution.py:590
  10.7 2.1 %collective-permute-done.2 = f32[2,7,16,128]{3,2,1,0:T(8,128)S(1)} collective-permute-done((f32[2,7,16,128]{3,2,1,0:T(8,128)S(1)}, f32[2,7,16,128]{3,2,1,0:T(8,128)S(1)}, u32[]{:S(2)}, u32[]{:S(2)}) %collective-permute-start.2) | collective-permute-done | bytes 114720 | tf_op jit(solution)/shard_map/ppermute | solution.py:590
  13.0 5.7 %collective-permute-start.4 = (f32[400,128]{1,0:T(8,128)S(1)}, f32[400,128]{1,0:T(8,128)S(1)}, u32[]{:S(2)}, u32[]{:S(2)}) collective-permute-start(f32[400,128]{1,0:T(8,128)S(1)} %get-tuple-element.58), channel_id=1, source_target_pairs={{8,0},{16,8},{24,16},{32,24},{40,32},{48,40},{56,48},{0,56},{9,1},... | collective-permute-start | bytes 614408 | tf_op jit(solution)/shard_map/ppermute | solution.py:590
  19.2 2.2 %collective-permute-done.4.upper = f32[400,128]{1,0:T(8,128)S(1)} collective-permute-done((f32[400,128]{1,0:T(8,128)S(1)}, f32[400,128]{1,0:T(8,128)S(1)}, u32[]{:S(2)}, u32[]{:S(2)}) %collective-permute-start.4) | collective-permute-done | bytes 204832 | tf_op jit(solution)/shard_map/ppermute | solution.py:590
  21.4 3.1 %collective-permute-done.5.lower = f32[400,128]{1,0:T(8,128)S(1)} collective-permute-done((f32[400,128]{1,0:T(8,128)S(1)}, f32[400,128]{1,0:T(8,128)S(1)}, u32[]{:S(2)}, u32[]{:S(2)}) %collective-permute-start.5) | collective-permute-done | bytes 204832 | tf_op jit(solution)/shard_map/ppermute | solution.py:590
  24.5 1.8 %shard_map.53 = (f32[26,16,256]{2,1,0:T(8,128)S(1)}, f32[26,8,256]{2,1,0:T(8,128)S(1)}, f32[12,8,256]{2,1,0:T(8,128)S(1)}, f32[26,24,256]{2,1,0:T(8,128)S(1)}, f...) custom-call(f32[1280,128]{1,0:T(8,128)S(1)} %bitcast.8, f32[400,128]{1,0:T(8,128)S(1)} %collective-permute-done.4.upper, ...), custom_call_target="tpu_custom_call" | custom-call | tf_op jit(solution)/shard_map/pallas_call | solution.py:646
  26.3 14.9 %all_to_all.10.gather = f32[32,2,8,128]{3,2,1,0:T(8,128)S(1)} all-to-all(f32[32,2,8,128]{3,2,1,0:T(8,128)S(1)} %broadcast_in_dim.10), channel_id=1, replica_groups=mesh['gx'=4,'gy'=8,'gz'=8] {'gx','gy'}, dimensions={0} | all-to-all | bytes 524288 | tf_op jit(solution)/shard_map/all_to_all | solution.py:620
  41.2 2.1 %shard_map.54 = (f32[4,16,256]{2,1,0:T(8,128)S(1)}, f32[16,16,128]{2,1,0:T(8,128)S(1)}, f32[16,16,128]{2,1,0:T(8,128)S(1)}, f32[24,128]{1,0:T(8,128)S(1)}, f32[1...) custom-call(f32[32,2,8,128]{3,2,1,0:T(8,128)S(1)} %all_to_all.10.gather, ...), custom_call_target="tpu_custom_call" | custom-call | tf_op jit(solution)/shard_map/pallas_call | solution.py:652
  43.4 6.4 %collective-permute-start.7 = (f32[48,128]{1,0:T(8,128)S(1)}, f32[48,128]{1,0:T(8,128)S(1)}, u32[]{:S(2)}, u32[]{:S(2)}) collective-permute-start(f32[48,128]{1,0:T(8,128)S(1)} %get-tuple-element.117), channel_id=1, source_target_pairs={{7,0},{0,1},{1,2},{2,3},{3,4},{4,5},{5,6},{6,7},{15,8},{8,9},{9,10... | collective-permute-start | bytes 73736 | tf_op jit(solution)/shard_map/ppermute | solution.py:590
  49.8 1.8 %collective-permute-start.6 = (f32[48,128]{1,0:T(8,128)S(1)}, f32[48,128]{1,0:T(8,128)S(1)}, u32[]{:S(2)}, u32[]{:S(2)}) collective-permute-start(f32[48,128]{1,0:T(8,128)S(1)} %get-tuple-element.118), channel_id=1, source_target_pairs={{1,0},{2,1},{3,2},{4,3},{5,4},{6,5},{7,6},{0,7},{9,8},{10,9},{11,1... | collective-permute-start | bytes 73736 | tf_op jit(solution)/shard_map/ppermute | solution.py:590
  53.1 4.7 %collective-permute-start.8 = (f32[8,128]{1,0:T(8,128)S(1)}, f32[8,128]{1,0:T(8,128)S(1)}, u32[]{:S(2)}, u32[]{:S(2)}) collective-permute-start(f32[8,128]{1,0:T(8,128)S(1)} %slice.58), channel_id=1, source_target_pairs={{4,0},{5,1},{6,2},{7,3},{0,4},{1,5},{2,6},{3,7},{12,8},{13,9},{14,... | collective-permute-start | bytes 12296 | tf_op jit(solution)/shard_map/ppermute | solution.py:590
  57.8 1.3 %collective-permute-start.11 = (f32[32,128]{1,0:T(8,128)S(1)}, f32[32,128]{1,0:T(8,128)S(1)}, u32[]{:S(2)}, u32[]{:S(2)}) collective-permute-start(f32[32,128]{1,0:T(8,128)S(1)} %get-tuple-element.73.small), channel_id=1, source_target_pairs={{128,0},{192,64},{0,128},{64,192},{129,1},{193,65},{1,129},{65,193... | collective-permute-start | bytes 49160 | tf_op jit(solution)/shard_map/ppermute | solution.py:590
  59.5 2.4 %collective-permute-start.10 = (f32[144,128]{1,0:T(8,128)S(1)}, f32[144,128]{1,0:T(8,128)S(1)}, u32[]{:S(2)}, u32[]{:S(2)}) collective-permute-start(f32[144,128]{1,0:T(8,128)S(1)} %get-tuple-element.75), channel_id=1, source_target_pairs={{64,0},{128,64},{192,128},{0,192},{65,1},{129,65},{193,129},{1,193... | collective-permute-start | bytes 221192 | tf_op jit(solution)/shard_map/ppermute | solution.py:590
  61.9 1.7 %collective-permute-done.9.before = f32[144,128]{1,0:T(8,128)S(1)} collective-permute-done((f32[144,128]{1,0:T(8,128)S(1)}, f32[144,128]{1,0:T(8,128)S(1)}, u32[]{:S(2)}, u32[]{:S(2)}) %collective-permute-start.9) | collective-permute-done | bytes 73760 | tf_op jit(solution)/shard_map/ppermute | solution.py:590
  63.7 1.5 %collective-permute-start.13 = (f32[216,128]{1,0:T(8,128)S(1)}, f32[216,128]{1,0:T(8,128)S(1)}, u32[]{:S(2)}, u32[]{:S(2)}) collective-permute-start(f32[216,128]{1,0:T(8,128)S(1)} %get-tuple-element.78), channel_id=1, source_target_pairs={{56,0},{0,8},{8,16},{16,24},{24,32},{32,40},{40,48},{48,56},{57,1}... | collective-permute-start | bytes 331784 | tf_op jit(solution)/shard_map/ppermute | solution.py:590
  65.2 1.3 %collective-permute-start.12 = (f32[216,128]{1,0:T(8,128)S(1)}, f32[216,128]{1,0:T(8,128)S(1)}, u32[]{:S(2)}, u32[]{:S(2)}) collective-permute-start(f32[216,128]{1,0:T(8,128)S(1)} %get-tuple-element.77.own), channel_id=1, source_target_pairs={{8,0},{16,8},{24,16},{32,24},{40,32},{48,40},{56,48},{0,56},{9,1},... | collective-permute-start | bytes 331784 | tf_op jit(solution)/shard_map/ppermute | solution.py:590
  66.8 2.1 %collective-permute-start.15 = (f32[32,128]{1,0:T(8,128)S(1)}, f32[32,128]{1,0:T(8,128)S(1)}, u32[]{:S(2)}, u32[]{:S(2)}) collective-permute-start(f32[32,128]{1,0:T(8,128)S(1)} %get-tuple-element.83), channel_id=1, source_target_pairs={{48,0},{56,8},{0,16},{8,24},{16,32},{24,40},{32,48},{40,56},{49,1}... | collective-permute-start | bytes 49160 | tf_op jit(solution)/shard_map/ppermute | solution.py:590
  68.9 1.5 %collective-permute-done.14.up2 = f32[32,128]{1,0:T(8,128)S(1)} collective-permute-done((f32[32,128]{1,0:T(8,128)S(1)}, f32[32,128]{1,0:T(8,128)S(1)}, u32[]{:S(2)}, u32[]{:S(2)}) %collective-permute-start.14) | collective-permute-done | bytes 16416 | tf_op jit(solution)/shard_map/ppermute | solution.py:590
  71.5 2.1 %shard_map.58 = (f32[16,16,128]{2,1,0:T(8,128)S(1)}, f32[16,16,128]{2,1,0:T(8,128)S(1)}, f32[24,128]{1,0:T(8,128)S(1)}, f32[16,128]{1,0:T(8,128)S(1)}, f32[16,128]{1,0:T(8,128)S(1)}) custom-call(f32[26,24,256]{2,1,0:T(8,128)S(1)} %get-tuple-element.80.x0, f32[12,24,256]{2,1,0:T(8,128)S(1)} %get-tuple-element.81.x1, f32[216,128]{1,0:T(8,128)S(1)} %get-tuple-element.77.own, ...), custom_call_target="tpu_custom_call" | custom-call | tf_op jit(solution)/shard_map/pallas_call | solution.py:665
  73.7 3.0 %collective-permute-start.17 = (f32[48,128]{1,0:T(8,128)S(1)}, f32[48,128]{1,0:T(8,128)S(1)}, u32[]{:S(2)}, u32[]{:S(2)}) collective-permute-start(f32[48,128]{1,0:T(8,128)S(1)} %concatenate.32), channel_id=1, source_target_pairs={{7,0},{0,1},{1,2},{2,3},{3,4},{4,5},{5,6},{6,7},{15,8},{8,9},{9,10... | collective-permute-start | bytes 73736 | tf_op jit(solution)/shard_map/ppermute | solution.py:590
  77.7 2.3 %collective-permute-done.16.above = f32[48,128]{1,0:T(8,128)S(1)} collective-permute-done((f32[48,128]{1,0:T(8,128)S(1)}, f32[48,128]{1,0:T(8,128)S(1)}, u32[]{:S(2)}, u32[]{:S(2)}) %collective-permute-start.16) | collective-permute-done | bytes 24608 | tf_op jit(solution)/shard_map/ppermute | solution.py:590
  80.9 2.3 %collective-permute-start.19 = (f32[144,128]{1,0:T(8,128)S(1)}, f32[144,128]{1,0:T(8,128)S(1)}, u32[]{:S(2)}, u32[]{:S(2)}) collective-permute-start(f32[144,128]{1,0:T(8,128)S(1)} %get-tuple-element.91), channel_id=1, source_target_pairs={{64,0},{128,64},{192,128},{0,192},{65,1},{129,65},{193,129},{1,193... | collective-permute-start | bytes 221192 | tf_op jit(solution)/shard_map/ppermute | solution.py:590
  84.3 3.0 %collective-permute-done.20.across = f32[32,128]{1,0:T(8,128)S(1)} collective-permute-done((f32[32,128]{1,0:T(8,128)S(1)}, f32[32,128]{1,0:T(8,128)S(1)}, u32[]{:S(2)}, u32[]{:S(2)}) %collective-permute-start.20) | collective-permute-done | bytes 16416 | tf_op jit(solution)/shard_map/ppermute | solution.py:590
  88.1 2.0 %collective-permute-start.21 = (f32[216,128]{1,0:T(8,128)S(1)}, f32[216,128]{1,0:T(8,128)S(1)}, u32[]{:S(2)}, u32[]{:S(2)}) collective-permute-start(f32[216,128]{1,0:T(8,128)S(1)} %get-tuple-element.93.own), channel_id=1, source_target_pairs={{8,0},{16,8},{24,16},{32,24},{40,32},{48,40},{56,48},{0,56},{9,1},... | collective-permute-start | bytes 331784 | tf_op jit(solution)/shard_map/ppermute | solution.py:590
  90.2 1.1 collective-permute-start.23
  91.3 1.2 collective-permute-start.24
  94.2 1.8 %collective-permute-done.24.down2 = f32[32,128]{1,0:T(8,128)S(1)} collective-permute-done((f32[32,128]{1,0:T(8,128)S(1)}, f32[32,128]{1,0:T(8,128)S(1)}, u32[]{:S(2)}, u32[]{:S(2)}) %collective-permute-start.24) | collective-permute-done | bytes 16416 | tf_op jit(solution)/shard_map/ppermute | solution.py:590
  96.0 1.7 %shard_map.62 = (f32[16,16,128]{2,1,0:T(8,128)S(1)}, f32[16,16,128]{2,1,0:T(8,128)S(1)}, f32[16,16,128]{2,1,0:T(8,128)S(1)}, f32[16,16,128]{2,1,0:T(8,128)S(1)},...) custom-call(f32[26,24,256]{2,1,0:T(8,128)S(1)} %get-tuple-element.95.x0, ...), custom_call_target="tpu_custom_call" | custom-call | tf_op jit(solution)/shard_map/pallas_call | solution.py:670
  97.8 23.4 %all_to_all.11 = f32[256,1,128]{2,1,0:T(1,128)S(1)} all-to-all(f32[256,1,128]{2,1,0:T(1,128)S(1)} %broadcast_in_dim.25), channel_id=1, replica_groups=mesh['gx'=4,'gy'=8,'gz'=8] {'gx','gy','gz'}, dimensions={0} | all-to-all | bytes 262144 | tf_op jit(solution)/shard_map/all_to_all | solution.py:626
  (62 shorter events, 12.7 us)
Async XLA Ops:
  2.6 4.2 %copy-start = (f32[2,16,16,128]{3,2,1,0:T(8,128)S(1)}, f32[2,16,16,128]{3,2,1,0:T(8,128)}, u32[]{:S(2)}) copy-start(f32[2,16,16,128]{3,2,1,0:T(8,128)} %get-tuple-element.55.both) | copy-start | bytes 786436
  2.6 5.2 %collective-permute-start = (f32[2,6,16,128]{3,2,1,0:T(8,128)}, f32[2,6,16,128]{3,2,1,0:T(8,128)S(1)}, u32[]{:S(2)}, u32[]{:S(2)}) collective-permute-start(f32[2,6,16,128]{3,2,1,0:T(8,128)} %get-tuple-element.56), channel_id=1, source_target_pairs={{1,0},{2,1},{3,2},{4,3},{5,4},{6,5},{7,6},{0,7},{9,8},{10,9},{11,1... | collective-permute-start | bytes 294920 | tf_op jit(solution)/shard_map/ppermute | solution.py:590
  5.8 2.0 %collective-permute-start.1 = (f32[2,6,16,128]{3,2,1,0:T(8,128)}, f32[2,6,16,128]{3,2,1,0:T(8,128)S(1)}, u32[]{:S(2)}, u32[]{:S(2)}) collective-permute-start(f32[2,6,16,128]{3,2,1,0:T(8,128)} %get-tuple-element.57), channel_id=1, source_target_pairs={{7,0},{0,1},{1,2},{2,3},{3,4},{4,5},{5,6},{6,7},{15,8},{8,9},{9,10... | collective-permute-start | bytes 294920 | tf_op jit(solution)/shard_map/ppermute | solution.py:590
  7.8 4.9 %collective-permute-start.2 = (f32[2,7,16,128]{3,2,1,0:T(8,128)S(1)}, f32[2,7,16,128]{3,2,1,0:T(8,128)S(1)}, u32[]{:S(2)}, u32[]{:S(2)}) collective-permute-start(f32[2,7,16,128]{3,2,1,0:T(8,128)S(1)} %pad_maximum_fusion), channel_id=1, source_target_pairs={{192,0},{0,64},{64,128},{128,192},{193,1},{1,65},{65,129},{129,193... | collective-permute-start | bytes 344072 | tf_op jit(solution)/shard_map/ppermute | solution.py:590
  9.1 3.7 %collective-permute-start.3 = (f32[2,7,16,128]{3,2,1,0:T(8,128)S(1)}, f32[2,7,16,128]{3,2,1,0:T(8,128)S(1)}, u32[]{:S(2)}, u32[]{:S(2)}) collective-permute-start(f32[2,7,16,128]{3,2,1,0:T(8,128)S(1)} %pad_maximum_fusion.1), channel_id=1, source_target_pairs={{64,0},{128,64},{192,128},{0,192},{65,1},{129,65},{193,129},{1,193... | collective-permute-start | bytes 344072 | tf_op jit(solution)/shard_map/ppermute | solution.py:590
  13.0 8.4 %collective-permute-start.4 = (f32[400,128]{1,0:T(8,128)S(1)}, f32[400,128]{1,0:T(8,128)S(1)}, u32[]{:S(2)}, u32[]{:S(2)}) collective-permute-start(f32[400,128]{1,0:T(8,128)S(1)} %get-tuple-element.58), channel_id=1, source_target_pairs={{8,0},{16,8},{24,16},{32,24},{40,32},{48,40},{56,48},{0,56},{9,1},... | collective-permute-start | bytes 614408 | tf_op jit(solution)/shard_map/ppermute | solution.py:590
  18.7 5.8 %collective-permute-start.5 = (f32[400,128]{1,0:T(8,128)S(1)}, f32[400,128]{1,0:T(8,128)S(1)}, u32[]{:S(2)}, u32[]{:S(2)}) collective-permute-start(f32[400,128]{1,0:T(8,128)S(1)} %get-tuple-element.59), channel_id=1, source_target_pairs={{56,0},{0,8},{8,16},{16,24},{24,32},{32,40},{40,48},{48,56},{57,1}... | collective-permute-start | bytes 614408 | tf_op jit(solution)/shard_map/ppermute | solution.py:590
  43.4 8.9 %collective-permute-start.7 = (f32[48,128]{1,0:T(8,128)S(1)}, f32[48,128]{1,0:T(8,128)S(1)}, u32[]{:S(2)}, u32[]{:S(2)}) collective-permute-start(f32[48,128]{1,0:T(8,128)S(1)} %get-tuple-element.117), channel_id=1, source_target_pairs={{7,0},{0,1},{1,2},{2,3},{3,4},{4,5},{5,6},{6,7},{15,8},{8,9},{9,10... | collective-permute-start | bytes 73736 | tf_op jit(solution)/shard_map/ppermute | solution.py:590
  49.8 3.3 %collective-permute-start.6 = (f32[48,128]{1,0:T(8,128)S(1)}, f32[48,128]{1,0:T(8,128)S(1)}, u32[]{:S(2)}, u32[]{:S(2)}) collective-permute-start(f32[48,128]{1,0:T(8,128)S(1)} %get-tuple-element.118), channel_id=1, source_target_pairs={{1,0},{2,1},{3,2},{4,3},{5,4},{6,5},{7,6},{0,7},{9,8},{10,9},{11,1... | collective-permute-start | bytes 73736 | tf_op jit(solution)/shard_map/ppermute | solution.py:590
  53.1 8.7 %collective-permute-start.8 = (f32[8,128]{1,0:T(8,128)S(1)}, f32[8,128]{1,0:T(8,128)S(1)}, u32[]{:S(2)}, u32[]{:S(2)}) collective-permute-start(f32[8,128]{1,0:T(8,128)S(1)} %slice.58), channel_id=1, source_target_pairs={{4,0},{5,1},{6,2},{7,3},{0,4},{1,5},{2,6},{3,7},{12,8},{13,9},{14,... | collective-permute-start | bytes 12296 | tf_op jit(solution)/shard_map/ppermute | solution.py:590
  57.8 4.1 %collective-permute-start.11 = (f32[32,128]{1,0:T(8,128)S(1)}, f32[32,128]{1,0:T(8,128)S(1)}, u32[]{:S(2)}, u32[]{:S(2)}) collective-permute-start(f32[32,128]{1,0:T(8,128)S(1)} %get-tuple-element.73.small), channel_id=1, source_target_pairs={{128,0},{192,64},{0,128},{64,192},{129,1},{193,65},{1,129},{65,193... | collective-permute-start | bytes 49160 | tf_op jit(solution)/shard_map/ppermute | solution.py:590
  59.1 4.5 %collective-permute-start.9 = (f32[144,128]{1,0:T(8,128)S(1)}, f32[144,128]{1,0:T(8,128)S(1)}, u32[]{:S(2)}, u32[]{:S(2)}) collective-permute-start(f32[144,128]{1,0:T(8,128)S(1)} %get-tuple-element.74), channel_id=1, source_target_pairs={{192,0},{0,64},{64,128},{128,192},{193,1},{1,65},{65,129},{129,193... | collective-permute-start | bytes 221192 | tf_op jit(solution)/shard_map/ppermute | solution.py:590
  59.5 4.2 %collective-permute-start.10 = (f32[144,128]{1,0:T(8,128)S(1)}, f32[144,128]{1,0:T(8,128)S(1)}, u32[]{:S(2)}, u32[]{:S(2)}) collective-permute-start(f32[144,128]{1,0:T(8,128)S(1)} %get-tuple-element.75), channel_id=1, source_target_pairs={{64,0},{128,64},{192,128},{0,192},{65,1},{129,65},{193,129},{1,193... | collective-permute-start | bytes 221192 | tf_op jit(solution)/shard_map/ppermute | solution.py:590
  63.7 6.6 %collective-permute-start.13 = (f32[216,128]{1,0:T(8,128)S(1)}, f32[216,128]{1,0:T(8,128)S(1)}, u32[]{:S(2)}, u32[]{:S(2)}) collective-permute-start(f32[216,128]{1,0:T(8,128)S(1)} %get-tuple-element.78), channel_id=1, source_target_pairs={{56,0},{0,8},{8,16},{16,24},{24,32},{32,40},{40,48},{48,56},{57,1}... | collective-permute-start | bytes 331784 | tf_op jit(solution)/shard_map/ppermute | solution.py:590
  65.2 5.1 %collective-permute-start.12 = (f32[216,128]{1,0:T(8,128)S(1)}, f32[216,128]{1,0:T(8,128)S(1)}, u32[]{:S(2)}, u32[]{:S(2)}) collective-permute-start(f32[216,128]{1,0:T(8,128)S(1)} %get-tuple-element.77.own), channel_id=1, source_target_pairs={{8,0},{16,8},{24,16},{32,24},{40,32},{48,40},{56,48},{0,56},{9,1},... | collective-permute-start | bytes 331784 | tf_op jit(solution)/shard_map/ppermute | solution.py:590
  66.5 3.8 %collective-permute-start.14 = (f32[32,128]{1,0:T(8,128)S(1)}, f32[32,128]{1,0:T(8,128)S(1)}, u32[]{:S(2)}, u32[]{:S(2)}) collective-permute-start(f32[32,128]{1,0:T(8,128)S(1)} %get-tuple-element.82), channel_id=1, source_target_pairs={{16,0},{24,8},{32,16},{40,24},{48,32},{56,40},{0,48},{8,56},{17,1}... | collective-permute-start | bytes 49160 | tf_op jit(solution)/shard_map/ppermute | solution.py:590
  66.8 4.7 %collective-permute-start.15 = (f32[32,128]{1,0:T(8,128)S(1)}, f32[32,128]{1,0:T(8,128)S(1)}, u32[]{:S(2)}, u32[]{:S(2)}) collective-permute-start(f32[32,128]{1,0:T(8,128)S(1)} %get-tuple-element.83), channel_id=1, source_target_pairs={{48,0},{56,8},{0,16},{8,24},{16,32},{24,40},{32,48},{40,56},{49,1}... | collective-permute-start | bytes 49160 | tf_op jit(solution)/shard_map/ppermute | solution.py:590
  73.7 4.0 %collective-permute-start.17 = (f32[48,128]{1,0:T(8,128)S(1)}, f32[48,128]{1,0:T(8,128)S(1)}, u32[]{:S(2)}, u32[]{:S(2)}) collective-permute-start(f32[48,128]{1,0:T(8,128)S(1)} %concatenate.32), channel_id=1, source_target_pairs={{7,0},{0,1},{1,2},{2,3},{3,4},{4,5},{5,6},{6,7},{15,8},{8,9},{9,10... | collective-permute-start | bytes 73736 | tf_op jit(solution)/shard_map/ppermute | solution.py:590
  76.7 3.3 %collective-permute-start.16 = (f32[48,128]{1,0:T(8,128)S(1)}, f32[48,128]{1,0:T(8,128)S(1)}, u32[]{:S(2)}, u32[]{:S(2)}) collective-permute-start(f32[48,128]{1,0:T(8,128)S(1)} %concatenate.31), channel_id=1, source_target_pairs={{1,0},{2,1},{3,2},{4,3},{5,4},{6,5},{7,6},{0,7},{9,8},{10,9},{11,1... | collective-permute-start | bytes 73736 | tf_op jit(solution)/shard_map/ppermute | solution.py:590
  80.0 7.3 %collective-permute-start.18 = (f32[144,128]{1,0:T(8,128)S(1)}, f32[144,128]{1,0:T(8,128)S(1)}, u32[]{:S(2)}, u32[]{:S(2)}) collective-permute-start(f32[144,128]{1,0:T(8,128)S(1)} %get-tuple-element.90), channel_id=1, source_target_pairs={{192,0},{0,64},{64,128},{128,192},{193,1},{1,65},{65,129},{129,193... | collective-permute-start | bytes 221192 | tf_op jit(solution)/shard_map/ppermute | solution.py:590
  80.9 6.4 %collective-permute-start.19 = (f32[144,128]{1,0:T(8,128)S(1)}, f32[144,128]{1,0:T(8,128)S(1)}, u32[]{:S(2)}, u32[]{:S(2)}) collective-permute-start(f32[144,128]{1,0:T(8,128)S(1)} %get-tuple-element.91), channel_id=1, source_target_pairs={{64,0},{128,64},{192,128},{0,192},{65,1},{129,65},{193,129},{1,193... | collective-permute-start | bytes 221192 | tf_op jit(solution)/shard_map/ppermute | solution.py:590
  83.2 4.1 %collective-permute-start.20 = (f32[32,128]{1,0:T(8,128)S(1)}, f32[32,128]{1,0:T(8,128)S(1)}, u32[]{:S(2)}, u32[]{:S(2)}) collective-permute-start(f32[32,128]{1,0:T(8,128)S(1)} %get-tuple-element.89.small), channel_id=1, source_target_pairs={{128,0},{192,64},{0,128},{64,192},{129,1},{193,65},{1,129},{65,193... | collective-permute-start | bytes 49160 | tf_op jit(solution)/shard_map/ppermute | solution.py:590
  87.4 5.1 %collective-permute-start.22 = (f32[216,128]{1,0:T(8,128)S(1)}, f32[216,128]{1,0:T(8,128)S(1)}, u32[]{:S(2)}, u32[]{:S(2)}) collective-permute-start(f32[216,128]{1,0:T(8,128)S(1)} %get-tuple-element.94), channel_id=1, source_target_pairs={{56,0},{0,8},{8,16},{16,24},{24,32},{32,40},{40,48},{48,56},{57,1}... | collective-permute-start | bytes 331784 | tf_op jit(solution)/shard_map/ppermute | solution.py:590
  88.1 4.4 %collective-permute-start.21 = (f32[216,128]{1,0:T(8,128)S(1)}, f32[216,128]{1,0:T(8,128)S(1)}, u32[]{:S(2)}, u32[]{:S(2)}) collective-permute-start(f32[216,128]{1,0:T(8,128)S(1)} %get-tuple-element.93.own), channel_id=1, source_target_pairs={{8,0},{16,8},{24,16},{32,24},{40,32},{48,40},{56,48},{0,56},{9,1},... | collective-permute-start | bytes 331784 | tf_op jit(solution)/shard_map/ppermute | solution.py:590
  90.2 4.0 %collective-permute-start.23 = (f32[32,128]{1,0:T(8,128)S(1)}, f32[32,128]{1,0:T(8,128)S(1)}, u32[]{:S(2)}, u32[]{:S(2)}) collective-permute-start(f32[32,128]{1,0:T(8,128)S(1)} %get-tuple-element.97), channel_id=1, source_target_pairs={{16,0},{24,8},{32,16},{40,24},{48,32},{56,40},{0,48},{8,56},{17,1}... | collective-permute-start | bytes 49160 | tf_op jit(solution)/shard_map/ppermute | solution.py:590
  91.3 4.7 %collective-permute-start.24 = (f32[32,128]{1,0:T(8,128)S(1)}, f32[32,128]{1,0:T(8,128)S(1)}, u32[]{:S(2)}, u32[]{:S(2)}) collective-permute-start(f32[32,128]{1,0:T(8,128)S(1)} %get-tuple-element.98), channel_id=1, source_target_pairs={{48,0},{56,8},{0,16},{8,24},{16,32},{24,40},{32,48},{40,56},{49,1}... | collective-permute-start | bytes 49160 | tf_op jit(solution)/shard_map/ppermute | solution.py:590

commit v10 on v9

--- a/solution.py
+++ b/solution.py
@@ -319,7 +319,8 @@
             share[pl.ds(12 + 6 * half + first, count)] = v
 
 
-def join_z_kernel(final, own, share, state, above, below, first, last, small):
+def join_z_kernel(final, own, low, above, below, first, last, small):
+    share, state = low[16:40], low[40:48]
     lane = iota((6, 128), 1)
     for s in (0, 12):
         main, side = pl.ds(16 + s, 6), pl.ds(22 + s, 6)
@@ -474,11 +475,17 @@
     return jnp.broadcast_to(jnp.sum(picked, axis=0, keepdims=True), (8, 128))
 
 
+def write_ends(w, weight0, weight1, low, high, *scratch):
+    pack_near(lambda k: w[k], low.at[pl.ds(0, 16)], high.at[pl.ds(0, 16)])
+    share_sweep(w, weight0, weight1, low.at[pl.ds(16, 24)], *scratch)
+    high[16:40] = low[16:40]
+
+
 def wide(row, k):
     return jnp.broadcast_to(row[:, MARK + k:MARK + k + 1], (16, 128))
 
 
-def first_up_kernel(gather, own0, halo0s, own1, halo1, x0, x1, both, weight2, u, w, share, low, high, dots, *scratch):
+def first_up_kernel(gather, own0, halo0s, own1, halo1, x0, x1, both, weight2, u, w, low, high, *scratch):
     (*scratch, full, y0, y1, z1, quads) = scratch
     weight0, weight1 = Joined(own0, halo0s), Joined(own1, halo1)
     row, lane = iota((16, 256), 0), iota((16, 256), 1)
@@ -492,9 +499,8 @@
         u[k] = v
         rz = rz + both[0, k] * v
         curve = curve + w[k] * v
-    dots[...] = lanes_of([rz, curve])
-    pack_near(lambda k: w[k], low, high)
-    share_sweep(w, weight0, weight1, share, y0, y1, z1, quads)
+    write_ends(w, weight0, weight1, low, high, y0, y1, z1, quads)
+    low[40:48] = high[40:48] = lanes_of([rz, curve])
 
 
 def near_kernel(body, up1, down1, own0, halo0, own1, halo1, x0, x1, r, tall, sides):
@@ -504,15 +510,20 @@
 
 
 def second_kernel(x0, x1, own, up1, down1, up2, down2, weight2, own0, halo0s, own1, halo1, both,
-                  m0, n0, share, low, high, *scratch):
+                  m0, n0, low, high, *scratch):
     weight0s, weight1 = Joined(own0, halo0s), Joined(own1, halo1)
     (full, *scratch, y0, y1, z1, quads) = scratch
     shares = (own, up1, down1, up2, down2)
     up_sweep(lambda *a: assemble_shares(*shares, *a), weight2, weight1, weight0s, x0, x1, both.at[1], full, n0, *scratch)
     for k in range(16):
         m0[k] = full[k + 5, :16, :128]
-    pack_near(lambda k: n0[k], low, high)
-    share_sweep(n0, weight0s, weight1, share, y0, y1, z1, quads)
+    write_ends(n0, weight0s, weight1, low, high, y0, y1, z1, quads)
+    ahead, behind = up1[208:210] + up2[24:26], down1[208:210] + own[208:210]
+    for ref in (low, high):
+        ref[40:42] = ahead + behind
+        ref[42:44] = ahead
+        ref[44:46] = behind
+        ref[46:48] = jnp.zeros((2, 128), F32)
 
 
 def third_kernel(x0, x1, own, up1, down1, up2, down2, weight2, own0, halo0s, own1, halo1, both, u0, w0, m0, n0,
@@ -600,12 +611,11 @@
     return body, shift(upper, "gy", 1), shift(lower, "gy", -1)
 
 
-def joint_exchange(own, share, low, high, state, final):
-    above = shift(jnp.concatenate([low, share, state]), "gz", 1)
-    below = shift(jnp.concatenate([high, share, state]), "gz", -1)
+def joint_exchange(own, low, high, final):
+    above, below = shift(low, "gz", 1), shift(high, "gz", -1)
     first, last, small = call(
-        functools.partial(join_z_kernel, final), [shape(144, 128), shape(144, 128), shape(32, 128)], count=5
-    )(own, share, state, above, below)
+        functools.partial(join_z_kernel, final), [shape(144, 128), shape(144, 128), shape(32, 128)], count=4
+    )(own, low, above, below)
     before, after, across = shift(last, "gx", -1), shift(first, "gx", 1), shift(small, "gx", 2)
     state = small[24:] if final else small[24:] + shift(small[24:], "gz", 4)
     body, upper, lower, ahead, behind = call(
@@ -647,10 +657,10 @@
         first_down_kernel, [shape(SLABS, 16, 256), shape(SLABS, 8, 256), shape(MIDS, 8, 256), short, mids, tile],
         scratch(SHORT, HALO, MID, (2, 4, 16, 128), (16 * UNITS, 128)), count=5,
     )(*halos, own0, own1)
-    share_outs = [shape(24, 128), shape(16, 128), shape(16, 128)]
+    ends = [shape(48, 128), shape(48, 128)]
     share_scratch = scratch(BLOCK, (10, 24, 256), (10, 24, 256), (2, 6, 24, 128))
-    weight2, u0, w0, share, low, high, dots = call(
-        first_up_kernel, [shape(4, 16, 256), block, block, *share_outs, tile], up_scratch + share_scratch, count=8
+    weight2, u0, w0, low, high = call(
+        first_up_kernel, [shape(4, 16, 256), block, block, *ends], up_scratch + share_scratch, count=8
     )(gather(jnp.stack([unit, unit2])), own0, halo0s, own1, halo1, x0, x1, both)
 
     def near(body, up1, down1):
@@ -658,14 +668,12 @@
             body, up1, down1, own0, halo0, own1, halo1
         )
 
-    body, own, up1, down1, up2, down2 = joint_exchange(w0, share, low, high, dots, False)
+    body, own, up1, down1, up2, down2 = joint_exchange(w0, low, high, False)
     x0, x1 = near(body, up1, down1)
-    ahead, behind = up1[208:210] + up2[24:26], down1[208:210] + own[208:210]
-    state = jnp.concatenate([ahead + behind, ahead, behind, jnp.zeros((2, 128), F32)])
-    m0, n0, share, low, high = call(
-        second_kernel, [block, block, *share_outs], scratch(SHORT) + up_scratch[:-1] + share_scratch, count=13
+    m0, n0, low, high = call(
+        second_kernel, [block, block, *ends], scratch(SHORT) + up_scratch[:-1] + share_scratch, count=13
     )(x0, x1, own, up1, down1, up2, down2, weight2, own0, halo0s, own1, halo1, both)
-    body, own, up1, down1, up2, down2 = joint_exchange(n0, share, low, high, state, True)
+    body, own, up1, down1, up2, down2 = joint_exchange(n0, low, high, True)
     x0, x1 = near(body, up1, down1)
     r1, u1, w1, m1, n1, first, dots = call(
         third_kernel, [block] * 5 + [tile, tile], scratch(SHORT, BLOCK) + up_scratch[:-1], count=17

time: 123 us -> 123 us (level)
  no operation moved by 1% of the time
where the time goes in v10:
time: 123 us; the launch traced here: 122 us
  starting transfers between devices  46.3 us (38%)
  blocking collectives  39.2 us (32%)
  waiting for transfers between devices  21.2 us (17%)
  Pallas kernels  13.5 us (11%)
    ppermute x25, starting transfers between devices, shift(): lax.ppermute(v, axis, [((i + distance) % count, i) for i in range(count)])  46.3 us
    all_to_all x1, blocking collectives, total(): lax.all_to_all(jnp.broadcast_to(v[None, :1], (count, 1, 128)), axes, 0, 0...  24.2 us
    ppermute x25, waiting for transfers between devices, shift(): lax.ppermute(v, axis, [((i + distance) % count, i) for i in range(count)])  21.2 us
    all_to_all x1, blocking collectives, gather(): lax.all_to_all(jnp.broadcast_to(unit[None], (count,) + unit.shape), ('gx'...  14.9 us
  transfers between devices with their start and end apart: 25, of which 16 were waited for; matrix products, arithmetic and copies ran while one was open for 1% of the time, Pallas kernels for 2%

profile of v10, /device:TPU:1, one launch (start us, length us, event | category | flops | bytes accessed | tf_op | source)
XLA Modules:
  0.0 122.4 jit_solution(1620484293868584787)
XLA Ops:
  0.6 1.9 %shard_map.50 = (f32[2,16,16,128]{3,2,1,0:T(8,128)}, f32[2,6,16,128]{3,2,1,0:T(8,128)}, f32[2,6,16,128]{3,2,1,0:T(8,128)}) custom-call(f32[16,16,128]{2,1,0:T(8,128)} %rhs_in.1, s32[16,16,128]{2,1,0:T(8,128)} %classes_in.1, f32[16]{0:T(128)} %table_in.1), custom_call_target="tpu_custom_call" | custom-call | tf_op jit(solution)/shard_map/pallas_call | solution.py:647
  2.6 3.3 %collective-permute-start = (f32[2,6,16,128]{3,2,1,0:T(8,128)}, f32[2,6,16,128]{3,2,1,0:T(8,128)S(1)}, u32[]{:S(2)}, u32[]{:S(2)}) collective-permute-start(f32[2,6,16,128]{3,2,1,0:T(8,128)} %get-tuple-element.53), channel_id=1, source_target_pairs={{1,0},{2,1},{3,2},{4,3},{5,4},{6,5},{7,6},{0,7},{9,8},{10,9},{11,1... | collective-permute-start | bytes 294920 | tf_op jit(solution)/shard_map/ppermute | solution.py:601
  7.8 1.3 %collective-permute-start.2 = (f32[2,7,16,128]{3,2,1,0:T(8,128)S(1)}, f32[2,7,16,128]{3,2,1,0:T(8,128)S(1)}, u32[]{:S(2)}, u32[]{:S(2)}) collective-permute-start(f32[2,7,16,128]{3,2,1,0:T(8,128)S(1)} %pad_maximum_fusion), channel_id=1, source_target_pairs={{192,0},{0,64},{64,128},{128,192},{193,1},{1,65},{65,129},{129,193... | collective-permute-start | bytes 344072 | tf_op jit(solution)/shard_map/ppermute | solution.py:601
  9.1 1.5 %collective-permute-start.3 = (f32[2,7,16,128]{3,2,1,0:T(8,128)S(1)}, f32[2,7,16,128]{3,2,1,0:T(8,128)S(1)}, u32[]{:S(2)}, u32[]{:S(2)}) collective-permute-start(f32[2,7,16,128]{3,2,1,0:T(8,128)S(1)} %pad_maximum_fusion.1), channel_id=1, source_target_pairs={{64,0},{128,64},{192,128},{0,192},{65,1},{129,65},{193,129},{1,193... | collective-permute-start | bytes 344072 | tf_op jit(solution)/shard_map/ppermute | solution.py:601
  10.7 2.1 %collective-permute-done.2 = f32[2,7,16,128]{3,2,1,0:T(8,128)S(1)} collective-permute-done((f32[2,7,16,128]{3,2,1,0:T(8,128)S(1)}, f32[2,7,16,128]{3,2,1,0:T(8,128)S(1)}, u32[]{:S(2)}, u32[]{:S(2)}) %collective-permute-start.2) | collective-permute-done | bytes 114720 | tf_op jit(solution)/shard_map/ppermute | solution.py:601
  13.0 5.7 %collective-permute-start.4 = (f32[400,128]{1,0:T(8,128)S(1)}, f32[400,128]{1,0:T(8,128)S(1)}, u32[]{:S(2)}, u32[]{:S(2)}) collective-permute-start(f32[400,128]{1,0:T(8,128)S(1)} %get-tuple-element.55), channel_id=1, source_target_pairs={{8,0},{16,8},{24,16},{32,24},{40,32},{48,40},{56,48},{0,56},{9,1},... | collective-permute-start | bytes 614408 | tf_op jit(solution)/shard_map/ppermute | solution.py:601
  19.2 2.2 %collective-permute-done.4.upper = f32[400,128]{1,0:T(8,128)S(1)} collective-permute-done((f32[400,128]{1,0:T(8,128)S(1)}, f32[400,128]{1,0:T(8,128)S(1)}, u32[]{:S(2)}, u32[]{:S(2)}) %collective-permute-start.4) | collective-permute-done | bytes 204832 | tf_op jit(solution)/shard_map/ppermute | solution.py:601
  21.4 3.1 %collective-permute-done.5.lower = f32[400,128]{1,0:T(8,128)S(1)} collective-permute-done((f32[400,128]{1,0:T(8,128)S(1)}, f32[400,128]{1,0:T(8,128)S(1)}, u32[]{:S(2)}, u32[]{:S(2)}) %collective-permute-start.5) | collective-permute-done | bytes 204832 | tf_op jit(solution)/shard_map/ppermute | solution.py:601
  24.5 1.8 %shard_map.53 = (f32[26,16,256]{2,1,0:T(8,128)S(1)}, f32[26,8,256]{2,1,0:T(8,128)S(1)}, f32[12,8,256]{2,1,0:T(8,128)S(1)}, f32[26,24,256]{2,1,0:T(8,128)S(1)}, f...) custom-call(f32[1280,128]{1,0:T(8,128)S(1)} %bitcast.8, f32[400,128]{1,0:T(8,128)S(1)} %collective-permute-done.4.upper, ...), custom_call_target="tpu_custom_call" | custom-call | tf_op jit(solution)/shard_map/pallas_call | solution.py:656
  26.3 14.9 %all_to_all.10.gather = f32[32,2,8,128]{3,2,1,0:T(8,128)S(1)} all-to-all(f32[32,2,8,128]{3,2,1,0:T(8,128)S(1)} %broadcast_in_dim.8), channel_id=1, replica_groups=mesh['gx'=4,'gy'=8,'gz'=8] {'gx','gy'}, dimensions={0} | all-to-all | bytes 524288 | tf_op jit(solution)/shard_map/all_to_all | solution.py:630
  41.2 2.1 %shard_map.54 = (f32[4,16,256]{2,1,0:T(8,128)S(1)}, f32[16,16,128]{2,1,0:T(8,128)S(1)}, f32[16,16,128]{2,1,0:T(8,128)S(1)}, f32[48,128]{1,0:T(8,128)S(1)}, f32[48,128]{1,0:T(8,128)S(1)}) custom-call(f32[32,2,8,128]{3,2,1,0:T(8,128)S(1)} %all_to_all.10.gather, f32[26,16,256]{2,1,0:T(8,128)S(1)} %get-tuple-element.57.own0, ...), custom_call_target="tpu_custom_call" | custom-call | tf_op jit(solution)/shard_map/pallas_call | solution.py:662
  43.4 6.4 %collective-permute-start.7 = (f32[48,128]{1,0:T(8,128)S(1)}, f32[48,128]{1,0:T(8,128)S(1)}, u32[]{:S(2)}, u32[]{:S(2)}) collective-permute-start(f32[48,128]{1,0:T(8,128)S(1)} %get-tuple-element.67), channel_id=1, source_target_pairs={{7,0},{0,1},{1,2},{2,3},{3,4},{4,5},{5,6},{6,7},{15,8},{8,9},{9,10... | collective-permute-start | bytes 73736 | tf_op jit(solution)/shard_map/ppermute | solution.py:601
  49.8 1.8 %collective-permute-start.6 = (f32[48,128]{1,0:T(8,128)S(1)}, f32[48,128]{1,0:T(8,128)S(1)}, u32[]{:S(2)}, u32[]{:S(2)}) collective-permute-start(f32[48,128]{1,0:T(8,128)S(1)} %get-tuple-element.66.low), channel_id=1, source_target_pairs={{1,0},{2,1},{3,2},{4,3},{5,4},{6,5},{7,6},{0,7},{9,8},{10,9},{11,1... | collective-permute-start | bytes 73736 | tf_op jit(solution)/shard_map/ppermute | solution.py:601
  53.1 4.7 %collective-permute-start.8 = (f32[8,128]{1,0:T(8,128)S(1)}, f32[8,128]{1,0:T(8,128)S(1)}, u32[]{:S(2)}, u32[]{:S(2)}) collective-permute-start(f32[8,128]{1,0:T(8,128)S(1)} %slice.46), channel_id=1, source_target_pairs={{4,0},{5,1},{6,2},{7,3},{0,4},{1,5},{2,6},{3,7},{12,8},{13,9},{14,... | collective-permute-start | bytes 12296 | tf_op jit(solution)/shard_map/ppermute | solution.py:601
  57.8 1.3 %collective-permute-start.11 = (f32[32,128]{1,0:T(8,128)S(1)}, f32[32,128]{1,0:T(8,128)S(1)}, u32[]{:S(2)}, u32[]{:S(2)}) collective-permute-start(f32[32,128]{1,0:T(8,128)S(1)} %get-tuple-element.68.small), channel_id=1, source_target_pairs={{128,0},{192,64},{0,128},{64,192},{129,1},{193,65},{1,129},{65,193... | collective-permute-start | bytes 49160 | tf_op jit(solution)/shard_map/ppermute | solution.py:601
  59.4 2.4 %collective-permute-start.10 = (f32[144,128]{1,0:T(8,128)S(1)}, f32[144,128]{1,0:T(8,128)S(1)}, u32[]{:S(2)}, u32[]{:S(2)}) collective-permute-start(f32[144,128]{1,0:T(8,128)S(1)} %get-tuple-element.70), channel_id=1, source_target_pairs={{64,0},{128,64},{192,128},{0,192},{65,1},{129,65},{193,129},{1,193... | collective-permute-start | bytes 221192 | tf_op jit(solution)/shard_map/ppermute | solution.py:601
  61.9 1.7 %collective-permute-done.9.before = f32[144,128]{1,0:T(8,128)S(1)} collective-permute-done((f32[144,128]{1,0:T(8,128)S(1)}, f32[144,128]{1,0:T(8,128)S(1)}, u32[]{:S(2)}, u32[]{:S(2)}) %collective-permute-start.9) | collective-permute-done | bytes 73760 | tf_op jit(solution)/shard_map/ppermute | solution.py:601
  63.7 1.5 %collective-permute-start.13 = (f32[216,128]{1,0:T(8,128)S(1)}, f32[216,128]{1,0:T(8,128)S(1)}, u32[]{:S(2)}, u32[]{:S(2)}) collective-permute-start(f32[216,128]{1,0:T(8,128)S(1)} %get-tuple-element.73), channel_id=1, source_target_pairs={{56,0},{0,8},{8,16},{16,24},{24,32},{32,40},{40,48},{48,56},{57,1}... | collective-permute-start | bytes 331784 | tf_op jit(solution)/shard_map/ppermute | solution.py:601
  65.2 1.3 %collective-permute-start.12 = (f32[216,128]{1,0:T(8,128)S(1)}, f32[216,128]{1,0:T(8,128)S(1)}, u32[]{:S(2)}, u32[]{:S(2)}) collective-permute-start(f32[216,128]{1,0:T(8,128)S(1)} %get-tuple-element.72.own), channel_id=1, source_target_pairs={{8,0},{16,8},{24,16},{32,24},{40,32},{48,40},{56,48},{0,56},{9,1},... | collective-permute-start | bytes 331784 | tf_op jit(solution)/shard_map/ppermute | solution.py:601
  66.8 2.1 %collective-permute-start.15 = (f32[32,128]{1,0:T(8,128)S(1)}, f32[32,128]{1,0:T(8,128)S(1)}, u32[]{:S(2)}, u32[]{:S(2)}) collective-permute-start(f32[32,128]{1,0:T(8,128)S(1)} %get-tuple-element.78), channel_id=1, source_target_pairs={{48,0},{56,8},{0,16},{8,24},{16,32},{24,40},{32,48},{40,56},{49,1}... | collective-permute-start | bytes 49160 | tf_op jit(solution)/shard_map/ppermute | solution.py:601
  69.7 1.0 shard_map.57
  71.5 2.2 %shard_map.58 = (f32[16,16,128]{2,1,0:T(8,128)S(1)}, f32[16,16,128]{2,1,0:T(8,128)S(1)}, f32[48,128]{1,0:T(8,128)S(1)}, f32[48,128]{1,0:T(8,128)S(1)}) custom-call(f32[26,24,256]{2,1,0:T(8,128)S(1)} %get-tuple-element.75.x0, f32[12,24,256]{2,1,0:T(8,128)S(1)} %get-tuple-element.76.x1, f32[216,128]{1,0:T(8,128)S(1)} %get-tuple-element.72.own, ...), custom_call_target="tpu_custom_call" | custom-call | tf_op jit(solution)/shard_map/pallas_call | solution.py:673
  73.7 3.0 %collective-permute-start.17 = (f32[48,128]{1,0:T(8,128)S(1)}, f32[48,128]{1,0:T(8,128)S(1)}, u32[]{:S(2)}, u32[]{:S(2)}) collective-permute-start(f32[48,128]{1,0:T(8,128)S(1)} %get-tuple-element.82), channel_id=1, source_target_pairs={{7,0},{0,1},{1,2},{2,3},{3,4},{4,5},{5,6},{6,7},{15,8},{8,9},{9,10... | collective-permute-start | bytes 73736 | tf_op jit(solution)/shard_map/ppermute | solution.py:601
  77.7 2.3 %collective-permute-done.16.above = f32[48,128]{1,0:T(8,128)S(1)} collective-permute-done((f32[48,128]{1,0:T(8,128)S(1)}, f32[48,128]{1,0:T(8,128)S(1)}, u32[]{:S(2)}, u32[]{:S(2)}) %collective-permute-start.16) | collective-permute-done | bytes 24608 | tf_op jit(solution)/shard_map/ppermute | solution.py:601
  80.9 2.3 %collective-permute-start.19 = (f32[144,128]{1,0:T(8,128)S(1)}, f32[144,128]{1,0:T(8,128)S(1)}, u32[]{:S(2)}, u32[]{:S(2)}) collective-permute-start(f32[144,128]{1,0:T(8,128)S(1)} %get-tuple-element.85), channel_id=1, source_target_pairs={{64,0},{128,64},{192,128},{0,192},{65,1},{129,65},{193,129},{1,193... | collective-permute-start | bytes 221192 | tf_op jit(solution)/shard_map/ppermute | solution.py:601
  83.2 1.1 collective-permute-start.20
  84.3 3.0 %collective-permute-done.20.across = f32[32,128]{1,0:T(8,128)S(1)} collective-permute-done((f32[32,128]{1,0:T(8,128)S(1)}, f32[32,128]{1,0:T(8,128)S(1)}, u32[]{:S(2)}, u32[]{:S(2)}) %collective-permute-start.20) | collective-permute-done | bytes 16416 | tf_op jit(solution)/shard_map/ppermute | solution.py:601
  88.1 2.0 %collective-permute-start.21 = (f32[216,128]{1,0:T(8,128)S(1)}, f32[216,128]{1,0:T(8,128)S(1)}, u32[]{:S(2)}, u32[]{:S(2)}) collective-permute-start(f32[216,128]{1,0:T(8,128)S(1)} %get-tuple-element.87.own), channel_id=1, source_target_pairs={{8,0},{16,8},{24,16},{32,24},{40,32},{48,40},{56,48},{0,56},{9,1},... | collective-permute-start | bytes 331784 | tf_op jit(solution)/shard_map/ppermute | solution.py:601
  90.4 2.1 %collective-permute-start.24 = (f32[32,128]{1,0:T(8,128)S(1)}, f32[32,128]{1,0:T(8,128)S(1)}, u32[]{:S(2)}, u32[]{:S(2)}) collective-permute-start(f32[32,128]{1,0:T(8,128)S(1)} %get-tuple-element.92), channel_id=1, source_target_pairs={{48,0},{56,8},{0,16},{8,24},{16,32},{24,40},{32,48},{40,56},{49,1}... | collective-permute-start | bytes 49160 | tf_op jit(solution)/shard_map/ppermute | solution.py:601
  92.5 1.0 shard_map.61
  95.2 1.7 %shard_map.62 = (f32[16,16,128]{2,1,0:T(8,128)S(1)}, f32[16,16,128]{2,1,0:T(8,128)S(1)}, f32[16,16,128]{2,1,0:T(8,128)S(1)}, f32[16,16,128]{2,1,0:T(8,128)S(1)},...) custom-call(f32[26,24,256]{2,1,0:T(8,128)S(1)} %get-tuple-element.89.x0, ...), custom_call_target="tpu_custom_call" | custom-call | tf_op jit(solution)/shard_map/pallas_call | solution.py:678
  97.0 24.2 %all_to_all.11 = f32[256,1,128]{2,1,0:T(1,128)S(1)} all-to-all(f32[256,1,128]{2,1,0:T(1,128)S(1)} %broadcast_in_dim.10), channel_id=1, replica_groups=mesh['gx'=4,'gy'=8,'gz'=8] {'gx','gy','gz'}, dimensions={0} | all-to-all | bytes 262144 | tf_op jit(solution)/shard_map/all_to_all | solution.py:636
  (56 shorter events, 12.3 us)
Async XLA Ops:
  2.6 4.2 %copy-start = (f32[2,16,16,128]{3,2,1,0:T(8,128)S(1)}, f32[2,16,16,128]{3,2,1,0:T(8,128)}, u32[]{:S(2)}) copy-start(f32[2,16,16,128]{3,2,1,0:T(8,128)} %get-tuple-element.52.both) | copy-start | bytes 786436
  2.6 5.2 %collective-permute-start = (f32[2,6,16,128]{3,2,1,0:T(8,128)}, f32[2,6,16,128]{3,2,1,0:T(8,128)S(1)}, u32[]{:S(2)}, u32[]{:S(2)}) collective-permute-start(f32[2,6,16,128]{3,2,1,0:T(8,128)} %get-tuple-element.53), channel_id=1, source_target_pairs={{1,0},{2,1},{3,2},{4,3},{5,4},{6,5},{7,6},{0,7},{9,8},{10,9},{11,1... | collective-permute-start | bytes 294920 | tf_op jit(solution)/shard_map/ppermute | solution.py:601
  5.8 2.0 %collective-permute-start.1 = (f32[2,6,16,128]{3,2,1,0:T(8,128)}, f32[2,6,16,128]{3,2,1,0:T(8,128)S(1)}, u32[]{:S(2)}, u32[]{:S(2)}) collective-permute-start(f32[2,6,16,128]{3,2,1,0:T(8,128)} %get-tuple-element.54), channel_id=1, source_target_pairs={{7,0},{0,1},{1,2},{2,3},{3,4},{4,5},{5,6},{6,7},{15,8},{8,9},{9,10... | collective-permute-start | bytes 294920 | tf_op jit(solution)/shard_map/ppermute | solution.py:601
  7.8 4.9 %collective-permute-start.2 = (f32[2,7,16,128]{3,2,1,0:T(8,128)S(1)}, f32[2,7,16,128]{3,2,1,0:T(8,128)S(1)}, u32[]{:S(2)}, u32[]{:S(2)}) collective-permute-start(f32[2,7,16,128]{3,2,1,0:T(8,128)S(1)} %pad_maximum_fusion), channel_id=1, source_target_pairs={{192,0},{0,64},{64,128},{128,192},{193,1},{1,65},{65,129},{129,193... | collective-permute-start | bytes 344072 | tf_op jit(solution)/shard_map/ppermute | solution.py:601
  9.1 3.7 %collective-permute-start.3 = (f32[2,7,16,128]{3,2,1,0:T(8,128)S(1)}, f32[2,7,16,128]{3,2,1,0:T(8,128)S(1)}, u32[]{:S(2)}, u32[]{:S(2)}) collective-permute-start(f32[2,7,16,128]{3,2,1,0:T(8,128)S(1)} %pad_maximum_fusion.1), channel_id=1, source_target_pairs={{64,0},{128,64},{192,128},{0,192},{65,1},{129,65},{193,129},{1,193... | collective-permute-start | bytes 344072 | tf_op jit(solution)/shard_map/ppermute | solution.py:601
  13.0 8.4 %collective-permute-start.4 = (f32[400,128]{1,0:T(8,128)S(1)}, f32[400,128]{1,0:T(8,128)S(1)}, u32[]{:S(2)}, u32[]{:S(2)}) collective-permute-start(f32[400,128]{1,0:T(8,128)S(1)} %get-tuple-element.55), channel_id=1, source_target_pairs={{8,0},{16,8},{24,16},{32,24},{40,32},{48,40},{56,48},{0,56},{9,1},... | collective-permute-start | bytes 614408 | tf_op jit(solution)/shard_map/ppermute | solution.py:601
  18.7 5.8 %collective-permute-start.5 = (f32[400,128]{1,0:T(8,128)S(1)}, f32[400,128]{1,0:T(8,128)S(1)}, u32[]{:S(2)}, u32[]{:S(2)}) collective-permute-start(f32[400,128]{1,0:T(8,128)S(1)} %get-tuple-element.56), channel_id=1, source_target_pairs={{56,0},{0,8},{8,16},{16,24},{24,32},{32,40},{40,48},{48,56},{57,1}... | collective-permute-start | bytes 614408 | tf_op jit(solution)/shard_map/ppermute | solution.py:601
  43.4 8.9 %collective-permute-start.7 = (f32[48,128]{1,0:T(8,128)S(1)}, f32[48,128]{1,0:T(8,128)S(1)}, u32[]{:S(2)}, u32[]{:S(2)}) collective-permute-start(f32[48,128]{1,0:T(8,128)S(1)} %get-tuple-element.67), channel_id=1, source_target_pairs={{7,0},{0,1},{1,2},{2,3},{3,4},{4,5},{5,6},{6,7},{15,8},{8,9},{9,10... | collective-permute-start | bytes 73736 | tf_op jit(solution)/shard_map/ppermute | solution.py:601
  49.8 3.3 %collective-permute-start.6 = (f32[48,128]{1,0:T(8,128)S(1)}, f32[48,128]{1,0:T(8,128)S(1)}, u32[]{:S(2)}, u32[]{:S(2)}) collective-permute-start(f32[48,128]{1,0:T(8,128)S(1)} %get-tuple-element.66.low), channel_id=1, source_target_pairs={{1,0},{2,1},{3,2},{4,3},{5,4},{6,5},{7,6},{0,7},{9,8},{10,9},{11,1... | collective-permute-start | bytes 73736 | tf_op jit(solution)/shard_map/ppermute | solution.py:601
  53.1 8.7 %collective-permute-start.8 = (f32[8,128]{1,0:T(8,128)S(1)}, f32[8,128]{1,0:T(8,128)S(1)}, u32[]{:S(2)}, u32[]{:S(2)}) collective-permute-start(f32[8,128]{1,0:T(8,128)S(1)} %slice.46), channel_id=1, source_target_pairs={{4,0},{5,1},{6,2},{7,3},{0,4},{1,5},{2,6},{3,7},{12,8},{13,9},{14,... | collective-permute-start | bytes 12296 | tf_op jit(solution)/shard_map/ppermute | solution.py:601
  57.8 4.1 %collective-permute-start.11 = (f32[32,128]{1,0:T(8,128)S(1)}, f32[32,128]{1,0:T(8,128)S(1)}, u32[]{:S(2)}, u32[]{:S(2)}) collective-permute-start(f32[32,128]{1,0:T(8,128)S(1)} %get-tuple-element.68.small), channel_id=1, source_target_pairs={{128,0},{192,64},{0,128},{64,192},{129,1},{193,65},{1,129},{65,193... | collective-permute-start | bytes 49160 | tf_op jit(solution)/shard_map/ppermute | solution.py:601
  59.1 4.5 %collective-permute-start.9 = (f32[144,128]{1,0:T(8,128)S(1)}, f32[144,128]{1,0:T(8,128)S(1)}, u32[]{:S(2)}, u32[]{:S(2)}) collective-permute-start(f32[144,128]{1,0:T(8,128)S(1)} %get-tuple-element.69), channel_id=1, source_target_pairs={{192,0},{0,64},{64,128},{128,192},{193,1},{1,65},{65,129},{129,193... | collective-permute-start | bytes 221192 | tf_op jit(solution)/shard_map/ppermute | solution.py:601
  59.4 4.2 %collective-permute-start.10 = (f32[144,128]{1,0:T(8,128)S(1)}, f32[144,128]{1,0:T(8,128)S(1)}, u32[]{:S(2)}, u32[]{:S(2)}) collective-permute-start(f32[144,128]{1,0:T(8,128)S(1)} %get-tuple-element.70), channel_id=1, source_target_pairs={{64,0},{128,64},{192,128},{0,192},{65,1},{129,65},{193,129},{1,193... | collective-permute-start | bytes 221192 | tf_op jit(solution)/shard_map/ppermute | solution.py:601
  63.7 5.9 %collective-permute-start.13 = (f32[216,128]{1,0:T(8,128)S(1)}, f32[216,128]{1,0:T(8,128)S(1)}, u32[]{:S(2)}, u32[]{:S(2)}) collective-permute-start(f32[216,128]{1,0:T(8,128)S(1)} %get-tuple-element.73), channel_id=1, source_target_pairs={{56,0},{0,8},{8,16},{16,24},{24,32},{32,40},{40,48},{48,56},{57,1}... | collective-permute-start | bytes 331784 | tf_op jit(solution)/shard_map/ppermute | solution.py:601
  65.2 4.5 %collective-permute-start.12 = (f32[216,128]{1,0:T(8,128)S(1)}, f32[216,128]{1,0:T(8,128)S(1)}, u32[]{:S(2)}, u32[]{:S(2)}) collective-permute-start(f32[216,128]{1,0:T(8,128)S(1)} %get-tuple-element.72.own), channel_id=1, source_target_pairs={{8,0},{16,8},{24,16},{32,24},{40,32},{48,40},{56,48},{0,56},{9,1},... | collective-permute-start | bytes 331784 | tf_op jit(solution)/shard_map/ppermute | solution.py:601
  66.5 4.2 %collective-permute-start.14 = (f32[32,128]{1,0:T(8,128)S(1)}, f32[32,128]{1,0:T(8,128)S(1)}, u32[]{:S(2)}, u32[]{:S(2)}) collective-permute-start(f32[32,128]{1,0:T(8,128)S(1)} %get-tuple-element.77), channel_id=1, source_target_pairs={{16,0},{24,8},{32,16},{40,24},{48,32},{56,40},{0,48},{8,56},{17,1}... | collective-permute-start | bytes 49160 | tf_op jit(solution)/shard_map/ppermute | solution.py:601
  66.8 4.7 %collective-permute-start.15 = (f32[32,128]{1,0:T(8,128)S(1)}, f32[32,128]{1,0:T(8,128)S(1)}, u32[]{:S(2)}, u32[]{:S(2)}) collective-permute-start(f32[32,128]{1,0:T(8,128)S(1)} %get-tuple-element.78), channel_id=1, source_target_pairs={{48,0},{56,8},{0,16},{8,24},{16,32},{24,40},{32,48},{40,56},{49,1}... | collective-permute-start | bytes 49160 | tf_op jit(solution)/shard_map/ppermute | solution.py:601
  73.7 4.0 %collective-permute-start.17 = (f32[48,128]{1,0:T(8,128)S(1)}, f32[48,128]{1,0:T(8,128)S(1)}, u32[]{:S(2)}, u32[]{:S(2)}) collective-permute-start(f32[48,128]{1,0:T(8,128)S(1)} %get-tuple-element.82), channel_id=1, source_target_pairs={{7,0},{0,1},{1,2},{2,3},{3,4},{4,5},{5,6},{6,7},{15,8},{8,9},{9,10... | collective-permute-start | bytes 73736 | tf_op jit(solution)/shard_map/ppermute | solution.py:601
  76.7 3.3 %collective-permute-start.16 = (f32[48,128]{1,0:T(8,128)S(1)}, f32[48,128]{1,0:T(8,128)S(1)}, u32[]{:S(2)}, u32[]{:S(2)}) collective-permute-start(f32[48,128]{1,0:T(8,128)S(1)} %get-tuple-element.81.low), channel_id=1, source_target_pairs={{1,0},{2,1},{3,2},{4,3},{5,4},{6,5},{7,6},{0,7},{9,8},{10,9},{11,1... | collective-permute-start | bytes 73736 | tf_op jit(solution)/shard_map/ppermute | solution.py:601
  80.0 7.3 %collective-permute-start.18 = (f32[144,128]{1,0:T(8,128)S(1)}, f32[144,128]{1,0:T(8,128)S(1)}, u32[]{:S(2)}, u32[]{:S(2)}) collective-permute-start(f32[144,128]{1,0:T(8,128)S(1)} %get-tuple-element.84), channel_id=1, source_target_pairs={{192,0},{0,64},{64,128},{128,192},{193,1},{1,65},{65,129},{129,193... | collective-permute-start | bytes 221192 | tf_op jit(solution)/shard_map/ppermute | solution.py:601
  80.9 6.4 %collective-permute-start.19 = (f32[144,128]{1,0:T(8,128)S(1)}, f32[144,128]{1,0:T(8,128)S(1)}, u32[]{:S(2)}, u32[]{:S(2)}) collective-permute-start(f32[144,128]{1,0:T(8,128)S(1)} %get-tuple-element.85), channel_id=1, source_target_pairs={{64,0},{128,64},{192,128},{0,192},{65,1},{129,65},{193,129},{1,193... | collective-permute-start | bytes 221192 | tf_op jit(solution)/shard_map/ppermute | solution.py:601
  83.2 4.1 %collective-permute-start.20 = (f32[32,128]{1,0:T(8,128)S(1)}, f32[32,128]{1,0:T(8,128)S(1)}, u32[]{:S(2)}, u32[]{:S(2)}) collective-permute-start(f32[32,128]{1,0:T(8,128)S(1)} %get-tuple-element.83.small), channel_id=1, source_target_pairs={{128,0},{192,64},{0,128},{64,192},{129,1},{193,65},{1,129},{65,193... | collective-permute-start | bytes 49160 | tf_op jit(solution)/shard_map/ppermute | solution.py:601
  87.4 5.1 %collective-permute-start.22 = (f32[216,128]{1,0:T(8,128)S(1)}, f32[216,128]{1,0:T(8,128)S(1)}, u32[]{:S(2)}, u32[]{:S(2)}) collective-permute-start(f32[216,128]{1,0:T(8,128)S(1)} %get-tuple-element.88), channel_id=1, source_target_pairs={{56,0},{0,8},{8,16},{16,24},{24,32},{32,40},{40,48},{48,56},{57,1}... | collective-permute-start | bytes 331784 | tf_op jit(solution)/shard_map/ppermute | solution.py:601
  88.1 4.4 %collective-permute-start.21 = (f32[216,128]{1,0:T(8,128)S(1)}, f32[216,128]{1,0:T(8,128)S(1)}, u32[]{:S(2)}, u32[]{:S(2)}) collective-permute-start(f32[216,128]{1,0:T(8,128)S(1)} %get-tuple-element.87.own), channel_id=1, source_target_pairs={{8,0},{16,8},{24,16},{32,24},{40,32},{48,40},{56,48},{0,56},{9,1},... | collective-permute-start | bytes 331784 | tf_op jit(solution)/shard_map/ppermute | solution.py:601
  90.1 4.1 %collective-permute-start.23 = (f32[32,128]{1,0:T(8,128)S(1)}, f32[32,128]{1,0:T(8,128)S(1)}, u32[]{:S(2)}, u32[]{:S(2)}) collective-permute-start(f32[32,128]{1,0:T(8,128)S(1)} %get-tuple-element.91), channel_id=1, source_target_pairs={{16,0},{24,8},{32,16},{40,24},{48,32},{56,40},{0,48},{8,56},{17,1}... | collective-permute-start | bytes 49160 | tf_op jit(solution)/shard_map/ppermute | solution.py:601
  90.4 4.8 %collective-permute-start.24 = (f32[32,128]{1,0:T(8,128)S(1)}, f32[32,128]{1,0:T(8,128)S(1)}, u32[]{:S(2)}, u32[]{:S(2)}) collective-permute-start(f32[32,128]{1,0:T(8,128)S(1)} %get-tuple-element.92), channel_id=1, source_target_pairs={{48,0},{56,8},{0,16},{8,24},{16,32},{24,40},{32,48},{40,56},{49,1}... | collective-permute-start | bytes 49160 | tf_op jit(solution)/shard_map/ppermute | solution.py:601

commit v11 on v10

--- a/solution.py
+++ b/solution.py
@@ -179,8 +179,31 @@
     return jnp.where(inside & (x >= 0) & (x < cells * sizes()[0]), OMEGA / (kap + extra), 0.0)
 
 
-def own_weights_kernel(body, weight0, weight1, unit, middle, quads):
-    here = units(body, 16 * UNITS, UNITS)
+def first_join_kernel(own, above, below, first, last, core, upper, lower):
+    for t in range(2):
+        for k in range(5):
+            first[t, k] = own[t, k]
+            last[t, k] = own[t, 11 + k]
+        for ref, pack in ((first, 4), (last, 5)):
+            ref[t, 5] = above[t, pack]
+            ref[t, 6] = below[t, pack]
+        for k in range(24):
+            source = own[t, k] if k < 16 else (above[t, k - 16] if k < 20 else below[t, k - 20])
+            core[pl.ds(16 * (24 * t + k), 16)] = source
+    pack_rows_kernel(core, upper, lower)
+
+
+def two_parts(core, rim, t):
+    return units(core, 24 * 16 * t, 24) + units(rim, 16 * 16 * t, 16)
+
+
+def two_sides(core_upper, core_lower, rim_upper, rim_lower, t, sides):
+    there = unpack_rows(core_upper, core_lower, 15 * t, sides.at[pl.ds(0, 384)])
+    return there + unpack_rows(rim_upper, rim_lower, 10 * t, sides.at[pl.ds(384, 256)])
+
+
+def own_weights_kernel(core, rim, weight0, weight1, unit, middle, quads):
+    here = two_parts(core, rim, 1)
     inside = inside_lanes(iota((16, 256), 1))
     for m in range(-1, MIDS + 1):
         pair = []
@@ -249,9 +272,10 @@
     lax.fori_loop(0, MIDS, middle_slab, 0, unroll=4)
 
 
-def first_down_kernel(body, upper, lower, own0, own1, halo0, halo0s, halo1, x0, x1, unit, r, tall, r1, quads, sides):
-    halo_weights(unpack_rows(upper, lower, 5 * UNITS // 8, sides), halo0, halo0s, halo1)
-    here, there = units(body, 0, UNITS), unpack_rows(upper, lower, 0, sides)
+def first_down_kernel(core, rim, core_upper, core_lower, rim_upper, rim_lower, own0, own1, halo0, halo0s, halo1, x0, x1, unit, r, tall, r1, quads, sides):
+    rows = (core_upper, core_lower, rim_upper, rim_lower)
+    halo_weights(two_sides(*rows, 1, sides), halo0, halo0s, halo1)
+    here, there = two_parts(core, rim, 0), two_sides(*rows, 0, sides)
     weight0, weight1 = Joined(own0, halo0), Joined(own1, halo1)
     near_sweep(lambda i: assemble_fine(here, there, i), weight0, weight1, x0, x1, r1, r, tall)
     for c in range(4):
@@ -603,12 +627,14 @@
 
 def fine_exchange(own, low, high):
     above, below = shift(low, "gz", 1), shift(high, "gz", -1)
-    first = jnp.concatenate([own[:, :5], above[:, 4:5], below[:, 4:5]], axis=1)
-    last = jnp.concatenate([own[:, 11:], above[:, 5:6], below[:, 5:6]], axis=1)
+    first, last, core, upper, lower = call(
+        first_join_kernel, [shape(2, 7, 16, 128), shape(2, 7, 16, 128), shape(768, 128), shape(240, 128), shape(240, 128)], count=3
+    )(own, above, below)
+    core_rows = shift(upper, "gy", 1), shift(lower, "gy", -1)
     before, after = shift(last, "gx", -1), shift(first, "gx", 1)
-    body = jnp.concatenate([own, above[:, :4], below[:, :4], before, after, own[:, :2]], axis=1).reshape(-1, 128)
-    upper, lower = call(pack_rows_kernel, [shape(10 * UNITS, 128)] * 2, count=1)(body)
-    return body, shift(upper, "gy", 1), shift(lower, "gy", -1)
+    rim = jnp.concatenate([before, after, own[:, :2]], axis=1).reshape(-1, 128)
+    upper, lower = call(pack_rows_kernel, [shape(160, 128)] * 2, count=1)(rim)
+    return core, rim, *core_rows, shift(upper, "gy", 1), shift(lower, "gy", -1)
 
 
 def joint_exchange(own, low, high, final):
@@ -651,11 +677,11 @@
     halos = fine_exchange(both, low, high)
     own0, own1, unit2 = call(
         own_weights_kernel, [shape(SLABS, 16, 256), shape(MIDS, 16, 256), tile],
-        scratch((MIDS, 16, 256), (2, 4, 16, 128)), count=1, flops=4_000_000,
-    )(halos[0])
+        scratch((MIDS, 16, 256), (2, 4, 16, 128)), count=2, flops=4_000_000,
+    )(*halos[:2])
     halo0, halo0s, halo1, x0, x1, unit = call(
         first_down_kernel, [shape(SLABS, 16, 256), shape(SLABS, 8, 256), shape(MIDS, 8, 256), short, mids, tile],
-        scratch(SHORT, HALO, MID, (2, 4, 16, 128), (16 * UNITS, 128)), count=5,
+        scratch(SHORT, HALO, MID, (2, 4, 16, 128), (16 * UNITS, 128)), count=8,
     )(*halos, own0, own1)
     ends = [shape(48, 128), shape(48, 128)]
     share_scratch = scratch(BLOCK, (10, 24, 256), (10, 24, 256), (2, 6, 24, 128))

time: 123 us -> 122 us (level)
  waiting for transfers between devices: 21.2 us -> 18.6 us
  starting transfers between devices: 46.3 us -> 48.1 us
    ppermute x25 -> x27, waiting for transfers between devices: 21.2 us -> 18.6 us  [shift(): lax.ppermute(v, axis, [((i + distance) % count, i) for i in range(count)])]
    ppermute x25 -> x27, starting transfers between devices: 46.3 us -> 48.1 us  [shift(): lax.ppermute(v, axis, [((i + distance) % count, i) for i in range(count)])]
  transfers between devices with their start and end apart: 25 -> 27, of which waited for: 16 -> 14; matrix products, arithmetic and copies ran while one was open for 1% -> 0% of each run, Pallas kernels for 2% -> 2%
where the time goes in v11:
time: 122 us
  starting transfers between devices  48.1 us (39%)
  blocking collectives  39.8 us (33%)
  waiting for transfers between devices  18.6 us (15%)
  Pallas kernels  13.6 us (11%)
    ppermute x27, starting transfers between devices, shift(): lax.ppermute(v, axis, [((i + distance) % count, i) for i in range(count)])  48.1 us
    all_to_all x1, blocking collectives, total(): lax.all_to_all(jnp.broadcast_to(v[None, :1], (count, 1, 128)), axes, 0, 0...  25 us
    ppermute x27, waiting for transfers between devices, shift(): lax.ppermute(v, axis, [((i + distance) % count, i) for i in range(count)])  18.6 us
    all_to_all x1, blocking collectives, gather(): lax.all_to_all(jnp.broadcast_to(unit[None], (count,) + unit.shape), ('gx'...  14.9 us
  transfers between devices with their start and end apart: 27, of which 14 were waited for; matrix products, arithmetic and copies ran while one was open for 0% of the time, Pallas kernels for 2%

profile of v11, /device:TPU:1, one launch (start us, length us, event | category | flops | bytes accessed | tf_op | source)
XLA Modules:
  0.0 122.2 jit_solution(12228127592151188267)
XLA Ops:
  0.6 1.9 %shard_map.50 = (f32[2,16,16,128]{3,2,1,0:T(8,128)}, f32[2,6,16,128]{3,2,1,0:T(8,128)}, f32[2,6,16,128]{3,2,1,0:T(8,128)}) custom-call(f32[16,16,128]{2,1,0:T(8,128)} %rhs_in.1, s32[16,16,128]{2,1,0:T(8,128)} %classes_in.1, f32[16]{0:T(128)} %table_in.1), custom_call_target="tpu_custom_call" | custom-call | tf_op jit(solution)/shard_map/pallas_call | solution.py:673
  2.6 3.3 %collective-permute-start = (f32[2,6,16,128]{3,2,1,0:T(8,128)}, f32[2,6,16,128]{3,2,1,0:T(8,128)S(1)}, u32[]{:S(2)}, u32[]{:S(2)}) collective-permute-start(f32[2,6,16,128]{3,2,1,0:T(8,128)} %get-tuple-element.58), channel_id=1, source_target_pairs={{1,0},{2,1},{3,2},{4,3},{5,4},{6,5},{7,6},{0,7},{9,8},{10,9},{11,1... | collective-permute-start | bytes 294920 | tf_op jit(solution)/shard_map/ppermute | solution.py:625
  5.8 2.0 %collective-permute-done.above = f32[2,6,16,128]{3,2,1,0:T(8,128)S(1)} collective-permute-done((f32[2,6,16,128]{3,2,1,0:T(8,128)}, f32[2,6,16,128]{3,2,1,0:T(8,128)S(1)}, u32[]{:S(2)}, u32[]{:S(2)}) %collective-permute-start) | collective-permute-done | bytes 98336 | tf_op jit(solution)/shard_map/ppermute | solution.py:625
  8.9 1.3 %collective-permute-start.2 = (f32[2,7,16,128]{3,2,1,0:T(8,128)S(1)}, f32[2,7,16,128]{3,2,1,0:T(8,128)S(1)}, u32[]{:S(2)}, u32[]{:S(2)}) collective-permute-start(f32[2,7,16,128]{3,2,1,0:T(8,128)S(1)} %get-tuple-element.61), channel_id=1, source_target_pairs={{192,0},{0,64},{64,128},{128,192},{193,1},{1,65},{65,129},{129,193... | collective-permute-start | bytes 344072 | tf_op jit(solution)/shard_map/ppermute | solution.py:625
  10.1 1.5 %collective-permute-start.3 = (f32[2,7,16,128]{3,2,1,0:T(8,128)S(1)}, f32[2,7,16,128]{3,2,1,0:T(8,128)S(1)}, u32[]{:S(2)}, u32[]{:S(2)}) collective-permute-start(f32[2,7,16,128]{3,2,1,0:T(8,128)S(1)} %get-tuple-element.62), channel_id=1, source_target_pairs={{64,0},{128,64},{192,128},{0,192},{65,1},{129,65},{193,129},{1,193... | collective-permute-start | bytes 344072 | tf_op jit(solution)/shard_map/ppermute | solution.py:625
  11.6 5.6 %collective-permute-start.4 = (f32[240,128]{1,0:T(8,128)S(1)}, f32[240,128]{1,0:T(8,128)S(1)}, u32[]{:S(2)}, u32[]{:S(2)}) collective-permute-start(f32[240,128]{1,0:T(8,128)S(1)} %get-tuple-element.63), channel_id=1, source_target_pairs={{8,0},{16,8},{24,16},{32,24},{40,32},{48,40},{56,48},{0,56},{9,1},... | collective-permute-start | bytes 368648 | tf_op jit(solution)/shard_map/ppermute | solution.py:625
  17.3 2.7 %collective-permute-start.6 = (f32[160,128]{1,0:T(8,128)S(1)}, f32[160,128]{1,0:T(8,128)S(1)}, u32[]{:S(2)}, u32[]{:S(2)}) collective-permute-start(f32[160,128]{1,0:T(8,128)S(1)} %get-tuple-element.65), channel_id=1, source_target_pairs={{8,0},{16,8},{24,16},{32,24},{40,32},{48,40},{56,48},{0,56},{9,1},... | collective-permute-start | bytes 245768 | tf_op jit(solution)/shard_map/ppermute | solution.py:625
  20.5 1.6 %collective-permute-done.5.core_lower = f32[240,128]{1,0:T(8,128)S(1)} collective-permute-done((f32[240,128]{1,0:T(8,128)S(1)}, f32[240,128]{1,0:T(8,128)S(1)}, u32[]{:S(2)}, u32[]{:S(2)}) %collective-permute-start.5) | collective-permute-done | bytes 122912 | tf_op jit(solution)/shard_map/ppermute | solution.py:625
  22.1 2.4 %collective-permute-done.7.rim_lower = f32[160,128]{1,0:T(8,128)S(1)} collective-permute-done((f32[160,128]{1,0:T(8,128)S(1)}, f32[160,128]{1,0:T(8,128)S(1)}, u32[]{:S(2)}, u32[]{:S(2)}) %collective-permute-start.7) | collective-permute-done | bytes 81952 | tf_op jit(solution)/shard_map/ppermute | solution.py:625
  24.5 1.8 %shard_map.54 = (f32[26,16,256]{2,1,0:T(8,128)S(1)}, f32[26,8,256]{2,1,0:T(8,128)S(1)}, f32[12,8,256]{2,1,0:T(8,128)S(1)}, f32[26,24,256]{2,1,0:T(8,128)S(1)}, f...) custom-call(f32[768,128]{1,0:T(8,128)S(1)} %get-tuple-element.60.core, f32[512,128]{1,0:T(8,128)S(1)} %bitcast.8, ...), custom_call_target="tpu_custom_call" | custom-call | tf_op jit(solution)/shard_map/pallas_call | solution.py:682
  26.4 14.9 %all_to_all.10.gather = f32[32,2,8,128]{3,2,1,0:T(8,128)S(1)} all-to-all(f32[32,2,8,128]{3,2,1,0:T(8,128)S(1)} %broadcast_in_dim.8), channel_id=1, replica_groups=mesh['gx'=4,'gy'=8,'gz'=8] {'gx','gy'}, dimensions={0} | all-to-all | bytes 524288 | tf_op jit(solution)/shard_map/all_to_all | solution.py:656
  41.2 2.1 %shard_map.55 = (f32[4,16,256]{2,1,0:T(8,128)S(1)}, f32[16,16,128]{2,1,0:T(8,128)S(1)}, f32[16,16,128]{2,1,0:T(8,128)S(1)}, f32[48,128]{1,0:T(8,128)S(1)}, f32[48,128]{1,0:T(8,128)S(1)}) custom-call(f32[32,2,8,128]{3,2,1,0:T(8,128)S(1)} %all_to_all.10.gather, f32[26,16,256]{2,1,0:T(8,128)S(1)} %get-tuple-element.67.own0, ...), custom_call_target="tpu_custom_call" | custom-call | tf_op jit(solution)/shard_map/pallas_call | solution.py:688
  43.3 5.8 %collective-permute-start.9 = (f32[48,128]{1,0:T(8,128)S(1)}, f32[48,128]{1,0:T(8,128)S(1)}, u32[]{:S(2)}, u32[]{:S(2)}) collective-permute-start(f32[48,128]{1,0:T(8,128)S(1)} %get-tuple-element.77), channel_id=1, source_target_pairs={{7,0},{0,1},{1,2},{2,3},{3,4},{4,5},{5,6},{6,7},{15,8},{8,9},{9,10... | collective-permute-start | bytes 73736 | tf_op jit(solution)/shard_map/ppermute | solution.py:625
  49.1 2.2 %collective-permute-start.8 = (f32[48,128]{1,0:T(8,128)S(1)}, f32[48,128]{1,0:T(8,128)S(1)}, u32[]{:S(2)}, u32[]{:S(2)}) collective-permute-start(f32[48,128]{1,0:T(8,128)S(1)} %get-tuple-element.76.low), channel_id=1, source_target_pairs={{1,0},{2,1},{3,2},{4,3},{5,4},{6,5},{7,6},{0,7},{9,8},{10,9},{11,1... | collective-permute-start | bytes 73736 | tf_op jit(solution)/shard_map/ppermute | solution.py:625
  52.4 3.9 %collective-permute-start.10 = (f32[8,128]{1,0:T(8,128)S(1)}, f32[8,128]{1,0:T(8,128)S(1)}, u32[]{:S(2)}, u32[]{:S(2)}) collective-permute-start(f32[8,128]{1,0:T(8,128)S(1)} %slice.14), channel_id=1, source_target_pairs={{4,0},{5,1},{6,2},{7,3},{0,4},{1,5},{2,6},{3,7},{12,8},{13,9},{14,... | collective-permute-start | bytes 12296 | tf_op jit(solution)/shard_map/ppermute | solution.py:625
  56.3 1.3 %collective-permute-start.13 = (f32[32,128]{1,0:T(8,128)S(1)}, f32[32,128]{1,0:T(8,128)S(1)}, u32[]{:S(2)}, u32[]{:S(2)}) collective-permute-start(f32[32,128]{1,0:T(8,128)S(1)} %get-tuple-element.78.small), channel_id=1, source_target_pairs={{128,0},{192,64},{0,128},{64,192},{129,1},{193,65},{1,129},{65,193... | collective-permute-start | bytes 49160 | tf_op jit(solution)/shard_map/ppermute | solution.py:625
  57.8 2.5 %collective-permute-start.12 = (f32[144,128]{1,0:T(8,128)S(1)}, f32[144,128]{1,0:T(8,128)S(1)}, u32[]{:S(2)}, u32[]{:S(2)}) collective-permute-start(f32[144,128]{1,0:T(8,128)S(1)} %get-tuple-element.80), channel_id=1, source_target_pairs={{64,0},{128,64},{192,128},{0,192},{65,1},{129,65},{193,129},{1,193... | collective-permute-start | bytes 221192 | tf_op jit(solution)/shard_map/ppermute | solution.py:625
  60.7 2.0 %collective-permute-done.11.before = f32[144,128]{1,0:T(8,128)S(1)} collective-permute-done((f32[144,128]{1,0:T(8,128)S(1)}, f32[144,128]{1,0:T(8,128)S(1)}, u32[]{:S(2)}, u32[]{:S(2)}) %collective-permute-start.11) | collective-permute-done | bytes 73760 | tf_op jit(solution)/shard_map/ppermute | solution.py:625
  63.5 2.3 %collective-permute-start.14 = (f32[216,128]{1,0:T(8,128)S(1)}, f32[216,128]{1,0:T(8,128)S(1)}, u32[]{:S(2)}, u32[]{:S(2)}) collective-permute-start(f32[216,128]{1,0:T(8,128)S(1)} %get-tuple-element.82.own), channel_id=1, source_target_pairs={{8,0},{16,8},{24,16},{32,24},{40,32},{48,40},{56,48},{0,56},{9,1},... | collective-permute-start | bytes 331784 | tf_op jit(solution)/shard_map/ppermute | solution.py:625
  65.8 2.4 %collective-permute-start.17 = (f32[32,128]{1,0:T(8,128)S(1)}, f32[32,128]{1,0:T(8,128)S(1)}, u32[]{:S(2)}, u32[]{:S(2)}) collective-permute-start(f32[32,128]{1,0:T(8,128)S(1)} %get-tuple-element.88), channel_id=1, source_target_pairs={{48,0},{56,8},{0,16},{8,24},{16,32},{24,40},{32,48},{40,56},{49,1}... | collective-permute-start | bytes 49160 | tf_op jit(solution)/shard_map/ppermute | solution.py:625
  70.5 2.2 %shard_map.59 = (f32[16,16,128]{2,1,0:T(8,128)S(1)}, f32[16,16,128]{2,1,0:T(8,128)S(1)}, f32[48,128]{1,0:T(8,128)S(1)}, f32[48,128]{1,0:T(8,128)S(1)}) custom-call(f32[26,24,256]{2,1,0:T(8,128)S(1)} %get-tuple-element.85.x0, f32[12,24,256]{2,1,0:T(8,128)S(1)} %get-tuple-element.86.x1, f32[216,128]{1,0:T(8,128)S(1)} %get-tuple-element.82.own, ...), custom_call_target="tpu_custom_call" | custom-call | tf_op jit(solution)/shard_map/pallas_call | solution.py:699
  72.7 2.6 %collective-permute-start.19 = (f32[48,128]{1,0:T(8,128)S(1)}, f32[48,128]{1,0:T(8,128)S(1)}, u32[]{:S(2)}, u32[]{:S(2)}) collective-permute-start(f32[48,128]{1,0:T(8,128)S(1)} %get-tuple-element.92), channel_id=1, source_target_pairs={{7,0},{0,1},{1,2},{2,3},{3,4},{4,5},{5,6},{6,7},{15,8},{8,9},{9,10... | collective-permute-start | bytes 73736 | tf_op jit(solution)/shard_map/ppermute | solution.py:625
  76.2 2.3 %collective-permute-done.18.above = f32[48,128]{1,0:T(8,128)S(1)} collective-permute-done((f32[48,128]{1,0:T(8,128)S(1)}, f32[48,128]{1,0:T(8,128)S(1)}, u32[]{:S(2)}, u32[]{:S(2)}) %collective-permute-start.18) | collective-permute-done | bytes 24608 | tf_op jit(solution)/shard_map/ppermute | solution.py:625
  78.5 1.2 collective-permute-start.20
  79.8 2.3 %collective-permute-start.21 = (f32[144,128]{1,0:T(8,128)S(1)}, f32[144,128]{1,0:T(8,128)S(1)}, u32[]{:S(2)}, u32[]{:S(2)}) collective-permute-start(f32[144,128]{1,0:T(8,128)S(1)} %get-tuple-element.95), channel_id=1, source_target_pairs={{64,0},{128,64},{192,128},{0,192},{65,1},{129,65},{193,129},{1,193... | collective-permute-start | bytes 221192 | tf_op jit(solution)/shard_map/ppermute | solution.py:625
  82.1 1.1 collective-permute-start.22
  83.2 3.1 %collective-permute-done.22.across = f32[32,128]{1,0:T(8,128)S(1)} collective-permute-done((f32[32,128]{1,0:T(8,128)S(1)}, f32[32,128]{1,0:T(8,128)S(1)}, u32[]{:S(2)}, u32[]{:S(2)}) %collective-permute-start.22) | collective-permute-done | bytes 16416 | tf_op jit(solution)/shard_map/ppermute | solution.py:625
  87.0 2.1 %collective-permute-start.23 = (f32[216,128]{1,0:T(8,128)S(1)}, f32[216,128]{1,0:T(8,128)S(1)}, u32[]{:S(2)}, u32[]{:S(2)}) collective-permute-start(f32[216,128]{1,0:T(8,128)S(1)} %get-tuple-element.97.own), channel_id=1, source_target_pairs={{8,0},{16,8},{24,16},{32,24},{40,32},{48,40},{56,48},{0,56},{9,1},... | collective-permute-start | bytes 331784 | tf_op jit(solution)/shard_map/ppermute | solution.py:625
  89.4 2.1 %collective-permute-start.26 = (f32[32,128]{1,0:T(8,128)S(1)}, f32[32,128]{1,0:T(8,128)S(1)}, u32[]{:S(2)}, u32[]{:S(2)}) collective-permute-start(f32[32,128]{1,0:T(8,128)S(1)} %get-tuple-element.102), channel_id=1, source_target_pairs={{48,0},{56,8},{0,16},{8,24},{16,32},{24,40},{32,48},{40,56},{49,1}... | collective-permute-start | bytes 49160 | tf_op jit(solution)/shard_map/ppermute | solution.py:625
  93.1 1.2 %collective-permute-done.26.down2 = f32[32,128]{1,0:T(8,128)S(1)} collective-permute-done((f32[32,128]{1,0:T(8,128)S(1)}, f32[32,128]{1,0:T(8,128)S(1)}, u32[]{:S(2)}, u32[]{:S(2)}) %collective-permute-start.26) | collective-permute-done | bytes 16416 | tf_op jit(solution)/shard_map/ppermute | solution.py:625
  94.3 1.7 %shard_map.63 = (f32[16,16,128]{2,1,0:T(8,128)S(1)}, f32[16,16,128]{2,1,0:T(8,128)S(1)}, f32[16,16,128]{2,1,0:T(8,128)S(1)}, f32[16,16,128]{2,1,0:T(8,128)S(1)},...) custom-call(f32[26,24,256]{2,1,0:T(8,128)S(1)} %get-tuple-element.99.x0, ...), custom_call_target="tpu_custom_call" | custom-call | tf_op jit(solution)/shard_map/pallas_call | solution.py:704
  96.1 25.0 %all_to_all.11 = f32[256,1,128]{2,1,0:T(1,128)S(1)} all-to-all(f32[256,1,128]{2,1,0:T(1,128)S(1)} %broadcast_in_dim.10), channel_id=1, replica_groups=mesh['gx'=4,'gy'=8,'gz'=8] {'gx','gy','gz'}, dimensions={0} | all-to-all | bytes 262144 | tf_op jit(solution)/shard_map/all_to_all | solution.py:662
  (54 shorter events, 10.9 us)
Async XLA Ops:
  2.6 5.2 %collective-permute-start = (f32[2,6,16,128]{3,2,1,0:T(8,128)}, f32[2,6,16,128]{3,2,1,0:T(8,128)S(1)}, u32[]{:S(2)}, u32[]{:S(2)}) collective-permute-start(f32[2,6,16,128]{3,2,1,0:T(8,128)} %get-tuple-element.58), channel_id=1, source_target_pairs={{1,0},{2,1},{3,2},{4,3},{5,4},{6,5},{7,6},{0,7},{9,8},{10,9},{11,1... | collective-permute-start | bytes 294920 | tf_op jit(solution)/shard_map/ppermute | solution.py:625
  5.8 2.0 %collective-permute-start.1 = (f32[2,6,16,128]{3,2,1,0:T(8,128)}, f32[2,6,16,128]{3,2,1,0:T(8,128)S(1)}, u32[]{:S(2)}, u32[]{:S(2)}) collective-permute-start(f32[2,6,16,128]{3,2,1,0:T(8,128)} %get-tuple-element.59), channel_id=1, source_target_pairs={{7,0},{0,1},{1,2},{2,3},{3,4},{4,5},{5,6},{6,7},{15,8},{8,9},{9,10... | collective-permute-start | bytes 294920 | tf_op jit(solution)/shard_map/ppermute | solution.py:625
  7.8 1.0 copy-start
  8.9 8.3 %collective-permute-start.2 = (f32[2,7,16,128]{3,2,1,0:T(8,128)S(1)}, f32[2,7,16,128]{3,2,1,0:T(8,128)S(1)}, u32[]{:S(2)}, u32[]{:S(2)}) collective-permute-start(f32[2,7,16,128]{3,2,1,0:T(8,128)S(1)} %get-tuple-element.61), channel_id=1, source_target_pairs={{192,0},{0,64},{64,128},{128,192},{193,1},{1,65},{65,129},{129,193... | collective-permute-start | bytes 344072 | tf_op jit(solution)/shard_map/ppermute | solution.py:625
  10.1 7.1 %collective-permute-start.3 = (f32[2,7,16,128]{3,2,1,0:T(8,128)S(1)}, f32[2,7,16,128]{3,2,1,0:T(8,128)S(1)}, u32[]{:S(2)}, u32[]{:S(2)}) collective-permute-start(f32[2,7,16,128]{3,2,1,0:T(8,128)S(1)} %get-tuple-element.62), channel_id=1, source_target_pairs={{64,0},{128,64},{192,128},{0,192},{65,1},{129,65},{193,129},{1,193... | collective-permute-start | bytes 344072 | tf_op jit(solution)/shard_map/ppermute | solution.py:625
  11.6 8.9 %collective-permute-start.4 = (f32[240,128]{1,0:T(8,128)S(1)}, f32[240,128]{1,0:T(8,128)S(1)}, u32[]{:S(2)}, u32[]{:S(2)}) collective-permute-start(f32[240,128]{1,0:T(8,128)S(1)} %get-tuple-element.63), channel_id=1, source_target_pairs={{8,0},{16,8},{24,16},{32,24},{40,32},{48,40},{56,48},{0,56},{9,1},... | collective-permute-start | bytes 368648 | tf_op jit(solution)/shard_map/ppermute | solution.py:625
  17.2 4.9 %collective-permute-start.5 = (f32[240,128]{1,0:T(8,128)S(1)}, f32[240,128]{1,0:T(8,128)S(1)}, u32[]{:S(2)}, u32[]{:S(2)}) collective-permute-start(f32[240,128]{1,0:T(8,128)S(1)} %get-tuple-element.64), channel_id=1, source_target_pairs={{56,0},{0,8},{8,16},{16,24},{24,32},{32,40},{40,48},{48,56},{57,1}... | collective-permute-start | bytes 368648 | tf_op jit(solution)/shard_map/ppermute | solution.py:625
  17.3 4.8 %collective-permute-start.6 = (f32[160,128]{1,0:T(8,128)S(1)}, f32[160,128]{1,0:T(8,128)S(1)}, u32[]{:S(2)}, u32[]{:S(2)}) collective-permute-start(f32[160,128]{1,0:T(8,128)S(1)} %get-tuple-element.65), channel_id=1, source_target_pairs={{8,0},{16,8},{24,16},{32,24},{40,32},{48,40},{56,48},{0,56},{9,1},... | collective-permute-start | bytes 245768 | tf_op jit(solution)/shard_map/ppermute | solution.py:625
  20.0 4.5 %collective-permute-start.7 = (f32[160,128]{1,0:T(8,128)S(1)}, f32[160,128]{1,0:T(8,128)S(1)}, u32[]{:S(2)}, u32[]{:S(2)}) collective-permute-start(f32[160,128]{1,0:T(8,128)S(1)} %get-tuple-element.66), channel_id=1, source_target_pairs={{56,0},{0,8},{8,16},{16,24},{24,32},{32,40},{40,48},{48,56},{57,1}... | collective-permute-start | bytes 245768 | tf_op jit(solution)/shard_map/ppermute | solution.py:625
  26.3 14.9 %copy-start.1 = (f32[2,16,16,128]{3,2,1,0:T(8,128)S(1)}, f32[2,16,16,128]{3,2,1,0:T(8,128)}, u32[]{:S(2)}) copy-start(f32[2,16,16,128]{3,2,1,0:T(8,128)} %get-tuple-element.57.own.both) | copy-start | bytes 786436
  43.3 8.6 %collective-permute-start.9 = (f32[48,128]{1,0:T(8,128)S(1)}, f32[48,128]{1,0:T(8,128)S(1)}, u32[]{:S(2)}, u32[]{:S(2)}) collective-permute-start(f32[48,128]{1,0:T(8,128)S(1)} %get-tuple-element.77), channel_id=1, source_target_pairs={{7,0},{0,1},{1,2},{2,3},{3,4},{4,5},{5,6},{6,7},{15,8},{8,9},{9,10... | collective-permute-start | bytes 73736 | tf_op jit(solution)/shard_map/ppermute | solution.py:625
  49.1 3.3 %collective-permute-start.8 = (f32[48,128]{1,0:T(8,128)S(1)}, f32[48,128]{1,0:T(8,128)S(1)}, u32[]{:S(2)}, u32[]{:S(2)}) collective-permute-start(f32[48,128]{1,0:T(8,128)S(1)} %get-tuple-element.76.low), channel_id=1, source_target_pairs={{1,0},{2,1},{3,2},{4,3},{5,4},{6,5},{7,6},{0,7},{9,8},{10,9},{11,1... | collective-permute-start | bytes 73736 | tf_op jit(solution)/shard_map/ppermute | solution.py:625
  52.4 7.9 %collective-permute-start.10 = (f32[8,128]{1,0:T(8,128)S(1)}, f32[8,128]{1,0:T(8,128)S(1)}, u32[]{:S(2)}, u32[]{:S(2)}) collective-permute-start(f32[8,128]{1,0:T(8,128)S(1)} %slice.14), channel_id=1, source_target_pairs={{4,0},{5,1},{6,2},{7,3},{0,4},{1,5},{2,6},{3,7},{12,8},{13,9},{14,... | collective-permute-start | bytes 12296 | tf_op jit(solution)/shard_map/ppermute | solution.py:625
  56.3 4.4 %collective-permute-start.13 = (f32[32,128]{1,0:T(8,128)S(1)}, f32[32,128]{1,0:T(8,128)S(1)}, u32[]{:S(2)}, u32[]{:S(2)}) collective-permute-start(f32[32,128]{1,0:T(8,128)S(1)} %get-tuple-element.78.small), channel_id=1, source_target_pairs={{128,0},{192,64},{0,128},{64,192},{129,1},{193,65},{1,129},{65,193... | collective-permute-start | bytes 49160 | tf_op jit(solution)/shard_map/ppermute | solution.py:625
  57.6 5.1 %collective-permute-start.11 = (f32[144,128]{1,0:T(8,128)S(1)}, f32[144,128]{1,0:T(8,128)S(1)}, u32[]{:S(2)}, u32[]{:S(2)}) collective-permute-start(f32[144,128]{1,0:T(8,128)S(1)} %get-tuple-element.79), channel_id=1, source_target_pairs={{192,0},{0,64},{64,128},{128,192},{193,1},{1,65},{65,129},{129,193... | collective-permute-start | bytes 221192 | tf_op jit(solution)/shard_map/ppermute | solution.py:625
  57.8 5.0 %collective-permute-start.12 = (f32[144,128]{1,0:T(8,128)S(1)}, f32[144,128]{1,0:T(8,128)S(1)}, u32[]{:S(2)}, u32[]{:S(2)}) collective-permute-start(f32[144,128]{1,0:T(8,128)S(1)} %get-tuple-element.80), channel_id=1, source_target_pairs={{64,0},{128,64},{192,128},{0,192},{65,1},{129,65},{193,129},{1,193... | collective-permute-start | bytes 221192 | tf_op jit(solution)/shard_map/ppermute | solution.py:625
  62.8 5.3 %collective-permute-start.15 = (f32[216,128]{1,0:T(8,128)S(1)}, f32[216,128]{1,0:T(8,128)S(1)}, u32[]{:S(2)}, u32[]{:S(2)}) collective-permute-start(f32[216,128]{1,0:T(8,128)S(1)} %get-tuple-element.83), channel_id=1, source_target_pairs={{56,0},{0,8},{8,16},{16,24},{24,32},{32,40},{40,48},{48,56},{57,1}... | collective-permute-start | bytes 331784 | tf_op jit(solution)/shard_map/ppermute | solution.py:625
  63.5 4.7 %collective-permute-start.14 = (f32[216,128]{1,0:T(8,128)S(1)}, f32[216,128]{1,0:T(8,128)S(1)}, u32[]{:S(2)}, u32[]{:S(2)}) collective-permute-start(f32[216,128]{1,0:T(8,128)S(1)} %get-tuple-element.82.own), channel_id=1, source_target_pairs={{8,0},{16,8},{24,16},{32,24},{40,32},{48,40},{56,48},{0,56},{9,1},... | collective-permute-start | bytes 331784 | tf_op jit(solution)/shard_map/ppermute | solution.py:625
  65.8 3.7 %collective-permute-start.16 = (f32[32,128]{1,0:T(8,128)S(1)}, f32[32,128]{1,0:T(8,128)S(1)}, u32[]{:S(2)}, u32[]{:S(2)}) collective-permute-start(f32[32,128]{1,0:T(8,128)S(1)} %get-tuple-element.87), channel_id=1, source_target_pairs={{16,0},{24,8},{32,16},{40,24},{48,32},{56,40},{0,48},{8,56},{17,1}... | collective-permute-start | bytes 49160 | tf_op jit(solution)/shard_map/ppermute | solution.py:625
  65.8 4.7 %collective-permute-start.17 = (f32[32,128]{1,0:T(8,128)S(1)}, f32[32,128]{1,0:T(8,128)S(1)}, u32[]{:S(2)}, u32[]{:S(2)}) collective-permute-start(f32[32,128]{1,0:T(8,128)S(1)} %get-tuple-element.88), channel_id=1, source_target_pairs={{48,0},{56,8},{0,16},{8,24},{16,32},{24,40},{32,48},{40,56},{49,1}... | collective-permute-start | bytes 49160 | tf_op jit(solution)/shard_map/ppermute | solution.py:625
  72.7 3.5 %collective-permute-start.19 = (f32[48,128]{1,0:T(8,128)S(1)}, f32[48,128]{1,0:T(8,128)S(1)}, u32[]{:S(2)}, u32[]{:S(2)}) collective-permute-start(f32[48,128]{1,0:T(8,128)S(1)} %get-tuple-element.92), channel_id=1, source_target_pairs={{7,0},{0,1},{1,2},{2,3},{3,4},{4,5},{5,6},{6,7},{15,8},{8,9},{9,10... | collective-permute-start | bytes 73736 | tf_op jit(solution)/shard_map/ppermute | solution.py:625
  75.3 3.3 %collective-permute-start.18 = (f32[48,128]{1,0:T(8,128)S(1)}, f32[48,128]{1,0:T(8,128)S(1)}, u32[]{:S(2)}, u32[]{:S(2)}) collective-permute-start(f32[48,128]{1,0:T(8,128)S(1)} %get-tuple-element.91.low), channel_id=1, source_target_pairs={{1,0},{2,1},{3,2},{4,3},{5,4},{6,5},{7,6},{0,7},{9,8},{10,9},{11,1... | collective-permute-start | bytes 73736 | tf_op jit(solution)/shard_map/ppermute | solution.py:625
  78.5 7.8 %collective-permute-start.20 = (f32[144,128]{1,0:T(8,128)S(1)}, f32[144,128]{1,0:T(8,128)S(1)}, u32[]{:S(2)}, u32[]{:S(2)}) collective-permute-start(f32[144,128]{1,0:T(8,128)S(1)} %get-tuple-element.94), channel_id=1, source_target_pairs={{192,0},{0,64},{64,128},{128,192},{193,1},{1,65},{65,129},{129,193... | collective-permute-start | bytes 221192 | tf_op jit(solution)/shard_map/ppermute | solution.py:625
  79.8 6.6 %collective-permute-start.21 = (f32[144,128]{1,0:T(8,128)S(1)}, f32[144,128]{1,0:T(8,128)S(1)}, u32[]{:S(2)}, u32[]{:S(2)}) collective-permute-start(f32[144,128]{1,0:T(8,128)S(1)} %get-tuple-element.95), channel_id=1, source_target_pairs={{64,0},{128,64},{192,128},{0,192},{65,1},{129,65},{193,129},{1,193... | collective-permute-start | bytes 221192 | tf_op jit(solution)/shard_map/ppermute | solution.py:625
  82.1 4.2 %collective-permute-start.22 = (f32[32,128]{1,0:T(8,128)S(1)}, f32[32,128]{1,0:T(8,128)S(1)}, u32[]{:S(2)}, u32[]{:S(2)}) collective-permute-start(f32[32,128]{1,0:T(8,128)S(1)} %get-tuple-element.93.small), channel_id=1, source_target_pairs={{128,0},{192,64},{0,128},{64,192},{129,1},{193,65},{1,129},{65,193... | collective-permute-start | bytes 49160 | tf_op jit(solution)/shard_map/ppermute | solution.py:625
  86.4 5.1 %collective-permute-start.24 = (f32[216,128]{1,0:T(8,128)S(1)}, f32[216,128]{1,0:T(8,128)S(1)}, u32[]{:S(2)}, u32[]{:S(2)}) collective-permute-start(f32[216,128]{1,0:T(8,128)S(1)} %get-tuple-element.98), channel_id=1, source_target_pairs={{56,0},{0,8},{8,16},{16,24},{24,32},{32,40},{40,48},{48,56},{57,1}... | collective-permute-start | bytes 331784 | tf_op jit(solution)/shard_map/ppermute | solution.py:625
  87.0 4.5 %collective-permute-start.23 = (f32[216,128]{1,0:T(8,128)S(1)}, f32[216,128]{1,0:T(8,128)S(1)}, u32[]{:S(2)}, u32[]{:S(2)}) collective-permute-start(f32[216,128]{1,0:T(8,128)S(1)} %get-tuple-element.97.own), channel_id=1, source_target_pairs={{8,0},{16,8},{24,16},{32,24},{40,32},{48,40},{56,48},{0,56},{9,1},... | collective-permute-start | bytes 331784 | tf_op jit(solution)/shard_map/ppermute | solution.py:625
  89.2 3.9 %collective-permute-start.25 = (f32[32,128]{1,0:T(8,128)S(1)}, f32[32,128]{1,0:T(8,128)S(1)}, u32[]{:S(2)}, u32[]{:S(2)}) collective-permute-start(f32[32,128]{1,0:T(8,128)S(1)} %get-tuple-element.101), channel_id=1, source_target_pairs={{16,0},{24,8},{32,16},{40,24},{48,32},{56,40},{0,48},{8,56},{17,1}... | collective-permute-start | bytes 49160 | tf_op jit(solution)/shard_map/ppermute | solution.py:625
  89.4 4.9 %collective-permute-start.26 = (f32[32,128]{1,0:T(8,128)S(1)}, f32[32,128]{1,0:T(8,128)S(1)}, u32[]{:S(2)}, u32[]{:S(2)}) collective-permute-start(f32[32,128]{1,0:T(8,128)S(1)} %get-tuple-element.102), channel_id=1, source_target_pairs={{48,0},{56,8},{0,16},{8,24},{16,32},{24,40},{32,48},{40,56},{49,1}... | collective-permute-start | bytes 49160 | tf_op jit(solution)/shard_map/ppermute | solution.py:625

commit v12 on v11

--- a/solution.py
+++ b/solution.py
@@ -191,6 +191,14 @@
             source = own[t, k] if k < 16 else (above[t, k - 16] if k < 20 else below[t, k - 20])
             core[pl.ds(16 * (24 * t + k), 16)] = source
     pack_rows_kernel(core, upper, lower)
+
+
+def rim_join_kernel(before, after, rim, upper, lower):
+    for t in range(2):
+        for k in range(16):
+            source = before[t, k] if k < 7 else (after[t, k - 7] if k < 14 else jnp.zeros((16, 128), F32))
+            rim[pl.ds(16 * (16 * t + k), 16)] = source
+    pack_rows_kernel(rim, upper, lower)
 
 
 def two_parts(core, rim, t):
@@ -632,8 +640,7 @@
     )(own, above, below)
     core_rows = shift(upper, "gy", 1), shift(lower, "gy", -1)
     before, after = shift(last, "gx", -1), shift(first, "gx", 1)
-    rim = jnp.concatenate([before, after, own[:, :2]], axis=1).reshape(-1, 128)
-    upper, lower = call(pack_rows_kernel, [shape(160, 128)] * 2, count=1)(rim)
+    rim, upper, lower = call(rim_join_kernel, [shape(512, 128), shape(160, 128), shape(160, 128)], count=2)(before, after)
     return core, rim, *core_rows, shift(upper, "gy", 1), shift(lower, "gy", -1)
 
 

time: 122 us -> 122 us (level)
  no operation moved by 1% of the time
where the time goes in v12:
time: 122 us
  starting transfers between devices  48.1 us (39%)
  blocking collectives  39.8 us (33%)
  waiting for transfers between devices  18.6 us (15%)
  Pallas kernels  13.6 us (11%)
    ppermute x27, starting transfers between devices, shift(): lax.ppermute(v, axis, [((i + distance) % count, i) for i in range(count)])  48.1 us
    all_to_all x1, blocking collectives, total(): lax.all_to_all(jnp.broadcast_to(v[None, :1], (count, 1, 128)), axes, 0, 0...  25 us
    ppermute x27, waiting for transfers between devices, shift(): lax.ppermute(v, axis, [((i + distance) % count, i) for i in range(count)])  18.6 us
    all_to_all x1, blocking collectives, gather(): lax.all_to_all(jnp.broadcast_to(unit[None], (count,) + unit.shape), ('gx'...  14.9 us
  transfers between devices with their start and end apart: 27, of which 14 were waited for; matrix products, arithmetic and copies ran while one was open for 0% of the time, Pallas kernels for 2%

profile of v12, /device:TPU:1, one launch (start us, length us, event | category | flops | bytes accessed | tf_op | source)
XLA Modules:
  0.0 122.2 jit_solution(13432438288742951147)
XLA Ops:
  0.6 1.9 %shard_map.50 = (f32[2,16,16,128]{3,2,1,0:T(8,128)}, f32[2,6,16,128]{3,2,1,0:T(8,128)}, f32[2,6,16,128]{3,2,1,0:T(8,128)}) custom-call(f32[16,16,128]{2,1,0:T(8,128)} %rhs_in.1, s32[16,16,128]{2,1,0:T(8,128)} %classes_in.1, f32[16]{0:T(128)} %table_in.1), custom_call_target="tpu_custom_call" | custom-call | tf_op jit(solution)/shard_map/pallas_call | solution.py:680
  2.6 3.3 %collective-permute-start = (f32[2,6,16,128]{3,2,1,0:T(8,128)}, f32[2,6,16,128]{3,2,1,0:T(8,128)S(1)}, u32[]{:S(2)}, u32[]{:S(2)}) collective-permute-start(f32[2,6,16,128]{3,2,1,0:T(8,128)} %get-tuple-element.59), channel_id=1, source_target_pairs={{1,0},{2,1},{3,2},{4,3},{5,4},{6,5},{7,6},{0,7},{9,8},{10,9},{11,1... | collective-permute-start | bytes 294920 | tf_op jit(solution)/shard_map/ppermute | solution.py:633
  5.8 2.0 %collective-permute-done.above = f32[2,6,16,128]{3,2,1,0:T(8,128)S(1)} collective-permute-done((f32[2,6,16,128]{3,2,1,0:T(8,128)}, f32[2,6,16,128]{3,2,1,0:T(8,128)S(1)}, u32[]{:S(2)}, u32[]{:S(2)}) %collective-permute-start) | collective-permute-done | bytes 98336 | tf_op jit(solution)/shard_map/ppermute | solution.py:633
  8.9 1.3 %collective-permute-start.2 = (f32[2,7,16,128]{3,2,1,0:T(8,128)S(1)}, f32[2,7,16,128]{3,2,1,0:T(8,128)S(1)}, u32[]{:S(2)}, u32[]{:S(2)}) collective-permute-start(f32[2,7,16,128]{3,2,1,0:T(8,128)S(1)} %get-tuple-element.62), channel_id=1, source_target_pairs={{192,0},{0,64},{64,128},{128,192},{193,1},{1,65},{65,129},{129,193... | collective-permute-start | bytes 344072 | tf_op jit(solution)/shard_map/ppermute | solution.py:633
  10.1 1.5 %collective-permute-start.3 = (f32[2,7,16,128]{3,2,1,0:T(8,128)S(1)}, f32[2,7,16,128]{3,2,1,0:T(8,128)S(1)}, u32[]{:S(2)}, u32[]{:S(2)}) collective-permute-start(f32[2,7,16,128]{3,2,1,0:T(8,128)S(1)} %get-tuple-element.63), channel_id=1, source_target_pairs={{64,0},{128,64},{192,128},{0,192},{65,1},{129,65},{193,129},{1,193... | collective-permute-start | bytes 344072 | tf_op jit(solution)/shard_map/ppermute | solution.py:633
  11.6 5.6 %collective-permute-start.4 = (f32[240,128]{1,0:T(8,128)S(1)}, f32[240,128]{1,0:T(8,128)S(1)}, u32[]{:S(2)}, u32[]{:S(2)}) collective-permute-start(f32[240,128]{1,0:T(8,128)S(1)} %get-tuple-element.65), channel_id=1, source_target_pairs={{8,0},{16,8},{24,16},{32,24},{40,32},{48,40},{56,48},{0,56},{9,1},... | collective-permute-start | bytes 368648 | tf_op jit(solution)/shard_map/ppermute | solution.py:633
  17.3 2.7 %collective-permute-start.6 = (f32[160,128]{1,0:T(8,128)S(1)}, f32[160,128]{1,0:T(8,128)S(1)}, u32[]{:S(2)}, u32[]{:S(2)}) collective-permute-start(f32[160,128]{1,0:T(8,128)S(1)} %get-tuple-element.67), channel_id=1, source_target_pairs={{8,0},{16,8},{24,16},{32,24},{40,32},{48,40},{56,48},{0,56},{9,1},... | collective-permute-start | bytes 245768 | tf_op jit(solution)/shard_map/ppermute | solution.py:633
  20.5 1.6 %collective-permute-done.5.core_lower = f32[240,128]{1,0:T(8,128)S(1)} collective-permute-done((f32[240,128]{1,0:T(8,128)S(1)}, f32[240,128]{1,0:T(8,128)S(1)}, u32[]{:S(2)}, u32[]{:S(2)}) %collective-permute-start.5) | collective-permute-done | bytes 122912 | tf_op jit(solution)/shard_map/ppermute | solution.py:633
  22.1 2.4 %collective-permute-done.7.rim_lower = f32[160,128]{1,0:T(8,128)S(1)} collective-permute-done((f32[160,128]{1,0:T(8,128)S(1)}, f32[160,128]{1,0:T(8,128)S(1)}, u32[]{:S(2)}, u32[]{:S(2)}) %collective-permute-start.7) | collective-permute-done | bytes 81952 | tf_op jit(solution)/shard_map/ppermute | solution.py:633
  24.5 1.8 %shard_map.54 = (f32[26,16,256]{2,1,0:T(8,128)S(1)}, f32[26,8,256]{2,1,0:T(8,128)S(1)}, f32[12,8,256]{2,1,0:T(8,128)S(1)}, f32[26,24,256]{2,1,0:T(8,128)S(1)}, f...) custom-call(f32[768,128]{1,0:T(8,128)S(1)} %get-tuple-element.61.core, f32[512,128]{1,0:T(8,128)S(1)} %get-tuple-element.64.rim, ...), custom_call_target="tpu_custom_call" | custom-call | tf_op jit(solution)/shard_map/pallas_call | solution.py:689
  26.3 14.9 %all_to_all.10.gather = f32[32,2,8,128]{3,2,1,0:T(8,128)S(1)} all-to-all(f32[32,2,8,128]{3,2,1,0:T(8,128)S(1)} %broadcast_in_dim.8), channel_id=1, replica_groups=mesh['gx'=4,'gy'=8,'gz'=8] {'gx','gy'}, dimensions={0} | all-to-all | bytes 524288 | tf_op jit(solution)/shard_map/all_to_all | solution.py:663
  41.2 2.1 %shard_map.55 = (f32[4,16,256]{2,1,0:T(8,128)S(1)}, f32[16,16,128]{2,1,0:T(8,128)S(1)}, f32[16,16,128]{2,1,0:T(8,128)S(1)}, f32[48,128]{1,0:T(8,128)S(1)}, f32[48,128]{1,0:T(8,128)S(1)}) custom-call(f32[32,2,8,128]{3,2,1,0:T(8,128)S(1)} %all_to_all.10.gather, f32[26,16,256]{2,1,0:T(8,128)S(1)} %get-tuple-element.69.own0, ...), custom_call_target="tpu_custom_call" | custom-call | tf_op jit(solution)/shard_map/pallas_call | solution.py:695
  43.3 5.8 %collective-permute-start.9 = (f32[48,128]{1,0:T(8,128)S(1)}, f32[48,128]{1,0:T(8,128)S(1)}, u32[]{:S(2)}, u32[]{:S(2)}) collective-permute-start(f32[48,128]{1,0:T(8,128)S(1)} %get-tuple-element.79), channel_id=1, source_target_pairs={{7,0},{0,1},{1,2},{2,3},{3,4},{4,5},{5,6},{6,7},{15,8},{8,9},{9,10... | collective-permute-start | bytes 73736 | tf_op jit(solution)/shard_map/ppermute | solution.py:633
  49.1 2.2 %collective-permute-start.8 = (f32[48,128]{1,0:T(8,128)S(1)}, f32[48,128]{1,0:T(8,128)S(1)}, u32[]{:S(2)}, u32[]{:S(2)}) collective-permute-start(f32[48,128]{1,0:T(8,128)S(1)} %get-tuple-element.78.low), channel_id=1, source_target_pairs={{1,0},{2,1},{3,2},{4,3},{5,4},{6,5},{7,6},{0,7},{9,8},{10,9},{11,1... | collective-permute-start | bytes 73736 | tf_op jit(solution)/shard_map/ppermute | solution.py:633
  52.4 3.9 %collective-permute-start.10 = (f32[8,128]{1,0:T(8,128)S(1)}, f32[8,128]{1,0:T(8,128)S(1)}, u32[]{:S(2)}, u32[]{:S(2)}) collective-permute-start(f32[8,128]{1,0:T(8,128)S(1)} %slice.10), channel_id=1, source_target_pairs={{4,0},{5,1},{6,2},{7,3},{0,4},{1,5},{2,6},{3,7},{12,8},{13,9},{14,... | collective-permute-start | bytes 12296 | tf_op jit(solution)/shard_map/ppermute | solution.py:633
  56.3 1.3 %collective-permute-start.13 = (f32[32,128]{1,0:T(8,128)S(1)}, f32[32,128]{1,0:T(8,128)S(1)}, u32[]{:S(2)}, u32[]{:S(2)}) collective-permute-start(f32[32,128]{1,0:T(8,128)S(1)} %get-tuple-element.80.small), channel_id=1, source_target_pairs={{128,0},{192,64},{0,128},{64,192},{129,1},{193,65},{1,129},{65,193... | collective-permute-start | bytes 49160 | tf_op jit(solution)/shard_map/ppermute | solution.py:633
  57.8 2.5 %collective-permute-start.12 = (f32[144,128]{1,0:T(8,128)S(1)}, f32[144,128]{1,0:T(8,128)S(1)}, u32[]{:S(2)}, u32[]{:S(2)}) collective-permute-start(f32[144,128]{1,0:T(8,128)S(1)} %get-tuple-element.82), channel_id=1, source_target_pairs={{64,0},{128,64},{192,128},{0,192},{65,1},{129,65},{193,129},{1,193... | collective-permute-start | bytes 221192 | tf_op jit(solution)/shard_map/ppermute | solution.py:633
  60.7 2.0 %collective-permute-done.11.before = f32[144,128]{1,0:T(8,128)S(1)} collective-permute-done((f32[144,128]{1,0:T(8,128)S(1)}, f32[144,128]{1,0:T(8,128)S(1)}, u32[]{:S(2)}, u32[]{:S(2)}) %collective-permute-start.11) | collective-permute-done | bytes 73760 | tf_op jit(solution)/shard_map/ppermute | solution.py:633
  63.5 2.3 %collective-permute-start.14 = (f32[216,128]{1,0:T(8,128)S(1)}, f32[216,128]{1,0:T(8,128)S(1)}, u32[]{:S(2)}, u32[]{:S(2)}) collective-permute-start(f32[216,128]{1,0:T(8,128)S(1)} %get-tuple-element.84.own), channel_id=1, source_target_pairs={{8,0},{16,8},{24,16},{32,24},{40,32},{48,40},{56,48},{0,56},{9,1},... | collective-permute-start | bytes 331784 | tf_op jit(solution)/shard_map/ppermute | solution.py:633
  65.8 2.4 %collective-permute-start.17 = (f32[32,128]{1,0:T(8,128)S(1)}, f32[32,128]{1,0:T(8,128)S(1)}, u32[]{:S(2)}, u32[]{:S(2)}) collective-permute-start(f32[32,128]{1,0:T(8,128)S(1)} %get-tuple-element.90), channel_id=1, source_target_pairs={{48,0},{56,8},{0,16},{8,24},{16,32},{24,40},{32,48},{40,56},{49,1}... | collective-permute-start | bytes 49160 | tf_op jit(solution)/shard_map/ppermute | solution.py:633
  70.5 2.2 %shard_map.59 = (f32[16,16,128]{2,1,0:T(8,128)S(1)}, f32[16,16,128]{2,1,0:T(8,128)S(1)}, f32[48,128]{1,0:T(8,128)S(1)}, f32[48,128]{1,0:T(8,128)S(1)}) custom-call(f32[26,24,256]{2,1,0:T(8,128)S(1)} %get-tuple-element.87.x0, f32[12,24,256]{2,1,0:T(8,128)S(1)} %get-tuple-element.88.x1, f32[216,128]{1,0:T(8,128)S(1)} %get-tuple-element.84.own, ...), custom_call_target="tpu_custom_call" | custom-call | tf_op jit(solution)/shard_map/pallas_call | solution.py:706
  72.7 2.6 %collective-permute-start.19 = (f32[48,128]{1,0:T(8,128)S(1)}, f32[48,128]{1,0:T(8,128)S(1)}, u32[]{:S(2)}, u32[]{:S(2)}) collective-permute-start(f32[48,128]{1,0:T(8,128)S(1)} %get-tuple-element.94), channel_id=1, source_target_pairs={{7,0},{0,1},{1,2},{2,3},{3,4},{4,5},{5,6},{6,7},{15,8},{8,9},{9,10... | collective-permute-start | bytes 73736 | tf_op jit(solution)/shard_map/ppermute | solution.py:633
  76.2 2.3 %collective-permute-done.18.above = f32[48,128]{1,0:T(8,128)S(1)} collective-permute-done((f32[48,128]{1,0:T(8,128)S(1)}, f32[48,128]{1,0:T(8,128)S(1)}, u32[]{:S(2)}, u32[]{:S(2)}) %collective-permute-start.18) | collective-permute-done | bytes 24608 | tf_op jit(solution)/shard_map/ppermute | solution.py:633
  78.5 1.2 collective-permute-start.20
  79.7 2.3 %collective-permute-start.21 = (f32[144,128]{1,0:T(8,128)S(1)}, f32[144,128]{1,0:T(8,128)S(1)}, u32[]{:S(2)}, u32[]{:S(2)}) collective-permute-start(f32[144,128]{1,0:T(8,128)S(1)} %get-tuple-element.97), channel_id=1, source_target_pairs={{64,0},{128,64},{192,128},{0,192},{65,1},{129,65},{193,129},{1,193... | collective-permute-start | bytes 221192 | tf_op jit(solution)/shard_map/ppermute | solution.py:633
  82.1 1.1 collective-permute-start.22
  83.2 3.1 %collective-permute-done.22.across = f32[32,128]{1,0:T(8,128)S(1)} collective-permute-done((f32[32,128]{1,0:T(8,128)S(1)}, f32[32,128]{1,0:T(8,128)S(1)}, u32[]{:S(2)}, u32[]{:S(2)}) %collective-permute-start.22) | collective-permute-done | bytes 16416 | tf_op jit(solution)/shard_map/ppermute | solution.py:633
  87.0 2.1 %collective-permute-start.23 = (f32[216,128]{1,0:T(8,128)S(1)}, f32[216,128]{1,0:T(8,128)S(1)}, u32[]{:S(2)}, u32[]{:S(2)}) collective-permute-start(f32[216,128]{1,0:T(8,128)S(1)} %get-tuple-element.99.own), channel_id=1, source_target_pairs={{8,0},{16,8},{24,16},{32,24},{40,32},{48,40},{56,48},{0,56},{9,1},... | collective-permute-start | bytes 331784 | tf_op jit(solution)/shard_map/ppermute | solution.py:633
  89.4 2.1 %collective-permute-start.26 = (f32[32,128]{1,0:T(8,128)S(1)}, f32[32,128]{1,0:T(8,128)S(1)}, u32[]{:S(2)}, u32[]{:S(2)}) collective-permute-start(f32[32,128]{1,0:T(8,128)S(1)} %get-tuple-element.104), channel_id=1, source_target_pairs={{48,0},{56,8},{0,16},{8,24},{16,32},{24,40},{32,48},{40,56},{49,1}... | collective-permute-start | bytes 49160 | tf_op jit(solution)/shard_map/ppermute | solution.py:633
  93.0 1.2 %collective-permute-done.26.down2 = f32[32,128]{1,0:T(8,128)S(1)} collective-permute-done((f32[32,128]{1,0:T(8,128)S(1)}, f32[32,128]{1,0:T(8,128)S(1)}, u32[]{:S(2)}, u32[]{:S(2)}) %collective-permute-start.26) | collective-permute-done | bytes 16416 | tf_op jit(solution)/shard_map/ppermute | solution.py:633
  94.3 1.7 %shard_map.63 = (f32[16,16,128]{2,1,0:T(8,128)S(1)}, f32[16,16,128]{2,1,0:T(8,128)S(1)}, f32[16,16,128]{2,1,0:T(8,128)S(1)}, f32[16,16,128]{2,1,0:T(8,128)S(1)},...) custom-call(f32[26,24,256]{2,1,0:T(8,128)S(1)} %get-tuple-element.101.x0, ...), custom_call_target="tpu_custom_call" | custom-call | tf_op jit(solution)/shard_map/pallas_call | solution.py:711
  96.1 25.0 %all_to_all.11 = f32[256,1,128]{2,1,0:T(1,128)S(1)} all-to-all(f32[256,1,128]{2,1,0:T(1,128)S(1)} %broadcast_in_dim.10), channel_id=1, replica_groups=mesh['gx'=4,'gy'=8,'gz'=8] {'gx','gy','gz'}, dimensions={0} | all-to-all | bytes 262144 | tf_op jit(solution)/shard_map/all_to_all | solution.py:669
  (52 shorter events, 10.9 us)
Async XLA Ops:
  2.6 5.2 %collective-permute-start = (f32[2,6,16,128]{3,2,1,0:T(8,128)}, f32[2,6,16,128]{3,2,1,0:T(8,128)S(1)}, u32[]{:S(2)}, u32[]{:S(2)}) collective-permute-start(f32[2,6,16,128]{3,2,1,0:T(8,128)} %get-tuple-element.59), channel_id=1, source_target_pairs={{1,0},{2,1},{3,2},{4,3},{5,4},{6,5},{7,6},{0,7},{9,8},{10,9},{11,1... | collective-permute-start | bytes 294920 | tf_op jit(solution)/shard_map/ppermute | solution.py:633
  5.8 2.0 %collective-permute-start.1 = (f32[2,6,16,128]{3,2,1,0:T(8,128)}, f32[2,6,16,128]{3,2,1,0:T(8,128)S(1)}, u32[]{:S(2)}, u32[]{:S(2)}) collective-permute-start(f32[2,6,16,128]{3,2,1,0:T(8,128)} %get-tuple-element.60), channel_id=1, source_target_pairs={{7,0},{0,1},{1,2},{2,3},{3,4},{4,5},{5,6},{6,7},{15,8},{8,9},{9,10... | collective-permute-start | bytes 294920 | tf_op jit(solution)/shard_map/ppermute | solution.py:633
  7.8 1.0 copy-start
  8.9 8.3 %collective-permute-start.2 = (f32[2,7,16,128]{3,2,1,0:T(8,128)S(1)}, f32[2,7,16,128]{3,2,1,0:T(8,128)S(1)}, u32[]{:S(2)}, u32[]{:S(2)}) collective-permute-start(f32[2,7,16,128]{3,2,1,0:T(8,128)S(1)} %get-tuple-element.62), channel_id=1, source_target_pairs={{192,0},{0,64},{64,128},{128,192},{193,1},{1,65},{65,129},{129,193... | collective-permute-start | bytes 344072 | tf_op jit(solution)/shard_map/ppermute | solution.py:633
  10.1 7.1 %collective-permute-start.3 = (f32[2,7,16,128]{3,2,1,0:T(8,128)S(1)}, f32[2,7,16,128]{3,2,1,0:T(8,128)S(1)}, u32[]{:S(2)}, u32[]{:S(2)}) collective-permute-start(f32[2,7,16,128]{3,2,1,0:T(8,128)S(1)} %get-tuple-element.63), channel_id=1, source_target_pairs={{64,0},{128,64},{192,128},{0,192},{65,1},{129,65},{193,129},{1,193... | collective-permute-start | bytes 344072 | tf_op jit(solution)/shard_map/ppermute | solution.py:633
  11.6 8.9 %collective-permute-start.4 = (f32[240,128]{1,0:T(8,128)S(1)}, f32[240,128]{1,0:T(8,128)S(1)}, u32[]{:S(2)}, u32[]{:S(2)}) collective-permute-start(f32[240,128]{1,0:T(8,128)S(1)} %get-tuple-element.65), channel_id=1, source_target_pairs={{8,0},{16,8},{24,16},{32,24},{40,32},{48,40},{56,48},{0,56},{9,1},... | collective-permute-start | bytes 368648 | tf_op jit(solution)/shard_map/ppermute | solution.py:633
  17.2 4.9 %collective-permute-start.5 = (f32[240,128]{1,0:T(8,128)S(1)}, f32[240,128]{1,0:T(8,128)S(1)}, u32[]{:S(2)}, u32[]{:S(2)}) collective-permute-start(f32[240,128]{1,0:T(8,128)S(1)} %get-tuple-element.66), channel_id=1, source_target_pairs={{56,0},{0,8},{8,16},{16,24},{24,32},{32,40},{40,48},{48,56},{57,1}... | collective-permute-start | bytes 368648 | tf_op jit(solution)/shard_map/ppermute | solution.py:633
  17.3 4.9 %collective-permute-start.6 = (f32[160,128]{1,0:T(8,128)S(1)}, f32[160,128]{1,0:T(8,128)S(1)}, u32[]{:S(2)}, u32[]{:S(2)}) collective-permute-start(f32[160,128]{1,0:T(8,128)S(1)} %get-tuple-element.67), channel_id=1, source_target_pairs={{8,0},{16,8},{24,16},{32,24},{40,32},{48,40},{56,48},{0,56},{9,1},... | collective-permute-start | bytes 245768 | tf_op jit(solution)/shard_map/ppermute | solution.py:633
  20.0 4.5 %collective-permute-start.7 = (f32[160,128]{1,0:T(8,128)S(1)}, f32[160,128]{1,0:T(8,128)S(1)}, u32[]{:S(2)}, u32[]{:S(2)}) collective-permute-start(f32[160,128]{1,0:T(8,128)S(1)} %get-tuple-element.68), channel_id=1, source_target_pairs={{56,0},{0,8},{8,16},{16,24},{24,32},{32,40},{40,48},{48,56},{57,1}... | collective-permute-start | bytes 245768 | tf_op jit(solution)/shard_map/ppermute | solution.py:633
  26.3 14.9 %copy-start.1 = (f32[2,16,16,128]{3,2,1,0:T(8,128)S(1)}, f32[2,16,16,128]{3,2,1,0:T(8,128)}, u32[]{:S(2)}) copy-start(f32[2,16,16,128]{3,2,1,0:T(8,128)} %get-tuple-element.58.own.both) | copy-start | bytes 786436
  43.3 8.6 %collective-permute-start.9 = (f32[48,128]{1,0:T(8,128)S(1)}, f32[48,128]{1,0:T(8,128)S(1)}, u32[]{:S(2)}, u32[]{:S(2)}) collective-permute-start(f32[48,128]{1,0:T(8,128)S(1)} %get-tuple-element.79), channel_id=1, source_target_pairs={{7,0},{0,1},{1,2},{2,3},{3,4},{4,5},{5,6},{6,7},{15,8},{8,9},{9,10... | collective-permute-start | bytes 73736 | tf_op jit(solution)/shard_map/ppermute | solution.py:633
  49.1 3.3 %collective-permute-start.8 = (f32[48,128]{1,0:T(8,128)S(1)}, f32[48,128]{1,0:T(8,128)S(1)}, u32[]{:S(2)}, u32[]{:S(2)}) collective-permute-start(f32[48,128]{1,0:T(8,128)S(1)} %get-tuple-element.78.low), channel_id=1, source_target_pairs={{1,0},{2,1},{3,2},{4,3},{5,4},{6,5},{7,6},{0,7},{9,8},{10,9},{11,1... | collective-permute-start | bytes 73736 | tf_op jit(solution)/shard_map/ppermute | solution.py:633
  52.4 7.9 %collective-permute-start.10 = (f32[8,128]{1,0:T(8,128)S(1)}, f32[8,128]{1,0:T(8,128)S(1)}, u32[]{:S(2)}, u32[]{:S(2)}) collective-permute-start(f32[8,128]{1,0:T(8,128)S(1)} %slice.10), channel_id=1, source_target_pairs={{4,0},{5,1},{6,2},{7,3},{0,4},{1,5},{2,6},{3,7},{12,8},{13,9},{14,... | collective-permute-start | bytes 12296 | tf_op jit(solution)/shard_map/ppermute | solution.py:633
  56.3 4.4 %collective-permute-start.13 = (f32[32,128]{1,0:T(8,128)S(1)}, f32[32,128]{1,0:T(8,128)S(1)}, u32[]{:S(2)}, u32[]{:S(2)}) collective-permute-start(f32[32,128]{1,0:T(8,128)S(1)} %get-tuple-element.80.small), channel_id=1, source_target_pairs={{128,0},{192,64},{0,128},{64,192},{129,1},{193,65},{1,129},{65,193... | collective-permute-start | bytes 49160 | tf_op jit(solution)/shard_map/ppermute | solution.py:633
  57.6 5.1 %collective-permute-start.11 = (f32[144,128]{1,0:T(8,128)S(1)}, f32[144,128]{1,0:T(8,128)S(1)}, u32[]{:S(2)}, u32[]{:S(2)}) collective-permute-start(f32[144,128]{1,0:T(8,128)S(1)} %get-tuple-element.81), channel_id=1, source_target_pairs={{192,0},{0,64},{64,128},{128,192},{193,1},{1,65},{65,129},{129,193... | collective-permute-start | bytes 221192 | tf_op jit(solution)/shard_map/ppermute | solution.py:633
  57.8 5.0 %collective-permute-start.12 = (f32[144,128]{1,0:T(8,128)S(1)}, f32[144,128]{1,0:T(8,128)S(1)}, u32[]{:S(2)}, u32[]{:S(2)}) collective-permute-start(f32[144,128]{1,0:T(8,128)S(1)} %get-tuple-element.82), channel_id=1, source_target_pairs={{64,0},{128,64},{192,128},{0,192},{65,1},{129,65},{193,129},{1,193... | collective-permute-start | bytes 221192 | tf_op jit(solution)/shard_map/ppermute | solution.py:633
  62.8 5.3 %collective-permute-start.15 = (f32[216,128]{1,0:T(8,128)S(1)}, f32[216,128]{1,0:T(8,128)S(1)}, u32[]{:S(2)}, u32[]{:S(2)}) collective-permute-start(f32[216,128]{1,0:T(8,128)S(1)} %get-tuple-element.85), channel_id=1, source_target_pairs={{56,0},{0,8},{8,16},{16,24},{24,32},{32,40},{40,48},{48,56},{57,1}... | collective-permute-start | bytes 331784 | tf_op jit(solution)/shard_map/ppermute | solution.py:633
  63.5 4.7 %collective-permute-start.14 = (f32[216,128]{1,0:T(8,128)S(1)}, f32[216,128]{1,0:T(8,128)S(1)}, u32[]{:S(2)}, u32[]{:S(2)}) collective-permute-start(f32[216,128]{1,0:T(8,128)S(1)} %get-tuple-element.84.own), channel_id=1, source_target_pairs={{8,0},{16,8},{24,16},{32,24},{40,32},{48,40},{56,48},{0,56},{9,1},... | collective-permute-start | bytes 331784 | tf_op jit(solution)/shard_map/ppermute | solution.py:633
  65.8 3.7 %collective-permute-start.16 = (f32[32,128]{1,0:T(8,128)S(1)}, f32[32,128]{1,0:T(8,128)S(1)}, u32[]{:S(2)}, u32[]{:S(2)}) collective-permute-start(f32[32,128]{1,0:T(8,128)S(1)} %get-tuple-element.89), channel_id=1, source_target_pairs={{16,0},{24,8},{32,16},{40,24},{48,32},{56,40},{0,48},{8,56},{17,1}... | collective-permute-start | bytes 49160 | tf_op jit(solution)/shard_map/ppermute | solution.py:633
  65.8 4.7 %collective-permute-start.17 = (f32[32,128]{1,0:T(8,128)S(1)}, f32[32,128]{1,0:T(8,128)S(1)}, u32[]{:S(2)}, u32[]{:S(2)}) collective-permute-start(f32[32,128]{1,0:T(8,128)S(1)} %get-tuple-element.90), channel_id=1, source_target_pairs={{48,0},{56,8},{0,16},{8,24},{16,32},{24,40},{32,48},{40,56},{49,1}... | collective-permute-start | bytes 49160 | tf_op jit(solution)/shard_map/ppermute | solution.py:633
  72.7 3.5 %collective-permute-start.19 = (f32[48,128]{1,0:T(8,128)S(1)}, f32[48,128]{1,0:T(8,128)S(1)}, u32[]{:S(2)}, u32[]{:S(2)}) collective-permute-start(f32[48,128]{1,0:T(8,128)S(1)} %get-tuple-element.94), channel_id=1, source_target_pairs={{7,0},{0,1},{1,2},{2,3},{3,4},{4,5},{5,6},{6,7},{15,8},{8,9},{9,10... | collective-permute-start | bytes 73736 | tf_op jit(solution)/shard_map/ppermute | solution.py:633
  75.3 3.3 %collective-permute-start.18 = (f32[48,128]{1,0:T(8,128)S(1)}, f32[48,128]{1,0:T(8,128)S(1)}, u32[]{:S(2)}, u32[]{:S(2)}) collective-permute-start(f32[48,128]{1,0:T(8,128)S(1)} %get-tuple-element.93.low), channel_id=1, source_target_pairs={{1,0},{2,1},{3,2},{4,3},{5,4},{6,5},{7,6},{0,7},{9,8},{10,9},{11,1... | collective-permute-start | bytes 73736 | tf_op jit(solution)/shard_map/ppermute | solution.py:633
  78.5 7.8 %collective-permute-start.20 = (f32[144,128]{1,0:T(8,128)S(1)}, f32[144,128]{1,0:T(8,128)S(1)}, u32[]{:S(2)}, u32[]{:S(2)}) collective-permute-start(f32[144,128]{1,0:T(8,128)S(1)} %get-tuple-element.96), channel_id=1, source_target_pairs={{192,0},{0,64},{64,128},{128,192},{193,1},{1,65},{65,129},{129,193... | collective-permute-start | bytes 221192 | tf_op jit(solution)/shard_map/ppermute | solution.py:633
  79.7 6.6 %collective-permute-start.21 = (f32[144,128]{1,0:T(8,128)S(1)}, f32[144,128]{1,0:T(8,128)S(1)}, u32[]{:S(2)}, u32[]{:S(2)}) collective-permute-start(f32[144,128]{1,0:T(8,128)S(1)} %get-tuple-element.97), channel_id=1, source_target_pairs={{64,0},{128,64},{192,128},{0,192},{65,1},{129,65},{193,129},{1,193... | collective-permute-start | bytes 221192 | tf_op jit(solution)/shard_map/ppermute | solution.py:633
  82.1 4.2 %collective-permute-start.22 = (f32[32,128]{1,0:T(8,128)S(1)}, f32[32,128]{1,0:T(8,128)S(1)}, u32[]{:S(2)}, u32[]{:S(2)}) collective-permute-start(f32[32,128]{1,0:T(8,128)S(1)} %get-tuple-element.95.small), channel_id=1, source_target_pairs={{128,0},{192,64},{0,128},{64,192},{129,1},{193,65},{1,129},{65,193... | collective-permute-start | bytes 49160 | tf_op jit(solution)/shard_map/ppermute | solution.py:633
  86.4 5.1 %collective-permute-start.24 = (f32[216,128]{1,0:T(8,128)S(1)}, f32[216,128]{1,0:T(8,128)S(1)}, u32[]{:S(2)}, u32[]{:S(2)}) collective-permute-start(f32[216,128]{1,0:T(8,128)S(1)} %get-tuple-element.100), channel_id=1, source_target_pairs={{56,0},{0,8},{8,16},{16,24},{24,32},{32,40},{40,48},{48,56},{57,1}... | collective-permute-start | bytes 331784 | tf_op jit(solution)/shard_map/ppermute | solution.py:633
  87.0 4.5 %collective-permute-start.23 = (f32[216,128]{1,0:T(8,128)S(1)}, f32[216,128]{1,0:T(8,128)S(1)}, u32[]{:S(2)}, u32[]{:S(2)}) collective-permute-start(f32[216,128]{1,0:T(8,128)S(1)} %get-tuple-element.99.own), channel_id=1, source_target_pairs={{8,0},{16,8},{24,16},{32,24},{40,32},{48,40},{56,48},{0,56},{9,1},... | collective-permute-start | bytes 331784 | tf_op jit(solution)/shard_map/ppermute | solution.py:633
  89.2 3.9 %collective-permute-start.25 = (f32[32,128]{1,0:T(8,128)S(1)}, f32[32,128]{1,0:T(8,128)S(1)}, u32[]{:S(2)}, u32[]{:S(2)}) collective-permute-start(f32[32,128]{1,0:T(8,128)S(1)} %get-tuple-element.103), channel_id=1, source_target_pairs={{16,0},{24,8},{32,16},{40,24},{48,32},{56,40},{0,48},{8,56},{17,1}... | collective-permute-start | bytes 49160 | tf_op jit(solution)/shard_map/ppermute | solution.py:633
  89.4 4.9 %collective-permute-start.26 = (f32[32,128]{1,0:T(8,128)S(1)}, f32[32,128]{1,0:T(8,128)S(1)}, u32[]{:S(2)}, u32[]{:S(2)}) collective-permute-start(f32[32,128]{1,0:T(8,128)S(1)} %get-tuple-element.104), channel_id=1, source_target_pairs={{48,0},{56,8},{0,16},{8,24},{16,32},{24,40},{32,48},{40,56},{49,1}... | collective-permute-start | bytes 49160 | tf_op jit(solution)/shard_map/ppermute | solution.py:633
